TPU v7x, 32 devices: a whole 2x2x4 slice. The times are simulated.
32 devices in a mesh: section: 4 (over z), tile: 4 (over x, core), rep: 2 (over y).
Axes of the slice: x: 2, y: 2, z: 4, core: 2. Of those that a mesh axis runs over, the one named last changes fastest.
Arguments:
- phase_shift: float32 [4, 4, 384, 384], P('section', 'tile'), may hold values from -3.140625 to 3.140625
- absorption: float32 [4, 4, 384, 384], P('section', 'tile'), may hold values from 0 to 0.5
- probe_wave: float32 [2, 256, 256], replicated, may hold values from -6 to 6
- positions: int32 [4, 2, 1, 2], P('tile', 'rep'), may hold values from 0 to 384
- counts: int32 [4, 2, 1, 256, 256], P('tile', 'rep'), may hold values from 0 to 7
Outputs:
- phase_gradient: float32 [4, 4, 384, 384], P('section', 'tile', 'rep')
- absorption_gradient: float32 [4, 4, 384, 384], P('section', 'tile', 'rep')
All inputs are finite; a program needn't handle non-finite values.
Results may differ from a plain program's by a relative error of at most 0.00027.
Values sent between devices are 32-bit elements; how exact they have to be, the bound alone decides.
No kernel may reach another device: no remote copies, remote signals or barrier semaphores. Data moves between devices by JAX's collectives and lax.ppermute only.
A program may use at most 64 MiB of HBM per device.

v0:
```python
import math

import jax
import jax.numpy as jnp
from jax import lax
from jax.sharding import PartitionSpec as P

HALO = 128


dead_time = 0.1
background = 0.1
loss_weight = 0.1
fresnel = 0.5
highest = lax.Precision.HIGHEST


def from_behind(value, axis, by):
    peers = lax.axis_size(axis)
    pairs = [(i, i + by) for i in range(peers) if 0 <= i + by < peers]
    return lax.ppermute(value, axis, pairs)


def left_product(matrix, frames):
    return jnp.einsum(
        "mk,bkn->bmn", matrix, frames, precision=highest, preferred_element_type=jnp.float32
    )


def right_product(frames, matrix):
    return jnp.einsum(
        "bmk,kn->bmn", frames, matrix, precision=highest, preferred_element_type=jnp.float32
    )


def sandwich(table_re, table_im, wave_re, wave_im):
    first_re = left_product(table_re, wave_re) - left_product(table_im, wave_im)
    first_im = left_product(table_re, wave_im) + left_product(table_im, wave_re)
    out_re = right_product(first_re, table_re) - right_product(first_im, table_im)
    out_im = right_product(first_re, table_im) + right_product(first_im, table_re)
    return (out_re, out_im)


def dft_tables(length):
    indices = jnp.arange(length, dtype=jnp.int32)
    product = indices[:, None] * indices[None, :] % length
    angles = product.astype(jnp.float32) * (2.0 * math.pi / length)
    cosine_table = jnp.cos(angles)
    sine_table = jnp.sin(angles)
    shifted = jnp.where(indices < length // 2, indices, indices - length).astype(jnp.float32)
    kernel = math.pi * fresnel * shifted * shifted / length

    def spread(weights):
        first_part = jnp.dot(cosine_table * weights[None, :], cosine_table, precision=highest)
        second_part = jnp.dot(sine_table * weights[None, :], sine_table, precision=highest)
        return (first_part + second_part) / length

    near_table = (spread(jnp.cos(kernel)), spread(jnp.sin(kernel)))
    norm_scale = 1.0 / math.sqrt(length)
    far_table = (cosine_table * norm_scale, -sine_table * norm_scale)
    return (near_table, far_table)


def likelihood_seed(far_re, far_im, observed):
    intensity = far_re * far_re + far_im * far_im
    shifted_total = intensity + background
    denominator = 1.0 + dead_time * shifted_total
    model_rate = shifted_total / denominator
    slope_term = loss_weight * (1.0 - observed / model_rate) / (denominator * denominator)
    return (2.0 * slope_term * far_re, 2.0 * slope_term * far_im)


def shards(phase_shift, absorption, probe_wave, positions, counts):
    slices_here = phase_shift.shape[0]
    tile_width = phase_shift.shape[2]
    frame_width = probe_wave.shape[1]
    frames_here = positions.shape[2]
    sections = lax.axis_size("section")
    tile_count = lax.axis_size("tile")
    grid_side = math.isqrt(tile_count)
    margin = HALO
    extent = tile_width + 2 * margin
    section_index = lax.axis_index("section")
    column = lax.axis_index("tile") % grid_side
    has_left = (column > 0).astype(jnp.float32)
    has_right = (column < grid_side - 1).astype(jnp.float32)
    is_last = section_index == sections - 1
    own_block = jnp.stack([phase_shift[:, 0], absorption[:, 0]])

    def fetch_rim(rim_strip, offset):
        return from_behind(rim_strip, "tile", offset)

    upper_rim = fetch_rim(own_block[:, :, tile_width - margin :, :], grid_side)
    lower_rim = fetch_rim(own_block[:, :, :margin, :], -grid_side)
    tall_block = jnp.concatenate([upper_rim, own_block, lower_rim], axis=2)
    left_rim = fetch_rim(tall_block[:, :, :, tile_width - margin :], 1) * has_left
    right_rim = fetch_rim(tall_block[:, :, :, :margin], -1) * has_right
    extended = jnp.concatenate([left_rim, tall_block, right_rim], axis=3)
    damping = jnp.exp(-extended[1])
    trans_re = damping * jnp.cos(extended[0])
    trans_im = damping * jnp.sin(extended[0])
    near_table, far_table = dft_tables(frame_width)
    last_re = jnp.where(is_last, far_table[0], near_table[0])
    last_im = jnp.where(is_last, far_table[1], near_table[1])

    def table_for():
        return (last_re, last_im)

    def windows(source_plane, corners):

        def cut_window(corner):
            return lax.dynamic_slice(
                source_plane, (corner[0], corner[1]), (frame_width, frame_width)
            )

        return jax.vmap(cut_window)(corners)

    def forward_batch(wave_re, wave_im, corners):
        object_re = windows(trans_re[0], corners)
        object_im = windows(trans_im[0], corners)
        exit_re = object_re * wave_re - object_im * wave_im
        exit_im = object_re * wave_im + object_im * wave_re
        exit_waves = [jnp.stack([exit_re, exit_im], axis=1)]
        table_re, table_im = table_for()
        wave_re, wave_im = sandwich(table_re, table_im, exit_re, exit_im)
        return (wave_re, wave_im, jnp.stack(exit_waves, axis=1))

    groups = frames_here // frames_here
    step_count = groups + sections - 1
    probe_block = probe_wave[:, None]
    corners_all = positions[0, 0]
    observed_all = counts[0, 0].astype(jnp.float32)
    saved_exits = jnp.zeros((frames_here, slices_here, 2, frame_width, frame_width), jnp.float32)
    seed_waves = jnp.zeros((frames_here, 2, frame_width, frame_width), jnp.float32)

    def forward_work(step_no, incoming, saved_now, seeds_now):
        group_no = step_no - section_index
        is_active = (group_no >= 0) & (group_no < groups)
        start_at = jnp.clip(group_no, 0, groups - 1) * frames_here
        wave_in = jnp.where(section_index == 0, probe_block, incoming)

        def forward_active(buffers):
            out_re, out_im, exit_waves = forward_batch(wave_in[0], wave_in[1], corners_all)
            seed_re, seed_im = likelihood_seed(out_re, out_im, observed_all)
            kept_exits = lax.dynamic_update_slice_in_dim(buffers[0], exit_waves, start_at, 0)
            kept_seeds = jnp.stack([seed_re, seed_im], axis=1)
            return (jnp.stack([out_re, out_im]), kept_exits, kept_seeds)

        def forward_resting(buffers):
            return (jnp.zeros_like(probe_block), buffers[0], buffers[1])

        return lax.cond(is_active, forward_active, forward_resting, (saved_now, seeds_now))

    def forward_step(step_no, loop_state):
        incoming, saved_now, seeds_now = loop_state
        outgoing, saved_now, seeds_now = forward_work(step_no, incoming, saved_now, seeds_now)
        incoming = from_behind(outgoing, "section", 1)
        return (incoming, saved_now, seeds_now)

    loop_state = lax.fori_loop(
        0, step_count - 1, forward_step, (jnp.zeros_like(probe_block), saved_exits, seed_waves)
    )
    unused_wave, saved_exits, seed_waves = forward_work(
        step_count - 1, loop_state[0], loop_state[1], loop_state[2]
    )
    grad_extended = jnp.zeros((2, slices_here, extent, extent), jnp.float32)

    def backward_work(step_no, incoming, grad_now):
        group_no = step_no - (sections - 1 - section_index)
        is_active = (group_no >= 0) & (group_no < groups)
        start_at = jnp.clip(group_no, 0, groups - 1) * frames_here

        def backward_active(grad_state):
            grad_re = jnp.where(is_last, seed_waves[:, 0], incoming[0])
            grad_im = jnp.where(is_last, seed_waves[:, 1], incoming[1])
            for slice_no in reversed(range(slices_here)):
                table_re, table_im = table_for()
                back_re, back_im = sandwich(table_re, -table_im, grad_re, grad_im)
                exit_re = saved_exits[:, slice_no, 0]
                exit_im = saved_exits[:, slice_no, 1]
                phase_term = back_im * exit_re - back_re * exit_im
                absorb_term = -(back_re * exit_re + back_im * exit_im)
                grad_terms = jnp.stack([phase_term, absorb_term], axis=1)
                corner = corners_all[0]
                current = lax.dynamic_slice(
                    grad_state,
                    (0, slice_no, corner[0], corner[1]),
                    (2, 1, frame_width, frame_width),
                )
                grad_state = lax.dynamic_update_slice(
                    grad_state,
                    current + grad_terms[0][:, None],
                    (0, slice_no, corner[0], corner[1]),
                )
                object_re = windows(trans_re[slice_no], corners_all)
                object_im = windows(trans_im[slice_no], corners_all)
                grad_re = object_re * back_re + object_im * back_im
                grad_im = object_re * back_im - object_im * back_re
            return (jnp.stack([grad_re, grad_im]), grad_state)

        def backward_resting(grad_state):
            return (jnp.zeros_like(probe_block), grad_state)

        return lax.cond(is_active, backward_active, backward_resting, grad_now)

    def backward_step(step_no, loop_state):
        incoming, grad_now = loop_state
        outgoing, grad_now = backward_work(step_no, incoming, grad_now)
        incoming = from_behind(outgoing, "section", -1)
        return (incoming, grad_now)

    loop_state = lax.fori_loop(
        0, step_count - 1, backward_step, (jnp.zeros_like(probe_block), grad_extended)
    )
    unused_grad, grad_extended = backward_work(step_count - 1, loop_state[0], loop_state[1])

    def give_back(rim_strip, offset):
        return from_behind(rim_strip, "tile", offset)

    from_below = give_back(grad_extended[:, :, :margin, :], -grid_side)
    from_above = give_back(grad_extended[:, :, tile_width + margin :, :], grid_side)
    body_rows = grad_extended[:, :, margin : margin + tile_width, :]
    body_rows = body_rows.at[:, :, :margin].add(from_above)
    body_rows = body_rows.at[:, :, tile_width - margin :].add(from_below)
    from_right = give_back(body_rows[..., :margin], -1) * has_right
    from_left = give_back(body_rows[..., tile_width + margin :], 1) * has_left
    middle = body_rows[..., margin : margin + tile_width]
    middle = middle.at[..., :margin].add(from_left)
    middle = middle.at[..., tile_width - margin :].add(from_right)
    shares = lax.psum_scatter(middle, "rep", scatter_dimension=2, tiled=True)
    return (shares[0][:, None], shares[1][:, None])


def solution(mesh):
    in_specs = (
        P("section", "tile", None, None),
        P("section", "tile", None, None),
        P(),
        P("tile", "rep", None, None),
        P("tile", "rep", None, None, None),
    )
    out_specs = (P("section", "tile", "rep", None), P("section", "tile", "rep", None))
    return jax.shard_map(shards, mesh=mesh, in_specs=in_specs, out_specs=out_specs, check_vma=False)
```

profile of v0, /device:TPU:13, one launch (start us, length us, event | category | flops | bytes accessed | tf_op | source)
XLA Modules:
  0.0 312.9 jit_solution(15010245331514969799)
XLA Ops:
  7.2 1.1 constant_dynamic-update-slice_fusion.1
  8.3 1.1 constant_dynamic-update-slice_fusion
  10.2 3.1 collective-permute-start.2
  13.4 1.3 collective-permute-start.3
  14.7 1.4 fusion.74
  16.2 1.4 fusion.68
  17.5 3.9 %collective-permute-done.2 = f32[2,1,128,384]{3,2,1,0:T(8,128)S(1)} collective-permute-done((f32[2,1,128,384]{3,2,1,0:T(8,128)}, f32[2,1,128,384]{3,2,1,0:T(8,128)S(1)}, u32[]{:S(2)}, u32[]{:S(2)}) %collective-permute-start.2) | collective-permute-done | bytes 393248 | tf_op jit(solution)/shard_map/ppermute | solution.py:21
  21.4 3.5 %collective-permute-done.3 = f32[2,1,128,384]{3,2,1,0:T(8,128)S(1)} collective-permute-done((f32[2,1,128,384]{3,2,1,0:T(8,128)S(1)}, f32[2,1,128,384]{3,2,1,0:T(8,128)S(1)}, u32[]{:S(2)}, u32[]{:S(2)}) %collective-permute-start.3) | collective-permute-done | bytes 393248 | tf_op jit(solution)/shard_map/ppermute | solution.py:21
  25.7 2.9 collective-permute-start.4
  28.6 2.4 collective-permute-start.5
  31.0 1.4 fusion.77
  32.4 1.4 fusion.67
  33.8 2.3 collective-permute-done.4
  36.1 4.4 %collective-permute-done.5 = f32[2,1,640,128]{3,2,1,0:T(8,128)S(1)} collective-permute-done((f32[2,1,640,128]{3,2,1,0:T(8,128)S(1)}, f32[2,1,640,128]{3,2,1,0:T(8,128)S(1)}, u32[]{:S(2)}, u32[]{:S(2)}) %collective-permute-start.5) | collective-permute-done | bytes 655392 | tf_op jit(solution)/shard_map/ppermute | solution.py:21
  40.8 6.7 %multiply_bitcast_fusion = (f32[1,640,640]{2,1,0:T(8,128)S(1)}, f32[1,640,640]{2,1,0:T(8,128)}) fusion(f32[2,1,640,640]{3,2,1,0:T(8,128)S(1)} %pad_maximum_fusion.4), kind=kLoop, calls=%fused_computation.135 | loop fusion | flops 1228800 | bytes 6553600 | tf_op jit(solution)/shard_map/mul | solution.py:101
  47.6 0.8 broadcast_in_dim.47
  48.5 69.7 %while.51 = (s32[]{:T(128)}, f32[2,1,256,256]{3,2,1,0:T(8,128)S(1)}, f32[1,1,2,256,256]{4,3,2,1,0:T(8,128)}, f32[1,2,256,256]{3,2,1,0:T(8,128)S(1)}, s32[]{:T(12...) while((s32[]{:T(128)}, ...), condition=%wide.region_3.4_spmd, body=%wide.region_0.3_spmd.sunk | while | flops 1613168640 | bytes 18612656 | solution.py:160
  48.5 0.8 conditional.8
  48.5 0.8 broadcast.181
  49.3 3.2 %collective-permute-start = (f32[2,1,256,256]{3,2,1,0:T(8,128)}, f32[2,1,256,256]{3,2,1,0:T(8,128)S(1)}, u32[]{:S(2)}, u32[]{:S(2)}) collective-permute-start(f32[2,1,256,256]{3,2,1,0:T(8,128)} %get-tuple-element.1097), channel_id=1, source_target_pairs={{0,8},{8,16},{16,24},{1,9},{9,17},{17,25},{2,10},{10,18},{18,26},{... | collective-permute-start | bytes 1572872 | tf_op jit(solution)/shard_map/while/body/eval_jaxpr/ppermute | solution.py:21
  52.5 18.7 %collective-permute-done = f32[2,1,256,256]{3,2,1,0:T(8,128)S(1)} collective-permute-done((f32[2,1,256,256]{3,2,1,0:T(8,128)}, f32[2,1,256,256]{3,2,1,0:T(8,128)S(1)}, u32[]{:S(2)}, u32[]{:S(2)}) %collective-permute-start) | collective-permute-done | bytes 524320 | tf_op jit(solution)/shard_map/while/body/eval_jaxpr/ppermute | solution.py:21
  71.2 13.5 %conditional.8 = (f32[2,1,256,256]{3,2,1,0:T(8,128)}, f32[1,1,2,256,256]{4,3,2,1,0:T(8,128)}, f32[1,2,256,256]{3,2,1,0:T(8,128)S(1)}) conditional(s32[]{:T(128)} %convert_element_type.122, (f32[1,1,2,256,256]{4,3,2,1,0:T(8,128)}, f32[1,2,256,256]{3,2,1,0:T(8,128)S(1)}) %tuple.178, (f32[1,640,640]{2,1,0:T(8,128)}, s32[1,2]{1,0:T(1,128)S(1)}, ...), branch_computations={%region_1.1_spmd, %region_2.2_spmd} | conditional | flops 1613168640 | bytes 16515197 | solution.py:152
  75.5 1.2 fusion.29
  76.7 1.2 fusion.26
  77.9 0.8 maximum_bitcast_fusion.1
  83.8 0.8 pad_maximum_fusion
  84.7 1.9 collective-permute-start
  86.6 8.7 %collective-permute-done = f32[2,1,256,256]{3,2,1,0:T(8,128)S(1)} collective-permute-done((f32[2,1,256,256]{3,2,1,0:T(8,128)}, f32[2,1,256,256]{3,2,1,0:T(8,128)S(1)}, u32[]{:S(2)}, u32[]{:S(2)}) %collective-permute-start) | collective-permute-done | bytes 524320 | tf_op jit(solution)/shard_map/while/body/eval_jaxpr/ppermute | solution.py:21
  95.3 0.8 conditional.8
  95.3 0.8 broadcast.181
  96.1 14.3 %collective-permute-start = (f32[2,1,256,256]{3,2,1,0:T(8,128)}, f32[2,1,256,256]{3,2,1,0:T(8,128)S(1)}, u32[]{:S(2)}, u32[]{:S(2)}) collective-permute-start(f32[2,1,256,256]{3,2,1,0:T(8,128)} %get-tuple-element.1097), channel_id=1, source_target_pairs={{0,8},{8,16},{16,24},{1,9},{9,17},{17,25},{2,10},{10,18},{18,26},{... | collective-permute-start | bytes 1572872 | tf_op jit(solution)/shard_map/while/body/eval_jaxpr/ppermute | solution.py:21
  110.4 7.8 %collective-permute-done = f32[2,1,256,256]{3,2,1,0:T(8,128)S(1)} collective-permute-done((f32[2,1,256,256]{3,2,1,0:T(8,128)}, f32[2,1,256,256]{3,2,1,0:T(8,128)S(1)}, u32[]{:S(2)}, u32[]{:S(2)}) %collective-permute-start) | collective-permute-done | bytes 524320 | tf_op jit(solution)/shard_map/while/body/eval_jaxpr/ppermute | solution.py:21
  118.2 1.9 broadcast_in_dim.46
  120.1 115.6 %while.52 = (s32[]{:T(128)}, f32[2,1,256,256]{3,2,1,0:T(8,128)S(1)}, f32[2,1,640,640]{3,2,0,1:T(8,128)}, s32[]{:T(128)}, f32[1,640,640]{2,1,0:T(8,128)}, /*index...) while((s32[]{:T(128)}, ...), condition=%wide.region_9.10_spmd, body=%wide.region_6.9_spmd.sunk | while | flops 1612644352 | bytes 18350624 | solution.py:212
  120.1 0.8 conditional.9
  120.1 0.8 broadcast.192
  120.9 1.9 collective-permute-start.1
  122.9 10.7 %collective-permute-done.1 = f32[2,1,256,256]{3,2,1,0:T(8,128)S(1)} collective-permute-done((f32[2,1,256,256]{3,2,1,0:T(8,128)}, f32[2,1,256,256]{3,2,1,0:T(8,128)S(1)}, u32[]{:S(2)}, u32[]{:S(2)}) %collective-permute-start.1) | collective-permute-done | bytes 524320 | tf_op jit(solution)/shard_map/while/body/eval_jaxpr/ppermute | solution.py:21
  133.5 0.8 conditional.9
  133.5 0.8 broadcast.192
  134.4 1.9 collective-permute-start.1
  136.3 64.2 %collective-permute-done.1 = f32[2,1,256,256]{3,2,1,0:T(8,128)S(1)} collective-permute-done((f32[2,1,256,256]{3,2,1,0:T(8,128)}, f32[2,1,256,256]{3,2,1,0:T(8,128)S(1)}, u32[]{:S(2)}, u32[]{:S(2)}) %collective-permute-start.1) | collective-permute-done | bytes 524320 | tf_op jit(solution)/shard_map/while/body/eval_jaxpr/ppermute | solution.py:21
  200.5 23.6 %conditional.9 = (f32[2,1,256,256]{3,2,1,0:T(8,128)}, f32[2,1,640,640]{3,2,0,1:T(8,128)}) conditional(s32[]{:T(128)} %convert_element_type.123, f32[2,1,640,640]{3,2,0,1:T(8,128)} %get-tuple-element.1191, (f32[1,640,640]{2,1,0:T(8,128)}, s32[1,2]{1,0:T(1,128)S(1)}, pred[]{:T(512)}, f32[1,2,256,256]{3,2,1,0:T(8,128)S(1)}, ...), branch_computations={%region_7.7_spmd, %region_8.8_spmd} | conditional | flops 1612644352 | bytes 16253164 | solution.py:204
  213.6 1.7 fusion.45
  215.3 1.4 fusion.43
  216.7 0.8 pad_maximum_fusion.3
  217.5 6.6 %dynamic_update_slice.4 = f32[2,1,640,640]{3,2,0,1:T(8,128)} dynamic-update-slice(f32[2,1,640,640]{3,2,0,1:T(8,128)} %get-tuple-element.744, f32[2,1,256,256]{3,2,0,1:T(8,128)S(1)} %fusion.43, s32[]{:T(128)} %constant.244.clone, s32[]{:T(128)} %constant.244.clone, s32[]{:T(128)S(6)} %select_n.157, s32[]{:T(128)S(6)} %select_n.158) | dynamic-update-slice | bytes 1048580 | tf_op jit(solution)/shard_map/while/body/eval_jaxpr/cond/branch_1_fun/dynamic_update_slice | solution.py:190
  224.1 1.9 collective-permute-start.1
  226.0 9.6 %collective-permute-done.1 = f32[2,1,256,256]{3,2,1,0:T(8,128)S(1)} collective-permute-done((f32[2,1,256,256]{3,2,1,0:T(8,128)}, f32[2,1,256,256]{3,2,1,0:T(8,128)S(1)}, u32[]{:S(2)}, u32[]{:S(2)}) %collective-permute-start.1) | collective-permute-done | bytes 524320 | tf_op jit(solution)/shard_map/while/body/eval_jaxpr/ppermute | solution.py:21
  235.7 1.4 fusion.120
  237.0 1.3 collective-permute-start.6
  238.4 1.3 collective-permute-start.7
  239.7 1.7 slice.365
  241.4 11.0 %collective-permute-done.6 = f32[2,1,128,640]{3,2,1,0:T(8,128)S(1)} collective-permute-done((f32[2,1,128,640]{3,2,1,0:T(8,128)S(1)}, f32[2,1,128,640]{3,2,1,0:T(8,128)S(1)}, u32[]{:S(2)}, u32[]{:S(2)}) %collective-permute-start.6) | collective-permute-done | bytes 655392 | tf_op jit(solution)/shard_map/ppermute | solution.py:21
  252.3 1.2 fusion.70
  253.5 2.7 collective-permute-done.7
  256.3 2.3 collective-permute-start.8
  258.7 2.2 collective-permute-start.9
  260.8 1.1 slice.370
  262.0 1.4 collective-permute-done.8
  264.2 3.6 %collective-permute-done.9 = f32[2,1,384,128]{3,2,1,0:T(8,128)S(1)} collective-permute-done((f32[2,1,384,128]{3,2,1,0:T(8,128)S(1)}, f32[2,1,384,128]{3,2,1,0:T(8,128)S(1)}, u32[]{:S(2)}, u32[]{:S(2)}) %collective-permute-start.9) | collective-permute-done | bytes 393248 | tf_op jit(solution)/shard_map/ppermute | solution.py:21
  267.8 1.8 fusion.71
  269.6 34.5 %reduce-scatter.2.cloned.1.call-done = f32[2,1,192,384]{3,2,1,0:T(8,128)} async-done(((f32[2,1,384,384]{3,2,1,0:T(8,128)}), f32[2,1,192,384]{3,2,1,0:T(8,128)}) %reduce-scatter.2.cloned.1.call-update) | async-done | bytes 589840 | tf_op jit(solution)/shard_map/reduce_scatter | solution.py:230
  304.1 1.9 fusion.123
  (49 shorter events, 14.2 us)
Async XLA Ops:
  7.2 296.9 %reduce-scatter.2.cloned.1.call-start = ((), (), s32[]{:S(2)}) async-start(), calls=%async_computation.1 | async-start | bytes 1769472 | tf_op jit(solution)/shard_map/reduce_scatter | solution.py:230
  10.2 11.2 %collective-permute-start.2 = (f32[2,1,128,384]{3,2,1,0:T(8,128)}, f32[2,1,128,384]{3,2,1,0:T(8,128)S(1)}, u32[]{:S(2)}, u32[]{:S(2)}) collective-permute-start(f32[2,1,128,384]{3,2,1,0:T(8,128)} %get-tuple-element.943), channel_id=1, source_target_pairs={{0,4},{2,6},{1,5},{3,7},{8,12},{10,14},{9,13},{11,15},{16,20},{18,... | collective-permute-start | bytes 1179656 | tf_op jit(solution)/shard_map/ppermute | solution.py:21
  13.4 11.6 %collective-permute-start.3 = (f32[2,1,128,384]{3,2,1,0:T(8,128)S(1)}, f32[2,1,128,384]{3,2,1,0:T(8,128)S(1)}, u32[]{:S(2)}, u32[]{:S(2)}) collective-permute-start(f32[2,1,128,384]{3,2,1,0:T(8,128)S(1)} %get-tuple-element.944), channel_id=1, source_target_pairs={{4,0},{6,2},{5,1},{7,3},{12,8},{14,10},{13,9},{15,11},{20,16},{22,... | collective-permute-start | bytes 1179656 | tf_op jit(solution)/shard_map/ppermute | solution.py:21
  17.5 11.0 %copy-start.5 = (s32[1,1,1,256,256]{4,3,2,1,0:T(8,128)S(1)}, s32[1,1,1,256,256]{4,3,2,1,0:T(8,128)}, u32[]{:S(2)}) copy-start(s32[1,1,1,256,256]{4,3,2,1,0:T(8,128)} %param.29) | copy-start | bytes 786436
  24.9 0.7 copy-start.2
  25.7 10.4 %collective-permute-start.4 = (f32[2,1,640,128]{3,2,1,0:T(8,128)S(1)}, f32[2,1,640,128]{3,2,1,0:T(8,128)S(1)}, u32[]{:S(2)}, u32[]{:S(2)}) collective-permute-start(f32[2,1,640,128]{3,2,1,0:T(8,128)S(1)} %get-tuple-element.941), channel_id=1, source_target_pairs={{0,2},{2,4},{4,6},{1,3},{3,5},{5,7},{8,10},{10,12},{12,14},{9,11},... | collective-permute-start | bytes 1966088 | tf_op jit(solution)/shard_map/ppermute | solution.py:21
  28.6 11.9 %collective-permute-start.5 = (f32[2,1,640,128]{3,2,1,0:T(8,128)S(1)}, f32[2,1,640,128]{3,2,1,0:T(8,128)S(1)}, u32[]{:S(2)}, u32[]{:S(2)}) collective-permute-start(f32[2,1,640,128]{3,2,1,0:T(8,128)S(1)} %get-tuple-element.942), channel_id=1, source_target_pairs={{2,0},{4,2},{6,4},{3,1},{5,3},{7,5},{10,8},{12,10},{14,12},{11,9},... | collective-permute-start | bytes 1966088 | tf_op jit(solution)/shard_map/ppermute | solution.py:21
  33.8 6.8 %copy-start.3 = (f32[2,1,128,384]{3,2,1,0:T(8,128)S(1)}, f32[2,1,128,384]{3,2,1,0:T(8,128)}, u32[]{:S(2)}) copy-start(f32[2,1,128,384]{3,2,1,0:T(8,128)} %copy-done.2) | copy-start | bytes 1179652
  40.8 7.7 %copy-start.4 = (s32[1,1,1,2]{3,2,1,0:T(1,128)S(1)}, s32[1,1,1,2]{3,2,1,0:T(1,128)}, u32[]{:S(2)}) copy-start(s32[1,1,1,2]{3,2,1,0:T(1,128)} %param.28) | copy-start | bytes 28
  49.3 21.9 %collective-permute-start = (f32[2,1,256,256]{3,2,1,0:T(8,128)}, f32[2,1,256,256]{3,2,1,0:T(8,128)S(1)}, u32[]{:S(2)}, u32[]{:S(2)}) collective-permute-start(f32[2,1,256,256]{3,2,1,0:T(8,128)} %get-tuple-element.1097), channel_id=1, source_target_pairs={{0,8},{8,16},{16,24},{1,9},{9,17},{17,25},{2,10},{10,18},{18,26},{... | collective-permute-start | bytes 1572872 | tf_op jit(solution)/shard_map/while/body/eval_jaxpr/ppermute | solution.py:21
  84.7 10.7 %collective-permute-start = (f32[2,1,256,256]{3,2,1,0:T(8,128)}, f32[2,1,256,256]{3,2,1,0:T(8,128)S(1)}, u32[]{:S(2)}, u32[]{:S(2)}) collective-permute-start(f32[2,1,256,256]{3,2,1,0:T(8,128)} %get-tuple-element.1097), channel_id=1, source_target_pairs={{0,8},{8,16},{16,24},{1,9},{9,17},{17,25},{2,10},{10,18},{18,26},{... | collective-permute-start | bytes 1572872 | tf_op jit(solution)/shard_map/while/body/eval_jaxpr/ppermute | solution.py:21
  96.1 22.0 %collective-permute-start = (f32[2,1,256,256]{3,2,1,0:T(8,128)}, f32[2,1,256,256]{3,2,1,0:T(8,128)S(1)}, u32[]{:S(2)}, u32[]{:S(2)}) collective-permute-start(f32[2,1,256,256]{3,2,1,0:T(8,128)} %get-tuple-element.1097), channel_id=1, source_target_pairs={{0,8},{8,16},{16,24},{1,9},{9,17},{17,25},{2,10},{10,18},{18,26},{... | collective-permute-start | bytes 1572872 | tf_op jit(solution)/shard_map/while/body/eval_jaxpr/ppermute | solution.py:21
  120.9 12.6 %collective-permute-start.1 = (f32[2,1,256,256]{3,2,1,0:T(8,128)}, f32[2,1,256,256]{3,2,1,0:T(8,128)S(1)}, u32[]{:S(2)}, u32[]{:S(2)}) collective-permute-start(f32[2,1,256,256]{3,2,1,0:T(8,128)} %get-tuple-element.1113), channel_id=1, source_target_pairs={{8,0},{16,8},{24,16},{9,1},{17,9},{25,17},{10,2},{18,10},{26,18},{... | collective-permute-start | bytes 1572872 | tf_op jit(solution)/shard_map/while/body/eval_jaxpr/ppermute | solution.py:21
  134.4 66.1 %collective-permute-start.1 = (f32[2,1,256,256]{3,2,1,0:T(8,128)}, f32[2,1,256,256]{3,2,1,0:T(8,128)S(1)}, u32[]{:S(2)}, u32[]{:S(2)}) collective-permute-start(f32[2,1,256,256]{3,2,1,0:T(8,128)} %get-tuple-element.1113), channel_id=1, source_target_pairs={{8,0},{16,8},{24,16},{9,1},{17,9},{25,17},{10,2},{18,10},{26,18},{... | collective-permute-start | bytes 1572872 | tf_op jit(solution)/shard_map/while/body/eval_jaxpr/ppermute | solution.py:21
  211.7 1.8 copy-start
  224.1 11.5 %collective-permute-start.1 = (f32[2,1,256,256]{3,2,1,0:T(8,128)}, f32[2,1,256,256]{3,2,1,0:T(8,128)S(1)}, u32[]{:S(2)}, u32[]{:S(2)}) collective-permute-start(f32[2,1,256,256]{3,2,1,0:T(8,128)} %get-tuple-element.1113), channel_id=1, source_target_pairs={{8,0},{16,8},{24,16},{9,1},{17,9},{25,17},{10,2},{18,10},{26,18},{... | collective-permute-start | bytes 1572872 | tf_op jit(solution)/shard_map/while/body/eval_jaxpr/ppermute | solution.py:21
  237.0 15.3 %collective-permute-start.6 = (f32[2,1,128,640]{3,2,1,0:T(8,128)S(1)}, f32[2,1,128,640]{3,2,1,0:T(8,128)S(1)}, u32[]{:S(2)}, u32[]{:S(2)}) collective-permute-start(f32[2,1,128,640]{3,2,1,0:T(8,128)S(1)} %get-tuple-element.936), channel_id=1, source_target_pairs={{0,4},{2,6},{1,5},{3,7},{8,12},{10,14},{9,13},{11,15},{16,20},{18,... | collective-permute-start | bytes 1966088 | tf_op jit(solution)/shard_map/ppermute | solution.py:21
  238.4 17.8 %collective-permute-start.7 = (f32[2,1,128,640]{3,2,1,0:T(8,128)S(1)}, f32[2,1,128,640]{3,2,1,0:T(8,128)S(1)}, u32[]{:S(2)}, u32[]{:S(2)}) collective-permute-start(f32[2,1,128,640]{3,2,1,0:T(8,128)S(1)} %get-tuple-element.935), channel_id=1, source_target_pairs={{4,0},{6,2},{5,1},{7,3},{12,8},{14,10},{13,9},{15,11},{20,16},{22,... | collective-permute-start | bytes 1966088 | tf_op jit(solution)/shard_map/ppermute | solution.py:21
  256.3 7.0 %collective-permute-start.8 = (f32[2,1,384,128]{3,2,1,0:T(8,128)S(1)}, f32[2,1,384,128]{3,2,1,0:T(8,128)S(1)}, u32[]{:S(2)}, u32[]{:S(2)}) collective-permute-start(f32[2,1,384,128]{3,2,1,0:T(8,128)S(1)} %get-tuple-element.940), channel_id=1, source_target_pairs={{0,2},{2,4},{4,6},{1,3},{3,5},{5,7},{8,10},{10,12},{12,14},{9,11},... | collective-permute-start | bytes 1179656 | tf_op jit(solution)/shard_map/ppermute | solution.py:21
  258.7 9.1 %collective-permute-start.9 = (f32[2,1,384,128]{3,2,1,0:T(8,128)S(1)}, f32[2,1,384,128]{3,2,1,0:T(8,128)S(1)}, u32[]{:S(2)}, u32[]{:S(2)}) collective-permute-start(f32[2,1,384,128]{3,2,1,0:T(8,128)S(1)} %get-tuple-element.939), channel_id=1, source_target_pairs={{2,0},{4,2},{6,4},{3,1},{5,3},{7,5},{10,8},{12,10},{14,12},{11,9},... | collective-permute-start | bytes 1179656 | tf_op jit(solution)/shard_map/ppermute | solution.py:21
Sparse Core Ops, SparseCore 0:
  269.7 34.3 reduce-scatter.1
where the time goes:
time: 318 us; the launch traced here: 313 us
  waiting for transfers between devices  187 us (59%)
  starting transfers between devices  41.9 us (13%)
  local copies, waits for them, and re-layouts  24.4 us (8%)
  other arithmetic  17.8 us (6%)
  matrix products  16.2 us (5%)
  between operations  14.3 us (4%)
  loops' own time  11.5 us (4%)
    ppermute x14, waiting for transfers between devices, from_behind(): return lax.ppermute(value, axis, pairs)  152 us
    ppermute x14, starting transfers between devices, from_behind(): return lax.ppermute(value, axis, pairs)  41.9 us
    reduce_scatter x1, waiting for transfers between devices, shards(): shares = lax.psum_scatter(middle, 'rep', scatter_dimension=2, tiled=True)  34.5 us
    another operation x4, loops' own time, backward_work(): return lax.cond(is_active, backward_active, backward_resting, grad_now)  7.66 us
    mul x1, other arithmetic, shards(): trans_im = damping * jnp.sin(extended[0])  6.72 us
    dynamic_update_slice x1, local copies, waits for them, and re-layouts, backward_active(): lax.dynamic_update_slice(grad_state, current + grad_terms[0][:, None], (0...  6.6 us
  transfers between devices with their start and end apart: 15, of which 15 were waited for; matrix products, arithmetic and copies ran while one was open for 3% of the time, Pallas kernels for 0%

commit v1 on v0

v1 whole, which is shorter than its diff:
```python
import math

import jax
import jax.numpy as jnp
import ml_dtypes
import numpy as np
from jax import lax
from jax.experimental import pallas as pl
from jax.experimental.pallas import tpu as pltpu
from jax.sharding import PartitionSpec as P

HALO = 128
LANES = 128
AXES = ("section", "tile", "rep")

dead_time = 0.1
background = 0.1
loss_weight = 0.1
fresnel = 0.5

f32 = jnp.float32
bf16 = jnp.bfloat16

SMEM = pl.BlockSpec(memory_space=pltpu.SMEM)
VMEM = pl.BlockSpec(memory_space=pltpu.VMEM)
ANY = pl.BlockSpec(memory_space=pl.ANY)


def two_parts(matrix):
    high = matrix.astype(ml_dtypes.bfloat16)
    low = (matrix - high.astype(np.float64)).astype(ml_dtypes.bfloat16)
    return np.stack([high, low])


def from_left(matrix):
    return np.block([[matrix.real, -matrix.imag], [matrix.imag, matrix.real]])


def from_right(matrix):
    return np.block([[matrix.real, matrix.imag], [-matrix.imag, matrix.real]])


def wave_tables(length):
    half = length // 2
    indices = np.arange(length)
    shifted = np.where(indices < half, indices, indices - length)
    kernel = np.exp(1j * math.pi * fresnel * shifted.astype(np.float64) ** 2 / length)
    spread = np.fft.ifft(kernel)
    circulant = spread[(indices[:, None] - indices[None, :]) % length]
    first, second = circulant[:half, :half], circulant[:half, half:]
    plus, minus = (first + second) / 2, (first - second) / 2
    near = [from_left(plus), from_left(minus), from_right(plus), from_right(minus)]
    turns = np.outer(indices[:half], indices[:half]) % half
    even = np.exp(-2j * math.pi * turns / half) / math.sqrt(length)
    odd = even * np.exp(-2j * math.pi * indices[:half] / length)[None, :]
    far = [from_left(even), from_left(odd), from_right(even.T), from_right(odd.T)]
    back = [from_left(even.T), from_left(odd.T), from_right(even), from_right(odd)]
    sort = np.zeros((length, length))
    sort[np.arange(half), 2 * np.arange(half)] = 1
    sort[half + np.arange(half), 2 * np.arange(half) + 1] = 1
    tables = np.stack([two_parts(m) for m in near + far + back])
    return tables, np.stack([sort, sort.T]).astype(ml_dtypes.bfloat16)


def fitted(function, degree):
    top = math.pi**2
    fit = np.polynomial.chebyshev.Chebyshev.interpolate(function, degree, domain=[0.0, top])
    return [float(c) for c in fit.convert(kind=np.polynomial.Polynomial).coef]


def sine_ratio(u):
    angle = np.sqrt(np.maximum(u, 1e-12))
    return np.sin(angle) / angle


SINE = fitted(sine_ratio, 8)
COSINE = fitted(lambda u: np.cos(np.sqrt(np.maximum(u, 0.0))), 8)


def polynomial(coefficients, u):
    total = jnp.full_like(u, coefficients[-1])
    for c in coefficients[-2::-1]:
        total = total * u + c
    return total


def cos_sin(angle):
    square = angle * angle
    return polynomial(COSINE, square), angle * polynomial(SINE, square)


def halves(value):
    high = value.astype(bf16)
    return high, (value - high.astype(f32)).astype(bf16)


def dot(a, b):
    return jnp.dot(a, b, preferred_element_type=f32)


def left_by(tables, index, value):
    high, low = halves(value)
    return dot(tables[index, 0], high) + dot(tables[index, 1], high) + dot(tables[index, 0], low)


def right_by(tables, index, value):
    high, low = halves(value)
    return dot(high, tables[index, 0]) + dot(high, tables[index, 1]) + dot(low, tables[index, 0])


def propagate(tables, at, re, im, fold, unfold):
    half = re.shape[0] // 2
    re0, re1, im0, im1 = re[:half], re[half:], im[:half], im[half:]
    if fold:
        re0, re1, im0, im1 = re0 + re1, re0 - re1, im0 + im1, im0 - im1
    first = left_by(tables, at, jnp.concatenate([re0, im0], 0))
    second = left_by(tables, at + 1, jnp.concatenate([re1, im1], 0))
    if unfold:
        first, second = first + second, first - second
    re = jnp.concatenate([first[:half], second[:half]], 0)
    im = jnp.concatenate([first[half:], second[half:]], 0)
    re0, re1, im0, im1 = re[:, :half], re[:, half:], im[:, :half], im[:, half:]
    if fold:
        re0, re1, im0, im1 = re0 + re1, re0 - re1, im0 + im1, im0 - im1
    first = right_by(tables, at + 2, jnp.concatenate([re0, im0], 1))
    second = right_by(tables, at + 3, jnp.concatenate([re1, im1], 1))
    if unfold:
        first, second = first + second, first - second
    re = jnp.concatenate([first[:, :half], second[:, :half]], 1)
    im = jnp.concatenate([first[:, half:], second[:, half:]], 1)
    return re, im


def near_field(tables, re, im):
    return propagate(tables, 0, re, im, True, True)


def far_field(tables, re, im):
    return propagate(tables, 4, re, im, True, False)


def far_back(tables, re, im):
    return propagate(tables, 8, re, im, False, True)


def likelihood_seed(far_re, far_im, observed):
    intensity = far_re * far_re + far_im * far_im
    shifted_total = intensity + background
    denominator = 1.0 + dead_time * shifted_total
    model_rate = shifted_total / denominator
    slope_term = loss_weight * (1.0 - observed / model_rate) / (denominator * denominator)
    return (2.0 * slope_term * far_re, 2.0 * slope_term * far_im)


def lane_part(column):
    block = jnp.minimum(column // LANES, 2)
    return pl.multiple_of(block * LANES, LANES), column - block * LANES


def cut_columns(read, column, width):
    start, rest = lane_part(column)
    wide = read(start, width + LANES)
    return pltpu.roll(wide, (width + LANES) - rest, 1)[:, :width]


def cut_rows(read, row, height, total):
    block = jnp.minimum(row // 8, (total - height) // 8 - 1)
    tall = read(pl.multiple_of(block * 8, 8), height + 8)
    return pltpu.roll(tall, (height + 8) - (row - block * 8), 0)[:height]


def put_columns(target, plane, rows, value, column):
    start, rest = lane_part(column)
    wide = jnp.concatenate([value, jnp.zeros((value.shape[0], LANES), f32)], 1)
    wide = pltpu.roll(wide, rest, 1)
    here = (plane, rows, pl.ds(start, wide.shape[1]))
    target[here] = target[here] + wide


class Place:
    def __init__(self, grid_side):
        self.grid_side = grid_side
        self.ways = 1 if grid_side == 2 else 2

    def section(self):
        return lax.axis_index("section")

    def rep(self):
        return lax.axis_index("rep")

    def row(self):
        return lax.axis_index("tile") // self.grid_side

    def column(self):
        return lax.axis_index("tile") % self.grid_side

    def owner(self):
        return 1 + self.column() % 2

    def sent(self, index, way):
        return 1 - index if self.ways == 1 else way

    def received(self, index, way):
        return 1 - index if self.ways == 1 else 1 - way


def solution(mesh):
    sections, tiles, reps = (mesh.shape[a] for a in AXES)
    grid_side = math.isqrt(tiles)
    place = Place(grid_side)
    ways = place.ways

    def everywhere(target_of):
        pairs = []
        for s in range(sections):
            for t in range(tiles):
                for r in range(reps):
                    target = target_of(s, t // grid_side, t % grid_side, r)
                    if target is None:
                        continue
                    ts, ty, tx, tr = target
                    if not (0 <= ty < grid_side and 0 <= tx < grid_side):
                        continue
                    pairs.append(
                        ((s * tiles + t) * reps + r, (ts * tiles + ty * grid_side + tx) * reps + tr)
                    )
        return pairs

    def move(value, target_of):
        return lax.ppermute(value, AXES, everywhere(target_of))

    def trade_rows(values):
        if ways == 1:
            return [move(values[0], lambda s, y, x, r: (s, 1 - y, x, r))]
        return [
            move(values[0], lambda s, y, x, r: (s, y - 1, x, r)),
            move(values[1], lambda s, y, x, r: (s, y + 1, x, r)),
        ]

    def trade_columns(values):
        if ways == 1:
            return [move(values[0], lambda s, y, x, r: (s, y, 1 - x, r))]
        return [
            move(values[0], lambda s, y, x, r: (s, y, x - 1, r)),
            move(values[1], lambda s, y, x, r: (s, y, x + 1, r)),
        ]

    def owner_of(x):
        return 1 + x % 2

    def shards(phase_shift, absorption, probe_wave, positions, counts):
        width = phase_shift.shape[2]
        frame = probe_wave.shape[1]
        extent = width + 2 * HALO
        half_rows = width // reps
        edge = width + HALO
        phase = phase_shift.reshape(width, width)
        absorb = absorption.reshape(width, width)
        spot = positions.reshape(1, 2)
        observed = counts.reshape(frame, frame)
        sds = jax.ShapeDtypeStruct

        spots_rows = trade_rows([spot] * ways)
        spots_rep = move(
            jnp.concatenate([spot] + spots_rows, 0), lambda s, y, x, r: (s, y, x, 1 - r)
        )

        def edge_kernel(phase_ref, absorb_ref, *refs):
            outs, sem = refs[:ways], refs[ways]
            copies = []
            for way in range(ways):
                side = place.sent(place.column(), way)
                start = pl.multiple_of(side * (width - HALO), LANES)
                for plane, ref in enumerate((phase_ref, absorb_ref)):
                    copy = pltpu.make_async_copy(
                        ref.at[:, pl.ds(start, HALO)], outs[way].at[plane], sem.at[2 * way + plane]
                    )
                    copy.start()
                    copies.append(copy)
            for copy in copies:
                copy.wait()

        edges = pl.pallas_call(
            edge_kernel,
            out_shape=[sds((2, width, HALO), f32)] * ways,
            in_specs=[ANY, ANY],
            out_specs=[VMEM] * ways,
            scratch_shapes=[pltpu.SemaphoreType.DMA((2 * ways,))],
            name="edge_columns",
        )(phase, absorb)
        sides = trade_columns(edges)

        def strip_kernel(phase_ref, absorb_ref, *refs):
            side_refs, spot_refs = refs[:ways], refs[ways : 2 * ways]
            outs, wide = refs[2 * ways : 3 * ways], refs[3 * ways]
            for way in range(ways):
                below = place.sent(place.row(), way)
                first = pl.multiple_of(below * (width - HALO), 8)
                rows = pl.ds(first, HALO)
                column = spot_refs[way if ways == 1 else 1 - way][0, 1]
                for plane, ref in enumerate((phase_ref, absorb_ref)):
                    if ways == 1:
                        wide[:, :HALO] = jnp.zeros((HALO, HALO), f32)
                        wide[:, edge:] = jnp.zeros((HALO, HALO), f32)
                    wide[:, HALO:edge] = ref[rows, :]
                    for other in range(ways):
                        start = place.received(place.column(), other) * edge
                        wide[:, pl.ds(pl.multiple_of(start, LANES), HALO)] = side_refs[other][
                            plane, rows, :
                        ]
                    outs[way][plane] = cut_columns(
                        lambda start, count: wide[:, pl.ds(start, count)], column, frame
                    )

        strips = pl.pallas_call(
            strip_kernel,
            out_shape=[sds((2, HALO, frame), f32)] * ways,
            in_specs=[VMEM] * (2 + ways) + [SMEM] * ways,
            out_specs=[VMEM] * ways,
            scratch_shapes=[pltpu.VMEM((HALO, extent), f32)],
            name="halo_rows",
        )(phase, absorb, *sides, *spots_rows)
        rims = trade_rows(strips)

        def window_kernel(spot_ref, phase_ref, absorb_ref, *refs):
            side_refs, rim_refs = refs[:ways], refs[ways : 2 * ways]
            out, wide, rim = refs[2 * ways :]
            row, column = spot_ref[0, 0], spot_ref[0, 1]
            values = []
            for plane, ref in enumerate((phase_ref, absorb_ref)):
                wide[:HALO, :] = jnp.zeros((HALO, extent), f32)
                wide[edge:, :] = jnp.zeros((HALO, extent), f32)
                if ways == 1:
                    wide[HALO:edge, :HALO] = jnp.zeros((width, HALO), f32)
                    wide[HALO:edge, edge:] = jnp.zeros((width, HALO), f32)
                    rim[:HALO, :] = jnp.zeros((HALO, frame), f32)
                    rim[edge:, :] = jnp.zeros((HALO, frame), f32)
                rim[HALO:edge, :] = jnp.zeros((width, frame), f32)
                wide[HALO:edge, HALO:edge] = ref[...]
                for way in range(ways):
                    start = place.received(place.column(), way) * edge
                    wide[HALO:edge, pl.ds(pl.multiple_of(start, LANES), HALO)] = side_refs[way][
                        plane
                    ]
                    start = place.received(place.row(), way) * edge
                    rim[pl.ds(pl.multiple_of(start, 8), HALO), :] = rim_refs[way][plane]

                def rows_of(top, tall):
                    cut = cut_columns(
                        lambda start, count: wide[pl.ds(top, tall), pl.ds(start, count)],
                        column,
                        frame,
                    )
                    return cut + rim[pl.ds(top, tall), :]

                values.append(cut_rows(rows_of, row, frame, extent))
            cosine, sine = cos_sin(values[0])
            damping = jnp.exp(-values[1])
            out[0] = damping * cosine
            out[1] = damping * sine

        window = pl.pallas_call(
            window_kernel,
            out_shape=sds((2, frame, frame), f32),
            in_specs=[SMEM] + [VMEM] * (2 + 2 * ways),
            out_specs=VMEM,
            scratch_shapes=[pltpu.VMEM((extent, extent), f32), pltpu.VMEM((extent, frame), f32)],
            name="window",
        )(spot, phase, absorb, *sides, *rims)

        def to_owner(section_of):
            return move(
                window,
                lambda s, y, x, r: (owner_of(x), y, x, r) if s == section_of(x) else None,
            )

        first = to_owner(lambda x: 0)
        other = to_owner(lambda x: 3 - owner_of(x))
        last = to_owner(lambda x: 3)

        def frame_kernel(first_ref, own_ref, other_ref, last_ref, probe, seen, tables, sort, *refs):
            out_first, out_own, out_other, out_last, fields, exits = refs
            own_is_second = place.owner() == 1
            fields[0] = jnp.where(own_is_second, own_ref[...], other_ref[...])
            fields[1] = jnp.where(own_is_second, other_ref[...], own_ref[...])
            objects = [first_ref, fields.at[0], fields.at[1], last_ref]
            re, im = probe[0], probe[1]
            for number, field in enumerate(objects):
                o_re, o_im = field[0], field[1]
                exit_re, exit_im = o_re * re - o_im * im, o_re * im + o_im * re
                exits[number, 0], exits[number, 1] = exit_re, exit_im
                if number < 3:
                    re, im = near_field(tables, exit_re, exit_im)
            re, im = far_field(tables, exit_re, exit_im)
            counted = dot(sort[0], seen[...].astype(f32).astype(bf16)).astype(bf16)
            re, im = likelihood_seed(re, im, dot(counted, sort[1]))
            im = -im
            for number in reversed(range(4)):
                if number == 3:
                    re, im = far_back(tables, re, im)
                else:
                    re, im = near_field(tables, re, im)
                exit_re, exit_im = exits[number, 0], exits[number, 1]
                phase_term = -(re * exit_im + im * exit_re)
                absorb_term = im * exit_im - re * exit_re
                if number == 3:
                    out_last[0], out_last[1] = phase_term, absorb_term
                elif number == 0:
                    out_first[0], out_first[1] = phase_term, absorb_term
                else:
                    if number == 2:
                        kept = (phase_term, absorb_term)
                    else:
                        for plane, term in enumerate((phase_term, absorb_term)):
                            out_own[plane] = jnp.where(own_is_second, term, exits[3, plane])
                            out_other[plane] = jnp.where(own_is_second, exits[3, plane], term)
                    if number == 2:
                        exits[3, 0], exits[3, 1] = kept
                if number > 0:
                    o_re, o_im = objects[number][0], objects[number][1]
                    re, im = o_re * re - o_im * im, o_re * im + o_im * re

        tables, sort = wave_tables(frame)
        terms = pl.pallas_call(
            frame_kernel,
            out_shape=[sds((2, frame, frame), f32)] * 4,
            in_specs=[VMEM] * 8,
            out_specs=[VMEM] * 4,
            scratch_shapes=[
                pltpu.VMEM((2, 2, frame, frame), f32),
                pltpu.VMEM((4, 2, frame, frame), f32),
            ],
            compiler_params=pltpu.CompilerParams(vmem_limit_bytes=48 << 20),
            name="frame",
        )(first, window, other, last, probe_wave, observed, tables, sort)

        def from_owner(value, section_of):
            return move(
                value,
                lambda s, y, x, r: (section_of(x), y, x, r) if s == owner_of(x) else None,
            )

        back_first = from_owner(terms[0], lambda x: 0)
        back_other = from_owner(terms[2], lambda x: 3 - owner_of(x))
        back_last = from_owner(terms[3], lambda x: 3)

        pad = frame

        def parts_kernel(spot_ref, first_ref, own_ref, other_ref, last_ref, *refs):
            keep, give, straight, across, term, padded, sem = refs
            section, rep, owner = place.section(), place.rep(), place.owner()
            choice = jnp.where(
                section == 0, 0, jnp.where(section == 3, 3, jnp.where(section == owner, 1, 2))
            )
            for number, ref in enumerate((first_ref, own_ref, other_ref, last_ref)):

                @pl.when(choice == number)
                def _():
                    copy = pltpu.make_async_copy(ref, term, sem)
                    copy.start()
                    copy.wait()

            row = spot_ref[0, 0]
            zeros = jnp.zeros((2, pad, frame), f32)
            padded[:, :pad] = zeros
            padded[:, pad + frame :] = zeros
            padded[:, pad : pad + frame] = term[...]
            mine = pad + HALO + half_rows * rep - row
            others = pad + HALO + half_rows * (1 - rep) - row
            above = jnp.maximum(pad - row, 0)
            below = jnp.minimum(pad + edge - row, pad + frame + HALO)
            cuts = (
                (keep, mine, half_rows),
                (give, others, half_rows),
                (straight, jnp.where(rep == 1, above, below), HALO),
                (across, jnp.where(rep == 1, below, above), HALO),
            )
            for out, start, height in cuts:
                for plane in range(2):
                    out[plane] = cut_rows(
                        lambda top, tall: padded[plane, pl.ds(top, tall), :],
                        start,
                        height,
                        frame + 2 * pad,
                    )

        keep, give, straight, across = pl.pallas_call(
            parts_kernel,
            out_shape=[sds((2, half_rows, frame), f32)] * 2 + [sds((2, HALO, frame), f32)] * 2,
            in_specs=[SMEM] + [ANY] * 4,
            out_specs=[VMEM] * 4,
            scratch_shapes=[
                pltpu.VMEM((2, frame, frame), f32),
                pltpu.VMEM((2, frame + 2 * pad, frame), f32),
                pltpu.SemaphoreType.DMA,
            ],
            name="parts",
        )(spot, back_first, terms[1], back_other, back_last)

        given = move(give, lambda s, y, x, r: (s, y, x, 1 - r))
        came_straight = move(straight, lambda s, y, x, r: (s, y + 1 - 2 * r, x, r))
        came_across = move(across, lambda s, y, x, r: (s, y - 1 + 2 * r, x, 1 - r))

        def gather_kernel(spot_ref, partner_ref, *refs):
            spot_refs = refs[:ways]
            keep_ref, given_ref, straight_ref, across_ref = refs[ways : ways + 4]
            middle, outs, total = refs[ways + 4], refs[ways + 5 : 2 * ways + 5], refs[-1]
            rep = place.rep()
            total[...] = jnp.zeros(total.shape, f32)
            if ways == 1:
                straight_column, across_column = spot_refs[0][0, 1], partner_ref[1, 1]
            else:
                straight_column = jnp.where(rep == 1, spot_refs[0][0, 1], spot_refs[1][0, 1])
                across_column = jnp.where(rep == 1, partner_ref[1, 1], partner_ref[2, 1])
            low = pl.ds(pl.multiple_of(rep * (half_rows - HALO), 8), HALO)
            every = pl.ds(0, half_rows)
            for plane in range(2):
                put_columns(total, plane, every, keep_ref[plane], spot_ref[0, 1])
                put_columns(total, plane, every, given_ref[plane], partner_ref[0, 1])
                put_columns(total, plane, low, straight_ref[plane], straight_column)
                put_columns(total, plane, low, across_ref[plane], across_column)
            middle[...] = total[:, :, HALO:edge]
            for way in range(ways):
                start = place.sent(place.column(), way) * edge
                outs[way][...] = total[:, :, pl.ds(pl.multiple_of(start, LANES), HALO)]

        middle, *leaving = pl.pallas_call(
            gather_kernel,
            out_shape=[sds((2, half_rows, width), f32)] + [sds((2, half_rows, HALO), f32)] * ways,
            in_specs=[SMEM] * (2 + ways) + [VMEM] * 4,
            out_specs=[VMEM] * (1 + ways),
            scratch_shapes=[pltpu.VMEM((2, half_rows, extent), f32)],
            name="gather_terms",
        )(spot, spots_rep, *spots_rows, keep, given, came_straight, came_across)
        arrived = trade_columns(leaving)

        def finish_kernel(middle_ref, *refs):
            arrived_refs, outs = refs[:ways], refs[ways:]
            for plane in range(2):
                outs[plane][...] = middle_ref[plane]
                for way in range(ways):
                    start = place.received(place.column(), way) * (width - HALO)
                    here = (slice(None), pl.ds(pl.multiple_of(start, LANES), HALO))
                    outs[plane][here] = outs[plane][here] + arrived_refs[way][plane]

        result = pl.pallas_call(
            finish_kernel,
            out_shape=[sds((half_rows, width), f32)] * 2,
            in_specs=[VMEM] * (1 + ways),
            out_specs=[VMEM] * 2,
            name="finish",
        )(middle, *arrived)
        return tuple(plane[None, None] for plane in result)

    in_specs = (
        P("section", "tile", None, None),
        P("section", "tile", None, None),
        P(),
        P("tile", "rep", None, None),
        P("tile", "rep", None, None, None),
    )
    out_specs = (P("section", "tile", "rep", None), P("section", "tile", "rep", None))
    return jax.shard_map(shards, mesh=mesh, in_specs=in_specs, out_specs=out_specs, check_vma=False)
```

time: 318 us -> 91.2 us (0.29); the launches traced: 313 us -> 90.8 us
  waiting for transfers between devices: 187 us -> 36.1 us
  Pallas kernels: 0 us -> 23.3 us
  local copies, waits for them, and re-layouts: 24.4 us -> 6.37 us
  starting transfers between devices: 41.9 us -> 24 us
  other arithmetic: 17.8 us -> 0.01 us
  matrix products: 16.2 us -> 0 us
  between operations: 14.3 us -> 0.87 us
  loops' own time: 11.5 us -> 0 us
    ppermute x14, waiting for transfers between devices: 152 us -> 36.1 us  [move(): return lax.ppermute(value, AXES, everywhere(target_of))]
    reduce_scatter x1 -> x0, waiting for transfers between devices: 34.5 us -> none  [shards(): shares = lax.psum_scatter(middle, 'rep', scatter_dimension=2, tiled=True)]
    pallas_call x0 -> x7, Pallas kernels: none -> 23.3 us  [the longest x1 8.12 us: shards(): pl.pallas_call(frame_kernel, out_shape=[sds((2, frame, frame), f32)] * 4,...]
    ppermute x14, starting transfers between devices: 41.9 us -> 24 us  [move(): return lax.ppermute(value, AXES, everywhere(target_of))]
    dot_general x20 -> x0, matrix products: 16.2 us -> none  [the longest x8 5.92 us: right_product(): jnp.einsum('bmk,kn->bmn', frames, matrix, precision=highest, preferred_el...]
    another operation x10 -> x0, loops' own time: 11.5 us -> none  [the longest x4 7.66 us: backward_work(): return lax.cond(is_active, backward_active, backward_resting, grad_now)]
    slice x9 -> x0, local copies, waits for them, and re-layouts: 8.73 us -> none  [the longest x1 1.9 us: shards(): return (shares[0][:, None], shares[1][:, None])]
    mul x3 -> x0, other arithmetic: 6.81 us -> none  [the longest x1 6.72 us: shards(): trans_im = damping * jnp.sin(extended[0])]
  transfers between devices with their start and end apart: 15 -> 14, of which waited for: 15 -> 6; matrix products, arithmetic and copies ran while one was open for 3% -> 0% of each run, Pallas kernels for 0% -> 0%
where the time goes in v1:
time: 91.2 us; the launch traced here: 90.8 us
  waiting for transfers between devices  36.1 us (40%)
  starting transfers between devices  24 us (26%)
  Pallas kernels  23.3 us (26%)
  local copies, waits for them, and re-layouts  6.37 us (7%)
    ppermute x14, waiting for transfers between devices, move(): return lax.ppermute(value, AXES, everywhere(target_of))  36.1 us
    ppermute x14, starting transfers between devices, move(): return lax.ppermute(value, AXES, everywhere(target_of))  24 us
    pallas_call x1, Pallas kernels, shards(): pl.pallas_call(frame_kernel, out_shape=[sds((2, frame, frame), f32)] * 4,...  8.12 us
    unnamed x36, local copies, waits for them, and re-layouts  6.37 us
    pallas_call x1, Pallas kernels, shards(): pl.pallas_call(window_kernel, out_shape=sds((2, frame, frame), f32), in_s...  3.38 us
    pallas_call x1, Pallas kernels, shards(): pl.pallas_call(parts_kernel, out_shape=[sds((2, half_rows, frame), f32)]...  3 us
    pallas_call x1, Pallas kernels, shards(): pl.pallas_call(gather_kernel, out_shape=[sds((2, half_rows, width), f32)]...  2.74 us
    pallas_call x1, Pallas kernels, shards(): pl.pallas_call(strip_kernel, out_shape=[sds((2, HALO, frame), f32)] * way...  2.28 us
  transfers between devices with their start and end apart: 14, of which 6 were waited for; matrix products, arithmetic and copies ran while one was open for 0% of the time, Pallas kernels for 0%

profile of v1, /device:TPU:13, one launch (start us, length us, event | category | flops | bytes accessed | tf_op | source)
XLA Modules:
  0.0 90.8 jit_solution(4617156309930435921)
XLA Ops:
  0.6 0.0 copy-start.4
  0.6 0.0 copy-start.3
  0.7 0.0 copy-start.1
  0.7 1.9 %edge_columns.1 = f32[2,384,128]{2,1,0:T(8,128)} custom-call(f32[384,384]{1,0:T(8,128)} %bitcast.7, f32[384,384]{1,0:T(8,128)} %bitcast.10), custom_call_target="tpu_custom_call" | custom-call | tf_op jit(solution)/shard_map/edge_columns/pallas_call | solution.py:283
  2.6 0.7 collective-permute-start.2
  3.3 1.2 %collective-permute-start = (s32[1,2]{1,0:T(1,128)}, s32[1,2]{1,0:T(1,128)S(1)}, u32[]{:S(2)}, u32[]{:S(2)}) collective-permute-start(s32[1,2]{1,0:T(1,128)} %bitcast.13), channel_id=1, source_target_pairs={{0,4},{1,5},{2,6},{3,7},{4,0},{5,1},{6,2},{7,3},{8,12},{9,13},{10,... | collective-permute-start | bytes 32 | tf_op jit(solution)/shard_map/ppermute | solution.py:230
  4.5 1.3 %collective-permute-done.refs_1_.refs_0_ = s32[1,2]{1,0:T(1,128)S(1)} collective-permute-done((s32[1,2]{1,0:T(1,128)}, s32[1,2]{1,0:T(1,128)S(1)}, u32[]{:S(2)}, u32[]{:S(2)}) %collective-permute-start) | collective-permute-done | bytes 40 | tf_op jit(solution)/shard_map/ppermute | solution.py:230
  5.8 0.0 copy-start.15
  5.8 0.0 collective-permute-done.2.refs_0_
  5.8 0.5 copy-done.15
  6.3 0.0 copy-start.5
  6.3 0.8 copy-done.5
  7.1 2.3 %halo_rows.1 = f32[2,128,256]{2,1,0:T(8,128)} custom-call(f32[384,384]{1,0:T(8,128)} %bitcast.8, f32[384,384]{1,0:T(8,128)} %bitcast.11, f32[2,384,128]{2,1,0:T(8,128)} %copy-done.5, s32[1,2]{1,0:T(1,128)} %copy-done.15), custom_call_target="tpu_custom_call" | custom-call | tf_op jit(solution)/shard_map/halo_rows/pallas_call | solution.py:315
  9.4 1.2 %collective-permute-start.3 = (f32[2,128,256]{2,1,0:T(8,128)}, f32[2,128,256]{2,1,0:T(8,128)S(1)}, u32[]{:S(2)}, u32[]{:S(2)}) collective-permute-start(f32[2,128,256]{2,1,0:T(8,128)} %halo_rows.1), channel_id=1, source_target_pairs={{0,4},{1,5},{2,6},{3,7},{4,0},{5,1},{6,2},{7,3},{8,12},{9,13},{10,... | collective-permute-start | bytes 786440 | tf_op jit(solution)/shard_map/ppermute | solution.py:230
  10.6 5.6 %collective-permute-done.3.refs_1_ = f32[2,128,256]{2,1,0:T(8,128)S(1)} collective-permute-done((f32[2,128,256]{2,1,0:T(8,128)}, f32[2,128,256]{2,1,0:T(8,128)S(1)}, u32[]{:S(2)}, u32[]{:S(2)}) %collective-permute-start.3) | collective-permute-done | bytes 262176 | tf_op jit(solution)/shard_map/ppermute | solution.py:230
  16.2 0.0 copy-start.12
  16.2 0.7 copy-done.12
  16.9 3.4 %window.1.own_ref = f32[2,256,256]{2,1,0:T(8,128)} custom-call(s32[1,2]{1,0:T(1,128)} %bitcast.14, f32[384,384]{1,0:T(8,128)} %bitcast.9, f32[384,384]{1,0:T(8,128)} %bitcast.12, f32[2,384,128]{2,1,0:T(8,128)} %copy-done.5, f32[2,128,256]{2,1,0:T(8,128)} %copy-done.12), custom_call_target="tpu_custom_call" | custom-call | tf_op jit(solution)/shard_map/window/pallas_call | solution.py:362
  20.3 0.7 collective-permute-start.4
  20.9 3.8 %collective-permute-start.5 = (f32[2,256,256]{2,1,0:T(8,128)}, f32[2,256,256]{2,1,0:T(8,128)S(1)}, u32[]{:S(2)}, u32[]{:S(2)}) collective-permute-start(f32[2,256,256]{2,1,0:T(8,128)} %window.1.own_ref), channel_id=1, source_target_pairs={{10,18},{11,19},{14,22},{15,23},{16,8},{17,9},{20,12},{21,13}} | collective-permute-start | bytes 1572872 | tf_op jit(solution)/shard_map/ppermute | solution.py:230
  24.8 0.7 collective-permute-start.6
  25.5 0.0 collective-permute-done.4.first_ref
  25.5 10.9 %collective-permute-done.5.other_ref = f32[2,256,256]{2,1,0:T(8,128)S(1)} collective-permute-done((f32[2,256,256]{2,1,0:T(8,128)}, f32[2,256,256]{2,1,0:T(8,128)S(1)}, u32[]{:S(2)}, u32[]{:S(2)}) %collective-permute-start.5) | collective-permute-done | bytes 524320 | tf_op jit(solution)/shard_map/ppermute | solution.py:230
  36.4 0.0 collective-permute-done.6.last_ref
  36.4 0.0 copy-done.4
  36.4 0.0 copy-done.3
  36.4 0.0 copy-done.1
  36.4 0.0 copy-start
  36.4 1.0 %copy-done = f32[2,256,256]{2,1,0:T(8,128)S(1)} copy-done((f32[2,256,256]{2,1,0:T(8,128)S(1)}, f32[2,256,256]{2,1,0:T(8,128)}, u32[]{:S(2)}) %copy-start) | copy-done | bytes 524312
  37.5 8.1 %frame.1 = (f32[2,256,256]{2,1,0:T(8,128)S(1)}, f32[2,256,256]{2,1,0:T(8,128)S(1)}, f32[2,256,256]{2,1,0:T(8,128)S(1)}, f32[2,256,256]{2,1,0:T(8,128)S(1)}) custom-call(f32[2,256,256]{2,1,0:T(8,128)S(1)} %collective-permute-done.4.first_ref, f32[2,256,256]{2,1,0:T(8,128)S(1)} %copy-done, f32[2,256,256]{2,1,0:T(8,128)S(1)} %collective-permute-done.5.other_ref, ...), custom_call_target="tpu_custom_call" | custom-call | tf_op jit(solution)/shard_map/frame/pallas_call | solution.py:424
  45.6 0.0 copy-start.2
  45.6 0.8 copy-done.2
  46.4 0.7 collective-permute-start.7
  47.1 1.3 %collective-permute-start.8 = (f32[2,256,256]{2,1,0:T(8,128)S(1)}, f32[2,256,256]{2,1,0:T(8,128)S(1)}, u32[]{:S(2)}, u32[]{:S(2)}) collective-permute-start(f32[2,256,256]{2,1,0:T(8,128)S(1)} %get-tuple-element.16), channel_id=1, source_target_pairs={{8,16},{9,17},{12,20},{13,21},{18,10},{19,11},{22,14},{23,15}} | collective-permute-start | bytes 1572872 | tf_op jit(solution)/shard_map/ppermute | solution.py:230
  48.4 0.7 collective-permute-start.9
  49.1 0.0 collective-permute-done.7.first_ref
  49.1 0.0 copy-start.6
  49.1 12.6 %collective-permute-done.8.other_ref = f32[2,256,256]{2,1,0:T(8,128)S(1)} collective-permute-done((f32[2,256,256]{2,1,0:T(8,128)S(1)}, f32[2,256,256]{2,1,0:T(8,128)S(1)}, u32[]{:S(2)}, u32[]{:S(2)}) %collective-permute-start.8) | collective-permute-done | bytes 524320 | tf_op jit(solution)/shard_map/ppermute | solution.py:230
  61.7 0.0 collective-permute-done.9.last_ref
  61.7 0.0 copy-done.6
  61.7 0.8 copy-done.7
  62.5 0.2 copy-done.8
  62.7 3.0 %parts.1 = (f32[2,192,256]{2,1,0:T(8,128)}, f32[2,192,256]{2,1,0:T(8,128)}, f32[2,128,256]{2,1,0:T(8,128)}, f32[2,128,256]{2,1,0:T(8,128)}) custom-call(s32[1,2]{1,0:T(1,128)} %bitcast.15, f32[2,256,256]{2,1,0:T(8,128)} %copy-done.6, f32[2,256,256]{2,1,0:T(8,128)} %copy-done.2, f32[2,256,256]{2,1,0:T(8,128)} %copy-done.7, f32[2,256,256]{2,1,0:T(8,128)} %copy-done.8), custom_call_target="tpu_custom_call" | custom-call | tf_op jit(solution)/shard_map/parts/pallas_call | solution.py:487
  65.7 0.3 collective-permute-start.10
  66.0 1.3 %collective-permute-start.11 = (f32[2,128,256]{2,1,0:T(8,128)}, f32[2,128,256]{2,1,0:T(8,128)S(1)}, u32[]{:S(2)}, u32[]{:S(2)}) collective-permute-start(f32[2,128,256]{2,1,0:T(8,128)} %get-tuple-element.20), channel_id=1, source_target_pairs={{0,4},{2,6},{5,1},{7,3},{8,12},{10,14},{13,9},{15,11},{16,20},{18,... | collective-permute-start | bytes 786440 | tf_op jit(solution)/shard_map/ppermute | solution.py:230
  67.2 4.1 %collective-permute-start.12 = (f32[2,128,256]{2,1,0:T(8,128)}, f32[2,128,256]{2,1,0:T(8,128)S(1)}, u32[]{:S(2)}, u32[]{:S(2)}) collective-permute-start(f32[2,128,256]{2,1,0:T(8,128)} %get-tuple-element.21), channel_id=1, source_target_pairs={{1,4},{3,6},{4,1},{6,3},{9,12},{11,14},{12,9},{14,11},{17,20},{19,... | collective-permute-start | bytes 786440 | tf_op jit(solution)/shard_map/ppermute | solution.py:230
  71.3 0.0 copy-done.14
  71.3 0.0 copy-done.16
  71.4 0.1 collective-permute-start.1
  71.4 4.4 %collective-permute-done.1.partner_ref = s32[2,2]{1,0:T(2,128)S(1)} collective-permute-done((s32[2,2]{1,0:T(2,128)S(1)}, s32[2,2]{1,0:T(2,128)S(1)}, u32[]{:S(2)}, u32[]{:S(2)}) %collective-permute-start.1) | collective-permute-done | bytes 48 | tf_op jit(solution)/shard_map/ppermute | solution.py:230
  75.9 0.0 collective-permute-done.11.refs_3_
  75.9 0.0 collective-permute-done.12.refs_4_
  75.9 0.0 copy-start.11
  75.9 0.0 collective-permute-done.10.refs_2_
  75.9 0.0 copy-start.9
  75.9 0.5 copy-done.17
  76.5 0.1 copy-done.10
  76.6 0.1 copy-done.11
  76.7 0.2 copy-done.9
  76.8 2.7 %gather_terms.1 = (f32[2,192,384]{2,1,0:T(8,128)}, f32[2,192,128]{2,1,0:T(8,128)}) custom-call(s32[1,2]{1,0:T(1,128)} %bitcast.16, s32[2,2]{1,0:T(2,128)} %copy-done.17, s32[1,2]{1,0:T(1,128)} %copy-done.15, f32[2,192,256]{2,1,0:T(8,128)} %get-tuple-element.18.refs_1_, f32[2,192,256]{2,1,0:T(8,128)} %copy-done.9, f32[2,128,256]{2,1,0:T(8,128)} %copy-done.10, ...), custom_call_target="tpu_custom_call" | custom-call | tf_op jit(solution)/shard_map/gather_terms/pallas_call | solution.py:527
  79.6 7.3 %collective-permute-start.13 = (f32[2,192,128]{2,1,0:T(8,128)}, f32[2,192,128]{2,1,0:T(8,128)S(1)}, u32[]{:S(2)}, u32[]{:S(2)}) collective-permute-start(f32[2,192,128]{2,1,0:T(8,128)} %get-tuple-element.23), channel_id=1, source_target_pairs={{0,2},{1,3},{2,0},{3,1},{4,6},{5,7},{6,4},{7,5},{8,10},{9,11},{10,... | collective-permute-start | bytes 589832 | tf_op jit(solution)/shard_map/ppermute | solution.py:230
  86.9 1.3 %collective-permute-done.13.refs_0_ = f32[2,192,128]{2,1,0:T(8,128)S(1)} collective-permute-done((f32[2,192,128]{2,1,0:T(8,128)}, f32[2,192,128]{2,1,0:T(8,128)S(1)}, u32[]{:S(2)}, u32[]{:S(2)}) %collective-permute-start.13) | collective-permute-done | bytes 196640 | tf_op jit(solution)/shard_map/ppermute | solution.py:230
  88.1 0.7 copy-done.13
  88.8 1.9 %finish.1 = (f32[192,384]{1,0:T(8,128)}, f32[192,384]{1,0:T(8,128)}) custom-call(f32[2,192,384]{2,1,0:T(8,128)} %get-tuple-element.22.middle_ref, f32[2,192,128]{2,1,0:T(8,128)} %copy-done.13), custom_call_target="tpu_custom_call" | custom-call | tf_op jit(solution)/shard_map/finish/pallas_call | solution.py:546
  (8 shorter events, 0.0 us)
Async XLA Ops:
  0.6 35.8 %copy-start.4 = (bf16[2,256,256]{2,1,0:T(8,128)(2,1)S(1)}, bf16[2,256,256]{2,1,0:T(8,128)(2,1)}, u32[]{:S(2)}) copy-start(bf16[2,256,256]{2,1,0:T(8,128)(2,1)} %constant.5.clone.sort) | copy-start | bytes 786436
  0.6 35.8 %copy-start.3 = (s32[1,1,1,256,256]{4,3,2,1,0:T(8,128)S(1)}, s32[1,1,1,256,256]{4,3,2,1,0:T(8,128)}, u32[]{:S(2)}) copy-start(s32[1,1,1,256,256]{4,3,2,1,0:T(8,128)} %param.11) | copy-start | bytes 786436
  0.7 35.8 %copy-start.1 = (f32[2,256,256]{2,1,0:T(8,128)S(1)}, f32[2,256,256]{2,1,0:T(8,128)}, u32[]{:S(2)}) copy-start(f32[2,256,256]{2,1,0:T(8,128)} %probe.1) | copy-start | bytes 1572868
  2.6 3.3 %collective-permute-start.2 = (f32[2,384,128]{2,1,0:T(8,128)}, f32[2,384,128]{2,1,0:T(8,128)S(1)}, u32[]{:S(2)}, u32[]{:S(2)}) collective-permute-start(f32[2,384,128]{2,1,0:T(8,128)} %edge_columns.1), channel_id=1, source_target_pairs={{0,2},{1,3},{2,0},{3,1},{4,6},{5,7},{6,4},{7,5},{8,10},{9,11},{10,... | collective-permute-start | bytes 1179656 | tf_op jit(solution)/shard_map/ppermute | solution.py:230
  3.3 2.5 %collective-permute-start = (s32[1,2]{1,0:T(1,128)}, s32[1,2]{1,0:T(1,128)S(1)}, u32[]{:S(2)}, u32[]{:S(2)}) collective-permute-start(s32[1,2]{1,0:T(1,128)} %bitcast.13), channel_id=1, source_target_pairs={{0,4},{1,5},{2,6},{3,7},{4,0},{5,1},{6,2},{7,3},{8,12},{9,13},{10,... | collective-permute-start | bytes 32 | tf_op jit(solution)/shard_map/ppermute | solution.py:230
  5.8 0.5 copy-start.15
  6.3 0.8 copy-start.5
  9.4 6.8 %collective-permute-start.3 = (f32[2,128,256]{2,1,0:T(8,128)}, f32[2,128,256]{2,1,0:T(8,128)S(1)}, u32[]{:S(2)}, u32[]{:S(2)}) collective-permute-start(f32[2,128,256]{2,1,0:T(8,128)} %halo_rows.1), channel_id=1, source_target_pairs={{0,4},{1,5},{2,6},{3,7},{4,0},{5,1},{6,2},{7,3},{8,12},{9,13},{10,... | collective-permute-start | bytes 786440 | tf_op jit(solution)/shard_map/ppermute | solution.py:230
  16.2 0.7 copy-start.12
  20.3 5.2 %collective-permute-start.4 = (f32[2,256,256]{2,1,0:T(8,128)}, f32[2,256,256]{2,1,0:T(8,128)S(1)}, u32[]{:S(2)}, u32[]{:S(2)}) collective-permute-start(f32[2,256,256]{2,1,0:T(8,128)} %window.1.own_ref), channel_id=1, source_target_pairs={{0,8},{1,9},{2,18},{3,19},{4,12},{5,13},{6,22},{7,23}} | collective-permute-start | bytes 1572872 | tf_op jit(solution)/shard_map/ppermute | solution.py:230
  20.9 15.4 %collective-permute-start.5 = (f32[2,256,256]{2,1,0:T(8,128)}, f32[2,256,256]{2,1,0:T(8,128)S(1)}, u32[]{:S(2)}, u32[]{:S(2)}) collective-permute-start(f32[2,256,256]{2,1,0:T(8,128)} %window.1.own_ref), channel_id=1, source_target_pairs={{10,18},{11,19},{14,22},{15,23},{16,8},{17,9},{20,12},{21,13}} | collective-permute-start | bytes 1572872 | tf_op jit(solution)/shard_map/ppermute | solution.py:230
  24.8 11.6 %collective-permute-start.6 = (f32[2,256,256]{2,1,0:T(8,128)}, f32[2,256,256]{2,1,0:T(8,128)S(1)}, u32[]{:S(2)}, u32[]{:S(2)}) collective-permute-start(f32[2,256,256]{2,1,0:T(8,128)} %window.1.own_ref), channel_id=1, source_target_pairs={{24,8},{25,9},{26,18},{27,19},{28,12},{29,13},{30,22},{31,23}} | collective-permute-start | bytes 1572872 | tf_op jit(solution)/shard_map/ppermute | solution.py:230
  36.4 1.0 %copy-start = (f32[2,256,256]{2,1,0:T(8,128)S(1)}, f32[2,256,256]{2,1,0:T(8,128)}, u32[]{:S(2)}) copy-start(f32[2,256,256]{2,1,0:T(8,128)} %window.1.own_ref) | copy-start | bytes 1572868
  37.5 33.9 %copy-start.14 = (s32[1,1,1,2]{3,2,1,0:T(1,128)S(1)}, s32[1,1,1,2]{3,2,1,0:T(1,128)}, u32[]{:S(2)}) copy-start(s32[1,1,1,2]{3,2,1,0:T(1,128)} %param.10) | copy-start | bytes 28
  37.5 33.9 %copy-start.16 = (s32[1,2]{1,0:T(1,128)S(1)}, s32[1,2]{1,0:T(1,128)}, u32[]{:S(2)}) copy-start(s32[1,2]{1,0:T(1,128)} %copy-done.15) | copy-start | bytes 28
  45.6 0.8 copy-start.2
  46.4 2.7 %collective-permute-start.7 = (f32[2,256,256]{2,1,0:T(8,128)S(1)}, f32[2,256,256]{2,1,0:T(8,128)S(1)}, u32[]{:S(2)}, u32[]{:S(2)}) collective-permute-start(f32[2,256,256]{2,1,0:T(8,128)S(1)} %get-tuple-element.14), channel_id=1, source_target_pairs={{8,0},{9,1},{12,4},{13,5},{18,2},{19,3},{22,6},{23,7}} | collective-permute-start | bytes 1572872 | tf_op jit(solution)/shard_map/ppermute | solution.py:230
  47.1 14.6 %collective-permute-start.8 = (f32[2,256,256]{2,1,0:T(8,128)S(1)}, f32[2,256,256]{2,1,0:T(8,128)S(1)}, u32[]{:S(2)}, u32[]{:S(2)}) collective-permute-start(f32[2,256,256]{2,1,0:T(8,128)S(1)} %get-tuple-element.16), channel_id=1, source_target_pairs={{8,16},{9,17},{12,20},{13,21},{18,10},{19,11},{22,14},{23,15}} | collective-permute-start | bytes 1572872 | tf_op jit(solution)/shard_map/ppermute | solution.py:230
  48.4 13.3 %collective-permute-start.9 = (f32[2,256,256]{2,1,0:T(8,128)S(1)}, f32[2,256,256]{2,1,0:T(8,128)S(1)}, u32[]{:S(2)}, u32[]{:S(2)}) collective-permute-start(f32[2,256,256]{2,1,0:T(8,128)S(1)} %get-tuple-element.17), channel_id=1, source_target_pairs={{8,24},{9,25},{12,28},{13,29},{18,26},{19,27},{22,30},{23,31}} | collective-permute-start | bytes 1572872 | tf_op jit(solution)/shard_map/ppermute | solution.py:230
  49.1 12.6 %copy-start.6 = (f32[2,256,256]{2,1,0:T(8,128)}, f32[2,256,256]{2,1,0:T(8,128)S(1)}, u32[]{:S(2)}) copy-start(f32[2,256,256]{2,1,0:T(8,128)S(1)} %collective-permute-done.7.first_ref) | copy-start | bytes 1572868
  61.7 0.8 copy-start.7
  61.7 1.0 %copy-start.8 = (f32[2,256,256]{2,1,0:T(8,128)}, f32[2,256,256]{2,1,0:T(8,128)S(1)}, u32[]{:S(2)}) copy-start(f32[2,256,256]{2,1,0:T(8,128)S(1)} %collective-permute-done.9.last_ref) | copy-start | bytes 1572868
  65.7 10.2 %collective-permute-start.10 = (f32[2,192,256]{2,1,0:T(8,128)}, f32[2,192,256]{2,1,0:T(8,128)S(1)}, u32[]{:S(2)}, u32[]{:S(2)}) collective-permute-start(f32[2,192,256]{2,1,0:T(8,128)} %get-tuple-element.19), channel_id=1, source_target_pairs={{0,1},{1,0},{2,3},{3,2},{4,5},{5,4},{6,7},{7,6},{8,9},{9,8},{10,11... | collective-permute-start | bytes 1179656 | tf_op jit(solution)/shard_map/ppermute | solution.py:230
  66.0 9.9 %collective-permute-start.11 = (f32[2,128,256]{2,1,0:T(8,128)}, f32[2,128,256]{2,1,0:T(8,128)S(1)}, u32[]{:S(2)}, u32[]{:S(2)}) collective-permute-start(f32[2,128,256]{2,1,0:T(8,128)} %get-tuple-element.20), channel_id=1, source_target_pairs={{0,4},{2,6},{5,1},{7,3},{8,12},{10,14},{13,9},{15,11},{16,20},{18,... | collective-permute-start | bytes 786440 | tf_op jit(solution)/shard_map/ppermute | solution.py:230
  67.2 8.6 %collective-permute-start.12 = (f32[2,128,256]{2,1,0:T(8,128)}, f32[2,128,256]{2,1,0:T(8,128)S(1)}, u32[]{:S(2)}, u32[]{:S(2)}) collective-permute-start(f32[2,128,256]{2,1,0:T(8,128)} %get-tuple-element.21), channel_id=1, source_target_pairs={{1,4},{3,6},{4,1},{6,3},{9,12},{11,14},{12,9},{14,11},{17,20},{19,... | collective-permute-start | bytes 786440 | tf_op jit(solution)/shard_map/ppermute | solution.py:230
  71.4 4.5 %collective-permute-start.1 = (s32[2,2]{1,0:T(2,128)S(1)}, s32[2,2]{1,0:T(2,128)S(1)}, u32[]{:S(2)}, u32[]{:S(2)}) collective-permute-start(s32[2,2]{1,0:T(2,128)S(1)} %pad_add_fusion), channel_id=1, source_target_pairs={{0,1},{1,0},{2,3},{3,2},{4,5},{5,4},{6,7},{7,6},{8,9},{9,8},{10,11... | collective-permute-start | bytes 56 | tf_op jit(solution)/shard_map/ppermute | solution.py:230
  75.9 0.6 copy-start.17
  75.9 0.7 copy-start.10
  75.9 0.8 copy-start.11
  75.9 0.9 %copy-start.9 = (f32[2,192,256]{2,1,0:T(8,128)}, f32[2,192,256]{2,1,0:T(8,128)S(1)}, u32[]{:S(2)}) copy-start(f32[2,192,256]{2,1,0:T(8,128)S(1)} %collective-permute-done.10.refs_2_) | copy-start | bytes 1179652
  79.6 8.6 %collective-permute-start.13 = (f32[2,192,128]{2,1,0:T(8,128)}, f32[2,192,128]{2,1,0:T(8,128)S(1)}, u32[]{:S(2)}, u32[]{:S(2)}) collective-permute-start(f32[2,192,128]{2,1,0:T(8,128)} %get-tuple-element.23), channel_id=1, source_target_pairs={{0,2},{1,3},{2,0},{3,1},{4,6},{5,7},{6,4},{7,5},{8,10},{9,11},{10,... | collective-permute-start | bytes 589832 | tf_op jit(solution)/shard_map/ppermute | solution.py:230
  88.1 0.7 copy-start.13

commit v2 on v1

v2 whole, which is shorter than its diff:
```python
import math

import jax
import jax.numpy as jnp
import ml_dtypes
import numpy as np
from jax import lax
from jax.experimental import pallas as pl
from jax.experimental.pallas import tpu as pltpu
from jax.sharding import PartitionSpec as P

HALO = 128
LANES = 128
AXES = ("section", "tile", "rep")

dead_time = 0.1
background = 0.1
loss_weight = 0.1
fresnel = 0.5

f32 = jnp.float32
bf16 = jnp.bfloat16

SMEM = pl.BlockSpec(memory_space=pltpu.SMEM)
VMEM = pl.BlockSpec(memory_space=pltpu.VMEM)
HBM = pl.BlockSpec(memory_space=pltpu.HBM)


def two_parts(matrix):
    high = matrix.astype(ml_dtypes.bfloat16)
    low = (matrix - high.astype(np.float64)).astype(ml_dtypes.bfloat16)
    return np.stack([high, low])


def from_left(matrix):
    return np.block([[matrix.real, -matrix.imag], [matrix.imag, matrix.real]])


def from_right(matrix):
    return np.block([[matrix.real, matrix.imag], [-matrix.imag, matrix.real]])


def wave_tables(length):
    half = length // 2
    indices = np.arange(length)
    shifted = np.where(indices < half, indices, indices - length)
    kernel = np.exp(1j * math.pi * fresnel * shifted.astype(np.float64) ** 2 / length)
    spread = np.fft.ifft(kernel)
    circulant = spread[(indices[:, None] - indices[None, :]) % length]
    first, second = circulant[:half, :half], circulant[:half, half:]
    plus, minus = (first + second) / 2, (first - second) / 2
    near = [from_left(plus), from_left(minus), from_right(plus), from_right(minus)]
    turns = np.outer(indices[:half], indices[:half]) % half
    even = np.exp(-2j * math.pi * turns / half) / math.sqrt(length)
    odd = even * np.exp(-2j * math.pi * indices[:half] / length)[None, :]
    far = [from_left(even), from_left(odd), from_right(even.T), from_right(odd.T)]
    back = [from_left(even.T), from_left(odd.T), from_right(even), from_right(odd)]
    sort = np.zeros((length, length))
    sort[np.arange(half), 2 * np.arange(half)] = 1
    sort[half + np.arange(half), 2 * np.arange(half) + 1] = 1
    tables = np.stack([two_parts(m) for m in near + far + back])
    return tables, np.stack([sort, sort.T]).astype(ml_dtypes.bfloat16)


def fitted(function, degree):
    top = math.pi**2
    fit = np.polynomial.chebyshev.Chebyshev.interpolate(function, degree, domain=[0.0, top])
    return [float(c) for c in fit.convert(kind=np.polynomial.Polynomial).coef]


def sine_ratio(u):
    angle = np.sqrt(np.maximum(u, 1e-12))
    return np.sin(angle) / angle


SINE = fitted(sine_ratio, 8)
COSINE = fitted(lambda u: np.cos(np.sqrt(np.maximum(u, 0.0))), 8)


def polynomial(coefficients, u):
    total = jnp.full_like(u, coefficients[-1])
    for c in coefficients[-2::-1]:
        total = total * u + c
    return total


def cos_sin(angle):
    square = angle * angle
    return polynomial(COSINE, square), angle * polynomial(SINE, square)


def halves(value):
    high = value.astype(bf16)
    return high, (value - high.astype(f32)).astype(bf16)


def dot(a, b):
    return jnp.dot(a, b, preferred_element_type=f32)


def left_by(tables, index, value):
    high, low = halves(value)
    return dot(tables[index, 0], high) + dot(tables[index, 1], high) + dot(tables[index, 0], low)


def right_by(tables, index, value):
    high, low = halves(value)
    return dot(high, tables[index, 0]) + dot(high, tables[index, 1]) + dot(low, tables[index, 0])


def propagate(tables, at, re, im, fold, unfold):
    half = re.shape[0] // 2
    re0, re1, im0, im1 = re[:half], re[half:], im[:half], im[half:]
    if fold:
        re0, re1, im0, im1 = re0 + re1, re0 - re1, im0 + im1, im0 - im1
    first = left_by(tables, at, jnp.concatenate([re0, im0], 0))
    second = left_by(tables, at + 1, jnp.concatenate([re1, im1], 0))
    if unfold:
        first, second = first + second, first - second
    re = jnp.concatenate([first[:half], second[:half]], 0)
    im = jnp.concatenate([first[half:], second[half:]], 0)
    re0, re1, im0, im1 = re[:, :half], re[:, half:], im[:, :half], im[:, half:]
    if fold:
        re0, re1, im0, im1 = re0 + re1, re0 - re1, im0 + im1, im0 - im1
    first = right_by(tables, at + 2, jnp.concatenate([re0, im0], 1))
    second = right_by(tables, at + 3, jnp.concatenate([re1, im1], 1))
    if unfold:
        first, second = first + second, first - second
    re = jnp.concatenate([first[:, :half], second[:, :half]], 1)
    im = jnp.concatenate([first[:, half:], second[:, half:]], 1)
    return re, im


def near_field(tables, re, im):
    return propagate(tables, 0, re, im, True, True)


def far_field(tables, re, im):
    return propagate(tables, 4, re, im, True, False)


def far_back(tables, re, im):
    return propagate(tables, 8, re, im, False, True)


def likelihood_seed(far_re, far_im, observed):
    intensity = far_re * far_re + far_im * far_im
    shifted_total = intensity + background
    denominator = 1.0 + dead_time * shifted_total
    model_rate = shifted_total / denominator
    slope_term = loss_weight * (1.0 - observed / model_rate) / (denominator * denominator)
    return (2.0 * slope_term * far_re, 2.0 * slope_term * far_im)


def in_band(index, offset, band):
    cell = index + (band // 2) * (2 * HALO)
    return (cell >= offset) & (cell < offset + 2 * HALO)


def lane_index(shape):
    return lax.broadcasted_iota(jnp.int32, shape, len(shape) - 1)


def row_index(shape):
    return lax.broadcasted_iota(jnp.int32, shape, len(shape) - 2)


def choose_columns(bands, offset):
    lane = lane_index(bands[1].shape)
    first = jnp.where(
        in_band(lane, offset, 0), bands[0], jnp.where(in_band(lane, offset, 2), bands[2], bands[4])
    )
    second = jnp.where(in_band(lane + HALO, offset, 1), bands[1], bands[3])
    return jnp.concatenate([first, second], 1)


def part_of_band(value, offset, band):
    start = (band % 2) * HALO
    half = value[:, start : start + HALO]
    return jnp.where(in_band(lane_index(half.shape) + start, offset, band), half, 0.0)


class Copies:
    def __init__(self, semaphores):
        self.semaphores = semaphores
        self.count = 0

    def start(self, source, target):
        copy = pltpu.make_async_copy(source, target, self.semaphores.at[self.count])
        self.count += 1
        copy.start()
        return copy


def wait_for(copies):
    for copy in copies:
        copy.wait()


class Place:
    def __init__(self, grid_side):
        self.grid_side = grid_side
        self.ways = 1 if grid_side == 2 else 2

    def section(self):
        return lax.axis_index("section")

    def rep(self):
        return lax.axis_index("rep")

    def row(self):
        return lax.axis_index("tile") // self.grid_side

    def column(self):
        return lax.axis_index("tile") % self.grid_side

    def owner(self):
        return 1 + self.column() % 2

    def sent(self, index, way):
        return 1 - index if self.ways == 1 else way

    def received(self, index, way):
        return 1 - index if self.ways == 1 else 1 - way


def solution(mesh):
    sections, tiles, reps = (mesh.shape[a] for a in AXES)
    grid_side = math.isqrt(tiles)
    place = Place(grid_side)
    ways = place.ways

    def everywhere(target_of):
        pairs = []
        for s in range(sections):
            for t in range(tiles):
                for r in range(reps):
                    target = target_of(s, t // grid_side, t % grid_side, r)
                    if target is None:
                        continue
                    ts, ty, tx, tr = target
                    if not (0 <= ty < grid_side and 0 <= tx < grid_side):
                        continue
                    pairs.append(
                        ((s * tiles + t) * reps + r, (ts * tiles + ty * grid_side + tx) * reps + tr)
                    )
        return pairs

    def move(value, target_of):
        return lax.ppermute(value, AXES, everywhere(target_of))

    def trade_rows(values):
        if ways == 1:
            return [move(values[0], lambda s, y, x, r: (s, 1 - y, x, r))]
        return [
            move(values[0], lambda s, y, x, r: (s, y - 1, x, r)),
            move(values[1], lambda s, y, x, r: (s, y + 1, x, r)),
        ]

    def trade_columns(values):
        if ways == 1:
            return [move(values[0], lambda s, y, x, r: (s, y, 1 - x, r))]
        return [
            move(values[0], lambda s, y, x, r: (s, y, x - 1, r)),
            move(values[1], lambda s, y, x, r: (s, y, x + 1, r)),
        ]

    def owner_of(x):
        return 1 + x % 2

    def shards(phase_shift, absorption, probe_wave, positions, counts):
        width = phase_shift.shape[2]
        frame = probe_wave.shape[1]
        half_rows = width // reps
        phase = phase_shift.reshape(width, width)
        absorb = absorption.reshape(width, width)
        spot = positions.reshape(1, 2)
        observed = counts.reshape(frame, frame)
        sds = jax.ShapeDtypeStruct
        small = pltpu.CompilerParams(vmem_limit_bytes=8 << 20)

        spots_rows = trade_rows([spot] * ways)
        spots_rep = move(
            jnp.concatenate([spot] + spots_rows, 0), lambda s, y, x, r: (s, y, x, 1 - r)
        )

        def edge(value, way):
            start = place.sent(place.column(), way) * (width - HALO)
            return lax.dynamic_slice_in_dim(value, start, HALO, 1)

        sides = [
            side
            for value in (phase, absorb)
            for side in trade_columns([edge(value, way) for way in range(ways)])
        ]

        def rows_of(refs, plane, rows):
            sides_here = [refs[2 + plane * ways + way][rows, :] for way in range(ways)]
            return refs[plane][rows, :], sides_here

        def bands_of(tile, margin):
            inner = [tile[:, i * HALO : (i + 1) * HALO] for i in range(3)]
            ends = []
            for side in range(2):
                if ways == 1:
                    there = place.received(place.column(), 0) == side
                    ends.append(jnp.where(there, margin[0], 0.0))
                else:
                    there = place.column() > 0 if side == 0 else place.column() < grid_side - 1
                    ends.append(jnp.where(there, margin[1 - side], 0.0))
            return [ends[0], *inner, ends[1]]

        def transmission(angle, loss):
            cosine, sine = cos_sin(angle)
            damping = jnp.exp(-loss)
            return damping * cosine, damping * sine

        def strip_kernel(*refs):
            loaded, spot_refs = refs[: 2 + 2 * ways], refs[2 + 2 * ways : 2 + 3 * ways]
            outs = refs[2 + 3 * ways :]
            for way in range(ways):
                below = place.sent(place.row(), way)
                rows = pl.ds(pl.multiple_of(below * (width - HALO), 8), HALO)
                column = spot_refs[way if ways == 1 else 1 - way][0, 1]
                cut = [
                    choose_columns(bands_of(*rows_of(loaded, plane, rows)), column)
                    for plane in range(2)
                ]
                outs[way][0], outs[way][1] = transmission(*cut)

        strips = pl.pallas_call(
            strip_kernel,
            out_shape=[sds((2, HALO, frame), f32)] * ways,
            in_specs=[VMEM] * (2 + 2 * ways) + [SMEM] * ways,
            out_specs=[VMEM] * ways,
            compiler_params=small,
            name="halo_rows",
        )(phase, absorb, *sides, *spots_rows)
        rims = trade_rows(strips)

        def window_kernel(spot_ref, *refs):
            loaded, (whole, part) = refs[:-2], refs[-2:]
            row, column = spot_ref[0, 0], spot_ref[0, 1]
            index = row_index((HALO, HALO))
            upper = in_band(index + HALO, row, 1)
            planes = []
            for plane in range(2):
                first = bands_of(*rows_of(loaded, plane, slice(0, HALO)))
                third = bands_of(*rows_of(loaded, plane, slice(2 * HALO, 3 * HALO)))
                bands = [jnp.where(upper, v, w) for v, w in zip(first, third)]
                planes.append(choose_columns(bands, column))
            whole[0], whole[1] = transmission(*planes)
            planes = []
            for plane in range(2):
                bands = bands_of(*rows_of(loaded, plane, slice(HALO, 2 * HALO)))
                planes.append(choose_columns(bands, column))
            real, imag = transmission(*planes)
            inside = in_band(row_index((HALO, frame)), row, 2)
            part[0], part[1] = jnp.where(inside, real, 1.0), jnp.where(inside, imag, 0.0)

        whole, part = pl.pallas_call(
            window_kernel,
            out_shape=[sds((2, HALO, frame), f32)] * 2,
            in_specs=[SMEM] + [VMEM] * (2 + 2 * ways),
            out_specs=[VMEM] * 2,
            compiler_params=small,
            name="window",
        )(spot, phase, absorb, *sides)

        def to_owner(value):
            return [
                move(
                    value,
                    lambda s, y, x, r: (owner_of(x), y, x, r) if s == section_of(x) else None,
                )
                for section_of in (lambda x: 0, lambda x: 3 - owner_of(x), lambda x: 3)
            ]

        wholes = to_owner(whole)

        def join_kernel(spot_ref, part_ref, *refs):
            rim_refs, out = refs[:ways], refs[ways]
            row = spot_ref[0, 0]
            index = row_index((HALO, frame))
            out[...] = part_ref[...]
            for way in range(ways):
                side = place.received(place.row(), way)
                there = jnp.where(side == 0, place.row() > 0, place.row() < grid_side - 1)
                shifted = index + jnp.where(side == 0, 0, 2 * (2 * HALO))
                near = (shifted >= row) & (shifted < row + jnp.where(there, 2 * HALO, 0))
                for plane in range(2):
                    out[plane] = jnp.where(near, rim_refs[way][plane], out[plane])

        joined = pl.pallas_call(
            join_kernel,
            out_shape=sds((2, HALO, frame), f32),
            in_specs=[SMEM] + [VMEM] * (1 + ways),
            out_specs=VMEM,
            compiler_params=small,
            name="join",
        )(spot, part, *rims)
        joineds = to_owner(joined)

        tables, sort = wave_tables(frame)

        def prepare_kernel(spot_ref, probe, seen, sort, rolled, counted):
            row, column = lax.rem(spot_ref[0, 0], frame), lax.rem(spot_ref[0, 1], frame)
            for plane in range(2):
                rolled[plane] = pltpu.roll(pltpu.roll(probe[plane], row, 0), column, 1)
            first = dot(sort[0], seen[...].astype(f32).astype(bf16)).astype(bf16)
            counted[...] = dot(first, sort[1])

        rolled, counted = pl.pallas_call(
            prepare_kernel,
            out_shape=[sds((2, frame, frame), f32), sds((frame, frame), f32)],
            in_specs=[SMEM] + [VMEM] * 3,
            out_specs=[VMEM] * 2,
            compiler_params=small,
            name="prepare",
        )(spot, probe_wave, observed, sort)

        def frame_kernel(probe, seen, tables, *refs):
            whole_refs, joined_refs, outs = refs[:4], refs[4:8], refs[8:12]
            fields, exits = refs[12:]
            own_is_second = place.owner() == 1
            for half, parts in ((slice(HALO, None), whole_refs), (slice(None, HALO), joined_refs)):
                for plane in range(2):
                    own, other = parts[1][plane], parts[2][plane]
                    fields[0, plane, half] = parts[0][plane]
                    fields[1, plane, half] = jnp.where(own_is_second, own, other)
                    fields[2, plane, half] = jnp.where(own_is_second, other, own)
                    fields[3, plane, half] = parts[3][plane]
            re, im = probe[0], probe[1]
            for number in range(4):
                o_re, o_im = fields[number, 0], fields[number, 1]
                exit_re, exit_im = o_re * re - o_im * im, o_re * im + o_im * re
                exits[number, 0], exits[number, 1] = exit_re, exit_im
                if number < 3:
                    re, im = near_field(tables, exit_re, exit_im)
            re, im = far_field(tables, exit_re, exit_im)
            re, im = likelihood_seed(re, im, seen[...])
            im = -im
            for number in reversed(range(4)):
                if number == 3:
                    re, im = far_back(tables, re, im)
                else:
                    re, im = near_field(tables, re, im)
                exit_re, exit_im = exits[number, 0], exits[number, 1]
                phase_term = -(re * exit_im + im * exit_re)
                absorb_term = im * exit_im - re * exit_re
                if number > 0:
                    o_re, o_im = fields[number, 0], fields[number, 1]
                    re, im = o_re * re - o_im * im, o_re * im + o_im * re
                if number in (0, 3):
                    outs[number][0], outs[number][1] = phase_term, absorb_term
                elif number == 2:
                    exits[2, 0], exits[2, 1] = phase_term, absorb_term
                else:
                    for plane, term in enumerate((phase_term, absorb_term)):
                        kept_term = exits[2, plane]
                        outs[1][plane] = jnp.where(own_is_second, term, kept_term)
                        outs[2][plane] = jnp.where(own_is_second, kept_term, term)

        terms = pl.pallas_call(
            frame_kernel,
            out_shape=[sds((2, frame, frame), f32)] * 4,
            in_specs=[VMEM] * 11,
            out_specs=[VMEM] * 4,
            scratch_shapes=[
                pltpu.VMEM((4, 2, frame, frame), f32),
                pltpu.VMEM((4, 2, frame, frame), f32),
            ],
            compiler_params=pltpu.CompilerParams(vmem_limit_bytes=16 << 20),
            name="frame",
        )(
            rolled, counted, tables,
            wholes[0], whole, wholes[1], wholes[2],
            joineds[0], joined, joineds[1], joineds[2],
        )

        def from_owner(value, section_of):
            return move(
                value,
                lambda s, y, x, r: (section_of(x), y, x, r) if s == owner_of(x) else None,
            )

        back = (
            from_owner(terms[0], lambda x: 0),
            terms[1],
            from_owner(terms[2], lambda x: 3 - owner_of(x)),
            from_owner(terms[3], lambda x: 3),
        )

        def load_term(refs, term):
            section, owner = place.section(), place.owner()
            choice = jnp.where(
                section == 0, 0, jnp.where(section == 3, 3, jnp.where(section == owner, 1, 2))
            )
            for number, ref in enumerate(refs):

                @pl.when(choice == number)
                def _():
                    term[...] = ref[...]

        def rows_for(term, plane, row, rep):
            index = row_index((frame, frame))
            middle = jnp.where(in_band(index, row, 2), term[plane], 0.0)
            later = middle[HALO // 2 :]
            earlier = jnp.where(in_band(index, row, 0), term[plane], 0.0)
            earlier = jnp.concatenate([earlier[HALO:], middle[: HALO // 2]], 0)
            return jnp.where(rep == 0, earlier, later)

        def parts_kernel(spot_ref, *refs):
            back_refs, (give, straight, across, term) = refs[:4], refs[4:]
            load_term(back_refs, term)
            rep, row = place.rep(), spot_ref[0, 0]
            index = row_index((HALO, frame))
            for plane in range(2):
                give[plane] = rows_for(term, plane, row, 1 - rep)
                first = term[plane, :HALO]
                above = jnp.where(in_band(index, row, 0), first, 0.0)
                below = jnp.where(in_band(index, row, 4), first, 0.0)
                straight[plane] = jnp.where(rep == 1, above, below)
                across[plane] = jnp.where(rep == 1, below, above)

        give, straight, across = pl.pallas_call(
            parts_kernel,
            out_shape=[sds((2, half_rows, frame), f32)] + [sds((2, HALO, frame), f32)] * 2,
            in_specs=[SMEM] + [VMEM] * 4,
            out_specs=[VMEM] * 3,
            scratch_shapes=[pltpu.VMEM((2, frame, frame), f32)],
            compiler_params=small,
            name="parts",
        )(spot, *back)

        given = move(give, lambda s, y, x, r: (s, y, x, 1 - r))
        came_straight = move(straight, lambda s, y, x, r: (s, y + 1 - 2 * r, x, r))
        came_across = move(across, lambda s, y, x, r: (s, y - 1 + 2 * r, x, 1 - r))

        def keep_kernel(spot_ref, *refs):
            back_refs, (mine, term) = refs[:4], refs[4:]
            load_term(back_refs, term)
            for plane in range(2):
                mine[plane] = rows_for(term, plane, spot_ref[0, 0], place.rep())

        kept = pl.pallas_call(
            keep_kernel,
            out_shape=sds((2, half_rows, frame), f32),
            in_specs=[SMEM] + [VMEM] * 4,
            out_specs=VMEM,
            scratch_shapes=[pltpu.VMEM((2, frame, frame), f32)],
            compiler_params=small,
            cost_estimate=pl.CostEstimate(flops=1 << 22, bytes_accessed=1 << 21, transcendentals=0),
            name="keep",
        )(spot, *back)

        def add_band(band, plane, refs):
            spot_ref, partner_ref, kept_ref, *spot_refs = refs[: 3 + ways]
            given, straight, across = refs[3 + ways : count]
            rep = place.rep()
            if ways == 1:
                straight_column, across_column = spot_refs[0][0, 1], partner_ref[1, 1]
            else:
                straight_column = jnp.where(rep == 1, spot_refs[0][0, 1], spot_refs[1][0, 1])
                across_column = jnp.where(rep == 1, partner_ref[1, 1], partner_ref[2, 1])
            total = part_of_band(kept_ref[plane], spot_ref[0, 1], band)
            total += part_of_band(given[plane], partner_ref[0, 1], band)
            strip = part_of_band(straight[plane], straight_column, band)
            strip += part_of_band(across[plane], across_column, band)
            gap = jnp.zeros((half_rows - HALO, HALO), f32)
            early, late = jnp.concatenate([strip, gap], 0), jnp.concatenate([gap, strip], 0)
            return total + jnp.where(rep == 1, late, early)

        pieces = (spot, spots_rep, kept, *spots_rows, given, came_straight, came_across)
        piece_specs = [SMEM, SMEM, VMEM] + [SMEM] * ways + [VMEM] * 3
        count = len(piece_specs)

        def edge_kernel(*refs):
            for way in range(ways):
                for plane in range(2):
                    if ways == 1:
                        value = jnp.where(
                            place.column() == 0,
                            add_band(4, plane, refs),
                            add_band(0, plane, refs),
                        )
                    else:
                        value = add_band(4 * way, plane, refs)
                    refs[count + way][plane] = value

        leaving = pl.pallas_call(
            edge_kernel,
            out_shape=[sds((2, half_rows, HALO), f32)] * ways,
            in_specs=piece_specs,
            out_specs=[VMEM] * ways,
            compiler_params=small,
            name="edge_terms",
        )(*pieces)
        arrived = trade_columns(leaving)

        def inner_kernel(*refs):
            outs, inner, total, semaphores = refs[count : count + 2], *refs[count + 2 :]
            copies = Copies(semaphores)
            started = []
            for plane in range(2):
                bands = [add_band(band, plane, refs) for band in (1, 2, 3)]
                for number, value in enumerate(bands):
                    total[plane, :, number * HALO : (number + 1) * HALO] = value
                started.append(copies.start(total.at[plane], outs[plane]))
                for way in range(ways):
                    first = place.received(place.column(), way) == 0
                    inner[way, plane] = jnp.where(first, bands[0], bands[2])
            wait_for(started)

        *results, inner = pl.pallas_call(
            inner_kernel,
            out_shape=[sds((half_rows, width), f32)] * 2
            + [sds((ways, 2, half_rows, HALO), f32)],
            in_specs=piece_specs,
            out_specs=[HBM] * 2 + [VMEM],
            scratch_shapes=[
                pltpu.VMEM((2, half_rows, width), f32),
                pltpu.SemaphoreType.DMA((2,)),
            ],
            compiler_params=small,
            cost_estimate=pl.CostEstimate(flops=1 << 22, bytes_accessed=1 << 21, transcendentals=0),
            name="inner_terms",
        )(*pieces)

        def finish_kernel(phase_in, absorb_in, inner_ref, *refs):
            arrived_refs, outs = refs[:ways], refs[ways : ways + 2]
            strips, semaphores = refs[ways + 2 :]
            copies = Copies(semaphores)
            leaving = []
            for way in range(ways):
                start = place.received(place.column(), way) * (width - HALO)
                for plane in range(2):
                    strips[way, plane] = arrived_refs[way][plane] + inner_ref[way, plane]
                    target = outs[plane].at[:, pl.ds(pl.multiple_of(start, LANES), HALO)]
                    leaving.append(copies.start(strips.at[way, plane], target))
            wait_for(leaving)

        result = pl.pallas_call(
            finish_kernel,
            out_shape=[sds((half_rows, width), f32)] * 2,
            in_specs=[HBM, HBM, VMEM] + [VMEM] * ways,
            out_specs=[HBM] * 2,
            scratch_shapes=[
                pltpu.VMEM((ways, 2, half_rows, HALO), f32),
                pltpu.SemaphoreType.DMA((2 * ways,)),
            ],
            input_output_aliases={0: 0, 1: 1},
            compiler_params=small,
            name="finish",
        )(*results, inner, *arrived)
        return tuple(plane[None, None] for plane in result)

    in_specs = (
        P("section", "tile", None, None),
        P("section", "tile", None, None),
        P(),
        P("tile", "rep", None, None),
        P("tile", "rep", None, None, None),
    )
    out_specs = (P("section", "tile", "rep", None), P("section", "tile", "rep", None))
    return jax.shard_map(shards, mesh=mesh, in_specs=in_specs, out_specs=out_specs, check_vma=False)
```

time: 91.2 us -> 74 us (0.81)
  waiting for transfers between devices: 36.1 us -> 21.3 us
  Pallas kernels: 23.3 us -> 13.7 us
  starting transfers between devices: 24 us -> 30.6 us
    ppermute x14 -> x18, waiting for transfers between devices: 36.1 us -> 21.3 us  [move(): return lax.ppermute(value, AXES, everywhere(target_of))]
    ppermute x14 -> x18, starting transfers between devices: 24 us -> 30.6 us  [move(): return lax.ppermute(value, AXES, everywhere(target_of))]
    pallas_call x3 -> x6, Pallas kernels: 8 us -> 5.29 us  [the longest x1 1.46 us: shards(): pl.pallas_call(inner_kernel, out_shape=[sds((half_rows, width), f32)] * 2...]
    pallas_call x1, Pallas kernels: 3 us -> 0.77 us  [shards(): pl.pallas_call(parts_kernel, out_shape=[sds((2, half_rows, frame), f32)]...]
    pallas_call x1, Pallas kernels: 8.12 us -> 6.17 us  [shards(): pl.pallas_call(frame_kernel, out_shape=[sds((2, frame, frame), f32)] * 4,...]
    dynamic_slice x0 -> x2, local copies, waits for them, and re-layouts: none -> 1.95 us  [edge(): return lax.dynamic_slice_in_dim(value, start, HALO, 1)]
    pallas_call x1, Pallas kernels: 2.28 us -> 0.76 us  [shards(): pl.pallas_call(strip_kernel, out_shape=[sds((2, HALO, frame), f32)] * way...]
    unnamed x36 -> x20, local copies, waits for them, and re-layouts: 6.37 us -> 4.93 us
  transfers between devices with their start and end apart: 14 -> 18, of which waited for: 6 -> 6; matrix products, arithmetic and copies ran while one was open for 0% -> 1% of each run, Pallas kernels for 0% -> 6%
where the time goes in v2:
time: 74 us; the launch traced here: 73.4 us
  starting transfers between devices  30.6 us (41%)
  waiting for transfers between devices  21.3 us (29%)
  Pallas kernels  13.7 us (19%)
  local copies, waits for them, and re-layouts  6.88 us (9%)
  between operations  0.93 us (1%)
    ppermute x18, starting transfers between devices, move(): return lax.ppermute(value, AXES, everywhere(target_of))  30.6 us
    ppermute x18, waiting for transfers between devices, move(): return lax.ppermute(value, AXES, everywhere(target_of))  21.3 us
    pallas_call x1, Pallas kernels, shards(): pl.pallas_call(frame_kernel, out_shape=[sds((2, frame, frame), f32)] * 4,...  6.17 us
    unnamed x20, local copies, waits for them, and re-layouts  4.93 us
    dynamic_slice x2, local copies, waits for them, and re-layouts, edge(): return lax.dynamic_slice_in_dim(value, start, HALO, 1)  1.95 us
  transfers between devices with their start and end apart: 18, of which 6 were waited for; matrix products, arithmetic and copies ran while one was open for 1% of the time, Pallas kernels for 6%

profile of v2, /device:TPU:13, one launch (start us, length us, event | category | flops | bytes accessed | tf_op | source)
XLA Modules:
  0.0 73.4 jit_solution(12929675871214682846)
XLA Ops:
  0.6 0.0 copy-start.6
  0.6 0.0 copy-start.5
  0.7 1.0 %dynamic-slice_bitcast_fusion.1 = f32[384,128]{1,0:T(8,128)S(1)} fusion(f32[1,1,384,384]{3,2,1,0:T(8,128)} %param.7, s32[]{:T(128)S(6)} %select_n.14), kind=kLoop, calls=%fused_computation.1 | loop fusion | bytes 393220 | tf_op jit(solution)/shard_map/dynamic_slice | solution.py:289
  1.7 0.7 %collective-permute-start.2 = (f32[384,128]{1,0:T(8,128)S(1)}, f32[384,128]{1,0:T(8,128)S(1)}, u32[]{:S(2)}, u32[]{:S(2)}) collective-permute-start(f32[384,128]{1,0:T(8,128)S(1)} %dynamic-slice_bitcast_fusion.1), channel_id=1, source_target_pairs={{0,2},{1,3},{2,0},{3,1},{4,6},{5,7},{6,4},{7,5},{8,10},{9,11},{10,... | collective-permute-start | bytes 589832 | tf_op jit(solution)/shard_map/ppermute | solution.py:250
  2.4 0.9 %dynamic-slice_bitcast_fusion = f32[384,128]{1,0:T(8,128)S(1)} fusion(f32[1,1,384,384]{3,2,1,0:T(8,128)} %param.8, s32[]{:T(128)S(6)} %select_n.14), kind=kLoop, calls=%fused_computation | loop fusion | bytes 393220 | tf_op jit(solution)/shard_map/dynamic_slice | solution.py:289
  3.4 0.1 collective-permute-start.3
  3.5 1.3 %collective-permute-start = (s32[1,2]{1,0:T(1,128)}, s32[1,2]{1,0:T(1,128)S(1)}, u32[]{:S(2)}, u32[]{:S(2)}) collective-permute-start(s32[1,2]{1,0:T(1,128)} %bitcast.15), channel_id=1, source_target_pairs={{0,4},{1,5},{2,6},{3,7},{4,0},{5,1},{6,2},{7,3},{8,12},{9,13},{10,... | collective-permute-start | bytes 32 | tf_op jit(solution)/shard_map/ppermute | solution.py:250
  4.7 1.3 %collective-permute-done.refs_4_.refs_3_ = s32[1,2]{1,0:T(1,128)S(1)} collective-permute-done((s32[1,2]{1,0:T(1,128)}, s32[1,2]{1,0:T(1,128)S(1)}, u32[]{:S(2)}, u32[]{:S(2)}) %collective-permute-start) | collective-permute-done | bytes 40 | tf_op jit(solution)/shard_map/ppermute | solution.py:250
  6.0 0.0 collective-permute-done.2.refs_2_
  6.0 0.0 collective-permute-done.3.refs_3_
  6.0 0.0 copy-start
  6.0 1.1 %copy-done = f32[1,1,384,384]{3,2,1,0:T(8,128)S(1)} copy-done((f32[1,1,384,384]{3,2,1,0:T(8,128)S(1)}, f32[1,1,384,384]{3,2,1,0:T(8,128)}, u32[]{:S(2)}) %copy-start) | copy-done | bytes 589848
  7.1 0.0 copy-start.2
  7.1 1.1 %copy-done.2 = f32[1,1,384,384]{3,2,1,0:T(8,128)S(1)} copy-done((f32[1,1,384,384]{3,2,1,0:T(8,128)S(1)}, f32[1,1,384,384]{3,2,1,0:T(8,128)}, u32[]{:S(2)}) %copy-start.2) | copy-done | bytes 589848
  8.2 0.0 copy-start.7
  8.2 0.8 %halo_rows.1 = f32[2,128,256]{2,1,0:T(8,128)S(1)} custom-call(f32[384,384]{1,0:T(8,128)S(1)} %bitcast.10, f32[384,384]{1,0:T(8,128)S(1)} %bitcast.12, f32[384,128]{1,0:T(8,128)S(1)} %collective-permute-done.2.refs_2_, f32[384,128]{1,0:T(8,128)S(1)} %collective-permute-done.3.refs_3_, s32[1,2]{1,0:T(1,128)S(1)} %collective-permute-done.refs_4_.refs_3_), custom_call_target="tpu_custom_call" | custom-call | tf_op jit(solution)/shard_map/halo_rows/pallas_call | solution.py:331
  8.9 1.3 %collective-permute-start.7 = (f32[2,128,256]{2,1,0:T(8,128)S(1)}, f32[2,128,256]{2,1,0:T(8,128)S(1)}, u32[]{:S(2)}, u32[]{:S(2)}) collective-permute-start(f32[2,128,256]{2,1,0:T(8,128)S(1)} %halo_rows.1), channel_id=1, source_target_pairs={{0,4},{1,5},{2,6},{3,7},{4,0},{5,1},{6,2},{7,3},{8,12},{9,13},{10,... | collective-permute-start | bytes 786440 | tf_op jit(solution)/shard_map/ppermute | solution.py:250
  10.2 1.1 %copy-done.1 = f32[1,1,384,384]{3,2,1,0:T(8,128)S(1)} copy-done((f32[1,1,384,384]{3,2,1,0:T(8,128)S(1)}, f32[1,1,384,384]{3,2,1,0:T(8,128)}, u32[]{:S(2)}) %copy-start.1) | copy-done | bytes 589848
  11.3 1.1 %copy-done.3 = f32[1,1,384,384]{3,2,1,0:T(8,128)S(1)} copy-done((f32[1,1,384,384]{3,2,1,0:T(8,128)S(1)}, f32[1,1,384,384]{3,2,1,0:T(8,128)}, u32[]{:S(2)}) %copy-start.3) | copy-done | bytes 589848
  12.3 0.7 copy-done.8
  13.0 1.0 %window.1 = (f32[2,128,256]{2,1,0:T(8,128)S(1)}, f32[2,128,256]{2,1,0:T(8,128)S(1)}) custom-call(s32[1,2]{1,0:T(1,128)S(1)} %bitcast.16, f32[384,384]{1,0:T(8,128)S(1)} %bitcast.11, f32[384,384]{1,0:T(8,128)S(1)} %bitcast.13, f32[384,128]{1,0:T(8,128)S(1)} %collective-permute-done.2.refs_2_, f32[384,128]{1,0:T(8,128)S(1)} %collective-permute-done.3.refs_3_), custom_call_target="tpu_custom_call" | custom-call | tf_op jit(solution)/shard_map/window/pallas_call | solution.py:361
  14.0 0.7 collective-permute-start.4
  14.7 3.8 %collective-permute-start.5 = (f32[2,128,256]{2,1,0:T(8,128)S(1)}, f32[2,128,256]{2,1,0:T(8,128)S(1)}, u32[]{:S(2)}, u32[]{:S(2)}) collective-permute-start(f32[2,128,256]{2,1,0:T(8,128)S(1)} %get-tuple-element.20.refs_1_), channel_id=1, source_target_pairs={{10,18},{11,19},{14,22},{15,23},{16,8},{17,9},{20,12},{21,13}} | collective-permute-start | bytes 786440 | tf_op jit(solution)/shard_map/ppermute | solution.py:250
  18.5 0.7 collective-permute-start.6
  19.2 0.0 collective-permute-done.7.refs_0_
  19.2 0.6 join.1.refs_5_
  19.8 0.7 collective-permute-start.10
  20.5 0.7 collective-permute-start.8
  21.2 0.0 collective-permute-done.4.refs_0_
  21.2 5.5 %collective-permute-start.9 = (f32[2,128,256]{2,1,0:T(8,128)S(1)}, f32[2,128,256]{2,1,0:T(8,128)S(1)}, u32[]{:S(2)}, u32[]{:S(2)}) collective-permute-start(f32[2,128,256]{2,1,0:T(8,128)S(1)} %join.1.refs_5_), channel_id=1, source_target_pairs={{10,18},{11,19},{14,22},{15,23},{16,8},{17,9},{20,12},{21,13}} | collective-permute-start | bytes 786440 | tf_op jit(solution)/shard_map/ppermute | solution.py:250
  26.7 0.0 copy-done.6
  26.7 0.0 copy-done.5
  26.7 0.0 copy-done.7
  26.7 0.9 %prepare.1 = (f32[2,256,256]{2,1,0:T(8,128)S(1)}, f32[256,256]{1,0:T(8,128)S(1)}) custom-call(s32[1,2]{1,0:T(1,128)S(1)} %bitcast.18, f32[2,256,256]{2,1,0:T(8,128)S(1)} %copy-done.5, s32[256,256]{1,0:T(8,128)S(1)} %bitcast.14, bf16[2,256,256]{2,1,0:T(8,128)(2,1)S(1)} %copy-done.7), custom_call_target="tpu_custom_call" | custom-call | tf_op jit(solution)/shard_map/prepare/pallas_call | solution.py:413
  27.6 0.0 copy-start.9
  27.6 0.0 collective-permute-done.5.refs_2_
  27.6 0.0 collective-permute-done.6.refs_3_
  27.6 0.0 collective-permute-done.10.refs_7_
  27.6 0.0 collective-permute-done.8.refs_4_
  27.7 3.1 %collective-permute-done.9.refs_6_ = f32[2,128,256]{2,1,0:T(8,128)S(1)} collective-permute-done((f32[2,128,256]{2,1,0:T(8,128)S(1)}, f32[2,128,256]{2,1,0:T(8,128)S(1)}, u32[]{:S(2)}, u32[]{:S(2)}) %collective-permute-start.9) | collective-permute-done | bytes 262176 | tf_op jit(solution)/shard_map/ppermute | solution.py:250
  30.7 0.0 copy-done.4
  30.7 6.2 %frame.1 = (f32[2,256,256]{2,1,0:T(8,128)S(1)}, f32[2,256,256]{2,1,0:T(8,128)S(1)}, f32[2,256,256]{2,1,0:T(8,128)S(1)}, f32[2,256,256]{2,1,0:T(8,128)S(1)}) custom-call(f32[2,256,256]{2,1,0:T(8,128)S(1)} %get-tuple-element.18.probe, f32[256,256]{1,0:T(8,128)S(1)} %get-tuple-element.19.seen, bf16[12,2,256,256]{3,2,1,0:T(8,128)(2,1)S(1)} %copy-done.4, ...), custom_call_target="tpu_custom_call" | custom-call | tf_op jit(solution)/shard_map/frame/pallas_call | solution.py:464
  36.9 0.7 collective-permute-start.11
  37.6 1.3 %collective-permute-start.12 = (f32[2,256,256]{2,1,0:T(8,128)S(1)}, f32[2,256,256]{2,1,0:T(8,128)S(1)}, u32[]{:S(2)}, u32[]{:S(2)}) collective-permute-start(f32[2,256,256]{2,1,0:T(8,128)S(1)} %get-tuple-element.24), channel_id=1, source_target_pairs={{8,16},{9,17},{12,20},{13,21},{18,10},{19,11},{22,14},{23,15}} | collective-permute-start | bytes 1572872 | tf_op jit(solution)/shard_map/ppermute | solution.py:250
  38.9 0.7 collective-permute-start.13
  39.6 0.0 collective-permute-done.11.refs_0_
  39.6 12.7 %collective-permute-done.12.refs_2_ = f32[2,256,256]{2,1,0:T(8,128)S(1)} collective-permute-done((f32[2,256,256]{2,1,0:T(8,128)S(1)}, f32[2,256,256]{2,1,0:T(8,128)S(1)}, u32[]{:S(2)}, u32[]{:S(2)}) %collective-permute-start.12) | collective-permute-done | bytes 524320 | tf_op jit(solution)/shard_map/ppermute | solution.py:250
  52.3 0.0 collective-permute-done.13.refs_3_
  52.3 0.0 copy-done.9
  52.3 0.8 %parts.1 = (f32[2,192,256]{2,1,0:T(8,128)S(1)}, f32[2,128,256]{2,1,0:T(8,128)S(1)}, f32[2,128,256]{2,1,0:T(8,128)S(1)}) custom-call(s32[1,2]{1,0:T(1,128)S(1)} %bitcast.19, f32[2,256,256]{2,1,0:T(8,128)S(1)} %collective-permute-done.11.refs_0_, f32[2,256,256]{2,1,0:T(8,128)S(1)} %get-tuple-element.23.refs_1_, ...), custom_call_target="tpu_custom_call" | custom-call | tf_op jit(solution)/shard_map/parts/pallas_call | solution.py:526
  53.1 0.3 collective-permute-start.14
  53.4 1.3 %collective-permute-start.15 = (f32[2,128,256]{2,1,0:T(8,128)S(1)}, f32[2,128,256]{2,1,0:T(8,128)S(1)}, u32[]{:S(2)}, u32[]{:S(2)}) collective-permute-start(f32[2,128,256]{2,1,0:T(8,128)S(1)} %get-tuple-element.27), channel_id=1, source_target_pairs={{0,4},{2,6},{5,1},{7,3},{8,12},{10,14},{13,9},{15,11},{16,20},{18,... | collective-permute-start | bytes 786440 | tf_op jit(solution)/shard_map/ppermute | solution.py:250
  54.6 3.1 %collective-permute-start.16 = (f32[2,128,256]{2,1,0:T(8,128)S(1)}, f32[2,128,256]{2,1,0:T(8,128)S(1)}, u32[]{:S(2)}, u32[]{:S(2)}) collective-permute-start(f32[2,128,256]{2,1,0:T(8,128)S(1)} %get-tuple-element.28), channel_id=1, source_target_pairs={{1,4},{3,6},{4,1},{6,3},{9,12},{11,14},{12,9},{14,11},{17,20},{19,... | collective-permute-start | bytes 786440 | tf_op jit(solution)/shard_map/ppermute | solution.py:250
  57.8 0.1 collective-permute-start.1
  57.9 0.7 keep.1.refs_2_
  58.6 1.8 %collective-permute-done.1.refs_1_ = s32[2,2]{1,0:T(2,128)S(1)} collective-permute-done((s32[2,2]{1,0:T(2,128)S(1)}, s32[2,2]{1,0:T(2,128)S(1)}, u32[]{:S(2)}, u32[]{:S(2)}) %collective-permute-start.1) | collective-permute-done | bytes 48 | tf_op jit(solution)/shard_map/ppermute | solution.py:250
  60.4 0.1 collective-permute-done.15.refs_5_
  60.5 2.3 %collective-permute-done.16.refs_6_ = f32[2,128,256]{2,1,0:T(8,128)S(1)} collective-permute-done((f32[2,128,256]{2,1,0:T(8,128)S(1)}, f32[2,128,256]{2,1,0:T(8,128)S(1)}, u32[]{:S(2)}, u32[]{:S(2)}) %collective-permute-start.16) | collective-permute-done | bytes 262176 | tf_op jit(solution)/shard_map/ppermute | solution.py:250
  62.8 0.0 collective-permute-done.14.refs_4_
  62.8 0.7 edge_terms.1
  63.4 7.7 %collective-permute-start.17 = (f32[2,192,128]{2,1,0:T(8,128)S(1)}, f32[2,192,128]{2,1,0:T(8,128)S(1)}, u32[]{:S(2)}, u32[]{:S(2)}) collective-permute-start(f32[2,192,128]{2,1,0:T(8,128)S(1)} %edge_terms.1), channel_id=1, source_target_pairs={{0,2},{1,3},{2,0},{3,1},{4,6},{5,7},{6,4},{7,5},{8,10},{9,11},{10,... | collective-permute-start | bytes 589832 | tf_op jit(solution)/shard_map/ppermute | solution.py:250
  71.2 1.5 %inner_terms.1 = (f32[192,384]{1,0:T(8,128)}, f32[192,384]{1,0:T(8,128)}, f32[1,2,192,128]{3,2,1,0:T(8,128)S(1)}) custom-call(s32[1,2]{1,0:T(1,128)S(1)} %bitcast.23, s32[2,2]{1,0:T(2,128)S(1)} %collective-permute-done.1.refs_1_, f32[2,192,256]{2,1,0:T(8,128)S(1)} %keep.1.refs_2_, s32[1,2]{1,0:T(1,128)S(1)} %collective-permute-done.refs_4_.refs_3_, ...), custom_call_target="tpu_custom_call" | custom-call | flops 4194304 | bytes 2097152 | tf_op jit(solution)/shard_map/inner_terms/pallas_call | solution.py:615
  72.7 0.0 collective-permute-done.17.refs_0_
  72.7 0.7 finish.1
  (5 shorter events, 0.0 us)
Async XLA Ops:
  0.6 26.1 %copy-start.6 = (s32[1,1,1,256,256]{4,3,2,1,0:T(8,128)S(1)}, s32[1,1,1,256,256]{4,3,2,1,0:T(8,128)}, u32[]{:S(2)}) copy-start(s32[1,1,1,256,256]{4,3,2,1,0:T(8,128)} %param.11) | copy-start | bytes 786436
  0.6 26.1 %copy-start.5 = (f32[2,256,256]{2,1,0:T(8,128)S(1)}, f32[2,256,256]{2,1,0:T(8,128)}, u32[]{:S(2)}) copy-start(f32[2,256,256]{2,1,0:T(8,128)} %probe.1) | copy-start | bytes 1572868
  1.7 4.4 %collective-permute-start.2 = (f32[384,128]{1,0:T(8,128)S(1)}, f32[384,128]{1,0:T(8,128)S(1)}, u32[]{:S(2)}, u32[]{:S(2)}) collective-permute-start(f32[384,128]{1,0:T(8,128)S(1)} %dynamic-slice_bitcast_fusion.1), channel_id=1, source_target_pairs={{0,2},{1,3},{2,0},{3,1},{4,6},{5,7},{6,4},{7,5},{8,10},{9,11},{10,... | collective-permute-start | bytes 589832 | tf_op jit(solution)/shard_map/ppermute | solution.py:250
  3.4 2.7 %collective-permute-start.3 = (f32[384,128]{1,0:T(8,128)S(1)}, f32[384,128]{1,0:T(8,128)S(1)}, u32[]{:S(2)}, u32[]{:S(2)}) collective-permute-start(f32[384,128]{1,0:T(8,128)S(1)} %dynamic-slice_bitcast_fusion), channel_id=1, source_target_pairs={{0,2},{1,3},{2,0},{3,1},{4,6},{5,7},{6,4},{7,5},{8,10},{9,11},{10,... | collective-permute-start | bytes 589832 | tf_op jit(solution)/shard_map/ppermute | solution.py:250
  3.5 2.6 %collective-permute-start = (s32[1,2]{1,0:T(1,128)}, s32[1,2]{1,0:T(1,128)S(1)}, u32[]{:S(2)}, u32[]{:S(2)}) collective-permute-start(s32[1,2]{1,0:T(1,128)} %bitcast.15), channel_id=1, source_target_pairs={{0,4},{1,5},{2,6},{3,7},{4,0},{5,1},{6,2},{7,3},{8,12},{9,13},{10,... | collective-permute-start | bytes 32 | tf_op jit(solution)/shard_map/ppermute | solution.py:250
  6.0 1.1 %copy-start = (f32[1,1,384,384]{3,2,1,0:T(8,128)S(1)}, f32[1,1,384,384]{3,2,1,0:T(8,128)}, u32[]{:S(2)}) copy-start(f32[1,1,384,384]{3,2,1,0:T(8,128)} %param.7) | copy-start | bytes 1769476
  7.1 1.1 %copy-start.2 = (f32[1,1,384,384]{3,2,1,0:T(8,128)S(1)}, f32[1,1,384,384]{3,2,1,0:T(8,128)}, u32[]{:S(2)}) copy-start(f32[1,1,384,384]{3,2,1,0:T(8,128)} %param.8) | copy-start | bytes 1769476
  8.2 18.5 %copy-start.7 = (bf16[2,256,256]{2,1,0:T(8,128)(2,1)S(1)}, bf16[2,256,256]{2,1,0:T(8,128)(2,1)}, u32[]{:S(2)}) copy-start(bf16[2,256,256]{2,1,0:T(8,128)(2,1)} %constant.33.clone.sort) | copy-start | bytes 786436
  8.9 10.3 %collective-permute-start.7 = (f32[2,128,256]{2,1,0:T(8,128)S(1)}, f32[2,128,256]{2,1,0:T(8,128)S(1)}, u32[]{:S(2)}, u32[]{:S(2)}) collective-permute-start(f32[2,128,256]{2,1,0:T(8,128)S(1)} %halo_rows.1), channel_id=1, source_target_pairs={{0,4},{1,5},{2,6},{3,7},{4,0},{5,1},{6,2},{7,3},{8,12},{9,13},{10,... | collective-permute-start | bytes 786440 | tf_op jit(solution)/shard_map/ppermute | solution.py:250
  10.2 1.1 %copy-start.1 = (f32[1,1,384,384]{3,2,1,0:T(8,128)S(1)}, f32[1,1,384,384]{3,2,1,0:T(8,128)}, u32[]{:S(2)}) copy-start(f32[1,1,384,384]{3,2,1,0:T(8,128)} %param.7) | copy-start | bytes 1769476
  11.3 1.1 %copy-start.3 = (f32[1,1,384,384]{3,2,1,0:T(8,128)S(1)}, f32[1,1,384,384]{3,2,1,0:T(8,128)}, u32[]{:S(2)}) copy-start(f32[1,1,384,384]{3,2,1,0:T(8,128)} %param.8) | copy-start | bytes 1769476
  12.3 0.7 copy-start.8
  13.0 17.7 %copy-start.4 = (bf16[12,2,256,256]{3,2,1,0:T(8,128)(2,1)S(1)}, bf16[12,2,256,256]{3,2,1,0:T(8,128)(2,1)}, u32[]{:S(2)}) copy-start(bf16[12,2,256,256]{3,2,1,0:T(8,128)(2,1)} %constant.34.clone.tables) | copy-start | bytes 9437188
  14.0 7.2 %collective-permute-start.4 = (f32[2,128,256]{2,1,0:T(8,128)S(1)}, f32[2,128,256]{2,1,0:T(8,128)S(1)}, u32[]{:S(2)}, u32[]{:S(2)}) collective-permute-start(f32[2,128,256]{2,1,0:T(8,128)S(1)} %get-tuple-element.20.refs_1_), channel_id=1, source_target_pairs={{0,8},{1,9},{2,18},{3,19},{4,12},{5,13},{6,22},{7,23}} | collective-permute-start | bytes 786440 | tf_op jit(solution)/shard_map/ppermute | solution.py:250
  14.7 12.9 %collective-permute-start.5 = (f32[2,128,256]{2,1,0:T(8,128)S(1)}, f32[2,128,256]{2,1,0:T(8,128)S(1)}, u32[]{:S(2)}, u32[]{:S(2)}) collective-permute-start(f32[2,128,256]{2,1,0:T(8,128)S(1)} %get-tuple-element.20.refs_1_), channel_id=1, source_target_pairs={{10,18},{11,19},{14,22},{15,23},{16,8},{17,9},{20,12},{21,13}} | collective-permute-start | bytes 786440 | tf_op jit(solution)/shard_map/ppermute | solution.py:250
  18.5 9.1 %collective-permute-start.6 = (f32[2,128,256]{2,1,0:T(8,128)S(1)}, f32[2,128,256]{2,1,0:T(8,128)S(1)}, u32[]{:S(2)}, u32[]{:S(2)}) collective-permute-start(f32[2,128,256]{2,1,0:T(8,128)S(1)} %get-tuple-element.20.refs_1_), channel_id=1, source_target_pairs={{24,8},{25,9},{26,18},{27,19},{28,12},{29,13},{30,22},{31,23}} | collective-permute-start | bytes 786440 | tf_op jit(solution)/shard_map/ppermute | solution.py:250
  19.8 7.8 %collective-permute-start.10 = (f32[2,128,256]{2,1,0:T(8,128)S(1)}, f32[2,128,256]{2,1,0:T(8,128)S(1)}, u32[]{:S(2)}, u32[]{:S(2)}) collective-permute-start(f32[2,128,256]{2,1,0:T(8,128)S(1)} %join.1.refs_5_), channel_id=1, source_target_pairs={{24,8},{25,9},{26,18},{27,19},{28,12},{29,13},{30,22},{31,23}} | collective-permute-start | bytes 786440 | tf_op jit(solution)/shard_map/ppermute | solution.py:250
  20.5 7.1 %collective-permute-start.8 = (f32[2,128,256]{2,1,0:T(8,128)S(1)}, f32[2,128,256]{2,1,0:T(8,128)S(1)}, u32[]{:S(2)}, u32[]{:S(2)}) collective-permute-start(f32[2,128,256]{2,1,0:T(8,128)S(1)} %join.1.refs_5_), channel_id=1, source_target_pairs={{0,8},{1,9},{2,18},{3,19},{4,12},{5,13},{6,22},{7,23}} | collective-permute-start | bytes 786440 | tf_op jit(solution)/shard_map/ppermute | solution.py:250
  21.2 9.5 %collective-permute-start.9 = (f32[2,128,256]{2,1,0:T(8,128)S(1)}, f32[2,128,256]{2,1,0:T(8,128)S(1)}, u32[]{:S(2)}, u32[]{:S(2)}) collective-permute-start(f32[2,128,256]{2,1,0:T(8,128)S(1)} %join.1.refs_5_), channel_id=1, source_target_pairs={{10,18},{11,19},{14,22},{15,23},{16,8},{17,9},{20,12},{21,13}} | collective-permute-start | bytes 786440 | tf_op jit(solution)/shard_map/ppermute | solution.py:250
  27.6 24.7 %copy-start.9 = (s32[1,1,1,2]{3,2,1,0:T(1,128)S(1)}, s32[1,1,1,2]{3,2,1,0:T(1,128)}, u32[]{:S(2)}) copy-start(s32[1,1,1,2]{3,2,1,0:T(1,128)} %param.10) | copy-start | bytes 28
  36.9 2.7 %collective-permute-start.11 = (f32[2,256,256]{2,1,0:T(8,128)S(1)}, f32[2,256,256]{2,1,0:T(8,128)S(1)}, u32[]{:S(2)}, u32[]{:S(2)}) collective-permute-start(f32[2,256,256]{2,1,0:T(8,128)S(1)} %get-tuple-element.22), channel_id=1, source_target_pairs={{8,0},{9,1},{12,4},{13,5},{18,2},{19,3},{22,6},{23,7}} | collective-permute-start | bytes 1572872 | tf_op jit(solution)/shard_map/ppermute | solution.py:250
  37.6 14.7 %collective-permute-start.12 = (f32[2,256,256]{2,1,0:T(8,128)S(1)}, f32[2,256,256]{2,1,0:T(8,128)S(1)}, u32[]{:S(2)}, u32[]{:S(2)}) collective-permute-start(f32[2,256,256]{2,1,0:T(8,128)S(1)} %get-tuple-element.24), channel_id=1, source_target_pairs={{8,16},{9,17},{12,20},{13,21},{18,10},{19,11},{22,14},{23,15}} | collective-permute-start | bytes 1572872 | tf_op jit(solution)/shard_map/ppermute | solution.py:250
  38.9 13.4 %collective-permute-start.13 = (f32[2,256,256]{2,1,0:T(8,128)S(1)}, f32[2,256,256]{2,1,0:T(8,128)S(1)}, u32[]{:S(2)}, u32[]{:S(2)}) collective-permute-start(f32[2,256,256]{2,1,0:T(8,128)S(1)} %get-tuple-element.25), channel_id=1, source_target_pairs={{8,24},{9,25},{12,28},{13,29},{18,26},{19,27},{22,30},{23,31}} | collective-permute-start | bytes 1572872 | tf_op jit(solution)/shard_map/ppermute | solution.py:250
  53.1 9.7 %collective-permute-start.14 = (f32[2,192,256]{2,1,0:T(8,128)S(1)}, f32[2,192,256]{2,1,0:T(8,128)S(1)}, u32[]{:S(2)}, u32[]{:S(2)}) collective-permute-start(f32[2,192,256]{2,1,0:T(8,128)S(1)} %get-tuple-element.26), channel_id=1, source_target_pairs={{0,1},{1,0},{2,3},{3,2},{4,5},{5,4},{6,7},{7,6},{8,9},{9,8},{10,11... | collective-permute-start | bytes 1179656 | tf_op jit(solution)/shard_map/ppermute | solution.py:250
  53.4 7.1 %collective-permute-start.15 = (f32[2,128,256]{2,1,0:T(8,128)S(1)}, f32[2,128,256]{2,1,0:T(8,128)S(1)}, u32[]{:S(2)}, u32[]{:S(2)}) collective-permute-start(f32[2,128,256]{2,1,0:T(8,128)S(1)} %get-tuple-element.27), channel_id=1, source_target_pairs={{0,4},{2,6},{5,1},{7,3},{8,12},{10,14},{13,9},{15,11},{16,20},{18,... | collective-permute-start | bytes 786440 | tf_op jit(solution)/shard_map/ppermute | solution.py:250
  54.6 8.1 %collective-permute-start.16 = (f32[2,128,256]{2,1,0:T(8,128)S(1)}, f32[2,128,256]{2,1,0:T(8,128)S(1)}, u32[]{:S(2)}, u32[]{:S(2)}) collective-permute-start(f32[2,128,256]{2,1,0:T(8,128)S(1)} %get-tuple-element.28), channel_id=1, source_target_pairs={{1,4},{3,6},{4,1},{6,3},{9,12},{11,14},{12,9},{14,11},{17,20},{19,... | collective-permute-start | bytes 786440 | tf_op jit(solution)/shard_map/ppermute | solution.py:250
  57.8 2.6 %collective-permute-start.1 = (s32[2,2]{1,0:T(2,128)S(1)}, s32[2,2]{1,0:T(2,128)S(1)}, u32[]{:S(2)}, u32[]{:S(2)}) collective-permute-start(s32[2,2]{1,0:T(2,128)S(1)} %pad_add_fusion), channel_id=1, source_target_pairs={{0,1},{1,0},{2,3},{3,2},{4,5},{5,4},{6,7},{7,6},{8,9},{9,8},{10,11... | collective-permute-start | bytes 56 | tf_op jit(solution)/shard_map/ppermute | solution.py:250
  63.4 9.2 %collective-permute-start.17 = (f32[2,192,128]{2,1,0:T(8,128)S(1)}, f32[2,192,128]{2,1,0:T(8,128)S(1)}, u32[]{:S(2)}, u32[]{:S(2)}) collective-permute-start(f32[2,192,128]{2,1,0:T(8,128)S(1)} %edge_terms.1), channel_id=1, source_target_pairs={{0,2},{1,3},{2,0},{3,1},{4,6},{5,7},{6,4},{7,5},{8,10},{9,11},{10,... | collective-permute-start | bytes 589832 | tf_op jit(solution)/shard_map/ppermute | solution.py:250

commit v3 on v2

--- a/solution.py
+++ b/solution.py
@@ -268,6 +268,15 @@
     def owner_of(x):
         return 1 + x % 2
 
+    def near_of(x):
+        return 3 * (x % 2)
+
+    def middle_of(x):
+        return 3 - owner_of(x)
+
+    def far_of(x):
+        return 3 - near_of(x)
+
     def shards(phase_shift, absorption, probe_wave, positions, counts):
         width = phase_shift.shape[2]
         frame = probe_wave.shape[1]
@@ -280,23 +289,26 @@
         small = pltpu.CompilerParams(vmem_limit_bytes=8 << 20)
 
         spots_rows = trade_rows([spot] * ways)
-        spots_rep = move(
-            jnp.concatenate([spot] + spots_rows, 0), lambda s, y, x, r: (s, y, x, 1 - r)
-        )
-
-        def edge(value, way):
-            start = place.sent(place.column(), way) * (width - HALO)
-            return lax.dynamic_slice_in_dim(value, start, HALO, 1)
-
-        sides = [
-            side
-            for value in (phase, absorb)
-            for side in trade_columns([edge(value, way) for way in range(ways)])
-        ]
+        def load_kernel(phase_ref, absorb_ref, tile, *refs):
+            edges, copies = refs[:ways], Copies(refs[ways])
+            wait_for([copies.start(phase_ref, tile.at[0]), copies.start(absorb_ref, tile.at[1])])
+            for way in range(ways):
+                start = place.sent(place.column(), way) * (width - HALO)
+                edges[way][...] = tile[:, :, pl.ds(pl.multiple_of(start, LANES), HALO)]
+
+        tile, *edges = pl.pallas_call(
+            load_kernel,
+            out_shape=[sds((2, width, width), f32)] + [sds((2, width, HALO), f32)] * ways,
+            in_specs=[HBM] * 2,
+            out_specs=[VMEM] * (1 + ways),
+            scratch_shapes=[pltpu.SemaphoreType.DMA((2,))],
+            compiler_params=small,
+            name="load",
+        )(phase, absorb)
+        sides = trade_columns(edges)
 
         def rows_of(refs, plane, rows):
-            sides_here = [refs[2 + plane * ways + way][rows, :] for way in range(ways)]
-            return refs[plane][rows, :], sides_here
+            return refs[0][plane, rows, :], [side[plane, rows, :] for side in refs[1:]]
 
         def bands_of(tile, margin):
             inner = [tile[:, i * HALO : (i + 1) * HALO] for i in range(3)]
@@ -316,8 +328,8 @@
             return damping * cosine, damping * sine
 
         def strip_kernel(*refs):
-            loaded, spot_refs = refs[: 2 + 2 * ways], refs[2 + 2 * ways : 2 + 3 * ways]
-            outs = refs[2 + 3 * ways :]
+            loaded, spot_refs = refs[: 1 + ways], refs[1 + ways : 1 + 2 * ways]
+            outs = refs[1 + 2 * ways :]
             for way in range(ways):
                 below = place.sent(place.row(), way)
                 rows = pl.ds(pl.multiple_of(below * (width - HALO), 8), HALO)
@@ -331,11 +343,11 @@
         strips = pl.pallas_call(
             strip_kernel,
             out_shape=[sds((2, HALO, frame), f32)] * ways,
-            in_specs=[VMEM] * (2 + 2 * ways) + [SMEM] * ways,
+            in_specs=[VMEM] * (1 + ways) + [SMEM] * ways,
             out_specs=[VMEM] * ways,
             compiler_params=small,
             name="halo_rows",
-        )(phase, absorb, *sides, *spots_rows)
+        )(tile, *sides, *spots_rows)
         rims = trade_rows(strips)
 
         def window_kernel(spot_ref, *refs):
@@ -361,11 +373,11 @@
         whole, part = pl.pallas_call(
             window_kernel,
             out_shape=[sds((2, HALO, frame), f32)] * 2,
-            in_specs=[SMEM] + [VMEM] * (2 + 2 * ways),
+            in_specs=[SMEM] + [VMEM] * (1 + ways),
             out_specs=[VMEM] * 2,
             compiler_params=small,
             name="window",
-        )(spot, phase, absorb, *sides)
+        )(spot, tile, *sides)
 
         def to_owner(value):
             return [
@@ -373,7 +385,7 @@
                     value,
                     lambda s, y, x, r: (owner_of(x), y, x, r) if s == section_of(x) else None,
                 )
-                for section_of in (lambda x: 0, lambda x: 3 - owner_of(x), lambda x: 3)
+                for section_of in (near_of, middle_of, far_of)
             ]
 
         wholes = to_owner(whole)
@@ -418,6 +430,10 @@
             compiler_params=small,
             name="prepare",
         )(spot, probe_wave, observed, sort)
+        places, counted = lax.optimization_barrier(
+            (jnp.concatenate([spot] + spots_rows, 0), counted)
+        )
+        spots_rep = move(places, lambda s, y, x, r: (s, y, x, 1 - r))
 
         def frame_kernel(probe, seen, tables, *refs):
             whole_refs, joined_refs, outs = refs[:4], refs[4:8], refs[8:12]
@@ -425,11 +441,11 @@
             own_is_second = place.owner() == 1
             for half, parts in ((slice(HALO, None), whole_refs), (slice(None, HALO), joined_refs)):
                 for plane in range(2):
-                    own, other = parts[1][plane], parts[2][plane]
-                    fields[0, plane, half] = parts[0][plane]
-                    fields[1, plane, half] = jnp.where(own_is_second, own, other)
-                    fields[2, plane, half] = jnp.where(own_is_second, other, own)
-                    fields[3, plane, half] = parts[3][plane]
+                    near, own, middle, far = (part[plane] for part in parts)
+                    fields[0, plane, half] = jnp.where(own_is_second, near, far)
+                    fields[1, plane, half] = jnp.where(own_is_second, own, middle)
+                    fields[2, plane, half] = jnp.where(own_is_second, middle, own)
+                    fields[3, plane, half] = jnp.where(own_is_second, far, near)
             re, im = probe[0], probe[1]
             for number in range(4):
                 o_re, o_im = fields[number, 0], fields[number, 1]
@@ -451,15 +467,13 @@
                 if number > 0:
                     o_re, o_im = fields[number, 0], fields[number, 1]
                     re, im = o_re * re - o_im * im, o_re * im + o_im * re
-                if number in (0, 3):
-                    outs[number][0], outs[number][1] = phase_term, absorb_term
-                elif number == 2:
-                    exits[2, 0], exits[2, 1] = phase_term, absorb_term
-                else:
-                    for plane, term in enumerate((phase_term, absorb_term)):
-                        kept_term = exits[2, plane]
-                        outs[1][plane] = jnp.where(own_is_second, term, kept_term)
-                        outs[2][plane] = jnp.where(own_is_second, kept_term, term)
+                exits[number, 0], exits[number, 1] = phase_term, absorb_term
+            for plane in range(2):
+                one, two, three, four = (exits[number, plane] for number in range(4))
+                outs[0][plane] = jnp.where(own_is_second, one, four)
+                outs[1][plane] = jnp.where(own_is_second, two, three)
+                outs[2][plane] = jnp.where(own_is_second, three, two)
+                outs[3][plane] = jnp.where(own_is_second, four, one)
 
         terms = pl.pallas_call(
             frame_kernel,
@@ -484,17 +498,19 @@
                 lambda s, y, x, r: (section_of(x), y, x, r) if s == owner_of(x) else None,
             )
 
+        far_terms = from_owner(terms[3], far_of)
         back = (
-            from_owner(terms[0], lambda x: 0),
+            far_terms,
+            from_owner(terms[0], near_of),
+            from_owner(terms[2], middle_of),
             terms[1],
-            from_owner(terms[2], lambda x: 3 - owner_of(x)),
-            from_owner(terms[3], lambda x: 3),
         )
 
         def load_term(refs, term):
             section, owner = place.section(), place.owner()
+            near = 3 * (owner - 1)
             choice = jnp.where(
-                section == 0, 0, jnp.where(section == 3, 3, jnp.where(section == owner, 1, 2))
+                section == 3 - near, 0, jnp.where(section == near, 1, jnp.where(section == owner, 3, 2))
             )
             for number, ref in enumerate(refs):
 

time: 74 us -> 69.7 us (0.942)
  starting transfers between devices: 30.6 us -> 23.6 us
  waiting for transfers between devices: 21.3 us -> 28.1 us
  local copies, waits for them, and re-layouts: 6.88 us -> 2.8 us
    ppermute x18 -> x17, starting transfers between devices: 30.6 us -> 23.6 us  [move(): return lax.ppermute(value, AXES, everywhere(target_of))]
    ppermute x18 -> x17, waiting for transfers between devices: 21.3 us -> 28.1 us  [move(): return lax.ppermute(value, AXES, everywhere(target_of))]
    unnamed x20 -> x16, local copies, waits for them, and re-layouts: 4.93 us -> 2.8 us
    dynamic_slice x2 -> x0, local copies, waits for them, and re-layouts: 1.95 us -> none  [edge(): return lax.dynamic_slice_in_dim(value, start, HALO, 1)]
  transfers between devices with their start and end apart: 18 -> 17, of which waited for: 6 -> 5; matrix products, arithmetic and copies ran while one was open for 1% -> 0% of each run, Pallas kernels for 6% -> 7%
where the time goes in v3:
time: 69.7 us; the launch traced here: 69.4 us
  waiting for transfers between devices  28.1 us (40%)
  starting transfers between devices  23.6 us (34%)
  Pallas kernels  14 us (20%)
  local copies, waits for them, and re-layouts  2.8 us (4%)
  between operations  0.9 us (1%)
    ppermute x17, waiting for transfers between devices, move(): return lax.ppermute(value, AXES, everywhere(target_of))  28.1 us
    ppermute x17, starting transfers between devices, move(): return lax.ppermute(value, AXES, everywhere(target_of))  23.6 us
    pallas_call x1, Pallas kernels, shards(): pl.pallas_call(frame_kernel, out_shape=[sds((2, frame, frame), f32)] * 4,...  6.15 us
    unnamed x16, local copies, waits for them, and re-layouts  2.8 us
    pallas_call x1, Pallas kernels, shards(): pl.pallas_call(inner_kernel, out_shape=[sds((half_rows, width), f32)] * 2...  1.46 us
  transfers between devices with their start and end apart: 17, of which 5 were waited for; matrix products, arithmetic and copies ran while one was open for 0% of the time, Pallas kernels for 7%

profile of v3, /device:TPU:13, one launch (start us, length us, event | category | flops | bytes accessed | tf_op | source)
XLA Modules:
  0.0 69.4 jit_solution(5234593361310066859)
XLA Ops:
  0.6 0.0 copy-start.7
  0.6 0.0 copy-start.1
  0.7 1.1 %copy-done.1 = f32[1,1,384,384]{3,2,1,0:T(8,128)S(1)} copy-done((f32[1,1,384,384]{3,2,1,0:T(8,128)S(1)}, f32[1,1,384,384]{3,2,1,0:T(8,128)}, u32[]{:S(2)}) %copy-start.1) | copy-done | bytes 589848
  1.7 0.0 copy-start.2
  1.7 1.1 %copy-done.2 = f32[1,1,384,384]{3,2,1,0:T(8,128)S(1)} copy-done((f32[1,1,384,384]{3,2,1,0:T(8,128)S(1)}, f32[1,1,384,384]{3,2,1,0:T(8,128)}, u32[]{:S(2)}) %copy-start.2) | copy-done | bytes 589848
  2.8 0.0 copy-start.3
  2.8 0.0 copy-start.4
  2.8 0.0 copy-start.5
  2.8 0.0 copy-start
  2.8 0.3 load.1
  3.1 0.7 %collective-permute-start.2 = (f32[2,384,128]{2,1,0:T(8,128)S(1)}, f32[2,384,128]{2,1,0:T(8,128)S(1)}, u32[]{:S(2)}, u32[]{:S(2)}) collective-permute-start(f32[2,384,128]{2,1,0:T(8,128)S(1)} %get-tuple-element.27), channel_id=1, source_target_pairs={{0,2},{1,3},{2,0},{3,1},{4,6},{5,7},{6,4},{7,5},{8,10},{9,11},{10,... | collective-permute-start | bytes 1179656 | tf_op jit(solution)/shard_map/ppermute | solution.py:250
  3.8 1.2 %collective-permute-start = (s32[1,2]{1,0:T(1,128)}, s32[1,2]{1,0:T(1,128)S(1)}, u32[]{:S(2)}, u32[]{:S(2)}) collective-permute-start(s32[1,2]{1,0:T(1,128)} %bitcast.9), channel_id=1, source_target_pairs={{0,4},{1,5},{2,6},{3,7},{4,0},{5,1},{6,2},{7,3},{8,12},{9,13},{10,... | collective-permute-start | bytes 32 | tf_op jit(solution)/shard_map/ppermute | solution.py:250
  5.1 1.3 %collective-permute-done.refs_2_.refs_3_ = s32[1,2]{1,0:T(1,128)S(1)} collective-permute-done((s32[1,2]{1,0:T(1,128)}, s32[1,2]{1,0:T(1,128)S(1)}, u32[]{:S(2)}, u32[]{:S(2)}) %collective-permute-start) | collective-permute-done | bytes 40 | tf_op jit(solution)/shard_map/ppermute | solution.py:250
  6.4 0.0 collective-permute-done.2.refs_1_
  6.4 0.8 %halo_rows.1 = f32[2,128,256]{2,1,0:T(8,128)S(1)} custom-call(f32[2,384,384]{2,1,0:T(8,128)S(1)} %get-tuple-element.26.refs_0_, f32[2,384,128]{2,1,0:T(8,128)S(1)} %collective-permute-done.2.refs_1_, s32[1,2]{1,0:T(1,128)S(1)} %collective-permute-done.refs_2_.refs_3_), custom_call_target="tpu_custom_call" | custom-call | tf_op jit(solution)/shard_map/halo_rows/pallas_call | solution.py:343
  7.1 1.3 %collective-permute-start.6 = (f32[2,128,256]{2,1,0:T(8,128)S(1)}, f32[2,128,256]{2,1,0:T(8,128)S(1)}, u32[]{:S(2)}, u32[]{:S(2)}) collective-permute-start(f32[2,128,256]{2,1,0:T(8,128)S(1)} %halo_rows.1), channel_id=1, source_target_pairs={{0,4},{1,5},{2,6},{3,7},{4,0},{5,1},{6,2},{7,3},{8,12},{9,13},{10,... | collective-permute-start | bytes 786440 | tf_op jit(solution)/shard_map/ppermute | solution.py:250
  8.4 0.0 copy-start.6
  8.4 0.7 copy-done.6
  9.1 1.0 %window.1 = (f32[2,128,256]{2,1,0:T(8,128)S(1)}, f32[2,128,256]{2,1,0:T(8,128)S(1)}) custom-call(s32[1,2]{1,0:T(1,128)S(1)} %bitcast.10, f32[2,384,384]{2,1,0:T(8,128)S(1)} %get-tuple-element.26.refs_0_, f32[2,384,128]{2,1,0:T(8,128)S(1)} %collective-permute-done.2.refs_1_), custom_call_target="tpu_custom_call" | custom-call | tf_op jit(solution)/shard_map/window/pallas_call | solution.py:373
  10.1 0.7 collective-permute-start.5
  10.8 3.8 %collective-permute-start.4 = (f32[2,128,256]{2,1,0:T(8,128)S(1)}, f32[2,128,256]{2,1,0:T(8,128)S(1)}, u32[]{:S(2)}, u32[]{:S(2)}) collective-permute-start(f32[2,128,256]{2,1,0:T(8,128)S(1)} %get-tuple-element.28.refs_1_), channel_id=1, source_target_pairs={{10,18},{11,19},{14,22},{15,23},{16,8},{17,9},{20,12},{21,13}} | collective-permute-start | bytes 786440 | tf_op jit(solution)/shard_map/ppermute | solution.py:250
  14.6 0.7 collective-permute-start.3
  15.3 0.0 collective-permute-done.6.refs_0_
  15.3 0.6 join.1.refs_5_
  15.9 0.7 collective-permute-start.9
  16.6 2.5 %collective-permute-start.8 = (f32[2,128,256]{2,1,0:T(8,128)S(1)}, f32[2,128,256]{2,1,0:T(8,128)S(1)}, u32[]{:S(2)}, u32[]{:S(2)}) collective-permute-start(f32[2,128,256]{2,1,0:T(8,128)S(1)} %join.1.refs_5_), channel_id=1, source_target_pairs={{10,18},{11,19},{14,22},{15,23},{16,8},{17,9},{20,12},{21,13}} | collective-permute-start | bytes 786440 | tf_op jit(solution)/shard_map/ppermute | solution.py:250
  19.1 0.0 collective-permute-done.5.refs_3_
  19.1 0.7 collective-permute-start.7
  19.8 0.0 copy-done.3
  19.8 0.0 copy-done.4
  19.8 0.0 copy-done.5
  19.8 0.9 %prepare.1 = (f32[2,256,256]{2,1,0:T(8,128)S(1)}, f32[256,256]{1,0:T(8,128)S(1)}) custom-call(s32[1,2]{1,0:T(1,128)S(1)} %bitcast.12, f32[2,256,256]{2,1,0:T(8,128)S(1)} %copy-done.3, s32[256,256]{1,0:T(8,128)S(1)} %bitcast.8, bf16[2,256,256]{2,1,0:T(8,128)(2,1)S(1)} %copy-done.5), custom_call_target="tpu_custom_call" | custom-call | tf_op jit(solution)/shard_map/prepare/pallas_call | solution.py:425
  20.7 0.0 copy-done.7
  20.7 0.5 collective-permute-done.4.refs_2_
  21.3 0.0 collective-permute-done.3.refs_0_
  21.3 0.0 collective-permute-done.9.refs_7_
  21.3 4.6 %collective-permute-done.8.refs_6_ = f32[2,128,256]{2,1,0:T(8,128)S(1)} collective-permute-done((f32[2,128,256]{2,1,0:T(8,128)S(1)}, f32[2,128,256]{2,1,0:T(8,128)S(1)}, u32[]{:S(2)}, u32[]{:S(2)}) %collective-permute-start.8) | collective-permute-done | bytes 262176 | tf_op jit(solution)/shard_map/ppermute | solution.py:250
  25.9 0.0 collective-permute-done.7.refs_4_
  25.9 0.0 copy-done
  25.9 6.2 %frame.1 = (f32[2,256,256]{2,1,0:T(8,128)S(1)}, f32[2,256,256]{2,1,0:T(8,128)S(1)}, f32[2,256,256]{2,1,0:T(8,128)S(1)}, f32[2,256,256]{2,1,0:T(8,128)S(1)}) custom-call(f32[2,256,256]{2,1,0:T(8,128)S(1)} %get-tuple-element.24.probe, f32[256,256]{1,0:T(8,128)S(1)} %get-tuple-element.25.seen, bf16[12,2,256,256]{3,2,1,0:T(8,128)(2,1)S(1)} %copy-done, ...), custom_call_target="tpu_custom_call" | custom-call | tf_op jit(solution)/shard_map/frame/pallas_call | solution.py:478
  32.1 0.7 %collective-permute-start.10 = (f32[2,256,256]{2,1,0:T(8,128)S(1)}, f32[2,256,256]{2,1,0:T(8,128)S(1)}, u32[]{:S(2)}, u32[]{:S(2)}) collective-permute-start(f32[2,256,256]{2,1,0:T(8,128)S(1)} %get-tuple-element.30), channel_id=1, source_target_pairs={{8,24},{9,25},{12,28},{13,29},{18,2},{19,3},{22,6},{23,7}} | collective-permute-start | bytes 1572872 | tf_op jit(solution)/shard_map/ppermute | solution.py:250
  32.8 0.7 %collective-permute-start.11 = (f32[2,256,256]{2,1,0:T(8,128)S(1)}, f32[2,256,256]{2,1,0:T(8,128)S(1)}, u32[]{:S(2)}, u32[]{:S(2)}) collective-permute-start(f32[2,256,256]{2,1,0:T(8,128)S(1)} %get-tuple-element.31), channel_id=1, source_target_pairs={{8,0},{9,1},{12,4},{13,5},{18,26},{19,27},{22,30},{23,31}} | collective-permute-start | bytes 1572872 | tf_op jit(solution)/shard_map/ppermute | solution.py:250
  33.5 1.3 %collective-permute-start.12 = (f32[2,256,256]{2,1,0:T(8,128)S(1)}, f32[2,256,256]{2,1,0:T(8,128)S(1)}, u32[]{:S(2)}, u32[]{:S(2)}) collective-permute-start(f32[2,256,256]{2,1,0:T(8,128)S(1)} %get-tuple-element.32), channel_id=1, source_target_pairs={{8,16},{9,17},{12,20},{13,21},{18,10},{19,11},{22,14},{23,15}} | collective-permute-start | bytes 1572872 | tf_op jit(solution)/shard_map/ppermute | solution.py:250
  34.8 0.0 collective-permute-done.10.refs_0_
  34.8 0.0 collective-permute-done.11.refs_1_
  34.8 13.6 %collective-permute-done.12.refs_2_ = f32[2,256,256]{2,1,0:T(8,128)S(1)} collective-permute-done((f32[2,256,256]{2,1,0:T(8,128)S(1)}, f32[2,256,256]{2,1,0:T(8,128)S(1)}, u32[]{:S(2)}, u32[]{:S(2)}) %collective-permute-start.12) | collective-permute-done | bytes 524320 | tf_op jit(solution)/shard_map/ppermute | solution.py:250
  48.4 0.8 %parts.1 = (f32[2,192,256]{2,1,0:T(8,128)S(1)}, f32[2,128,256]{2,1,0:T(8,128)S(1)}, f32[2,128,256]{2,1,0:T(8,128)S(1)}) custom-call(s32[1,2]{1,0:T(1,128)S(1)} %bitcast.14, f32[2,256,256]{2,1,0:T(8,128)S(1)} %collective-permute-done.10.refs_0_, f32[2,256,256]{2,1,0:T(8,128)S(1)} %collective-permute-done.11.refs_1_, ...), custom_call_target="tpu_custom_call" | custom-call | tf_op jit(solution)/shard_map/parts/pallas_call | solution.py:542
  49.2 0.3 collective-permute-start.13
  49.4 1.3 %collective-permute-start.14 = (f32[2,128,256]{2,1,0:T(8,128)S(1)}, f32[2,128,256]{2,1,0:T(8,128)S(1)}, u32[]{:S(2)}, u32[]{:S(2)}) collective-permute-start(f32[2,128,256]{2,1,0:T(8,128)S(1)} %get-tuple-element.35), channel_id=1, source_target_pairs={{0,4},{2,6},{5,1},{7,3},{8,12},{10,14},{13,9},{15,11},{16,20},{18,... | collective-permute-start | bytes 786440 | tf_op jit(solution)/shard_map/ppermute | solution.py:250
  50.7 3.5 %collective-permute-start.15 = (f32[2,128,256]{2,1,0:T(8,128)S(1)}, f32[2,128,256]{2,1,0:T(8,128)S(1)}, u32[]{:S(2)}, u32[]{:S(2)}) collective-permute-start(f32[2,128,256]{2,1,0:T(8,128)S(1)} %get-tuple-element.36), channel_id=1, source_target_pairs={{1,4},{3,6},{4,1},{6,3},{9,12},{11,14},{12,9},{14,11},{17,20},{19,... | collective-permute-start | bytes 786440 | tf_op jit(solution)/shard_map/ppermute | solution.py:250
  54.2 0.1 collective-permute-start.1
  54.3 0.7 keep.1.refs_2_
  55.0 8.0 %collective-permute-done.1.refs_1_ = s32[2,2]{1,0:T(2,128)S(1)} collective-permute-done((s32[2,2]{1,0:T(2,128)S(1)}, s32[2,2]{1,0:T(2,128)S(1)}, u32[]{:S(2)}, u32[]{:S(2)}) %collective-permute-start.1) | collective-permute-done | bytes 48 | tf_op jit(solution)/shard_map/ppermute | solution.py:250
  63.0 0.0 collective-permute-done.14.refs_5_
  63.0 0.0 collective-permute-done.15.refs_6_
  63.0 0.0 collective-permute-done.13.refs_4_
  63.0 0.7 edge_terms.1
  63.6 3.5 %collective-permute-start.16 = (f32[2,192,128]{2,1,0:T(8,128)S(1)}, f32[2,192,128]{2,1,0:T(8,128)S(1)}, u32[]{:S(2)}, u32[]{:S(2)}) collective-permute-start(f32[2,192,128]{2,1,0:T(8,128)S(1)} %edge_terms.1), channel_id=1, source_target_pairs={{0,2},{1,3},{2,0},{3,1},{4,6},{5,7},{6,4},{7,5},{8,10},{9,11},{10,... | collective-permute-start | bytes 589832 | tf_op jit(solution)/shard_map/ppermute | solution.py:250
  67.2 1.5 %inner_terms.1 = (f32[192,384]{1,0:T(8,128)}, f32[192,384]{1,0:T(8,128)}, f32[1,2,192,128]{3,2,1,0:T(8,128)S(1)}) custom-call(s32[1,2]{1,0:T(1,128)S(1)} %bitcast.17, s32[2,2]{1,0:T(2,128)S(1)} %collective-permute-done.1.refs_1_, f32[2,192,256]{2,1,0:T(8,128)S(1)} %keep.1.refs_2_, s32[1,2]{1,0:T(1,128)S(1)} %collective-permute-done.refs_2_.refs_3_, ...), custom_call_target="tpu_custom_call" | custom-call | flops 4194304 | bytes 2097152 | tf_op jit(solution)/shard_map/inner_terms/pallas_call | solution.py:631
  68.7 0.0 collective-permute-done.16.refs_0_
  68.7 0.7 %finish.1 = (f32[192,384]{1,0:T(8,128)}, f32[192,384]{1,0:T(8,128)}) custom-call(f32[192,384]{1,0:T(8,128)} %get-tuple-element.37.phase_in, f32[192,384]{1,0:T(8,128)} %get-tuple-element.38.absorb_in, f32[1,2,192,128]{3,2,1,0:T(8,128)S(1)} %get-tuple-element.39.inner_ref, ...), custom_call_target="tpu_custom_call", output_to_operand_aliasing={{0}: (0, {}), {1}: (1, {})} | custom-call | tf_op jit(solution)/shard_map/finish/pallas_call | solution.py:659
  (1 shorter events, 0.0 us)
Async XLA Ops:
  0.6 20.1 %copy-start.7 = (s32[1,1,1,2]{3,2,1,0:T(1,128)S(1)}, s32[1,1,1,2]{3,2,1,0:T(1,128)}, u32[]{:S(2)}) copy-start(s32[1,1,1,2]{3,2,1,0:T(1,128)} %param.10) | copy-start | bytes 28
  0.6 1.1 %copy-start.1 = (f32[1,1,384,384]{3,2,1,0:T(8,128)S(1)}, f32[1,1,384,384]{3,2,1,0:T(8,128)}, u32[]{:S(2)}) copy-start(f32[1,1,384,384]{3,2,1,0:T(8,128)} %param.7) | copy-start | bytes 1769476
  1.7 1.1 %copy-start.2 = (f32[1,1,384,384]{3,2,1,0:T(8,128)S(1)}, f32[1,1,384,384]{3,2,1,0:T(8,128)}, u32[]{:S(2)}) copy-start(f32[1,1,384,384]{3,2,1,0:T(8,128)} %param.8) | copy-start | bytes 1769476
  2.8 17.0 %copy-start.3 = (f32[2,256,256]{2,1,0:T(8,128)S(1)}, f32[2,256,256]{2,1,0:T(8,128)}, u32[]{:S(2)}) copy-start(f32[2,256,256]{2,1,0:T(8,128)} %probe.1) | copy-start | bytes 1572868
  2.8 17.0 %copy-start.4 = (s32[1,1,1,256,256]{4,3,2,1,0:T(8,128)S(1)}, s32[1,1,1,256,256]{4,3,2,1,0:T(8,128)}, u32[]{:S(2)}) copy-start(s32[1,1,1,256,256]{4,3,2,1,0:T(8,128)} %param.11) | copy-start | bytes 786436
  2.8 17.0 %copy-start.5 = (bf16[2,256,256]{2,1,0:T(8,128)(2,1)S(1)}, bf16[2,256,256]{2,1,0:T(8,128)(2,1)}, u32[]{:S(2)}) copy-start(bf16[2,256,256]{2,1,0:T(8,128)(2,1)} %constant.4.clone.sort) | copy-start | bytes 786436
  2.8 23.1 %copy-start = (bf16[12,2,256,256]{3,2,1,0:T(8,128)(2,1)S(1)}, bf16[12,2,256,256]{3,2,1,0:T(8,128)(2,1)}, u32[]{:S(2)}) copy-start(bf16[12,2,256,256]{3,2,1,0:T(8,128)(2,1)} %constant.5.clone.tables) | copy-start | bytes 9437188
  3.1 3.3 %collective-permute-start.2 = (f32[2,384,128]{2,1,0:T(8,128)S(1)}, f32[2,384,128]{2,1,0:T(8,128)S(1)}, u32[]{:S(2)}, u32[]{:S(2)}) collective-permute-start(f32[2,384,128]{2,1,0:T(8,128)S(1)} %get-tuple-element.27), channel_id=1, source_target_pairs={{0,2},{1,3},{2,0},{3,1},{4,6},{5,7},{6,4},{7,5},{8,10},{9,11},{10,... | collective-permute-start | bytes 1179656 | tf_op jit(solution)/shard_map/ppermute | solution.py:250
  3.8 2.5 %collective-permute-start = (s32[1,2]{1,0:T(1,128)}, s32[1,2]{1,0:T(1,128)S(1)}, u32[]{:S(2)}, u32[]{:S(2)}) collective-permute-start(s32[1,2]{1,0:T(1,128)} %bitcast.9), channel_id=1, source_target_pairs={{0,4},{1,5},{2,6},{3,7},{4,0},{5,1},{6,2},{7,3},{8,12},{9,13},{10,... | collective-permute-start | bytes 32 | tf_op jit(solution)/shard_map/ppermute | solution.py:250
  7.1 8.1 %collective-permute-start.6 = (f32[2,128,256]{2,1,0:T(8,128)S(1)}, f32[2,128,256]{2,1,0:T(8,128)S(1)}, u32[]{:S(2)}, u32[]{:S(2)}) collective-permute-start(f32[2,128,256]{2,1,0:T(8,128)S(1)} %halo_rows.1), channel_id=1, source_target_pairs={{0,4},{1,5},{2,6},{3,7},{4,0},{5,1},{6,2},{7,3},{8,12},{9,13},{10,... | collective-permute-start | bytes 786440 | tf_op jit(solution)/shard_map/ppermute | solution.py:250
  8.4 0.7 copy-start.6
  10.1 9.0 %collective-permute-start.5 = (f32[2,128,256]{2,1,0:T(8,128)S(1)}, f32[2,128,256]{2,1,0:T(8,128)S(1)}, u32[]{:S(2)}, u32[]{:S(2)}) collective-permute-start(f32[2,128,256]{2,1,0:T(8,128)S(1)} %get-tuple-element.28.refs_1_), channel_id=1, source_target_pairs={{2,18},{3,19},{6,22},{7,23},{24,8},{25,9},{28,12},{29,13}} | collective-permute-start | bytes 786440 | tf_op jit(solution)/shard_map/ppermute | solution.py:250
  10.8 10.5 %collective-permute-start.4 = (f32[2,128,256]{2,1,0:T(8,128)S(1)}, f32[2,128,256]{2,1,0:T(8,128)S(1)}, u32[]{:S(2)}, u32[]{:S(2)}) collective-permute-start(f32[2,128,256]{2,1,0:T(8,128)S(1)} %get-tuple-element.28.refs_1_), channel_id=1, source_target_pairs={{10,18},{11,19},{14,22},{15,23},{16,8},{17,9},{20,12},{21,13}} | collective-permute-start | bytes 786440 | tf_op jit(solution)/shard_map/ppermute | solution.py:250
  14.6 6.7 %collective-permute-start.3 = (f32[2,128,256]{2,1,0:T(8,128)S(1)}, f32[2,128,256]{2,1,0:T(8,128)S(1)}, u32[]{:S(2)}, u32[]{:S(2)}) collective-permute-start(f32[2,128,256]{2,1,0:T(8,128)S(1)} %get-tuple-element.28.refs_1_), channel_id=1, source_target_pairs={{0,8},{1,9},{4,12},{5,13},{26,18},{27,19},{30,22},{31,23}} | collective-permute-start | bytes 786440 | tf_op jit(solution)/shard_map/ppermute | solution.py:250
  15.9 5.4 %collective-permute-start.9 = (f32[2,128,256]{2,1,0:T(8,128)S(1)}, f32[2,128,256]{2,1,0:T(8,128)S(1)}, u32[]{:S(2)}, u32[]{:S(2)}) collective-permute-start(f32[2,128,256]{2,1,0:T(8,128)S(1)} %join.1.refs_5_), channel_id=1, source_target_pairs={{2,18},{3,19},{6,22},{7,23},{24,8},{25,9},{28,12},{29,13}} | collective-permute-start | bytes 786440 | tf_op jit(solution)/shard_map/ppermute | solution.py:250
  16.6 9.3 %collective-permute-start.8 = (f32[2,128,256]{2,1,0:T(8,128)S(1)}, f32[2,128,256]{2,1,0:T(8,128)S(1)}, u32[]{:S(2)}, u32[]{:S(2)}) collective-permute-start(f32[2,128,256]{2,1,0:T(8,128)S(1)} %join.1.refs_5_), channel_id=1, source_target_pairs={{10,18},{11,19},{14,22},{15,23},{16,8},{17,9},{20,12},{21,13}} | collective-permute-start | bytes 786440 | tf_op jit(solution)/shard_map/ppermute | solution.py:250
  19.1 6.8 %collective-permute-start.7 = (f32[2,128,256]{2,1,0:T(8,128)S(1)}, f32[2,128,256]{2,1,0:T(8,128)S(1)}, u32[]{:S(2)}, u32[]{:S(2)}) collective-permute-start(f32[2,128,256]{2,1,0:T(8,128)S(1)} %join.1.refs_5_), channel_id=1, source_target_pairs={{0,8},{1,9},{4,12},{5,13},{26,18},{27,19},{30,22},{31,23}} | collective-permute-start | bytes 786440 | tf_op jit(solution)/shard_map/ppermute | solution.py:250
  32.1 2.7 %collective-permute-start.10 = (f32[2,256,256]{2,1,0:T(8,128)S(1)}, f32[2,256,256]{2,1,0:T(8,128)S(1)}, u32[]{:S(2)}, u32[]{:S(2)}) collective-permute-start(f32[2,256,256]{2,1,0:T(8,128)S(1)} %get-tuple-element.30), channel_id=1, source_target_pairs={{8,24},{9,25},{12,28},{13,29},{18,2},{19,3},{22,6},{23,7}} | collective-permute-start | bytes 1572872 | tf_op jit(solution)/shard_map/ppermute | solution.py:250
  32.8 2.0 %collective-permute-start.11 = (f32[2,256,256]{2,1,0:T(8,128)S(1)}, f32[2,256,256]{2,1,0:T(8,128)S(1)}, u32[]{:S(2)}, u32[]{:S(2)}) collective-permute-start(f32[2,256,256]{2,1,0:T(8,128)S(1)} %get-tuple-element.31), channel_id=1, source_target_pairs={{8,0},{9,1},{12,4},{13,5},{18,26},{19,27},{22,30},{23,31}} | collective-permute-start | bytes 1572872 | tf_op jit(solution)/shard_map/ppermute | solution.py:250
  33.5 14.9 %collective-permute-start.12 = (f32[2,256,256]{2,1,0:T(8,128)S(1)}, f32[2,256,256]{2,1,0:T(8,128)S(1)}, u32[]{:S(2)}, u32[]{:S(2)}) collective-permute-start(f32[2,256,256]{2,1,0:T(8,128)S(1)} %get-tuple-element.32), channel_id=1, source_target_pairs={{8,16},{9,17},{12,20},{13,21},{18,10},{19,11},{22,14},{23,15}} | collective-permute-start | bytes 1572872 | tf_op jit(solution)/shard_map/ppermute | solution.py:250
  49.2 13.8 %collective-permute-start.13 = (f32[2,192,256]{2,1,0:T(8,128)S(1)}, f32[2,192,256]{2,1,0:T(8,128)S(1)}, u32[]{:S(2)}, u32[]{:S(2)}) collective-permute-start(f32[2,192,256]{2,1,0:T(8,128)S(1)} %get-tuple-element.34), channel_id=1, source_target_pairs={{0,1},{1,0},{2,3},{3,2},{4,5},{5,4},{6,7},{7,6},{8,9},{9,8},{10,11... | collective-permute-start | bytes 1179656 | tf_op jit(solution)/shard_map/ppermute | solution.py:250
  49.4 13.5 %collective-permute-start.14 = (f32[2,128,256]{2,1,0:T(8,128)S(1)}, f32[2,128,256]{2,1,0:T(8,128)S(1)}, u32[]{:S(2)}, u32[]{:S(2)}) collective-permute-start(f32[2,128,256]{2,1,0:T(8,128)S(1)} %get-tuple-element.35), channel_id=1, source_target_pairs={{0,4},{2,6},{5,1},{7,3},{8,12},{10,14},{13,9},{15,11},{16,20},{18,... | collective-permute-start | bytes 786440 | tf_op jit(solution)/shard_map/ppermute | solution.py:250
  50.7 12.2 %collective-permute-start.15 = (f32[2,128,256]{2,1,0:T(8,128)S(1)}, f32[2,128,256]{2,1,0:T(8,128)S(1)}, u32[]{:S(2)}, u32[]{:S(2)}) collective-permute-start(f32[2,128,256]{2,1,0:T(8,128)S(1)} %get-tuple-element.36), channel_id=1, source_target_pairs={{1,4},{3,6},{4,1},{6,3},{9,12},{11,14},{12,9},{14,11},{17,20},{19,... | collective-permute-start | bytes 786440 | tf_op jit(solution)/shard_map/ppermute | solution.py:250
  54.2 8.8 %collective-permute-start.1 = (s32[2,2]{1,0:T(2,128)S(1)}, s32[2,2]{1,0:T(2,128)S(1)}, u32[]{:S(2)}, u32[]{:S(2)}) collective-permute-start(s32[2,2]{1,0:T(2,128)S(1)} %pad_add_fusion), channel_id=1, source_target_pairs={{0,1},{1,0},{2,3},{3,2},{4,5},{5,4},{6,7},{7,6},{8,9},{9,8},{10,11... | collective-permute-start | bytes 56 | tf_op jit(solution)/shard_map/ppermute | solution.py:250
  63.6 5.0 %collective-permute-start.16 = (f32[2,192,128]{2,1,0:T(8,128)S(1)}, f32[2,192,128]{2,1,0:T(8,128)S(1)}, u32[]{:S(2)}, u32[]{:S(2)}) collective-permute-start(f32[2,192,128]{2,1,0:T(8,128)S(1)} %edge_terms.1), channel_id=1, source_target_pairs={{0,2},{1,3},{2,0},{3,1},{4,6},{5,7},{6,4},{7,5},{8,10},{9,11},{10,... | collective-permute-start | bytes 589832 | tf_op jit(solution)/shard_map/ppermute | solution.py:250

commit v4 on v3

--- a/solution.py
+++ b/solution.py
@@ -157,6 +157,14 @@
     return (cell >= offset) & (cell < offset + 2 * HALO)
 
 
+def row_at(ref, number=0):
+    return ref[2 * number, :1, :1]
+
+
+def column_at(ref, number=0):
+    return ref[2 * number + 1, :1, :1]
+
+
 def lane_index(shape):
     return lax.broadcasted_iota(jnp.int32, shape, len(shape) - 1)
 
@@ -284,11 +292,12 @@
         phase = phase_shift.reshape(width, width)
         absorb = absorption.reshape(width, width)
         spot = positions.reshape(1, 2)
+        spot_tiles = jnp.broadcast_to(positions.reshape(2, 1, 1), (2, 8, LANES))
         observed = counts.reshape(frame, frame)
         sds = jax.ShapeDtypeStruct
         small = pltpu.CompilerParams(vmem_limit_bytes=8 << 20)
 
-        spots_rows = trade_rows([spot] * ways)
+        spots_rows = trade_rows([spot_tiles] * ways)
         def load_kernel(phase_ref, absorb_ref, tile, *refs):
             edges, copies = refs[:ways], Copies(refs[ways])
             wait_for([copies.start(phase_ref, tile.at[0]), copies.start(absorb_ref, tile.at[1])])
@@ -333,7 +342,7 @@
             for way in range(ways):
                 below = place.sent(place.row(), way)
                 rows = pl.ds(pl.multiple_of(below * (width - HALO), 8), HALO)
-                column = spot_refs[way if ways == 1 else 1 - way][0, 1]
+                column = column_at(spot_refs[way if ways == 1 else 1 - way])
                 cut = [
                     choose_columns(bands_of(*rows_of(loaded, plane, rows)), column)
                     for plane in range(2)
@@ -343,7 +352,7 @@
         strips = pl.pallas_call(
             strip_kernel,
             out_shape=[sds((2, HALO, frame), f32)] * ways,
-            in_specs=[VMEM] * (1 + ways) + [SMEM] * ways,
+            in_specs=[VMEM] * (1 + 2 * ways),
             out_specs=[VMEM] * ways,
             compiler_params=small,
             name="halo_rows",
@@ -352,7 +361,7 @@
 
         def window_kernel(spot_ref, *refs):
             loaded, (whole, part) = refs[:-2], refs[-2:]
-            row, column = spot_ref[0, 0], spot_ref[0, 1]
+            row, column = row_at(spot_ref), column_at(spot_ref)
             index = row_index((HALO, HALO))
             upper = in_band(index + HALO, row, 1)
             planes = []
@@ -373,11 +382,11 @@
         whole, part = pl.pallas_call(
             window_kernel,
             out_shape=[sds((2, HALO, frame), f32)] * 2,
-            in_specs=[SMEM] + [VMEM] * (1 + ways),
+            in_specs=[VMEM] * (2 + ways),
             out_specs=[VMEM] * 2,
             compiler_params=small,
             name="window",
-        )(spot, tile, *sides)
+        )(spot_tiles, tile, *sides)
 
         def to_owner(value):
             return [
@@ -392,7 +401,7 @@
 
         def join_kernel(spot_ref, part_ref, *refs):
             rim_refs, out = refs[:ways], refs[ways]
-            row = spot_ref[0, 0]
+            row = row_at(spot_ref)
             index = row_index((HALO, frame))
             out[...] = part_ref[...]
             for way in range(ways):
@@ -406,11 +415,11 @@
         joined = pl.pallas_call(
             join_kernel,
             out_shape=sds((2, HALO, frame), f32),
-            in_specs=[SMEM] + [VMEM] * (1 + ways),
+            in_specs=[VMEM] * (2 + ways),
             out_specs=VMEM,
             compiler_params=small,
             name="join",
-        )(spot, part, *rims)
+        )(spot_tiles, part, *rims)
         joineds = to_owner(joined)
 
         tables, sort = wave_tables(frame)
@@ -431,11 +440,11 @@
             name="prepare",
         )(spot, probe_wave, observed, sort)
         places, counted = lax.optimization_barrier(
-            (jnp.concatenate([spot] + spots_rows, 0), counted)
+            (jnp.concatenate([spot_tiles] + spots_rows, 0), counted)
         )
         spots_rep = move(places, lambda s, y, x, r: (s, y, x, 1 - r))
 
-        def frame_kernel(probe, seen, tables, *refs):
+        def frame_kernel(partner_ref, probe, seen, tables, *refs):
             whole_refs, joined_refs, outs = refs[:4], refs[4:8], refs[8:12]
             fields, exits = refs[12:]
             own_is_second = place.owner() == 1
@@ -478,7 +487,7 @@
         terms = pl.pallas_call(
             frame_kernel,
             out_shape=[sds((2, frame, frame), f32)] * 4,
-            in_specs=[VMEM] * 11,
+            in_specs=[VMEM] * 12,
             out_specs=[VMEM] * 4,
             scratch_shapes=[
                 pltpu.VMEM((4, 2, frame, frame), f32),
@@ -487,7 +496,7 @@
             compiler_params=pltpu.CompilerParams(vmem_limit_bytes=16 << 20),
             name="frame",
         )(
-            rolled, counted, tables,
+            spots_rep, rolled, counted, tables,
             wholes[0], whole, wholes[1], wholes[2],
             joineds[0], joined, joineds[1], joineds[2],
         )
@@ -527,9 +536,12 @@
             return jnp.where(rep == 0, earlier, later)
 
         def parts_kernel(spot_ref, *refs):
-            back_refs, (give, straight, across, term) = refs[:4], refs[4:]
-            load_term(back_refs, term)
-            rep, row = place.rep(), spot_ref[0, 0]
+            back_refs, (give, straight, across, term) = refs[:-4], refs[-4:]
+            if len(back_refs) > 1:
+                load_term(back_refs, term)
+            else:
+                term = back_refs[0]
+            rep, row = place.rep(), row_at(spot_ref)
             index = row_index((HALO, frame))
             for plane in range(2):
                 give[plane] = rows_for(term, plane, row, 1 - rep)
@@ -539,56 +551,73 @@
                 straight[plane] = jnp.where(rep == 1, above, below)
                 across[plane] = jnp.where(rep == 1, below, above)
 
-        give, straight, across = pl.pallas_call(
-            parts_kernel,
-            out_shape=[sds((2, half_rows, frame), f32)] + [sds((2, HALO, frame), f32)] * 2,
-            in_specs=[SMEM] + [VMEM] * 4,
-            out_specs=[VMEM] * 3,
-            scratch_shapes=[pltpu.VMEM((2, frame, frame), f32)],
-            compiler_params=small,
-            name="parts",
-        )(spot, *back)
-
-        given = move(give, lambda s, y, x, r: (s, y, x, 1 - r))
-        came_straight = move(straight, lambda s, y, x, r: (s, y + 1 - 2 * r, x, r))
-        came_across = move(across, lambda s, y, x, r: (s, y - 1 + 2 * r, x, 1 - r))
+        def exchange(terms_here, owners, name):
+            give, straight, across = pl.pallas_call(
+                parts_kernel,
+                out_shape=[sds((2, half_rows, frame), f32)] + [sds((2, HALO, frame), f32)] * 2,
+                in_specs=[VMEM] * (1 + len(terms_here)),
+                out_specs=[VMEM] * 3,
+                scratch_shapes=[pltpu.VMEM((2, frame, frame), f32)],
+                compiler_params=small,
+                name=name,
+            )(spot_tiles, *terms_here)
+
+            def of_those(target_of):
+                return lambda s, y, x, r: (
+                    target_of(s, y, x, r) if (s == owner_of(x)) == owners else None
+                )
+
+            return (
+                move(give, of_those(lambda s, y, x, r: (s, y, x, 1 - r))),
+                move(straight, of_those(lambda s, y, x, r: (s, y + 1 - 2 * r, x, r))),
+                move(across, of_those(lambda s, y, x, r: (s, y - 1 + 2 * r, x, 1 - r))),
+            )
+
+        came_early = exchange(terms[1:2], True, "own_parts")
+        came_late = exchange(back[:3], False, "parts")
 
         def keep_kernel(spot_ref, *refs):
             back_refs, (mine, term) = refs[:4], refs[4:]
             load_term(back_refs, term)
             for plane in range(2):
-                mine[plane] = rows_for(term, plane, spot_ref[0, 0], place.rep())
+                mine[plane] = rows_for(term, plane, row_at(spot_ref), place.rep())
 
         kept = pl.pallas_call(
             keep_kernel,
             out_shape=sds((2, half_rows, frame), f32),
-            in_specs=[SMEM] + [VMEM] * 4,
+            in_specs=[VMEM] * 5,
             out_specs=VMEM,
             scratch_shapes=[pltpu.VMEM((2, frame, frame), f32)],
             compiler_params=small,
             cost_estimate=pl.CostEstimate(flops=1 << 22, bytes_accessed=1 << 21, transcendentals=0),
             name="keep",
-        )(spot, *back)
+        )(spot_tiles, *back)
 
         def add_band(band, plane, refs):
             spot_ref, partner_ref, kept_ref, *spot_refs = refs[: 3 + ways]
-            given, straight, across = refs[3 + ways : count]
+            early, late = refs[3 + ways : 6 + ways], refs[6 + ways : count]
+            is_owner = place.section() == place.owner()
+            given, straight, across = (
+                jnp.where(is_owner, a[plane], b[plane]) for a, b in zip(early, late)
+            )
             rep = place.rep()
             if ways == 1:
-                straight_column, across_column = spot_refs[0][0, 1], partner_ref[1, 1]
+                straight_column, across_column = column_at(spot_refs[0]), column_at(partner_ref, 1)
             else:
-                straight_column = jnp.where(rep == 1, spot_refs[0][0, 1], spot_refs[1][0, 1])
-                across_column = jnp.where(rep == 1, partner_ref[1, 1], partner_ref[2, 1])
-            total = part_of_band(kept_ref[plane], spot_ref[0, 1], band)
-            total += part_of_band(given[plane], partner_ref[0, 1], band)
-            strip = part_of_band(straight[plane], straight_column, band)
-            strip += part_of_band(across[plane], across_column, band)
+                straight_column = jnp.where(rep == 1, column_at(spot_refs[0]), column_at(spot_refs[1]))
+                across_column = jnp.where(
+                    rep == 1, column_at(partner_ref, 1), column_at(partner_ref, 2)
+                )
+            total = part_of_band(kept_ref[plane], column_at(spot_ref), band)
+            total += part_of_band(given, column_at(partner_ref), band)
+            strip = part_of_band(straight, straight_column, band)
+            strip += part_of_band(across, across_column, band)
             gap = jnp.zeros((half_rows - HALO, HALO), f32)
             early, late = jnp.concatenate([strip, gap], 0), jnp.concatenate([gap, strip], 0)
             return total + jnp.where(rep == 1, late, early)
 
-        pieces = (spot, spots_rep, kept, *spots_rows, given, came_straight, came_across)
-        piece_specs = [SMEM, SMEM, VMEM] + [SMEM] * ways + [VMEM] * 3
+        pieces = (spot_tiles, spots_rep, kept, *spots_rows, *came_early, *came_late)
+        piece_specs = [VMEM] * (9 + ways)
         count = len(piece_specs)
 
         def edge_kernel(*refs):

time: 69.7 us -> 66.9 us (0.960)
  the two profiles are of different devices: /device:TPU:13 before, /device:TPU:21 now
where the time goes in v4:
time: 66.9 us; the launch traced here: 66.5 us
  starting transfers between devices  33.6 us (50%)
  waiting for transfers between devices  18 us (27%)
  Pallas kernels  10.9 us (16%)
  local copies, waits for them, and re-layouts  3.07 us (5%)
  between operations  0.94 us (1%)
    ppermute x20, starting transfers between devices, move(): return lax.ppermute(value, AXES, everywhere(target_of))  33.6 us
    ppermute x20, waiting for transfers between devices, move(): return lax.ppermute(value, AXES, everywhere(target_of))  18 us
    pallas_call x1, Pallas kernels, shards(): pl.pallas_call(frame_kernel, out_shape=[sds((2, frame, frame), f32)] * 4,...  6.18 us
    unnamed x14, local copies, waits for them, and re-layouts  2.15 us
  transfers between devices with their start and end apart: 20, of which 9 were waited for; matrix products, arithmetic and copies ran while one was open for 1% of the time, Pallas kernels for 5%

profile of v4, /device:TPU:21, one launch (start us, length us, event | category | flops | bytes accessed | tf_op | source)
XLA Modules:
  0.0 66.5 jit_solution(12256413380102665736)
XLA Ops:
  0.6 0.0 copy-start.6
  0.6 0.0 copy-start.1
  0.7 1.1 %copy-done.1 = f32[1,1,384,384]{3,2,1,0:T(8,128)S(1)} copy-done((f32[1,1,384,384]{3,2,1,0:T(8,128)S(1)}, f32[1,1,384,384]{3,2,1,0:T(8,128)}, u32[]{:S(2)}) %copy-start.1) | copy-done | bytes 589848
  1.7 0.0 copy-start.2
  1.7 1.1 %copy-done.2 = f32[1,1,384,384]{3,2,1,0:T(8,128)S(1)} copy-done((f32[1,1,384,384]{3,2,1,0:T(8,128)S(1)}, f32[1,1,384,384]{3,2,1,0:T(8,128)}, u32[]{:S(2)}) %copy-start.2) | copy-done | bytes 589848
  2.8 0.0 copy-start.3
  2.8 0.3 load.1
  3.1 0.7 %collective-permute-start.2 = (f32[2,384,128]{2,1,0:T(8,128)S(1)}, f32[2,384,128]{2,1,0:T(8,128)S(1)}, u32[]{:S(2)}, u32[]{:S(2)}) collective-permute-start(f32[2,384,128]{2,1,0:T(8,128)S(1)} %get-tuple-element.30), channel_id=1, source_target_pairs={{0,2},{1,3},{2,0},{3,1},{4,6},{5,7},{6,4},{7,5},{8,10},{9,11},{10,... | collective-permute-start | bytes 1179656 | tf_op jit(solution)/shard_map/ppermute | solution.py:258
  3.8 0.9 %broadcast_in_dim.14.spot_ref.refs_0_ = s32[2,8,128]{2,1,0:T(8,128)S(1)} broadcast(s32[2]{0:T(128)} %bitcast.10), dimensions={0} | broadcast | bytes 8200 | tf_op jit(solution)/shard_map/broadcast_in_dim | solution.py:295
  4.8 1.2 %collective-permute-start = (s32[2,8,128]{2,1,0:T(8,128)S(1)}, s32[2,8,128]{2,1,0:T(8,128)S(1)}, u32[]{:S(2)}, u32[]{:S(2)}) collective-permute-start(s32[2,8,128]{2,1,0:T(8,128)S(1)} %broadcast_in_dim.14.spot_ref.refs_0_), channel_id=1, source_target_pairs={{0,4},{1,5},{2,6},{3,7},{4,0},{5,1},{6,2},{7,3},{8,12},{9,13},{10,... | collective-permute-start | bytes 24584 | tf_op jit(solution)/shard_map/ppermute | solution.py:258
  6.0 1.3 %collective-permute-done.refs_2_.refs_3_ = s32[2,8,128]{2,1,0:T(8,128)S(1)} collective-permute-done((s32[2,8,128]{2,1,0:T(8,128)S(1)}, s32[2,8,128]{2,1,0:T(8,128)S(1)}, u32[]{:S(2)}, u32[]{:S(2)}) %collective-permute-start) | collective-permute-done | bytes 8224 | tf_op jit(solution)/shard_map/ppermute | solution.py:258
  7.3 0.0 collective-permute-done.2.refs_1_
  7.3 0.2 halo_rows.1
  7.5 1.3 %collective-permute-start.6 = (f32[2,128,256]{2,1,0:T(8,128)S(1)}, f32[2,128,256]{2,1,0:T(8,128)S(1)}, u32[]{:S(2)}, u32[]{:S(2)}) collective-permute-start(f32[2,128,256]{2,1,0:T(8,128)S(1)} %halo_rows.1), channel_id=1, source_target_pairs={{0,4},{1,5},{2,6},{3,7},{4,0},{5,1},{6,2},{7,3},{8,12},{9,13},{10,... | collective-permute-start | bytes 786440 | tf_op jit(solution)/shard_map/ppermute | solution.py:258
  8.8 0.6 window.1
  9.4 1.3 %collective-permute-start.5 = (f32[2,128,256]{2,1,0:T(8,128)S(1)}, f32[2,128,256]{2,1,0:T(8,128)S(1)}, u32[]{:S(2)}, u32[]{:S(2)}) collective-permute-start(f32[2,128,256]{2,1,0:T(8,128)S(1)} %get-tuple-element.31.refs_1_), channel_id=1, source_target_pairs={{2,18},{3,19},{6,22},{7,23},{24,8},{25,9},{28,12},{29,13}} | collective-permute-start | bytes 786440 | tf_op jit(solution)/shard_map/ppermute | solution.py:258
  10.7 0.0 copy-done.6
  10.7 0.0 copy-done.3
  10.7 0.0 copy-done.4
  10.7 0.0 copy-done.5
  10.7 0.9 %prepare.1 = (f32[2,256,256]{2,1,0:T(8,128)S(1)}, f32[256,256]{1,0:T(8,128)S(1)}) custom-call(s32[1,2]{1,0:T(1,128)S(1)} %bitcast.11, f32[2,256,256]{2,1,0:T(8,128)S(1)} %copy-done.3, s32[256,256]{1,0:T(8,128)S(1)} %bitcast.9, bf16[2,256,256]{2,1,0:T(8,128)(2,1)S(1)} %copy-done.5), custom_call_target="tpu_custom_call" | custom-call | tf_op jit(solution)/shard_map/prepare/pallas_call | solution.py:434
  11.6 0.3 collective-permute-start.1
  11.9 1.3 %collective-permute-start.4 = (f32[2,128,256]{2,1,0:T(8,128)S(1)}, f32[2,128,256]{2,1,0:T(8,128)S(1)}, u32[]{:S(2)}, u32[]{:S(2)}) collective-permute-start(f32[2,128,256]{2,1,0:T(8,128)S(1)} %get-tuple-element.31.refs_1_), channel_id=1, source_target_pairs={{10,18},{11,19},{14,22},{15,23},{16,8},{17,9},{20,12},{21,13}} | collective-permute-start | bytes 786440 | tf_op jit(solution)/shard_map/ppermute | solution.py:258
  13.2 1.3 %collective-permute-start.3 = (f32[2,128,256]{2,1,0:T(8,128)S(1)}, f32[2,128,256]{2,1,0:T(8,128)S(1)}, u32[]{:S(2)}, u32[]{:S(2)}) collective-permute-start(f32[2,128,256]{2,1,0:T(8,128)S(1)} %get-tuple-element.31.refs_1_), channel_id=1, source_target_pairs={{0,8},{1,9},{4,12},{5,13},{26,18},{27,19},{30,22},{31,23}} | collective-permute-start | bytes 786440 | tf_op jit(solution)/shard_map/ppermute | solution.py:258
  14.5 0.0 collective-permute-done.6.refs_0_
  14.5 0.1 join.1.refs_5_
  14.6 1.3 %collective-permute-start.9 = (f32[2,128,256]{2,1,0:T(8,128)S(1)}, f32[2,128,256]{2,1,0:T(8,128)S(1)}, u32[]{:S(2)}, u32[]{:S(2)}) collective-permute-start(f32[2,128,256]{2,1,0:T(8,128)S(1)} %join.1.refs_5_), channel_id=1, source_target_pairs={{2,18},{3,19},{6,22},{7,23},{24,8},{25,9},{28,12},{29,13}} | collective-permute-start | bytes 786440 | tf_op jit(solution)/shard_map/ppermute | solution.py:258
  15.9 0.0 collective-permute-done.1.partner_ref.refs_1_
  15.9 1.3 %collective-permute-start.8 = (f32[2,128,256]{2,1,0:T(8,128)S(1)}, f32[2,128,256]{2,1,0:T(8,128)S(1)}, u32[]{:S(2)}, u32[]{:S(2)}) collective-permute-start(f32[2,128,256]{2,1,0:T(8,128)S(1)} %join.1.refs_5_), channel_id=1, source_target_pairs={{10,18},{11,19},{14,22},{15,23},{16,8},{17,9},{20,12},{21,13}} | collective-permute-start | bytes 786440 | tf_op jit(solution)/shard_map/ppermute | solution.py:258
  17.2 0.3 collective-permute-done.5.refs_3_
  17.5 1.3 %collective-permute-start.7 = (f32[2,128,256]{2,1,0:T(8,128)S(1)}, f32[2,128,256]{2,1,0:T(8,128)S(1)}, u32[]{:S(2)}, u32[]{:S(2)}) collective-permute-start(f32[2,128,256]{2,1,0:T(8,128)S(1)} %join.1.refs_5_), channel_id=1, source_target_pairs={{0,8},{1,9},{4,12},{5,13},{26,18},{27,19},{30,22},{31,23}} | collective-permute-start | bytes 786440 | tf_op jit(solution)/shard_map/ppermute | solution.py:258
  18.8 1.8 %collective-permute-done.4.refs_2_ = f32[2,128,256]{2,1,0:T(8,128)S(1)} collective-permute-done((f32[2,128,256]{2,1,0:T(8,128)S(1)}, f32[2,128,256]{2,1,0:T(8,128)S(1)}, u32[]{:S(2)}, u32[]{:S(2)}) %collective-permute-start.4) | collective-permute-done | bytes 262176 | tf_op jit(solution)/shard_map/ppermute | solution.py:258
  20.6 0.5 collective-permute-done.3.refs_0_
  21.1 4.2 %collective-permute-done.9.refs_7_ = f32[2,128,256]{2,1,0:T(8,128)S(1)} collective-permute-done((f32[2,128,256]{2,1,0:T(8,128)S(1)}, f32[2,128,256]{2,1,0:T(8,128)S(1)}, u32[]{:S(2)}, u32[]{:S(2)}) %collective-permute-start.9) | collective-permute-done | bytes 262176 | tf_op jit(solution)/shard_map/ppermute | solution.py:258
  25.3 0.5 collective-permute-done.8.refs_6_
  25.8 0.9 %collective-permute-done.7.refs_4_ = f32[2,128,256]{2,1,0:T(8,128)S(1)} collective-permute-done((f32[2,128,256]{2,1,0:T(8,128)S(1)}, f32[2,128,256]{2,1,0:T(8,128)S(1)}, u32[]{:S(2)}, u32[]{:S(2)}) %collective-permute-start.7) | collective-permute-done | bytes 262176 | tf_op jit(solution)/shard_map/ppermute | solution.py:258
  26.7 0.0 copy-done
  26.7 6.2 %frame.1 = (f32[2,256,256]{2,1,0:T(8,128)S(1)}, f32[2,256,256]{2,1,0:T(8,128)S(1)}, f32[2,256,256]{2,1,0:T(8,128)S(1)}, f32[2,256,256]{2,1,0:T(8,128)S(1)}) custom-call(s32[4,8,128]{2,1,0:T(8,128)S(1)} %collective-permute-done.1.partner_ref.refs_1_, f32[2,256,256]{2,1,0:T(8,128)S(1)} %get-tuple-element.27.probe, f32[256,256]{1,0:T(8,128)S(1)} %get-tuple-element.28.seen, ...), custom_call_target="tpu_custom_call" | custom-call | tf_op jit(solution)/shard_map/frame/pallas_call | solution.py:487
  32.9 1.3 %collective-permute-start.10 = (f32[2,256,256]{2,1,0:T(8,128)S(1)}, f32[2,256,256]{2,1,0:T(8,128)S(1)}, u32[]{:S(2)}, u32[]{:S(2)}) collective-permute-start(f32[2,256,256]{2,1,0:T(8,128)S(1)} %get-tuple-element.33), channel_id=1, source_target_pairs={{8,24},{9,25},{12,28},{13,29},{18,2},{19,3},{22,6},{23,7}} | collective-permute-start | bytes 1572872 | tf_op jit(solution)/shard_map/ppermute | solution.py:258
  34.3 1.3 %collective-permute-start.11 = (f32[2,256,256]{2,1,0:T(8,128)S(1)}, f32[2,256,256]{2,1,0:T(8,128)S(1)}, u32[]{:S(2)}, u32[]{:S(2)}) collective-permute-start(f32[2,256,256]{2,1,0:T(8,128)S(1)} %get-tuple-element.34), channel_id=1, source_target_pairs={{8,0},{9,1},{12,4},{13,5},{18,26},{19,27},{22,30},{23,31}} | collective-permute-start | bytes 1572872 | tf_op jit(solution)/shard_map/ppermute | solution.py:258
  35.6 1.3 %collective-permute-start.12 = (f32[2,256,256]{2,1,0:T(8,128)S(1)}, f32[2,256,256]{2,1,0:T(8,128)S(1)}, u32[]{:S(2)}, u32[]{:S(2)}) collective-permute-start(f32[2,256,256]{2,1,0:T(8,128)S(1)} %get-tuple-element.35), channel_id=1, source_target_pairs={{8,16},{9,17},{12,20},{13,21},{18,10},{19,11},{22,14},{23,15}} | collective-permute-start | bytes 1572872 | tf_op jit(solution)/shard_map/ppermute | solution.py:258
  36.9 0.2 own_parts.1
  37.2 1.3 %collective-permute-start.14 = (f32[2,128,256]{2,1,0:T(8,128)S(1)}, f32[2,128,256]{2,1,0:T(8,128)S(1)}, u32[]{:S(2)}, u32[]{:S(2)}) collective-permute-start(f32[2,128,256]{2,1,0:T(8,128)S(1)} %get-tuple-element.38), channel_id=1, source_target_pairs={{8,12},{13,9},{18,22},{23,19}} | collective-permute-start | bytes 786440 | tf_op jit(solution)/shard_map/ppermute | solution.py:258
  38.5 3.9 %collective-permute-start.13 = (f32[2,192,256]{2,1,0:T(8,128)S(1)}, f32[2,192,256]{2,1,0:T(8,128)S(1)}, u32[]{:S(2)}, u32[]{:S(2)}) collective-permute-start(f32[2,192,256]{2,1,0:T(8,128)S(1)} %get-tuple-element.37), channel_id=1, source_target_pairs={{8,9},{9,8},{12,13},{13,12},{18,19},{19,18},{22,23},{23,22}} | collective-permute-start | bytes 1179656 | tf_op jit(solution)/shard_map/ppermute | solution.py:258
  42.4 0.0 collective-permute-done.10.refs_0_
  42.4 4.9 %collective-permute-done.11.refs_1_ = f32[2,256,256]{2,1,0:T(8,128)S(1)} collective-permute-done((f32[2,256,256]{2,1,0:T(8,128)S(1)}, f32[2,256,256]{2,1,0:T(8,128)S(1)}, u32[]{:S(2)}, u32[]{:S(2)}) %collective-permute-start.11) | collective-permute-done | bytes 524320 | tf_op jit(solution)/shard_map/ppermute | solution.py:258
  47.3 0.0 collective-permute-done.12.refs_2_
  47.3 0.2 parts.1
  47.5 0.7 %collective-permute-start.16 = (f32[2,192,256]{2,1,0:T(8,128)S(1)}, f32[2,192,256]{2,1,0:T(8,128)S(1)}, u32[]{:S(2)}, u32[]{:S(2)}) collective-permute-start(f32[2,192,256]{2,1,0:T(8,128)S(1)} %get-tuple-element.40), channel_id=1, source_target_pairs={{0,1},{1,0},{2,3},{3,2},{4,5},{5,4},{6,7},{7,6},{10,11},{11,10},{1... | collective-permute-start | bytes 1179656 | tf_op jit(solution)/shard_map/ppermute | solution.py:258
  48.2 3.0 %collective-permute-start.15 = (f32[2,128,256]{2,1,0:T(8,128)S(1)}, f32[2,128,256]{2,1,0:T(8,128)S(1)}, u32[]{:S(2)}, u32[]{:S(2)}) collective-permute-start(f32[2,128,256]{2,1,0:T(8,128)S(1)} %get-tuple-element.39), channel_id=1, source_target_pairs={{9,12},{12,9},{19,22},{22,19}} | collective-permute-start | bytes 786440 | tf_op jit(solution)/shard_map/ppermute | solution.py:258
  51.2 0.7 %collective-permute-start.17 = (f32[2,128,256]{2,1,0:T(8,128)S(1)}, f32[2,128,256]{2,1,0:T(8,128)S(1)}, u32[]{:S(2)}, u32[]{:S(2)}) collective-permute-start(f32[2,128,256]{2,1,0:T(8,128)S(1)} %get-tuple-element.41), channel_id=1, source_target_pairs={{0,4},{2,6},{5,1},{7,3},{10,14},{15,11},{16,20},{21,17},{24,28},{2... | collective-permute-start | bytes 786440 | tf_op jit(solution)/shard_map/ppermute | solution.py:258
  51.9 0.0 collective-permute-done.14.refs_5_
  51.9 0.7 %collective-permute-start.18 = (f32[2,128,256]{2,1,0:T(8,128)S(1)}, f32[2,128,256]{2,1,0:T(8,128)S(1)}, u32[]{:S(2)}, u32[]{:S(2)}) collective-permute-start(f32[2,128,256]{2,1,0:T(8,128)S(1)} %get-tuple-element.42), channel_id=1, source_target_pairs={{1,4},{3,6},{4,1},{6,3},{11,14},{14,11},{17,20},{20,17},{25,28},{2... | collective-permute-start | bytes 786440 | tf_op jit(solution)/shard_map/ppermute | solution.py:258
  52.6 0.2 keep.1.refs_2_
  52.8 3.5 %collective-permute-done.15.refs_6_ = f32[2,128,256]{2,1,0:T(8,128)S(1)} collective-permute-done((f32[2,128,256]{2,1,0:T(8,128)S(1)}, f32[2,128,256]{2,1,0:T(8,128)S(1)}, u32[]{:S(2)}, u32[]{:S(2)}) %collective-permute-start.15) | collective-permute-done | bytes 262176 | tf_op jit(solution)/shard_map/ppermute | solution.py:258
  56.3 0.0 collective-permute-done.13.refs_4_
  56.3 0.0 collective-permute-done.17.refs_8_
  56.3 0.0 collective-permute-done.18.refs_9_
  56.3 0.0 collective-permute-done.16.refs_7_
  56.4 0.2 edge_terms.1
  56.6 8.1 %collective-permute-start.19 = (f32[2,192,128]{2,1,0:T(8,128)S(1)}, f32[2,192,128]{2,1,0:T(8,128)S(1)}, u32[]{:S(2)}, u32[]{:S(2)}) collective-permute-start(f32[2,192,128]{2,1,0:T(8,128)S(1)} %edge_terms.1), channel_id=1, source_target_pairs={{0,2},{1,3},{2,0},{3,1},{4,6},{5,7},{6,4},{7,5},{8,10},{9,11},{10,... | collective-permute-start | bytes 589832 | tf_op jit(solution)/shard_map/ppermute | solution.py:258
  64.7 1.0 %inner_terms.1 = (f32[192,384]{1,0:T(8,128)}, f32[192,384]{1,0:T(8,128)}, f32[1,2,192,128]{3,2,1,0:T(8,128)S(1)}) custom-call(s32[2,8,128]{2,1,0:T(8,128)S(1)} %broadcast_in_dim.14.spot_ref.refs_0_, s32[4,8,128]{2,1,0:T(8,128)S(1)} %collective-permute-done.1.partner_ref.refs_1_, f32[2,192,256]{2,1,0:T(8,128)S(1)} %keep.1.refs_2_, ...), custom_call_target="tpu_custom_call" | custom-call | flops 4194304 | bytes 2097152 | tf_op jit(solution)/shard_map/inner_terms/pallas_call | solution.py:660
  65.7 0.0 collective-permute-done.19.refs_0_
  65.8 0.7 %finish.1 = (f32[192,384]{1,0:T(8,128)}, f32[192,384]{1,0:T(8,128)}) custom-call(f32[192,384]{1,0:T(8,128)} %get-tuple-element.43.phase_in, f32[192,384]{1,0:T(8,128)} %get-tuple-element.44.absorb_in, f32[1,2,192,128]{3,2,1,0:T(8,128)S(1)} %get-tuple-element.45.inner_ref, ...), custom_call_target="tpu_custom_call", output_to_operand_aliasing={{0}: (0, {}), {1}: (1, {})} | custom-call | tf_op jit(solution)/shard_map/finish/pallas_call | solution.py:688
  (4 shorter events, 0.0 us)
Async XLA Ops:
  0.6 10.1 %copy-start.6 = (s32[1,1,1,2]{3,2,1,0:T(1,128)S(1)}, s32[1,1,1,2]{3,2,1,0:T(1,128)}, u32[]{:S(2)}) copy-start(s32[1,1,1,2]{3,2,1,0:T(1,128)} %param.10) | copy-start | bytes 28
  0.6 1.1 %copy-start.1 = (f32[1,1,384,384]{3,2,1,0:T(8,128)S(1)}, f32[1,1,384,384]{3,2,1,0:T(8,128)}, u32[]{:S(2)}) copy-start(f32[1,1,384,384]{3,2,1,0:T(8,128)} %param.7) | copy-start | bytes 1769476
  1.7 1.1 %copy-start.2 = (f32[1,1,384,384]{3,2,1,0:T(8,128)S(1)}, f32[1,1,384,384]{3,2,1,0:T(8,128)}, u32[]{:S(2)}) copy-start(f32[1,1,384,384]{3,2,1,0:T(8,128)} %param.8) | copy-start | bytes 1769476
  2.8 7.9 %copy-start.3 = (f32[2,256,256]{2,1,0:T(8,128)S(1)}, f32[2,256,256]{2,1,0:T(8,128)}, u32[]{:S(2)}) copy-start(f32[2,256,256]{2,1,0:T(8,128)} %probe.1) | copy-start | bytes 1572868
  2.8 7.9 %copy-start.4 = (s32[1,1,1,256,256]{4,3,2,1,0:T(8,128)S(1)}, s32[1,1,1,256,256]{4,3,2,1,0:T(8,128)}, u32[]{:S(2)}) copy-start(s32[1,1,1,256,256]{4,3,2,1,0:T(8,128)} %param.11) | copy-start | bytes 786436
  2.8 7.9 %copy-start.5 = (bf16[2,256,256]{2,1,0:T(8,128)(2,1)S(1)}, bf16[2,256,256]{2,1,0:T(8,128)(2,1)}, u32[]{:S(2)}) copy-start(bf16[2,256,256]{2,1,0:T(8,128)(2,1)} %constant.4.clone.sort) | copy-start | bytes 786436
  2.8 23.9 %copy-start = (bf16[12,2,256,256]{3,2,1,0:T(8,128)(2,1)S(1)}, bf16[12,2,256,256]{3,2,1,0:T(8,128)(2,1)}, u32[]{:S(2)}) copy-start(bf16[12,2,256,256]{3,2,1,0:T(8,128)(2,1)} %constant.5.clone.tables) | copy-start | bytes 9437188
  3.1 4.2 %collective-permute-start.2 = (f32[2,384,128]{2,1,0:T(8,128)S(1)}, f32[2,384,128]{2,1,0:T(8,128)S(1)}, u32[]{:S(2)}, u32[]{:S(2)}) collective-permute-start(f32[2,384,128]{2,1,0:T(8,128)S(1)} %get-tuple-element.30), channel_id=1, source_target_pairs={{0,2},{1,3},{2,0},{3,1},{4,6},{5,7},{6,4},{7,5},{8,10},{9,11},{10,... | collective-permute-start | bytes 1179656 | tf_op jit(solution)/shard_map/ppermute | solution.py:258
  4.8 2.5 %collective-permute-start = (s32[2,8,128]{2,1,0:T(8,128)S(1)}, s32[2,8,128]{2,1,0:T(8,128)S(1)}, u32[]{:S(2)}, u32[]{:S(2)}) collective-permute-start(s32[2,8,128]{2,1,0:T(8,128)S(1)} %broadcast_in_dim.14.spot_ref.refs_0_), channel_id=1, source_target_pairs={{0,4},{1,5},{2,6},{3,7},{4,0},{5,1},{6,2},{7,3},{8,12},{9,13},{10,... | collective-permute-start | bytes 24584 | tf_op jit(solution)/shard_map/ppermute | solution.py:258
  7.5 7.0 %collective-permute-start.6 = (f32[2,128,256]{2,1,0:T(8,128)S(1)}, f32[2,128,256]{2,1,0:T(8,128)S(1)}, u32[]{:S(2)}, u32[]{:S(2)}) collective-permute-start(f32[2,128,256]{2,1,0:T(8,128)S(1)} %halo_rows.1), channel_id=1, source_target_pairs={{0,4},{1,5},{2,6},{3,7},{4,0},{5,1},{6,2},{7,3},{8,12},{9,13},{10,... | collective-permute-start | bytes 786440 | tf_op jit(solution)/shard_map/ppermute | solution.py:258
  9.4 8.1 %collective-permute-start.5 = (f32[2,128,256]{2,1,0:T(8,128)S(1)}, f32[2,128,256]{2,1,0:T(8,128)S(1)}, u32[]{:S(2)}, u32[]{:S(2)}) collective-permute-start(f32[2,128,256]{2,1,0:T(8,128)S(1)} %get-tuple-element.31.refs_1_), channel_id=1, source_target_pairs={{2,18},{3,19},{6,22},{7,23},{24,8},{25,9},{28,12},{29,13}} | collective-permute-start | bytes 786440 | tf_op jit(solution)/shard_map/ppermute | solution.py:258
  11.6 4.3 %collective-permute-start.1 = (s32[4,8,128]{2,1,0:T(8,128)S(1)}, s32[4,8,128]{2,1,0:T(8,128)S(1)}, u32[]{:S(2)}, u32[]{:S(2)}) collective-permute-start(s32[4,8,128]{2,1,0:T(8,128)S(1)} %pad_add_fusion), channel_id=1, source_target_pairs={{0,1},{1,0},{2,3},{3,2},{4,5},{5,4},{6,7},{7,6},{8,9},{9,8},{10,11... | collective-permute-start | bytes 49160 | tf_op jit(solution)/shard_map/ppermute | solution.py:258
  11.9 8.7 %collective-permute-start.4 = (f32[2,128,256]{2,1,0:T(8,128)S(1)}, f32[2,128,256]{2,1,0:T(8,128)S(1)}, u32[]{:S(2)}, u32[]{:S(2)}) collective-permute-start(f32[2,128,256]{2,1,0:T(8,128)S(1)} %get-tuple-element.31.refs_1_), channel_id=1, source_target_pairs={{10,18},{11,19},{14,22},{15,23},{16,8},{17,9},{20,12},{21,13}} | collective-permute-start | bytes 786440 | tf_op jit(solution)/shard_map/ppermute | solution.py:258
  13.2 7.9 %collective-permute-start.3 = (f32[2,128,256]{2,1,0:T(8,128)S(1)}, f32[2,128,256]{2,1,0:T(8,128)S(1)}, u32[]{:S(2)}, u32[]{:S(2)}) collective-permute-start(f32[2,128,256]{2,1,0:T(8,128)S(1)} %get-tuple-element.31.refs_1_), channel_id=1, source_target_pairs={{0,8},{1,9},{4,12},{5,13},{26,18},{27,19},{30,22},{31,23}} | collective-permute-start | bytes 786440 | tf_op jit(solution)/shard_map/ppermute | solution.py:258
  14.6 10.7 %collective-permute-start.9 = (f32[2,128,256]{2,1,0:T(8,128)S(1)}, f32[2,128,256]{2,1,0:T(8,128)S(1)}, u32[]{:S(2)}, u32[]{:S(2)}) collective-permute-start(f32[2,128,256]{2,1,0:T(8,128)S(1)} %join.1.refs_5_), channel_id=1, source_target_pairs={{2,18},{3,19},{6,22},{7,23},{24,8},{25,9},{28,12},{29,13}} | collective-permute-start | bytes 786440 | tf_op jit(solution)/shard_map/ppermute | solution.py:258
  15.9 9.9 %collective-permute-start.8 = (f32[2,128,256]{2,1,0:T(8,128)S(1)}, f32[2,128,256]{2,1,0:T(8,128)S(1)}, u32[]{:S(2)}, u32[]{:S(2)}) collective-permute-start(f32[2,128,256]{2,1,0:T(8,128)S(1)} %join.1.refs_5_), channel_id=1, source_target_pairs={{10,18},{11,19},{14,22},{15,23},{16,8},{17,9},{20,12},{21,13}} | collective-permute-start | bytes 786440 | tf_op jit(solution)/shard_map/ppermute | solution.py:258
  17.5 9.2 %collective-permute-start.7 = (f32[2,128,256]{2,1,0:T(8,128)S(1)}, f32[2,128,256]{2,1,0:T(8,128)S(1)}, u32[]{:S(2)}, u32[]{:S(2)}) collective-permute-start(f32[2,128,256]{2,1,0:T(8,128)S(1)} %join.1.refs_5_), channel_id=1, source_target_pairs={{0,8},{1,9},{4,12},{5,13},{26,18},{27,19},{30,22},{31,23}} | collective-permute-start | bytes 786440 | tf_op jit(solution)/shard_map/ppermute | solution.py:258
  32.9 9.4 %collective-permute-start.10 = (f32[2,256,256]{2,1,0:T(8,128)S(1)}, f32[2,256,256]{2,1,0:T(8,128)S(1)}, u32[]{:S(2)}, u32[]{:S(2)}) collective-permute-start(f32[2,256,256]{2,1,0:T(8,128)S(1)} %get-tuple-element.33), channel_id=1, source_target_pairs={{8,24},{9,25},{12,28},{13,29},{18,2},{19,3},{22,6},{23,7}} | collective-permute-start | bytes 1572872 | tf_op jit(solution)/shard_map/ppermute | solution.py:258
  34.3 13.0 %collective-permute-start.11 = (f32[2,256,256]{2,1,0:T(8,128)S(1)}, f32[2,256,256]{2,1,0:T(8,128)S(1)}, u32[]{:S(2)}, u32[]{:S(2)}) collective-permute-start(f32[2,256,256]{2,1,0:T(8,128)S(1)} %get-tuple-element.34), channel_id=1, source_target_pairs={{8,0},{9,1},{12,4},{13,5},{18,26},{19,27},{22,30},{23,31}} | collective-permute-start | bytes 1572872 | tf_op jit(solution)/shard_map/ppermute | solution.py:258
  35.6 11.7 %collective-permute-start.12 = (f32[2,256,256]{2,1,0:T(8,128)S(1)}, f32[2,256,256]{2,1,0:T(8,128)S(1)}, u32[]{:S(2)}, u32[]{:S(2)}) collective-permute-start(f32[2,256,256]{2,1,0:T(8,128)S(1)} %get-tuple-element.35), channel_id=1, source_target_pairs={{8,16},{9,17},{12,20},{13,21},{18,10},{19,11},{22,14},{23,15}} | collective-permute-start | bytes 1572872 | tf_op jit(solution)/shard_map/ppermute | solution.py:258
  37.2 14.7 %collective-permute-start.14 = (f32[2,128,256]{2,1,0:T(8,128)S(1)}, f32[2,128,256]{2,1,0:T(8,128)S(1)}, u32[]{:S(2)}, u32[]{:S(2)}) collective-permute-start(f32[2,128,256]{2,1,0:T(8,128)S(1)} %get-tuple-element.38), channel_id=1, source_target_pairs={{8,12},{13,9},{18,22},{23,19}} | collective-permute-start | bytes 786440 | tf_op jit(solution)/shard_map/ppermute | solution.py:258
  38.5 17.9 %collective-permute-start.13 = (f32[2,192,256]{2,1,0:T(8,128)S(1)}, f32[2,192,256]{2,1,0:T(8,128)S(1)}, u32[]{:S(2)}, u32[]{:S(2)}) collective-permute-start(f32[2,192,256]{2,1,0:T(8,128)S(1)} %get-tuple-element.37), channel_id=1, source_target_pairs={{8,9},{9,8},{12,13},{13,12},{18,19},{19,18},{22,23},{23,22}} | collective-permute-start | bytes 1179656 | tf_op jit(solution)/shard_map/ppermute | solution.py:258
  47.5 8.8 %collective-permute-start.16 = (f32[2,192,256]{2,1,0:T(8,128)S(1)}, f32[2,192,256]{2,1,0:T(8,128)S(1)}, u32[]{:S(2)}, u32[]{:S(2)}) collective-permute-start(f32[2,192,256]{2,1,0:T(8,128)S(1)} %get-tuple-element.40), channel_id=1, source_target_pairs={{0,1},{1,0},{2,3},{3,2},{4,5},{5,4},{6,7},{7,6},{10,11},{11,10},{1... | collective-permute-start | bytes 1179656 | tf_op jit(solution)/shard_map/ppermute | solution.py:258
  48.2 8.1 %collective-permute-start.15 = (f32[2,128,256]{2,1,0:T(8,128)S(1)}, f32[2,128,256]{2,1,0:T(8,128)S(1)}, u32[]{:S(2)}, u32[]{:S(2)}) collective-permute-start(f32[2,128,256]{2,1,0:T(8,128)S(1)} %get-tuple-element.39), channel_id=1, source_target_pairs={{9,12},{12,9},{19,22},{22,19}} | collective-permute-start | bytes 786440 | tf_op jit(solution)/shard_map/ppermute | solution.py:258
  51.2 5.1 %collective-permute-start.17 = (f32[2,128,256]{2,1,0:T(8,128)S(1)}, f32[2,128,256]{2,1,0:T(8,128)S(1)}, u32[]{:S(2)}, u32[]{:S(2)}) collective-permute-start(f32[2,128,256]{2,1,0:T(8,128)S(1)} %get-tuple-element.41), channel_id=1, source_target_pairs={{0,4},{2,6},{5,1},{7,3},{10,14},{15,11},{16,20},{21,17},{24,28},{2... | collective-permute-start | bytes 786440 | tf_op jit(solution)/shard_map/ppermute | solution.py:258
  51.9 4.4 %collective-permute-start.18 = (f32[2,128,256]{2,1,0:T(8,128)S(1)}, f32[2,128,256]{2,1,0:T(8,128)S(1)}, u32[]{:S(2)}, u32[]{:S(2)}) collective-permute-start(f32[2,128,256]{2,1,0:T(8,128)S(1)} %get-tuple-element.42), channel_id=1, source_target_pairs={{1,4},{3,6},{4,1},{6,3},{11,14},{14,11},{17,20},{20,17},{25,28},{2... | collective-permute-start | bytes 786440 | tf_op jit(solution)/shard_map/ppermute | solution.py:258
  56.6 9.2 %collective-permute-start.19 = (f32[2,192,128]{2,1,0:T(8,128)S(1)}, f32[2,192,128]{2,1,0:T(8,128)S(1)}, u32[]{:S(2)}, u32[]{:S(2)}) collective-permute-start(f32[2,192,128]{2,1,0:T(8,128)S(1)} %edge_terms.1), channel_id=1, source_target_pairs={{0,2},{1,3},{2,0},{3,1},{4,6},{5,7},{6,4},{7,5},{8,10},{9,11},{10,... | collective-permute-start | bytes 589832 | tf_op jit(solution)/shard_map/ppermute | solution.py:258

commit v5 on v4

--- a/solution.py
+++ b/solution.py
@@ -292,12 +292,15 @@
         phase = phase_shift.reshape(width, width)
         absorb = absorption.reshape(width, width)
         spot = positions.reshape(1, 2)
-        spot_tiles = jnp.broadcast_to(positions.reshape(2, 1, 1), (2, 8, LANES))
+        def tiles_of(spots):
+            return jnp.broadcast_to(spots.reshape(-1, 1, 1), (spots.size, 8, LANES))
+
+        spot_tiles = tiles_of(spot)
         observed = counts.reshape(frame, frame)
         sds = jax.ShapeDtypeStruct
         small = pltpu.CompilerParams(vmem_limit_bytes=8 << 20)
 
-        spots_rows = trade_rows([spot_tiles] * ways)
+        spots_rows = [tiles_of(spots) for spots in trade_rows([spot] * ways)]
         def load_kernel(phase_ref, absorb_ref, tile, *refs):
             edges, copies = refs[:ways], Copies(refs[ways])
             wait_for([copies.start(phase_ref, tile.at[0]), copies.start(absorb_ref, tile.at[1])])
@@ -314,6 +317,7 @@
             compiler_params=small,
             name="load",
         )(phase, absorb)
+        edges, spots_rows = lax.optimization_barrier((edges, spots_rows))
         sides = trade_columns(edges)
 
         def rows_of(refs, plane, rows):
@@ -420,6 +424,7 @@
             compiler_params=small,
             name="join",
         )(spot_tiles, part, *rims)
+        joined, probe_late = lax.optimization_barrier((joined, probe_wave))
         joineds = to_owner(joined)
 
         tables, sort = wave_tables(frame)
@@ -438,7 +443,7 @@
             out_specs=[VMEM] * 2,
             compiler_params=small,
             name="prepare",
-        )(spot, probe_wave, observed, sort)
+        )(spot, probe_late, observed, sort)
         places, counted = lax.optimization_barrier(
             (jnp.concatenate([spot_tiles] + spots_rows, 0), counted)
         )
@@ -535,46 +540,60 @@
             earlier = jnp.concatenate([earlier[HALO:], middle[: HALO // 2]], 0)
             return jnp.where(rep == 0, earlier, later)
 
-        def parts_kernel(spot_ref, *refs):
-            back_refs, (give, straight, across, term) = refs[:-4], refs[-4:]
-            if len(back_refs) > 1:
-                load_term(back_refs, term)
-            else:
-                term = back_refs[0]
-            rep, row = place.rep(), row_at(spot_ref)
+        def split_strips(term, row, straight, across):
+            rep = place.rep()
             index = row_index((HALO, frame))
             for plane in range(2):
-                give[plane] = rows_for(term, plane, row, 1 - rep)
                 first = term[plane, :HALO]
                 above = jnp.where(in_band(index, row, 0), first, 0.0)
                 below = jnp.where(in_band(index, row, 4), first, 0.0)
                 straight[plane] = jnp.where(rep == 1, above, below)
                 across[plane] = jnp.where(rep == 1, below, above)
 
-        def exchange(terms_here, owners, name):
-            give, straight, across = pl.pallas_call(
-                parts_kernel,
-                out_shape=[sds((2, half_rows, frame), f32)] + [sds((2, HALO, frame), f32)] * 2,
-                in_specs=[VMEM] * (1 + len(terms_here)),
-                out_specs=[VMEM] * 3,
-                scratch_shapes=[pltpu.VMEM((2, frame, frame), f32)],
-                compiler_params=small,
-                name=name,
-            )(spot_tiles, *terms_here)
-
+        def own_kernel(spot_ref, own, straight, across):
+            split_strips(own, row_at(spot_ref), straight, across)
+
+        def parts_kernel(spot_ref, *refs):
+            back_refs, (give, straight, across, term) = refs[:-4], refs[-4:]
+            load_term(back_refs, term)
+            for plane in range(2):
+                give[plane] = rows_for(term, plane, row_at(spot_ref), 1 - place.rep())
+            split_strips(term, row_at(spot_ref), straight, across)
+
+        def exchange(straight, across, owners):
             def of_those(target_of):
                 return lambda s, y, x, r: (
                     target_of(s, y, x, r) if (s == owner_of(x)) == owners else None
                 )
 
             return (
-                move(give, of_those(lambda s, y, x, r: (s, y, x, 1 - r))),
                 move(straight, of_those(lambda s, y, x, r: (s, y + 1 - 2 * r, x, r))),
                 move(across, of_those(lambda s, y, x, r: (s, y - 1 + 2 * r, x, 1 - r))),
             )
 
-        came_early = exchange(terms[1:2], True, "own_parts")
-        came_late = exchange(back[:3], False, "parts")
+        strip = sds((2, HALO, frame), f32)
+        own_strips = pl.pallas_call(
+            own_kernel,
+            out_shape=[strip] * 2,
+            in_specs=[VMEM] * 2,
+            out_specs=[VMEM] * 2,
+            compiler_params=small,
+            name="own_parts",
+        )(spot_tiles, terms[1])
+        came_early = exchange(*own_strips, True)
+        back, came_early = lax.optimization_barrier((back, came_early))
+        give, *strips = pl.pallas_call(
+            parts_kernel,
+            out_shape=[sds((2, half_rows, frame), f32), strip, strip],
+            in_specs=[VMEM] * 5,
+            out_specs=[VMEM] * 3,
+            scratch_shapes=[pltpu.VMEM((2, frame, frame), f32)],
+            compiler_params=small,
+            name="parts",
+        )(spot_tiles, *back)
+
+        came_late = exchange(*strips, False)
+        given = move(give, lambda s, y, x, r: (s, y, x, 1 - r))
 
         def keep_kernel(spot_ref, *refs):
             back_refs, (mine, term) = refs[:4], refs[4:]
@@ -595,9 +614,9 @@
 
         def add_band(band, plane, refs):
             spot_ref, partner_ref, kept_ref, *spot_refs = refs[: 3 + ways]
-            early, late = refs[3 + ways : 6 + ways], refs[6 + ways : count]
+            given, early, late = refs[3 + ways], refs[4 + ways : 6 + ways], refs[6 + ways : count]
             is_owner = place.section() == place.owner()
-            given, straight, across = (
+            straight, across = (
                 jnp.where(is_owner, a[plane], b[plane]) for a, b in zip(early, late)
             )
             rep = place.rep()
@@ -609,15 +628,15 @@
                     rep == 1, column_at(partner_ref, 1), column_at(partner_ref, 2)
                 )
             total = part_of_band(kept_ref[plane], column_at(spot_ref), band)
-            total += part_of_band(given, column_at(partner_ref), band)
+            total += part_of_band(given[plane], column_at(partner_ref), band)
             strip = part_of_band(straight, straight_column, band)
             strip += part_of_band(across, across_column, band)
             gap = jnp.zeros((half_rows - HALO, HALO), f32)
             early, late = jnp.concatenate([strip, gap], 0), jnp.concatenate([gap, strip], 0)
             return total + jnp.where(rep == 1, late, early)
 
-        pieces = (spot_tiles, spots_rep, kept, *spots_rows, *came_early, *came_late)
-        piece_specs = [VMEM] * (9 + ways)
+        pieces = (spot_tiles, spots_rep, kept, *spots_rows, given, *came_early, *came_late)
+        piece_specs = [VMEM] * (8 + ways)
         count = len(piece_specs)
 
         def edge_kernel(*refs):

time: 66.9 us -> 64.5 us (0.964)
  the two profiles are of different devices: /device:TPU:21 before, /device:TPU:13 now
where the time goes in v5:
time: 64.5 us; the launch traced here: 64.1 us
  starting transfers between devices  26.3 us (41%)
  waiting for transfers between devices  23.2 us (36%)
  Pallas kernels  10.7 us (17%)
  local copies, waits for them, and re-layouts  2.94 us (5%)
  between operations  0.93 us (1%)
    ppermute x19, starting transfers between devices, move(): return lax.ppermute(value, AXES, everywhere(target_of))  26.3 us
    ppermute x19, waiting for transfers between devices, move(): return lax.ppermute(value, AXES, everywhere(target_of))  23.2 us
    pallas_call x1, Pallas kernels, shards(): pl.pallas_call(frame_kernel, out_shape=[sds((2, frame, frame), f32)] * 4,...  6.15 us
    unnamed x14, local copies, waits for them, and re-layouts  2.15 us
  transfers between devices with their start and end apart: 19, of which 9 were waited for; matrix products, arithmetic and copies ran while one was open for 1% of the time, Pallas kernels for 5%

profile of v5, /device:TPU:13, one launch (start us, length us, event | category | flops | bytes accessed | tf_op | source)
XLA Modules:
  0.0 64.1 jit_solution(13056710938310491716)
XLA Ops:
  0.6 0.0 copy-start.6
  0.6 1.3 %collective-permute-start = (s32[1,2]{1,0:T(1,128)}, s32[1,2]{1,0:T(1,128)S(1)}, u32[]{:S(2)}, u32[]{:S(2)}) collective-permute-start(s32[1,2]{1,0:T(1,128)} %bitcast.11), channel_id=1, source_target_pairs={{0,4},{1,5},{2,6},{3,7},{4,0},{5,1},{6,2},{7,3},{8,12},{9,13},{10,... | collective-permute-start | bytes 32 | tf_op jit(solution)/shard_map/ppermute | solution.py:258
  1.9 0.0 copy-start.1
  1.9 1.1 %copy-done.1 = f32[1,1,384,384]{3,2,1,0:T(8,128)S(1)} copy-done((f32[1,1,384,384]{3,2,1,0:T(8,128)S(1)}, f32[1,1,384,384]{3,2,1,0:T(8,128)}, u32[]{:S(2)}) %copy-start.1) | copy-done | bytes 589848
  3.0 0.0 copy-start.2
  3.0 1.1 %copy-done.2 = f32[1,1,384,384]{3,2,1,0:T(8,128)S(1)} copy-done((f32[1,1,384,384]{3,2,1,0:T(8,128)S(1)}, f32[1,1,384,384]{3,2,1,0:T(8,128)}, u32[]{:S(2)}) %copy-start.2) | copy-done | bytes 589848
  4.0 0.0 copy-start.3
  4.1 0.0 copy-start.4
  4.1 0.3 load.1
  4.4 0.0 collective-permute-done
  4.4 0.1 broadcast_in_dim.23.refs_2_.refs_3_
  4.5 1.0 %collective-permute-start.1 = (f32[2,384,128]{2,1,0:T(8,128)S(1)}, f32[2,384,128]{2,1,0:T(8,128)S(1)}, u32[]{:S(2)}, u32[]{:S(2)}) collective-permute-start(f32[2,384,128]{2,1,0:T(8,128)S(1)} %get-tuple-element.37), channel_id=1, source_target_pairs={{0,2},{1,3},{2,0},{3,1},{4,6},{5,7},{6,4},{7,5},{8,10},{9,11},{10,... | collective-permute-start | bytes 1179656 | tf_op jit(solution)/shard_map/ppermute | solution.py:258
  5.4 1.3 %collective-permute-done.1.refs_1_ = f32[2,384,128]{2,1,0:T(8,128)S(1)} collective-permute-done((f32[2,384,128]{2,1,0:T(8,128)S(1)}, f32[2,384,128]{2,1,0:T(8,128)S(1)}, u32[]{:S(2)}, u32[]{:S(2)}) %collective-permute-start.1) | collective-permute-done | bytes 393248 | tf_op jit(solution)/shard_map/ppermute | solution.py:258
  6.8 0.2 halo_rows.1
  7.0 1.0 %collective-permute-start.2 = (f32[2,128,256]{2,1,0:T(8,128)S(1)}, f32[2,128,256]{2,1,0:T(8,128)S(1)}, u32[]{:S(2)}, u32[]{:S(2)}) collective-permute-start(f32[2,128,256]{2,1,0:T(8,128)S(1)} %halo_rows.1), channel_id=1, source_target_pairs={{0,4},{1,5},{2,6},{3,7},{4,0},{5,1},{6,2},{7,3},{8,12},{9,13},{10,... | collective-permute-start | bytes 786440 | tf_op jit(solution)/shard_map/ppermute | solution.py:258
  8.0 0.7 %broadcast_in_dim.21.spot_ref.refs_0_ = s32[2,8,128]{2,1,0:T(8,128)S(1)} broadcast(s32[2]{0:T(128)} %bitcast.12), dimensions={0} | broadcast | bytes 8200 | tf_op jit(solution)/shard_map/broadcast_in_dim | solution.py:296
  8.7 0.6 window.1
  9.3 0.7 %collective-permute-start.6 = (f32[2,128,256]{2,1,0:T(8,128)S(1)}, f32[2,128,256]{2,1,0:T(8,128)S(1)}, u32[]{:S(2)}, u32[]{:S(2)}) collective-permute-start(f32[2,128,256]{2,1,0:T(8,128)S(1)} %get-tuple-element.44.refs_1_), channel_id=1, source_target_pairs={{2,18},{3,19},{6,22},{7,23},{24,8},{25,9},{28,12},{29,13}} | collective-permute-start | bytes 786440 | tf_op jit(solution)/shard_map/ppermute | solution.py:258
  10.0 3.8 %collective-permute-start.5 = (f32[2,128,256]{2,1,0:T(8,128)S(1)}, f32[2,128,256]{2,1,0:T(8,128)S(1)}, u32[]{:S(2)}, u32[]{:S(2)}) collective-permute-start(f32[2,128,256]{2,1,0:T(8,128)S(1)} %get-tuple-element.44.refs_1_), channel_id=1, source_target_pairs={{10,18},{11,19},{14,22},{15,23},{16,8},{17,9},{20,12},{21,13}} | collective-permute-start | bytes 786440 | tf_op jit(solution)/shard_map/ppermute | solution.py:258
  13.9 0.7 %collective-permute-start.4 = (f32[2,128,256]{2,1,0:T(8,128)S(1)}, f32[2,128,256]{2,1,0:T(8,128)S(1)}, u32[]{:S(2)}, u32[]{:S(2)}) collective-permute-start(f32[2,128,256]{2,1,0:T(8,128)S(1)} %get-tuple-element.44.refs_1_), channel_id=1, source_target_pairs={{0,8},{1,9},{4,12},{5,13},{26,18},{27,19},{30,22},{31,23}} | collective-permute-start | bytes 786440 | tf_op jit(solution)/shard_map/ppermute | solution.py:258
  14.5 0.1 collective-permute-done.2.refs_0_
  14.6 0.1 join.1.refs_5_
  14.7 0.7 %collective-permute-start.9 = (f32[2,128,256]{2,1,0:T(8,128)S(1)}, f32[2,128,256]{2,1,0:T(8,128)S(1)}, u32[]{:S(2)}, u32[]{:S(2)}) collective-permute-start(f32[2,128,256]{2,1,0:T(8,128)S(1)} %join.1.refs_5_), channel_id=1, source_target_pairs={{2,18},{3,19},{6,22},{7,23},{24,8},{25,9},{28,12},{29,13}} | collective-permute-start | bytes 786440 | tf_op jit(solution)/shard_map/ppermute | solution.py:258
  15.4 3.8 %collective-permute-start.8 = (f32[2,128,256]{2,1,0:T(8,128)S(1)}, f32[2,128,256]{2,1,0:T(8,128)S(1)}, u32[]{:S(2)}, u32[]{:S(2)}) collective-permute-start(f32[2,128,256]{2,1,0:T(8,128)S(1)} %join.1.refs_5_), channel_id=1, source_target_pairs={{10,18},{11,19},{14,22},{15,23},{16,8},{17,9},{20,12},{21,13}} | collective-permute-start | bytes 786440 | tf_op jit(solution)/shard_map/ppermute | solution.py:258
  19.2 0.0 collective-permute-done.6.refs_3_
  19.2 0.7 %collective-permute-start.7 = (f32[2,128,256]{2,1,0:T(8,128)S(1)}, f32[2,128,256]{2,1,0:T(8,128)S(1)}, u32[]{:S(2)}, u32[]{:S(2)}) collective-permute-start(f32[2,128,256]{2,1,0:T(8,128)S(1)} %join.1.refs_5_), channel_id=1, source_target_pairs={{0,8},{1,9},{4,12},{5,13},{26,18},{27,19},{30,22},{31,23}} | collective-permute-start | bytes 786440 | tf_op jit(solution)/shard_map/ppermute | solution.py:258
  19.9 0.0 copy-done.6
  19.9 0.0 copy-done.3
  19.9 0.0 copy-done.4
  19.9 0.0 copy-done.5
  19.9 0.9 %prepare.1 = (f32[2,256,256]{2,1,0:T(8,128)S(1)}, f32[256,256]{1,0:T(8,128)S(1)}) custom-call(s32[1,2]{1,0:T(1,128)S(1)} %bitcast.13, f32[2,256,256]{2,1,0:T(8,128)S(1)} %copy-done.3, s32[256,256]{1,0:T(8,128)S(1)} %bitcast.10, bf16[2,256,256]{2,1,0:T(8,128)(2,1)S(1)} %copy-done.5), custom_call_target="tpu_custom_call" | custom-call | tf_op jit(solution)/shard_map/prepare/pallas_call | solution.py:439
  20.8 0.0 collective-permute-done.5.refs_2_
  20.8 0.3 collective-permute-start.3
  21.1 0.0 collective-permute-done.4.refs_0_
  21.1 2.7 %collective-permute-done.3.partner_ref.refs_1_ = s32[4,8,128]{2,1,0:T(8,128)S(1)} collective-permute-done((s32[4,8,128]{2,1,0:T(8,128)S(1)}, s32[4,8,128]{2,1,0:T(8,128)S(1)}, u32[]{:S(2)}, u32[]{:S(2)}) %collective-permute-start.3) | collective-permute-done | bytes 16416 | tf_op jit(solution)/shard_map/ppermute | solution.py:258
  23.8 0.0 collective-permute-done.9.refs_7_
  23.8 1.4 %collective-permute-done.8.refs_6_ = f32[2,128,256]{2,1,0:T(8,128)S(1)} collective-permute-done((f32[2,128,256]{2,1,0:T(8,128)S(1)}, f32[2,128,256]{2,1,0:T(8,128)S(1)}, u32[]{:S(2)}, u32[]{:S(2)}) %collective-permute-start.8) | collective-permute-done | bytes 262176 | tf_op jit(solution)/shard_map/ppermute | solution.py:258
  25.2 0.0 collective-permute-done.7.refs_4_
  25.2 0.0 copy-done
  25.2 6.2 %frame.1 = (f32[2,256,256]{2,1,0:T(8,128)S(1)}, f32[2,256,256]{2,1,0:T(8,128)S(1)}, f32[2,256,256]{2,1,0:T(8,128)S(1)}, f32[2,256,256]{2,1,0:T(8,128)S(1)}) custom-call(s32[4,8,128]{2,1,0:T(8,128)S(1)} %collective-permute-done.3.partner_ref.refs_1_, f32[2,256,256]{2,1,0:T(8,128)S(1)} %get-tuple-element.42.probe, f32[256,256]{1,0:T(8,128)S(1)} %get-tuple-element.43.seen, ...), custom_call_target="tpu_custom_call" | custom-call | tf_op jit(solution)/shard_map/frame/pallas_call | solution.py:492
  31.3 0.7 %collective-permute-start.10 = (f32[2,256,256]{2,1,0:T(8,128)S(1)}, f32[2,256,256]{2,1,0:T(8,128)S(1)}, u32[]{:S(2)}, u32[]{:S(2)}) collective-permute-start(f32[2,256,256]{2,1,0:T(8,128)S(1)} %get-tuple-element.46), channel_id=1, source_target_pairs={{8,24},{9,25},{12,28},{13,29},{18,2},{19,3},{22,6},{23,7}} | collective-permute-start | bytes 1572872 | tf_op jit(solution)/shard_map/ppermute | solution.py:258
  32.0 0.7 %collective-permute-start.11 = (f32[2,256,256]{2,1,0:T(8,128)S(1)}, f32[2,256,256]{2,1,0:T(8,128)S(1)}, u32[]{:S(2)}, u32[]{:S(2)}) collective-permute-start(f32[2,256,256]{2,1,0:T(8,128)S(1)} %get-tuple-element.47), channel_id=1, source_target_pairs={{8,0},{9,1},{12,4},{13,5},{18,26},{19,27},{22,30},{23,31}} | collective-permute-start | bytes 1572872 | tf_op jit(solution)/shard_map/ppermute | solution.py:258
  32.7 1.3 %collective-permute-start.12 = (f32[2,256,256]{2,1,0:T(8,128)S(1)}, f32[2,256,256]{2,1,0:T(8,128)S(1)}, u32[]{:S(2)}, u32[]{:S(2)}) collective-permute-start(f32[2,256,256]{2,1,0:T(8,128)S(1)} %get-tuple-element.48), channel_id=1, source_target_pairs={{8,16},{9,17},{12,20},{13,21},{18,10},{19,11},{22,14},{23,15}} | collective-permute-start | bytes 1572872 | tf_op jit(solution)/shard_map/ppermute | solution.py:258
  34.0 0.1 own_parts.1
  34.1 0.7 %collective-permute-start.13 = (f32[2,128,256]{2,1,0:T(8,128)S(1)}, f32[2,128,256]{2,1,0:T(8,128)S(1)}, u32[]{:S(2)}, u32[]{:S(2)}) collective-permute-start(f32[2,128,256]{2,1,0:T(8,128)S(1)} %get-tuple-element.50), channel_id=1, source_target_pairs={{8,12},{13,9},{18,22},{23,19}} | collective-permute-start | bytes 786440 | tf_op jit(solution)/shard_map/ppermute | solution.py:258
  34.8 0.7 %collective-permute-start.14 = (f32[2,128,256]{2,1,0:T(8,128)S(1)}, f32[2,128,256]{2,1,0:T(8,128)S(1)}, u32[]{:S(2)}, u32[]{:S(2)}) collective-permute-start(f32[2,128,256]{2,1,0:T(8,128)S(1)} %get-tuple-element.51), channel_id=1, source_target_pairs={{9,12},{12,9},{19,22},{22,19}} | collective-permute-start | bytes 786440 | tf_op jit(solution)/shard_map/ppermute | solution.py:258
  35.5 0.0 collective-permute-done.13.refs_5_
  35.5 0.0 collective-permute-done.14.refs_6_
  35.5 0.0 collective-permute-done.10.refs_0_
  35.6 0.0 collective-permute-done.11.refs_1_
  35.6 11.9 %collective-permute-done.12.refs_2_ = f32[2,256,256]{2,1,0:T(8,128)S(1)} collective-permute-done((f32[2,256,256]{2,1,0:T(8,128)S(1)}, f32[2,256,256]{2,1,0:T(8,128)S(1)}, u32[]{:S(2)}, u32[]{:S(2)}) %collective-permute-start.12) | collective-permute-done | bytes 524320 | tf_op jit(solution)/shard_map/ppermute | solution.py:258
  47.4 0.3 parts.1
  47.7 0.1 collective-permute-start.15
  47.8 1.3 %collective-permute-start.16 = (f32[2,128,256]{2,1,0:T(8,128)S(1)}, f32[2,128,256]{2,1,0:T(8,128)S(1)}, u32[]{:S(2)}, u32[]{:S(2)}) collective-permute-start(f32[2,128,256]{2,1,0:T(8,128)S(1)} %get-tuple-element.59), channel_id=1, source_target_pairs={{0,4},{2,6},{5,1},{7,3},{10,14},{15,11},{16,20},{21,17},{24,28},{2... | collective-permute-start | bytes 786440 | tf_op jit(solution)/shard_map/ppermute | solution.py:258
  49.1 3.7 %collective-permute-start.17 = (f32[2,128,256]{2,1,0:T(8,128)S(1)}, f32[2,128,256]{2,1,0:T(8,128)S(1)}, u32[]{:S(2)}, u32[]{:S(2)}) collective-permute-start(f32[2,128,256]{2,1,0:T(8,128)S(1)} %get-tuple-element.60), channel_id=1, source_target_pairs={{1,4},{3,6},{4,1},{6,3},{11,14},{14,11},{17,20},{20,17},{25,28},{2... | collective-permute-start | bytes 786440 | tf_op jit(solution)/shard_map/ppermute | solution.py:258
  52.8 0.2 keep.1.refs_2_
  53.0 2.2 %collective-permute-done.16.refs_7_ = f32[2,128,256]{2,1,0:T(8,128)S(1)} collective-permute-done((f32[2,128,256]{2,1,0:T(8,128)S(1)}, f32[2,128,256]{2,1,0:T(8,128)S(1)}, u32[]{:S(2)}, u32[]{:S(2)}) %collective-permute-start.16) | collective-permute-done | bytes 262176 | tf_op jit(solution)/shard_map/ppermute | solution.py:258
  55.2 2.0 %collective-permute-done.17.refs_8_ = f32[2,128,256]{2,1,0:T(8,128)S(1)} collective-permute-done((f32[2,128,256]{2,1,0:T(8,128)S(1)}, f32[2,128,256]{2,1,0:T(8,128)S(1)}, u32[]{:S(2)}, u32[]{:S(2)}) %collective-permute-start.17) | collective-permute-done | bytes 262176 | tf_op jit(solution)/shard_map/ppermute | solution.py:258
  57.2 1.6 %collective-permute-done.15.refs_4_ = f32[2,192,256]{2,1,0:T(8,128)S(1)} collective-permute-done((f32[2,192,256]{2,1,0:T(8,128)S(1)}, f32[2,192,256]{2,1,0:T(8,128)S(1)}, u32[]{:S(2)}, u32[]{:S(2)}) %collective-permute-start.15) | collective-permute-done | bytes 393248 | tf_op jit(solution)/shard_map/ppermute | solution.py:258
  58.8 0.2 edge_terms.1
  59.0 3.4 %collective-permute-start.18 = (f32[2,192,128]{2,1,0:T(8,128)S(1)}, f32[2,192,128]{2,1,0:T(8,128)S(1)}, u32[]{:S(2)}, u32[]{:S(2)}) collective-permute-start(f32[2,192,128]{2,1,0:T(8,128)S(1)} %edge_terms.1), channel_id=1, source_target_pairs={{0,2},{1,3},{2,0},{3,1},{4,6},{5,7},{6,4},{7,5},{8,10},{9,11},{10,... | collective-permute-start | bytes 589832 | tf_op jit(solution)/shard_map/ppermute | solution.py:258
  62.4 1.0 %inner_terms.1 = (f32[192,384]{1,0:T(8,128)}, f32[192,384]{1,0:T(8,128)}, f32[1,2,192,128]{3,2,1,0:T(8,128)S(1)}) custom-call(s32[2,8,128]{2,1,0:T(8,128)S(1)} %broadcast_in_dim.21.spot_ref.refs_0_, s32[4,8,128]{2,1,0:T(8,128)S(1)} %collective-permute-done.3.partner_ref.refs_1_, f32[2,192,256]{2,1,0:T(8,128)S(1)} %keep.1.refs_2_, ...), custom_call_target="tpu_custom_call" | custom-call | flops 4194304 | bytes 2097152 | tf_op jit(solution)/shard_map/inner_terms/pallas_call | solution.py:679
  63.4 0.1 collective-permute-done.18.refs_0_
  63.4 0.7 %finish.1 = (f32[192,384]{1,0:T(8,128)}, f32[192,384]{1,0:T(8,128)}) custom-call(f32[192,384]{1,0:T(8,128)} %get-tuple-element.61.phase_in, f32[192,384]{1,0:T(8,128)} %get-tuple-element.62.absorb_in, f32[1,2,192,128]{3,2,1,0:T(8,128)S(1)} %get-tuple-element.63.inner_ref, ...), custom_call_target="tpu_custom_call", output_to_operand_aliasing={{0}: (0, {}), {1}: (1, {})} | custom-call | tf_op jit(solution)/shard_map/finish/pallas_call | solution.py:707
  (3 shorter events, 0.0 us)
Async XLA Ops:
  0.6 19.3 %copy-start.6 = (s32[1,1,1,2]{3,2,1,0:T(1,128)S(1)}, s32[1,1,1,2]{3,2,1,0:T(1,128)}, u32[]{:S(2)}) copy-start(s32[1,1,1,2]{3,2,1,0:T(1,128)} %param.10) | copy-start | bytes 28
  0.6 3.7 %collective-permute-start = (s32[1,2]{1,0:T(1,128)}, s32[1,2]{1,0:T(1,128)S(1)}, u32[]{:S(2)}, u32[]{:S(2)}) collective-permute-start(s32[1,2]{1,0:T(1,128)} %bitcast.11), channel_id=1, source_target_pairs={{0,4},{1,5},{2,6},{3,7},{4,0},{5,1},{6,2},{7,3},{8,12},{9,13},{10,... | collective-permute-start | bytes 32 | tf_op jit(solution)/shard_map/ppermute | solution.py:258
  1.9 1.1 %copy-start.1 = (f32[1,1,384,384]{3,2,1,0:T(8,128)S(1)}, f32[1,1,384,384]{3,2,1,0:T(8,128)}, u32[]{:S(2)}) copy-start(f32[1,1,384,384]{3,2,1,0:T(8,128)} %param.7) | copy-start | bytes 1769476
  3.0 1.1 %copy-start.2 = (f32[1,1,384,384]{3,2,1,0:T(8,128)S(1)}, f32[1,1,384,384]{3,2,1,0:T(8,128)}, u32[]{:S(2)}) copy-start(f32[1,1,384,384]{3,2,1,0:T(8,128)} %param.8) | copy-start | bytes 1769476
  4.0 15.9 %copy-start.3 = (f32[2,256,256]{2,1,0:T(8,128)S(1)}, f32[2,256,256]{2,1,0:T(8,128)}, u32[]{:S(2)}) copy-start(f32[2,256,256]{2,1,0:T(8,128)} %probe) | copy-start | bytes 1572868
  4.1 15.9 %copy-start.4 = (s32[1,1,1,256,256]{4,3,2,1,0:T(8,128)S(1)}, s32[1,1,1,256,256]{4,3,2,1,0:T(8,128)}, u32[]{:S(2)}) copy-start(s32[1,1,1,256,256]{4,3,2,1,0:T(8,128)} %param.11) | copy-start | bytes 786436
  4.1 15.9 %copy-start.5 = (bf16[2,256,256]{2,1,0:T(8,128)(2,1)S(1)}, bf16[2,256,256]{2,1,0:T(8,128)(2,1)}, u32[]{:S(2)}) copy-start(bf16[2,256,256]{2,1,0:T(8,128)(2,1)} %constant.4.clone.sort) | copy-start | bytes 786436
  4.1 21.1 %copy-start = (bf16[12,2,256,256]{3,2,1,0:T(8,128)(2,1)S(1)}, bf16[12,2,256,256]{3,2,1,0:T(8,128)(2,1)}, u32[]{:S(2)}) copy-start(bf16[12,2,256,256]{3,2,1,0:T(8,128)(2,1)} %constant.5.clone.tables) | copy-start | bytes 9437188
  4.5 2.3 %collective-permute-start.1 = (f32[2,384,128]{2,1,0:T(8,128)S(1)}, f32[2,384,128]{2,1,0:T(8,128)S(1)}, u32[]{:S(2)}, u32[]{:S(2)}) collective-permute-start(f32[2,384,128]{2,1,0:T(8,128)S(1)} %get-tuple-element.37), channel_id=1, source_target_pairs={{0,2},{1,3},{2,0},{3,1},{4,6},{5,7},{6,4},{7,5},{8,10},{9,11},{10,... | collective-permute-start | bytes 1179656 | tf_op jit(solution)/shard_map/ppermute | solution.py:258
  7.0 7.6 %collective-permute-start.2 = (f32[2,128,256]{2,1,0:T(8,128)S(1)}, f32[2,128,256]{2,1,0:T(8,128)S(1)}, u32[]{:S(2)}, u32[]{:S(2)}) collective-permute-start(f32[2,128,256]{2,1,0:T(8,128)S(1)} %halo_rows.1), channel_id=1, source_target_pairs={{0,4},{1,5},{2,6},{3,7},{4,0},{5,1},{6,2},{7,3},{8,12},{9,13},{10,... | collective-permute-start | bytes 786440 | tf_op jit(solution)/shard_map/ppermute | solution.py:258
  9.3 9.9 %collective-permute-start.6 = (f32[2,128,256]{2,1,0:T(8,128)S(1)}, f32[2,128,256]{2,1,0:T(8,128)S(1)}, u32[]{:S(2)}, u32[]{:S(2)}) collective-permute-start(f32[2,128,256]{2,1,0:T(8,128)S(1)} %get-tuple-element.44.refs_1_), channel_id=1, source_target_pairs={{2,18},{3,19},{6,22},{7,23},{24,8},{25,9},{28,12},{29,13}} | collective-permute-start | bytes 786440 | tf_op jit(solution)/shard_map/ppermute | solution.py:258
  10.0 10.8 %collective-permute-start.5 = (f32[2,128,256]{2,1,0:T(8,128)S(1)}, f32[2,128,256]{2,1,0:T(8,128)S(1)}, u32[]{:S(2)}, u32[]{:S(2)}) collective-permute-start(f32[2,128,256]{2,1,0:T(8,128)S(1)} %get-tuple-element.44.refs_1_), channel_id=1, source_target_pairs={{10,18},{11,19},{14,22},{15,23},{16,8},{17,9},{20,12},{21,13}} | collective-permute-start | bytes 786440 | tf_op jit(solution)/shard_map/ppermute | solution.py:258
  13.9 7.3 %collective-permute-start.4 = (f32[2,128,256]{2,1,0:T(8,128)S(1)}, f32[2,128,256]{2,1,0:T(8,128)S(1)}, u32[]{:S(2)}, u32[]{:S(2)}) collective-permute-start(f32[2,128,256]{2,1,0:T(8,128)S(1)} %get-tuple-element.44.refs_1_), channel_id=1, source_target_pairs={{0,8},{1,9},{4,12},{5,13},{26,18},{27,19},{30,22},{31,23}} | collective-permute-start | bytes 786440 | tf_op jit(solution)/shard_map/ppermute | solution.py:258
  14.7 9.1 %collective-permute-start.9 = (f32[2,128,256]{2,1,0:T(8,128)S(1)}, f32[2,128,256]{2,1,0:T(8,128)S(1)}, u32[]{:S(2)}, u32[]{:S(2)}) collective-permute-start(f32[2,128,256]{2,1,0:T(8,128)S(1)} %join.1.refs_5_), channel_id=1, source_target_pairs={{2,18},{3,19},{6,22},{7,23},{24,8},{25,9},{28,12},{29,13}} | collective-permute-start | bytes 786440 | tf_op jit(solution)/shard_map/ppermute | solution.py:258
  15.4 9.8 %collective-permute-start.8 = (f32[2,128,256]{2,1,0:T(8,128)S(1)}, f32[2,128,256]{2,1,0:T(8,128)S(1)}, u32[]{:S(2)}, u32[]{:S(2)}) collective-permute-start(f32[2,128,256]{2,1,0:T(8,128)S(1)} %join.1.refs_5_), channel_id=1, source_target_pairs={{10,18},{11,19},{14,22},{15,23},{16,8},{17,9},{20,12},{21,13}} | collective-permute-start | bytes 786440 | tf_op jit(solution)/shard_map/ppermute | solution.py:258
  19.2 6.0 %collective-permute-start.7 = (f32[2,128,256]{2,1,0:T(8,128)S(1)}, f32[2,128,256]{2,1,0:T(8,128)S(1)}, u32[]{:S(2)}, u32[]{:S(2)}) collective-permute-start(f32[2,128,256]{2,1,0:T(8,128)S(1)} %join.1.refs_5_), channel_id=1, source_target_pairs={{0,8},{1,9},{4,12},{5,13},{26,18},{27,19},{30,22},{31,23}} | collective-permute-start | bytes 786440 | tf_op jit(solution)/shard_map/ppermute | solution.py:258
  20.8 2.9 %collective-permute-start.3 = (s32[4,8,128]{2,1,0:T(8,128)S(1)}, s32[4,8,128]{2,1,0:T(8,128)S(1)}, u32[]{:S(2)}, u32[]{:S(2)}) collective-permute-start(s32[4,8,128]{2,1,0:T(8,128)S(1)} %pad_add_fusion), channel_id=1, source_target_pairs={{0,1},{1,0},{2,3},{3,2},{4,5},{5,4},{6,7},{7,6},{8,9},{9,8},{10,11... | collective-permute-start | bytes 49160 | tf_op jit(solution)/shard_map/ppermute | solution.py:258
  31.3 4.2 %collective-permute-start.10 = (f32[2,256,256]{2,1,0:T(8,128)S(1)}, f32[2,256,256]{2,1,0:T(8,128)S(1)}, u32[]{:S(2)}, u32[]{:S(2)}) collective-permute-start(f32[2,256,256]{2,1,0:T(8,128)S(1)} %get-tuple-element.46), channel_id=1, source_target_pairs={{8,24},{9,25},{12,28},{13,29},{18,2},{19,3},{22,6},{23,7}} | collective-permute-start | bytes 1572872 | tf_op jit(solution)/shard_map/ppermute | solution.py:258
  32.0 3.5 %collective-permute-start.11 = (f32[2,256,256]{2,1,0:T(8,128)S(1)}, f32[2,256,256]{2,1,0:T(8,128)S(1)}, u32[]{:S(2)}, u32[]{:S(2)}) collective-permute-start(f32[2,256,256]{2,1,0:T(8,128)S(1)} %get-tuple-element.47), channel_id=1, source_target_pairs={{8,0},{9,1},{12,4},{13,5},{18,26},{19,27},{22,30},{23,31}} | collective-permute-start | bytes 1572872 | tf_op jit(solution)/shard_map/ppermute | solution.py:258
  32.7 14.7 %collective-permute-start.12 = (f32[2,256,256]{2,1,0:T(8,128)S(1)}, f32[2,256,256]{2,1,0:T(8,128)S(1)}, u32[]{:S(2)}, u32[]{:S(2)}) collective-permute-start(f32[2,256,256]{2,1,0:T(8,128)S(1)} %get-tuple-element.48), channel_id=1, source_target_pairs={{8,16},{9,17},{12,20},{13,21},{18,10},{19,11},{22,14},{23,15}} | collective-permute-start | bytes 1572872 | tf_op jit(solution)/shard_map/ppermute | solution.py:258
  34.1 1.4 %collective-permute-start.13 = (f32[2,128,256]{2,1,0:T(8,128)S(1)}, f32[2,128,256]{2,1,0:T(8,128)S(1)}, u32[]{:S(2)}, u32[]{:S(2)}) collective-permute-start(f32[2,128,256]{2,1,0:T(8,128)S(1)} %get-tuple-element.50), channel_id=1, source_target_pairs={{8,12},{13,9},{18,22},{23,19}} | collective-permute-start | bytes 786440 | tf_op jit(solution)/shard_map/ppermute | solution.py:258
  34.8 0.7 %collective-permute-start.14 = (f32[2,128,256]{2,1,0:T(8,128)S(1)}, f32[2,128,256]{2,1,0:T(8,128)S(1)}, u32[]{:S(2)}, u32[]{:S(2)}) collective-permute-start(f32[2,128,256]{2,1,0:T(8,128)S(1)} %get-tuple-element.51), channel_id=1, source_target_pairs={{9,12},{12,9},{19,22},{22,19}} | collective-permute-start | bytes 786440 | tf_op jit(solution)/shard_map/ppermute | solution.py:258
  47.7 11.1 %collective-permute-start.15 = (f32[2,192,256]{2,1,0:T(8,128)S(1)}, f32[2,192,256]{2,1,0:T(8,128)S(1)}, u32[]{:S(2)}, u32[]{:S(2)}) collective-permute-start(f32[2,192,256]{2,1,0:T(8,128)S(1)} %get-tuple-element.56), channel_id=1, source_target_pairs={{0,1},{1,0},{2,3},{3,2},{4,5},{5,4},{6,7},{7,6},{8,9},{9,8},{10,11... | collective-permute-start | bytes 1179656 | tf_op jit(solution)/shard_map/ppermute | solution.py:258
  47.8 7.4 %collective-permute-start.16 = (f32[2,128,256]{2,1,0:T(8,128)S(1)}, f32[2,128,256]{2,1,0:T(8,128)S(1)}, u32[]{:S(2)}, u32[]{:S(2)}) collective-permute-start(f32[2,128,256]{2,1,0:T(8,128)S(1)} %get-tuple-element.59), channel_id=1, source_target_pairs={{0,4},{2,6},{5,1},{7,3},{10,14},{15,11},{16,20},{21,17},{24,28},{2... | collective-permute-start | bytes 786440 | tf_op jit(solution)/shard_map/ppermute | solution.py:258
  49.1 8.1 %collective-permute-start.17 = (f32[2,128,256]{2,1,0:T(8,128)S(1)}, f32[2,128,256]{2,1,0:T(8,128)S(1)}, u32[]{:S(2)}, u32[]{:S(2)}) collective-permute-start(f32[2,128,256]{2,1,0:T(8,128)S(1)} %get-tuple-element.60), channel_id=1, source_target_pairs={{1,4},{3,6},{4,1},{6,3},{11,14},{14,11},{17,20},{20,17},{25,28},{2... | collective-permute-start | bytes 786440 | tf_op jit(solution)/shard_map/ppermute | solution.py:258
  59.0 4.4 %collective-permute-start.18 = (f32[2,192,128]{2,1,0:T(8,128)S(1)}, f32[2,192,128]{2,1,0:T(8,128)S(1)}, u32[]{:S(2)}, u32[]{:S(2)}) collective-permute-start(f32[2,192,128]{2,1,0:T(8,128)S(1)} %edge_terms.1), channel_id=1, source_target_pairs={{0,2},{1,3},{2,0},{3,1},{4,6},{5,7},{6,4},{7,5},{8,10},{9,11},{10,... | collective-permute-start | bytes 589832 | tf_op jit(solution)/shard_map/ppermute | solution.py:258

commit v6 on v5

--- a/solution.py
+++ b/solution.py
@@ -301,22 +301,21 @@
         small = pltpu.CompilerParams(vmem_limit_bytes=8 << 20)
 
         spots_rows = [tiles_of(spots) for spots in trade_rows([spot] * ways)]
-        def load_kernel(phase_ref, absorb_ref, tile, *refs):
-            edges, copies = refs[:ways], Copies(refs[ways])
-            wait_for([copies.start(phase_ref, tile.at[0]), copies.start(absorb_ref, tile.at[1])])
+        tile = jnp.stack([phase, absorb])
+
+        def load_kernel(tile, *edges):
             for way in range(ways):
                 start = place.sent(place.column(), way) * (width - HALO)
                 edges[way][...] = tile[:, :, pl.ds(pl.multiple_of(start, LANES), HALO)]
 
-        tile, *edges = pl.pallas_call(
+        edges = pl.pallas_call(
             load_kernel,
-            out_shape=[sds((2, width, width), f32)] + [sds((2, width, HALO), f32)] * ways,
-            in_specs=[HBM] * 2,
-            out_specs=[VMEM] * (1 + ways),
-            scratch_shapes=[pltpu.SemaphoreType.DMA((2,))],
-            compiler_params=small,
-            name="load",
-        )(phase, absorb)
+            out_shape=[sds((2, width, HALO), f32)] * ways,
+            in_specs=[VMEM],
+            out_specs=[VMEM] * ways,
+            compiler_params=small,
+            name="edges",
+        )(tile)
         edges, spots_rows = lax.optimization_barrier((edges, spots_rows))
         sides = trade_columns(edges)
 
@@ -453,16 +452,19 @@
             whole_refs, joined_refs, outs = refs[:4], refs[4:8], refs[8:12]
             fields, exits = refs[12:]
             own_is_second = place.owner() == 1
-            for half, parts in ((slice(HALO, None), whole_refs), (slice(None, HALO), joined_refs)):
-                for plane in range(2):
-                    near, own, middle, far = (part[plane] for part in parts)
-                    fields[0, plane, half] = jnp.where(own_is_second, near, far)
-                    fields[1, plane, half] = jnp.where(own_is_second, own, middle)
-                    fields[2, plane, half] = jnp.where(own_is_second, middle, own)
-                    fields[3, plane, half] = jnp.where(own_is_second, far, near)
+            far, middle, own, near = zip(joined_refs[::-1], whole_refs)
+            choices = ((near, far), (own, middle), (middle, own), (far, near))
+
+            def field(number, plane):
+                first, second = choices[number]
+                return jnp.concatenate(
+                    [jnp.where(own_is_second, a[plane], b[plane]) for a, b in zip(first, second)], 0
+                )
+
             re, im = probe[0], probe[1]
             for number in range(4):
-                o_re, o_im = fields[number, 0], fields[number, 1]
+                o_re, o_im = field(number, 0), field(number, 1)
+                fields[number, 0], fields[number, 1] = o_re, o_im
                 exit_re, exit_im = o_re * re - o_im * im, o_re * im + o_im * re
                 exits[number, 0], exits[number, 1] = exit_re, exit_im
                 if number < 3:
@@ -476,18 +478,19 @@
                 else:
                     re, im = near_field(tables, re, im)
                 exit_re, exit_im = exits[number, 0], exits[number, 1]
-                phase_term = -(re * exit_im + im * exit_re)
-                absorb_term = im * exit_im - re * exit_re
+                found = -(re * exit_im + im * exit_re), im * exit_im - re * exit_re
                 if number > 0:
                     o_re, o_im = fields[number, 0], fields[number, 1]
                     re, im = o_re * re - o_im * im, o_re * im + o_im * re
-                exits[number, 0], exits[number, 1] = phase_term, absorb_term
-            for plane in range(2):
-                one, two, three, four = (exits[number, plane] for number in range(4))
-                outs[0][plane] = jnp.where(own_is_second, one, four)
-                outs[1][plane] = jnp.where(own_is_second, two, three)
-                outs[2][plane] = jnp.where(own_is_second, three, two)
-                outs[3][plane] = jnp.where(own_is_second, four, one)
+                one, other = (0, 3) if number in (0, 3) else (1, 2)
+                for plane, term in enumerate(found):
+                    if number >= 2:
+                        outs[one][plane] = term
+                        outs[other][plane] = term
+                    else:
+                        kept_term = outs[one][plane]
+                        outs[one][plane] = jnp.where(own_is_second, term, kept_term)
+                        outs[other][plane] = jnp.where(own_is_second, kept_term, term)
 
         terms = pl.pallas_call(
             frame_kernel,
@@ -502,7 +505,7 @@
             name="frame",
         )(
             spots_rep, rolled, counted, tables,
-            wholes[0], whole, wholes[1], wholes[2],
+            wholes[2], wholes[1], whole, wholes[0],
             joineds[0], joined, joineds[1], joineds[2],
         )
 

time: 64.5 us -> 64.1 us (level)
  local copies, waits for them, and re-layouts: 2.94 us -> 0.16 us
  other arithmetic: 0.01 us -> 1.32 us
  waiting for transfers between devices: 23.2 us -> 24.2 us
    unnamed x14 -> x10, local copies, waits for them, and re-layouts: 2.15 us -> 0.02 us
    another operation x0 -> x1, other arithmetic: none -> 1.32 us  [shards(): tile = jnp.stack([phase, absorb])]
    ppermute x19, waiting for transfers between devices: 23.2 us -> 24.2 us  [move(): return lax.ppermute(value, AXES, everywhere(target_of))]
    broadcast_in_dim x2, local copies, waits for them, and re-layouts: 0.79 us -> 0.14 us  [tiles_of(): return jnp.broadcast_to(spots.reshape(-1, 1, 1), (spots.size, 8, LANES))]
  transfers between devices with their start and end apart: 19 -> 19, of which waited for: 9 -> 9; matrix products, arithmetic and copies ran while one was open for 1% -> 2% of each run, Pallas kernels for 5% -> 5%
where the time goes in v6:
time: 64.1 us; the launch traced here: 63.8 us
  starting transfers between devices  26.7 us (42%)
  waiting for transfers between devices  24.2 us (38%)
  Pallas kernels  10.5 us (16%)
  other arithmetic  1.32 us (2%)
  between operations  0.92 us (1%)
    ppermute x19, starting transfers between devices, move(): return lax.ppermute(value, AXES, everywhere(target_of))  26.7 us
    ppermute x19, waiting for transfers between devices, move(): return lax.ppermute(value, AXES, everywhere(target_of))  24.2 us
    pallas_call x1, Pallas kernels, shards(): pl.pallas_call(frame_kernel, out_shape=[sds((2, frame, frame), f32)] * 4,...  6.15 us
    another operation x1, other arithmetic, shards(): tile = jnp.stack([phase, absorb])  1.32 us
  transfers between devices with their start and end apart: 19, of which 9 were waited for; matrix products, arithmetic and copies ran while one was open for 2% of the time, Pallas kernels for 5%

profile of v6, /device:TPU:13, one launch (start us, length us, event | category | flops | bytes accessed | tf_op | source)
XLA Modules:
  0.0 63.8 jit_solution(18347524763007945184)
XLA Ops:
  0.6 1.3 %collective-permute-start = (s32[1,2]{1,0:T(1,128)}, s32[1,2]{1,0:T(1,128)S(1)}, u32[]{:S(2)}, u32[]{:S(2)}) collective-permute-start(s32[1,2]{1,0:T(1,128)} %bitcast.9), channel_id=1, source_target_pairs={{0,4},{1,5},{2,6},{3,7},{4,0},{5,1},{6,2},{7,3},{8,12},{9,13},{10,... | collective-permute-start | bytes 32 | tf_op jit(solution)/shard_map/ppermute | solution.py:258
  1.9 1.3 %pad_maximum_fusion.tile.refs_0_ = f32[2,384,384]{2,1,0:T(8,128)S(1)} fusion(f32[1,384,384]{2,1,0:T(8,128)} %bitcast.12, f32[1,384,384]{2,1,0:T(8,128)} %bitcast.13), kind=kLoop, calls=%fused_computation | loop fusion | flops 294912 | bytes 2359296 | tf_op jit(solution)/shard_map/stack | solution.py:304
  3.3 0.0 copy-start.4
  3.3 0.0 collective-permute-done
  3.3 0.1 broadcast_in_dim.23.refs_2_.refs_3_
  3.4 1.7 %collective-permute-start.1 = (f32[2,384,128]{2,1,0:T(8,128)S(1)}, f32[2,384,128]{2,1,0:T(8,128)S(1)}, u32[]{:S(2)}, u32[]{:S(2)}) collective-permute-start(f32[2,384,128]{2,1,0:T(8,128)S(1)} %edges.1), channel_id=1, source_target_pairs={{0,2},{1,3},{2,0},{3,1},{4,6},{5,7},{6,4},{7,5},{8,10},{9,11},{10,... | collective-permute-start | bytes 1179656 | tf_op jit(solution)/shard_map/ppermute | solution.py:258
  5.1 1.3 %collective-permute-done.1.refs_1_ = f32[2,384,128]{2,1,0:T(8,128)S(1)} collective-permute-done((f32[2,384,128]{2,1,0:T(8,128)S(1)}, f32[2,384,128]{2,1,0:T(8,128)S(1)}, u32[]{:S(2)}, u32[]{:S(2)}) %collective-permute-start.1) | collective-permute-done | bytes 393248 | tf_op jit(solution)/shard_map/ppermute | solution.py:258
  6.5 0.0 copy-start.1
  6.5 0.0 copy-start.2
  6.5 0.0 copy-start.3
  6.5 0.2 halo_rows.1
  6.7 1.3 %collective-permute-start.2 = (f32[2,128,256]{2,1,0:T(8,128)S(1)}, f32[2,128,256]{2,1,0:T(8,128)S(1)}, u32[]{:S(2)}, u32[]{:S(2)}) collective-permute-start(f32[2,128,256]{2,1,0:T(8,128)S(1)} %halo_rows.1), channel_id=1, source_target_pairs={{0,4},{1,5},{2,6},{3,7},{4,0},{5,1},{6,2},{7,3},{8,12},{9,13},{10,... | collective-permute-start | bytes 786440 | tf_op jit(solution)/shard_map/ppermute | solution.py:258
  8.0 0.0 copy-done.4
  8.0 0.1 broadcast_in_dim.21.spot_ref.refs_0_
  8.1 0.0 copy-start
  8.1 0.6 window.1
  8.7 0.8 %collective-permute-start.6 = (f32[2,128,256]{2,1,0:T(8,128)S(1)}, f32[2,128,256]{2,1,0:T(8,128)S(1)}, u32[]{:S(2)}, u32[]{:S(2)}) collective-permute-start(f32[2,128,256]{2,1,0:T(8,128)S(1)} %get-tuple-element.40.refs_2_), channel_id=1, source_target_pairs={{0,8},{1,9},{4,12},{5,13},{26,18},{27,19},{30,22},{31,23}} | collective-permute-start | bytes 786440 | tf_op jit(solution)/shard_map/ppermute | solution.py:258
  9.5 3.8 %collective-permute-start.5 = (f32[2,128,256]{2,1,0:T(8,128)S(1)}, f32[2,128,256]{2,1,0:T(8,128)S(1)}, u32[]{:S(2)}, u32[]{:S(2)}) collective-permute-start(f32[2,128,256]{2,1,0:T(8,128)S(1)} %get-tuple-element.40.refs_2_), channel_id=1, source_target_pairs={{10,18},{11,19},{14,22},{15,23},{16,8},{17,9},{20,12},{21,13}} | collective-permute-start | bytes 786440 | tf_op jit(solution)/shard_map/ppermute | solution.py:258
  13.3 0.7 %collective-permute-start.4 = (f32[2,128,256]{2,1,0:T(8,128)S(1)}, f32[2,128,256]{2,1,0:T(8,128)S(1)}, u32[]{:S(2)}, u32[]{:S(2)}) collective-permute-start(f32[2,128,256]{2,1,0:T(8,128)S(1)} %get-tuple-element.40.refs_2_), channel_id=1, source_target_pairs={{2,18},{3,19},{6,22},{7,23},{24,8},{25,9},{28,12},{29,13}} | collective-permute-start | bytes 786440 | tf_op jit(solution)/shard_map/ppermute | solution.py:258
  14.0 0.3 collective-permute-done.2.refs_0_
  14.3 0.1 join.1.refs_5_
  14.4 0.7 %collective-permute-start.9 = (f32[2,128,256]{2,1,0:T(8,128)S(1)}, f32[2,128,256]{2,1,0:T(8,128)S(1)}, u32[]{:S(2)}, u32[]{:S(2)}) collective-permute-start(f32[2,128,256]{2,1,0:T(8,128)S(1)} %join.1.refs_5_), channel_id=1, source_target_pairs={{2,18},{3,19},{6,22},{7,23},{24,8},{25,9},{28,12},{29,13}} | collective-permute-start | bytes 786440 | tf_op jit(solution)/shard_map/ppermute | solution.py:258
  15.1 3.8 %collective-permute-start.8 = (f32[2,128,256]{2,1,0:T(8,128)S(1)}, f32[2,128,256]{2,1,0:T(8,128)S(1)}, u32[]{:S(2)}, u32[]{:S(2)}) collective-permute-start(f32[2,128,256]{2,1,0:T(8,128)S(1)} %join.1.refs_5_), channel_id=1, source_target_pairs={{10,18},{11,19},{14,22},{15,23},{16,8},{17,9},{20,12},{21,13}} | collective-permute-start | bytes 786440 | tf_op jit(solution)/shard_map/ppermute | solution.py:258
  18.9 0.0 collective-permute-done.6.refs_3_
  18.9 0.7 %collective-permute-start.7 = (f32[2,128,256]{2,1,0:T(8,128)S(1)}, f32[2,128,256]{2,1,0:T(8,128)S(1)}, u32[]{:S(2)}, u32[]{:S(2)}) collective-permute-start(f32[2,128,256]{2,1,0:T(8,128)S(1)} %join.1.refs_5_), channel_id=1, source_target_pairs={{0,8},{1,9},{4,12},{5,13},{26,18},{27,19},{30,22},{31,23}} | collective-permute-start | bytes 786440 | tf_op jit(solution)/shard_map/ppermute | solution.py:258
  19.6 0.0 copy-done.1
  19.6 0.0 copy-done.2
  19.6 0.0 copy-done.3
  19.6 0.9 %prepare.1 = (f32[2,256,256]{2,1,0:T(8,128)S(1)}, f32[256,256]{1,0:T(8,128)S(1)}) custom-call(s32[1,2]{1,0:T(1,128)S(1)} %bitcast.11, f32[2,256,256]{2,1,0:T(8,128)S(1)} %copy-done.1, s32[256,256]{1,0:T(8,128)S(1)} %bitcast.8, bf16[2,256,256]{2,1,0:T(8,128)(2,1)S(1)} %copy-done.3), custom_call_target="tpu_custom_call" | custom-call | tf_op jit(solution)/shard_map/prepare/pallas_call | solution.py:438
  20.5 0.0 collective-permute-done.5.refs_1_
  20.5 0.3 collective-permute-start.3
  20.8 0.0 collective-permute-done.4.refs_0_
  20.8 2.7 %collective-permute-done.3.partner_ref.refs_1_ = s32[4,8,128]{2,1,0:T(8,128)S(1)} collective-permute-done((s32[4,8,128]{2,1,0:T(8,128)S(1)}, s32[4,8,128]{2,1,0:T(8,128)S(1)}, u32[]{:S(2)}, u32[]{:S(2)}) %collective-permute-start.3) | collective-permute-done | bytes 16416 | tf_op jit(solution)/shard_map/ppermute | solution.py:258
  23.5 0.0 collective-permute-done.9.refs_7_
  23.5 1.5 %collective-permute-done.8.refs_6_ = f32[2,128,256]{2,1,0:T(8,128)S(1)} collective-permute-done((f32[2,128,256]{2,1,0:T(8,128)S(1)}, f32[2,128,256]{2,1,0:T(8,128)S(1)}, u32[]{:S(2)}, u32[]{:S(2)}) %collective-permute-start.8) | collective-permute-done | bytes 262176 | tf_op jit(solution)/shard_map/ppermute | solution.py:258
  25.0 0.0 collective-permute-done.7.refs_4_
  25.0 0.0 copy-done
  25.0 6.2 %frame.1 = (f32[2,256,256]{2,1,0:T(8,128)S(1)}, f32[2,256,256]{2,1,0:T(8,128)S(1)}, f32[2,256,256]{2,1,0:T(8,128)S(1)}, f32[2,256,256]{2,1,0:T(8,128)S(1)}) custom-call(s32[4,8,128]{2,1,0:T(8,128)S(1)} %collective-permute-done.3.partner_ref.refs_1_, f32[2,256,256]{2,1,0:T(8,128)S(1)} %get-tuple-element.38.probe, f32[256,256]{1,0:T(8,128)S(1)} %get-tuple-element.39.seen, ...), custom_call_target="tpu_custom_call" | custom-call | tf_op jit(solution)/shard_map/frame/pallas_call | solution.py:495
  31.2 0.7 %collective-permute-start.10 = (f32[2,256,256]{2,1,0:T(8,128)S(1)}, f32[2,256,256]{2,1,0:T(8,128)S(1)}, u32[]{:S(2)}, u32[]{:S(2)}) collective-permute-start(f32[2,256,256]{2,1,0:T(8,128)S(1)} %get-tuple-element.42), channel_id=1, source_target_pairs={{8,24},{9,25},{12,28},{13,29},{18,2},{19,3},{22,6},{23,7}} | collective-permute-start | bytes 1572872 | tf_op jit(solution)/shard_map/ppermute | solution.py:258
  31.9 0.7 %collective-permute-start.11 = (f32[2,256,256]{2,1,0:T(8,128)S(1)}, f32[2,256,256]{2,1,0:T(8,128)S(1)}, u32[]{:S(2)}, u32[]{:S(2)}) collective-permute-start(f32[2,256,256]{2,1,0:T(8,128)S(1)} %get-tuple-element.43), channel_id=1, source_target_pairs={{8,0},{9,1},{12,4},{13,5},{18,26},{19,27},{22,30},{23,31}} | collective-permute-start | bytes 1572872 | tf_op jit(solution)/shard_map/ppermute | solution.py:258
  32.6 1.3 %collective-permute-start.12 = (f32[2,256,256]{2,1,0:T(8,128)S(1)}, f32[2,256,256]{2,1,0:T(8,128)S(1)}, u32[]{:S(2)}, u32[]{:S(2)}) collective-permute-start(f32[2,256,256]{2,1,0:T(8,128)S(1)} %get-tuple-element.44), channel_id=1, source_target_pairs={{8,16},{9,17},{12,20},{13,21},{18,10},{19,11},{22,14},{23,15}} | collective-permute-start | bytes 1572872 | tf_op jit(solution)/shard_map/ppermute | solution.py:258
  33.9 0.1 own_parts.1
  34.0 0.7 %collective-permute-start.13 = (f32[2,128,256]{2,1,0:T(8,128)S(1)}, f32[2,128,256]{2,1,0:T(8,128)S(1)}, u32[]{:S(2)}, u32[]{:S(2)}) collective-permute-start(f32[2,128,256]{2,1,0:T(8,128)S(1)} %get-tuple-element.46), channel_id=1, source_target_pairs={{8,12},{13,9},{18,22},{23,19}} | collective-permute-start | bytes 786440 | tf_op jit(solution)/shard_map/ppermute | solution.py:258
  34.7 0.7 %collective-permute-start.14 = (f32[2,128,256]{2,1,0:T(8,128)S(1)}, f32[2,128,256]{2,1,0:T(8,128)S(1)}, u32[]{:S(2)}, u32[]{:S(2)}) collective-permute-start(f32[2,128,256]{2,1,0:T(8,128)S(1)} %get-tuple-element.47), channel_id=1, source_target_pairs={{9,12},{12,9},{19,22},{22,19}} | collective-permute-start | bytes 786440 | tf_op jit(solution)/shard_map/ppermute | solution.py:258
  35.4 0.0 collective-permute-done.13.refs_5_
  35.4 0.0 collective-permute-done.14.refs_6_
  35.4 0.0 collective-permute-done.10.refs_0_
  35.4 0.0 collective-permute-done.11.refs_1_
  35.4 11.7 %collective-permute-done.12.refs_2_ = f32[2,256,256]{2,1,0:T(8,128)S(1)} collective-permute-done((f32[2,256,256]{2,1,0:T(8,128)S(1)}, f32[2,256,256]{2,1,0:T(8,128)S(1)}, u32[]{:S(2)}, u32[]{:S(2)}) %collective-permute-start.12) | collective-permute-done | bytes 524320 | tf_op jit(solution)/shard_map/ppermute | solution.py:258
  47.1 0.3 parts.1
  47.4 0.1 collective-permute-start.15
  47.5 1.3 %collective-permute-start.16 = (f32[2,128,256]{2,1,0:T(8,128)S(1)}, f32[2,128,256]{2,1,0:T(8,128)S(1)}, u32[]{:S(2)}, u32[]{:S(2)}) collective-permute-start(f32[2,128,256]{2,1,0:T(8,128)S(1)} %get-tuple-element.55), channel_id=1, source_target_pairs={{0,4},{2,6},{5,1},{7,3},{10,14},{15,11},{16,20},{21,17},{24,28},{2... | collective-permute-start | bytes 786440 | tf_op jit(solution)/shard_map/ppermute | solution.py:258
  48.8 4.0 %collective-permute-start.17 = (f32[2,128,256]{2,1,0:T(8,128)S(1)}, f32[2,128,256]{2,1,0:T(8,128)S(1)}, u32[]{:S(2)}, u32[]{:S(2)}) collective-permute-start(f32[2,128,256]{2,1,0:T(8,128)S(1)} %get-tuple-element.56), channel_id=1, source_target_pairs={{1,4},{3,6},{4,1},{6,3},{11,14},{14,11},{17,20},{20,17},{25,28},{2... | collective-permute-start | bytes 786440 | tf_op jit(solution)/shard_map/ppermute | solution.py:258
  52.8 0.2 keep.1.refs_2_
  53.0 1.9 %collective-permute-done.16.refs_7_ = f32[2,128,256]{2,1,0:T(8,128)S(1)} collective-permute-done((f32[2,128,256]{2,1,0:T(8,128)S(1)}, f32[2,128,256]{2,1,0:T(8,128)S(1)}, u32[]{:S(2)}, u32[]{:S(2)}) %collective-permute-start.16) | collective-permute-done | bytes 262176 | tf_op jit(solution)/shard_map/ppermute | solution.py:258
  54.9 2.0 %collective-permute-done.17.refs_8_ = f32[2,128,256]{2,1,0:T(8,128)S(1)} collective-permute-done((f32[2,128,256]{2,1,0:T(8,128)S(1)}, f32[2,128,256]{2,1,0:T(8,128)S(1)}, u32[]{:S(2)}, u32[]{:S(2)}) %collective-permute-start.17) | collective-permute-done | bytes 262176 | tf_op jit(solution)/shard_map/ppermute | solution.py:258
  56.9 2.7 %collective-permute-done.15.refs_4_ = f32[2,192,256]{2,1,0:T(8,128)S(1)} collective-permute-done((f32[2,192,256]{2,1,0:T(8,128)S(1)}, f32[2,192,256]{2,1,0:T(8,128)S(1)}, u32[]{:S(2)}, u32[]{:S(2)}) %collective-permute-start.15) | collective-permute-done | bytes 393248 | tf_op jit(solution)/shard_map/ppermute | solution.py:258
  59.6 0.2 edge_terms.1
  59.8 2.2 %collective-permute-start.18 = (f32[2,192,128]{2,1,0:T(8,128)S(1)}, f32[2,192,128]{2,1,0:T(8,128)S(1)}, u32[]{:S(2)}, u32[]{:S(2)}) collective-permute-start(f32[2,192,128]{2,1,0:T(8,128)S(1)} %edge_terms.1), channel_id=1, source_target_pairs={{0,2},{1,3},{2,0},{3,1},{4,6},{5,7},{6,4},{7,5},{8,10},{9,11},{10,... | collective-permute-start | bytes 589832 | tf_op jit(solution)/shard_map/ppermute | solution.py:258
  62.0 1.0 %inner_terms.1 = (f32[192,384]{1,0:T(8,128)}, f32[192,384]{1,0:T(8,128)}, f32[1,2,192,128]{3,2,1,0:T(8,128)S(1)}) custom-call(s32[2,8,128]{2,1,0:T(8,128)S(1)} %broadcast_in_dim.21.spot_ref.refs_0_, s32[4,8,128]{2,1,0:T(8,128)S(1)} %collective-permute-done.3.partner_ref.refs_1_, f32[2,192,256]{2,1,0:T(8,128)S(1)} %keep.1.refs_2_, ...), custom_call_target="tpu_custom_call" | custom-call | flops 4194304 | bytes 2097152 | tf_op jit(solution)/shard_map/inner_terms/pallas_call | solution.py:682
  63.1 0.1 collective-permute-done.18.refs_0_
  63.1 0.7 %finish.1 = (f32[192,384]{1,0:T(8,128)}, f32[192,384]{1,0:T(8,128)}) custom-call(f32[192,384]{1,0:T(8,128)} %get-tuple-element.57.phase_in, f32[192,384]{1,0:T(8,128)} %get-tuple-element.58.absorb_in, f32[1,2,192,128]{3,2,1,0:T(8,128)S(1)} %get-tuple-element.59.inner_ref, ...), custom_call_target="tpu_custom_call", output_to_operand_aliasing={{0}: (0, {}), {1}: (1, {})} | custom-call | tf_op jit(solution)/shard_map/finish/pallas_call | solution.py:710
  (2 shorter events, 0.0 us)
Async XLA Ops:
  0.6 2.7 %collective-permute-start = (s32[1,2]{1,0:T(1,128)}, s32[1,2]{1,0:T(1,128)S(1)}, u32[]{:S(2)}, u32[]{:S(2)}) collective-permute-start(s32[1,2]{1,0:T(1,128)} %bitcast.9), channel_id=1, source_target_pairs={{0,4},{1,5},{2,6},{3,7},{4,0},{5,1},{6,2},{7,3},{8,12},{9,13},{10,... | collective-permute-start | bytes 32 | tf_op jit(solution)/shard_map/ppermute | solution.py:258
  3.3 4.7 %copy-start.4 = (s32[1,1,1,2]{3,2,1,0:T(1,128)S(1)}, s32[1,1,1,2]{3,2,1,0:T(1,128)}, u32[]{:S(2)}) copy-start(s32[1,1,1,2]{3,2,1,0:T(1,128)} %param.10) | copy-start | bytes 28
  3.4 3.1 %collective-permute-start.1 = (f32[2,384,128]{2,1,0:T(8,128)S(1)}, f32[2,384,128]{2,1,0:T(8,128)S(1)}, u32[]{:S(2)}, u32[]{:S(2)}) collective-permute-start(f32[2,384,128]{2,1,0:T(8,128)S(1)} %edges.1), channel_id=1, source_target_pairs={{0,2},{1,3},{2,0},{3,1},{4,6},{5,7},{6,4},{7,5},{8,10},{9,11},{10,... | collective-permute-start | bytes 1179656 | tf_op jit(solution)/shard_map/ppermute | solution.py:258
  6.5 13.2 %copy-start.1 = (f32[2,256,256]{2,1,0:T(8,128)S(1)}, f32[2,256,256]{2,1,0:T(8,128)}, u32[]{:S(2)}) copy-start(f32[2,256,256]{2,1,0:T(8,128)} %probe) | copy-start | bytes 1572868
  6.5 13.2 %copy-start.2 = (s32[1,1,1,256,256]{4,3,2,1,0:T(8,128)S(1)}, s32[1,1,1,256,256]{4,3,2,1,0:T(8,128)}, u32[]{:S(2)}) copy-start(s32[1,1,1,256,256]{4,3,2,1,0:T(8,128)} %param.11) | copy-start | bytes 786436
  6.5 13.2 %copy-start.3 = (bf16[2,256,256]{2,1,0:T(8,128)(2,1)S(1)}, bf16[2,256,256]{2,1,0:T(8,128)(2,1)}, u32[]{:S(2)}) copy-start(bf16[2,256,256]{2,1,0:T(8,128)(2,1)} %constant.4.clone.sort) | copy-start | bytes 786436
  6.7 7.6 %collective-permute-start.2 = (f32[2,128,256]{2,1,0:T(8,128)S(1)}, f32[2,128,256]{2,1,0:T(8,128)S(1)}, u32[]{:S(2)}, u32[]{:S(2)}) collective-permute-start(f32[2,128,256]{2,1,0:T(8,128)S(1)} %halo_rows.1), channel_id=1, source_target_pairs={{0,4},{1,5},{2,6},{3,7},{4,0},{5,1},{6,2},{7,3},{8,12},{9,13},{10,... | collective-permute-start | bytes 786440 | tf_op jit(solution)/shard_map/ppermute | solution.py:258
  8.1 17.0 %copy-start = (bf16[12,2,256,256]{3,2,1,0:T(8,128)(2,1)S(1)}, bf16[12,2,256,256]{3,2,1,0:T(8,128)(2,1)}, u32[]{:S(2)}) copy-start(bf16[12,2,256,256]{3,2,1,0:T(8,128)(2,1)} %constant.5.clone.tables) | copy-start | bytes 9437188
  8.7 10.2 %collective-permute-start.6 = (f32[2,128,256]{2,1,0:T(8,128)S(1)}, f32[2,128,256]{2,1,0:T(8,128)S(1)}, u32[]{:S(2)}, u32[]{:S(2)}) collective-permute-start(f32[2,128,256]{2,1,0:T(8,128)S(1)} %get-tuple-element.40.refs_2_), channel_id=1, source_target_pairs={{0,8},{1,9},{4,12},{5,13},{26,18},{27,19},{30,22},{31,23}} | collective-permute-start | bytes 786440 | tf_op jit(solution)/shard_map/ppermute | solution.py:258
  9.5 11.0 %collective-permute-start.5 = (f32[2,128,256]{2,1,0:T(8,128)S(1)}, f32[2,128,256]{2,1,0:T(8,128)S(1)}, u32[]{:S(2)}, u32[]{:S(2)}) collective-permute-start(f32[2,128,256]{2,1,0:T(8,128)S(1)} %get-tuple-element.40.refs_2_), channel_id=1, source_target_pairs={{10,18},{11,19},{14,22},{15,23},{16,8},{17,9},{20,12},{21,13}} | collective-permute-start | bytes 786440 | tf_op jit(solution)/shard_map/ppermute | solution.py:258
  13.3 7.5 %collective-permute-start.4 = (f32[2,128,256]{2,1,0:T(8,128)S(1)}, f32[2,128,256]{2,1,0:T(8,128)S(1)}, u32[]{:S(2)}, u32[]{:S(2)}) collective-permute-start(f32[2,128,256]{2,1,0:T(8,128)S(1)} %get-tuple-element.40.refs_2_), channel_id=1, source_target_pairs={{2,18},{3,19},{6,22},{7,23},{24,8},{25,9},{28,12},{29,13}} | collective-permute-start | bytes 786440 | tf_op jit(solution)/shard_map/ppermute | solution.py:258
  14.4 9.1 %collective-permute-start.9 = (f32[2,128,256]{2,1,0:T(8,128)S(1)}, f32[2,128,256]{2,1,0:T(8,128)S(1)}, u32[]{:S(2)}, u32[]{:S(2)}) collective-permute-start(f32[2,128,256]{2,1,0:T(8,128)S(1)} %join.1.refs_5_), channel_id=1, source_target_pairs={{2,18},{3,19},{6,22},{7,23},{24,8},{25,9},{28,12},{29,13}} | collective-permute-start | bytes 786440 | tf_op jit(solution)/shard_map/ppermute | solution.py:258
  15.1 10.0 %collective-permute-start.8 = (f32[2,128,256]{2,1,0:T(8,128)S(1)}, f32[2,128,256]{2,1,0:T(8,128)S(1)}, u32[]{:S(2)}, u32[]{:S(2)}) collective-permute-start(f32[2,128,256]{2,1,0:T(8,128)S(1)} %join.1.refs_5_), channel_id=1, source_target_pairs={{10,18},{11,19},{14,22},{15,23},{16,8},{17,9},{20,12},{21,13}} | collective-permute-start | bytes 786440 | tf_op jit(solution)/shard_map/ppermute | solution.py:258
  18.9 6.1 %collective-permute-start.7 = (f32[2,128,256]{2,1,0:T(8,128)S(1)}, f32[2,128,256]{2,1,0:T(8,128)S(1)}, u32[]{:S(2)}, u32[]{:S(2)}) collective-permute-start(f32[2,128,256]{2,1,0:T(8,128)S(1)} %join.1.refs_5_), channel_id=1, source_target_pairs={{0,8},{1,9},{4,12},{5,13},{26,18},{27,19},{30,22},{31,23}} | collective-permute-start | bytes 786440 | tf_op jit(solution)/shard_map/ppermute | solution.py:258
  20.5 2.9 %collective-permute-start.3 = (s32[4,8,128]{2,1,0:T(8,128)S(1)}, s32[4,8,128]{2,1,0:T(8,128)S(1)}, u32[]{:S(2)}, u32[]{:S(2)}) collective-permute-start(s32[4,8,128]{2,1,0:T(8,128)S(1)} %pad_add_fusion), channel_id=1, source_target_pairs={{0,1},{1,0},{2,3},{3,2},{4,5},{5,4},{6,7},{7,6},{8,9},{9,8},{10,11... | collective-permute-start | bytes 49160 | tf_op jit(solution)/shard_map/ppermute | solution.py:258
  31.2 4.2 %collective-permute-start.10 = (f32[2,256,256]{2,1,0:T(8,128)S(1)}, f32[2,256,256]{2,1,0:T(8,128)S(1)}, u32[]{:S(2)}, u32[]{:S(2)}) collective-permute-start(f32[2,256,256]{2,1,0:T(8,128)S(1)} %get-tuple-element.42), channel_id=1, source_target_pairs={{8,24},{9,25},{12,28},{13,29},{18,2},{19,3},{22,6},{23,7}} | collective-permute-start | bytes 1572872 | tf_op jit(solution)/shard_map/ppermute | solution.py:258
  31.9 3.5 %collective-permute-start.11 = (f32[2,256,256]{2,1,0:T(8,128)S(1)}, f32[2,256,256]{2,1,0:T(8,128)S(1)}, u32[]{:S(2)}, u32[]{:S(2)}) collective-permute-start(f32[2,256,256]{2,1,0:T(8,128)S(1)} %get-tuple-element.43), channel_id=1, source_target_pairs={{8,0},{9,1},{12,4},{13,5},{18,26},{19,27},{22,30},{23,31}} | collective-permute-start | bytes 1572872 | tf_op jit(solution)/shard_map/ppermute | solution.py:258
  32.6 14.5 %collective-permute-start.12 = (f32[2,256,256]{2,1,0:T(8,128)S(1)}, f32[2,256,256]{2,1,0:T(8,128)S(1)}, u32[]{:S(2)}, u32[]{:S(2)}) collective-permute-start(f32[2,256,256]{2,1,0:T(8,128)S(1)} %get-tuple-element.44), channel_id=1, source_target_pairs={{8,16},{9,17},{12,20},{13,21},{18,10},{19,11},{22,14},{23,15}} | collective-permute-start | bytes 1572872 | tf_op jit(solution)/shard_map/ppermute | solution.py:258
  34.0 1.4 %collective-permute-start.13 = (f32[2,128,256]{2,1,0:T(8,128)S(1)}, f32[2,128,256]{2,1,0:T(8,128)S(1)}, u32[]{:S(2)}, u32[]{:S(2)}) collective-permute-start(f32[2,128,256]{2,1,0:T(8,128)S(1)} %get-tuple-element.46), channel_id=1, source_target_pairs={{8,12},{13,9},{18,22},{23,19}} | collective-permute-start | bytes 786440 | tf_op jit(solution)/shard_map/ppermute | solution.py:258
  34.7 0.7 %collective-permute-start.14 = (f32[2,128,256]{2,1,0:T(8,128)S(1)}, f32[2,128,256]{2,1,0:T(8,128)S(1)}, u32[]{:S(2)}, u32[]{:S(2)}) collective-permute-start(f32[2,128,256]{2,1,0:T(8,128)S(1)} %get-tuple-element.47), channel_id=1, source_target_pairs={{9,12},{12,9},{19,22},{22,19}} | collective-permute-start | bytes 786440 | tf_op jit(solution)/shard_map/ppermute | solution.py:258
  47.4 12.2 %collective-permute-start.15 = (f32[2,192,256]{2,1,0:T(8,128)S(1)}, f32[2,192,256]{2,1,0:T(8,128)S(1)}, u32[]{:S(2)}, u32[]{:S(2)}) collective-permute-start(f32[2,192,256]{2,1,0:T(8,128)S(1)} %get-tuple-element.52), channel_id=1, source_target_pairs={{0,1},{1,0},{2,3},{3,2},{4,5},{5,4},{6,7},{7,6},{8,9},{9,8},{10,11... | collective-permute-start | bytes 1179656 | tf_op jit(solution)/shard_map/ppermute | solution.py:258
  47.5 7.4 %collective-permute-start.16 = (f32[2,128,256]{2,1,0:T(8,128)S(1)}, f32[2,128,256]{2,1,0:T(8,128)S(1)}, u32[]{:S(2)}, u32[]{:S(2)}) collective-permute-start(f32[2,128,256]{2,1,0:T(8,128)S(1)} %get-tuple-element.55), channel_id=1, source_target_pairs={{0,4},{2,6},{5,1},{7,3},{10,14},{15,11},{16,20},{21,17},{24,28},{2... | collective-permute-start | bytes 786440 | tf_op jit(solution)/shard_map/ppermute | solution.py:258
  48.8 8.1 %collective-permute-start.17 = (f32[2,128,256]{2,1,0:T(8,128)S(1)}, f32[2,128,256]{2,1,0:T(8,128)S(1)}, u32[]{:S(2)}, u32[]{:S(2)}) collective-permute-start(f32[2,128,256]{2,1,0:T(8,128)S(1)} %get-tuple-element.56), channel_id=1, source_target_pairs={{1,4},{3,6},{4,1},{6,3},{11,14},{14,11},{17,20},{20,17},{25,28},{2... | collective-permute-start | bytes 786440 | tf_op jit(solution)/shard_map/ppermute | solution.py:258
  59.8 3.3 %collective-permute-start.18 = (f32[2,192,128]{2,1,0:T(8,128)S(1)}, f32[2,192,128]{2,1,0:T(8,128)S(1)}, u32[]{:S(2)}, u32[]{:S(2)}) collective-permute-start(f32[2,192,128]{2,1,0:T(8,128)S(1)} %edge_terms.1), channel_id=1, source_target_pairs={{0,2},{1,3},{2,0},{3,1},{4,6},{5,7},{6,4},{7,5},{8,10},{9,11},{10,... | collective-permute-start | bytes 589832 | tf_op jit(solution)/shard_map/ppermute | solution.py:258

commit v7 on v6

--- a/solution.py
+++ b/solution.py
@@ -306,21 +306,25 @@
         def load_kernel(tile, *edges):
             for way in range(ways):
                 start = place.sent(place.column(), way) * (width - HALO)
-                edges[way][...] = tile[:, :, pl.ds(pl.multiple_of(start, LANES), HALO)]
+                columns = pl.ds(pl.multiple_of(start, LANES), HALO)
+                for plane in range(2):
+                    edges[plane * ways + way][...] = tile[plane, :, columns]
 
         edges = pl.pallas_call(
             load_kernel,
-            out_shape=[sds((2, width, HALO), f32)] * ways,
+            out_shape=[sds((width, HALO), f32)] * (2 * ways),
             in_specs=[VMEM],
-            out_specs=[VMEM] * ways,
+            out_specs=[VMEM] * (2 * ways),
             compiler_params=small,
             name="edges",
         )(tile)
-        edges, spots_rows = lax.optimization_barrier((edges, spots_rows))
-        sides = trade_columns(edges)
+        phase_edges, absorb_edges = edges[:ways], edges[ways:]
+        absorb_edges, spots_rows = lax.optimization_barrier((absorb_edges, spots_rows))
+        sides = trade_columns(phase_edges) + trade_columns(absorb_edges)
 
         def rows_of(refs, plane, rows):
-            return refs[0][plane, rows, :], [side[plane, rows, :] for side in refs[1:]]
+            sides_here = refs[1 + plane * ways : 1 + (plane + 1) * ways]
+            return refs[0][plane, rows, :], [side[rows, :] for side in sides_here]
 
         def bands_of(tile, margin):
             inner = [tile[:, i * HALO : (i + 1) * HALO] for i in range(3)]
@@ -340,8 +344,8 @@
             return damping * cosine, damping * sine
 
         def strip_kernel(*refs):
-            loaded, spot_refs = refs[: 1 + ways], refs[1 + ways : 1 + 2 * ways]
-            outs = refs[1 + 2 * ways :]
+            loaded, spot_refs = refs[: 1 + 2 * ways], refs[1 + 2 * ways : 1 + 3 * ways]
+            outs = refs[1 + 3 * ways :]
             for way in range(ways):
                 below = place.sent(place.row(), way)
                 rows = pl.ds(pl.multiple_of(below * (width - HALO), 8), HALO)
@@ -355,7 +359,7 @@
         strips = pl.pallas_call(
             strip_kernel,
             out_shape=[sds((2, HALO, frame), f32)] * ways,
-            in_specs=[VMEM] * (1 + 2 * ways),
+            in_specs=[VMEM] * (1 + 3 * ways),
             out_specs=[VMEM] * ways,
             compiler_params=small,
             name="halo_rows",
@@ -385,7 +389,7 @@
         whole, part = pl.pallas_call(
             window_kernel,
             out_shape=[sds((2, HALO, frame), f32)] * 2,
-            in_specs=[VMEM] * (2 + ways),
+            in_specs=[VMEM] * (2 + 2 * ways),
             out_specs=[VMEM] * 2,
             compiler_params=small,
             name="window",
@@ -543,60 +547,66 @@
             earlier = jnp.concatenate([earlier[HALO:], middle[: HALO // 2]], 0)
             return jnp.where(rep == 0, earlier, later)
 
-        def split_strips(term, row, straight, across):
-            rep = place.rep()
+        def strips_of(term, plane, row):
             index = row_index((HALO, frame))
+            first = term[plane, :HALO]
+            bands = (in_band(index, row, band) for band in (0, 4))
+            return [jnp.where(band, first, 0.0) for band in bands]
+
+        def own_kernel(spot_ref, own, across):
             for plane in range(2):
-                first = term[plane, :HALO]
-                above = jnp.where(in_band(index, row, 0), first, 0.0)
-                below = jnp.where(in_band(index, row, 4), first, 0.0)
+                above, below = strips_of(own, plane, row_at(spot_ref))
+                across[plane] = jnp.where(place.rep() == 1, below, above)
+
+        def parts_kernel(spot_ref, *refs):
+            back_refs, (give, straight, across, term) = refs[:4], refs[4:]
+            load_term(back_refs, term)
+            rep, row = place.rep(), row_at(spot_ref)
+            for plane in range(2):
+                give[plane] = rows_for(term, plane, row, 1 - rep)
+                above, below = strips_of(term, plane, row)
                 straight[plane] = jnp.where(rep == 1, above, below)
                 across[plane] = jnp.where(rep == 1, below, above)
 
-        def own_kernel(spot_ref, own, straight, across):
-            split_strips(own, row_at(spot_ref), straight, across)
-
-        def parts_kernel(spot_ref, *refs):
-            back_refs, (give, straight, across, term) = refs[:-4], refs[-4:]
-            load_term(back_refs, term)
-            for plane in range(2):
-                give[plane] = rows_for(term, plane, row_at(spot_ref), 1 - place.rep())
-            split_strips(term, row_at(spot_ref), straight, across)
-
-        def exchange(straight, across, owners):
-            def of_those(target_of):
-                return lambda s, y, x, r: (
-                    target_of(s, y, x, r) if (s == owner_of(x)) == owners else None
-                )
-
-            return (
-                move(straight, of_those(lambda s, y, x, r: (s, y + 1 - 2 * r, x, r))),
-                move(across, of_those(lambda s, y, x, r: (s, y - 1 + 2 * r, x, 1 - r))),
+        routes = (
+            lambda s, y, x, r: (s, y, x, 1 - r),
+            lambda s, y, x, r: (s, y + 1 - 2 * r, x, r),
+            lambda s, y, x, r: (s, y - 1 + 2 * r, x, 1 - r),
+        )
+
+        def exchange(value, number, owners=None):
+            return move(
+                value,
+                lambda s, y, x, r: (
+                    routes[number](s, y, x, r)
+                    if owners is None or (s == owner_of(x)) == owners
+                    else None
+                ),
             )
 
         strip = sds((2, HALO, frame), f32)
-        own_strips = pl.pallas_call(
+        part_shapes = [sds((2, half_rows, frame), f32), strip, strip]
+        own_across = pl.pallas_call(
             own_kernel,
-            out_shape=[strip] * 2,
+            out_shape=strip,
             in_specs=[VMEM] * 2,
-            out_specs=[VMEM] * 2,
+            out_specs=VMEM,
             compiler_params=small,
             name="own_parts",
         )(spot_tiles, terms[1])
-        came_early = exchange(*own_strips, True)
-        back, came_early = lax.optimization_barrier((back, came_early))
-        give, *strips = pl.pallas_call(
+        early_across = exchange(own_across, 2, True)
+        give, straight, across = pl.pallas_call(
             parts_kernel,
-            out_shape=[sds((2, half_rows, frame), f32), strip, strip],
+            out_shape=part_shapes,
             in_specs=[VMEM] * 5,
             out_specs=[VMEM] * 3,
             scratch_shapes=[pltpu.VMEM((2, frame, frame), f32)],
             compiler_params=small,
             name="parts",
         )(spot_tiles, *back)
-
-        came_late = exchange(*strips, False)
-        given = move(give, lambda s, y, x, r: (s, y, x, 1 - r))
+        given = exchange(give, 0)
+        straight, across, early_across = lax.optimization_barrier((straight, across, early_across))
+        came_straight, late_across = exchange(straight, 1), exchange(across, 2, False)
 
         def keep_kernel(spot_ref, *refs):
             back_refs, (mine, term) = refs[:4], refs[4:]
@@ -617,11 +627,9 @@
 
         def add_band(band, plane, refs):
             spot_ref, partner_ref, kept_ref, *spot_refs = refs[: 3 + ways]
-            given, early, late = refs[3 + ways], refs[4 + ways : 6 + ways], refs[6 + ways : count]
             is_owner = place.section() == place.owner()
-            straight, across = (
-                jnp.where(is_owner, a[plane], b[plane]) for a, b in zip(early, late)
-            )
+            given, straight, late, early = (ref[plane] for ref in refs[3 + ways : count])
+            across = jnp.where(is_owner, early, late)
             rep = place.rep()
             if ways == 1:
                 straight_column, across_column = column_at(spot_refs[0]), column_at(partner_ref, 1)
@@ -631,15 +639,15 @@
                     rep == 1, column_at(partner_ref, 1), column_at(partner_ref, 2)
                 )
             total = part_of_band(kept_ref[plane], column_at(spot_ref), band)
-            total += part_of_band(given[plane], column_at(partner_ref), band)
+            total += part_of_band(given, column_at(partner_ref), band)
             strip = part_of_band(straight, straight_column, band)
             strip += part_of_band(across, across_column, band)
             gap = jnp.zeros((half_rows - HALO, HALO), f32)
             early, late = jnp.concatenate([strip, gap], 0), jnp.concatenate([gap, strip], 0)
             return total + jnp.where(rep == 1, late, early)
 
-        pieces = (spot_tiles, spots_rep, kept, *spots_rows, given, *came_early, *came_late)
-        piece_specs = [VMEM] * (8 + ways)
+        pieces = (spot_tiles, spots_rep, kept, *spots_rows, given, came_straight, late_across, early_across)
+        piece_specs = [VMEM] * len(pieces)
         count = len(piece_specs)
 
         def edge_kernel(*refs):

time: 64.1 us -> 63.6 us (level)
  starting transfers between devices: 26.7 us -> 25.6 us
  waiting for transfers between devices: 24.2 us -> 24.9 us
    ppermute x19, starting transfers between devices: 26.7 us -> 25.6 us  [move(): return lax.ppermute(value, AXES, everywhere(target_of))]
  transfers between devices with their start and end apart: 19 -> 19, of which waited for: 9 -> 10; matrix products, arithmetic and copies ran while one was open for 2% -> 2% of each run, Pallas kernels for 5% -> 5%
where the time goes in v7:
time: 63.6 us; the launch traced here: 63.3 us
  starting transfers between devices  25.6 us (40%)
  waiting for transfers between devices  24.9 us (39%)
  Pallas kernels  10.5 us (17%)
  other arithmetic  1.32 us (2%)
  between operations  0.89 us (1%)
    ppermute x19, starting transfers between devices, move(): return lax.ppermute(value, AXES, everywhere(target_of))  25.6 us
    ppermute x19, waiting for transfers between devices, move(): return lax.ppermute(value, AXES, everywhere(target_of))  24.9 us
    pallas_call x1, Pallas kernels, shards(): pl.pallas_call(frame_kernel, out_shape=[sds((2, frame, frame), f32)] * 4,...  6.15 us
    another operation x1, other arithmetic, shards(): tile = jnp.stack([phase, absorb])  1.32 us
  transfers between devices with their start and end apart: 19, of which 10 were waited for; matrix products, arithmetic and copies ran while one was open for 2% of the time, Pallas kernels for 5%

profile of v7, /device:TPU:13, one launch (start us, length us, event | category | flops | bytes accessed | tf_op | source)
XLA Modules:
  0.0 63.3 jit_solution(3284166374839949992)
XLA Ops:
  0.6 1.3 %collective-permute-start = (s32[1,2]{1,0:T(1,128)}, s32[1,2]{1,0:T(1,128)S(1)}, u32[]{:S(2)}, u32[]{:S(2)}) collective-permute-start(s32[1,2]{1,0:T(1,128)} %bitcast.9), channel_id=1, source_target_pairs={{0,4},{1,5},{2,6},{3,7},{4,0},{5,1},{6,2},{7,3},{8,12},{9,13},{10,... | collective-permute-start | bytes 32 | tf_op jit(solution)/shard_map/ppermute | solution.py:258
  1.9 1.3 %pad_maximum_fusion.tile.refs_0_ = f32[2,384,384]{2,1,0:T(8,128)S(1)} fusion(f32[1,384,384]{2,1,0:T(8,128)} %bitcast.12, f32[1,384,384]{2,1,0:T(8,128)} %bitcast.13), kind=kLoop, calls=%fused_computation | loop fusion | flops 294912 | bytes 2359296 | tf_op jit(solution)/shard_map/stack | solution.py:304
  3.3 0.0 copy-start.4
  3.3 1.0 %collective-permute-start.1 = (f32[384,128]{1,0:T(8,128)S(1)}, f32[384,128]{1,0:T(8,128)S(1)}, u32[]{:S(2)}, u32[]{:S(2)}) collective-permute-start(f32[384,128]{1,0:T(8,128)S(1)} %get-tuple-element.31), channel_id=1, source_target_pairs={{0,2},{1,3},{2,0},{3,1},{4,6},{5,7},{6,4},{7,5},{8,10},{9,11},{10,... | collective-permute-start | bytes 589832 | tf_op jit(solution)/shard_map/ppermute | solution.py:258
  4.3 0.0 collective-permute-done
  4.3 0.1 broadcast_in_dim.23.refs_3_
  4.4 0.7 %collective-permute-start.2 = (f32[384,128]{1,0:T(8,128)S(1)}, f32[384,128]{1,0:T(8,128)S(1)}, u32[]{:S(2)}, u32[]{:S(2)}) collective-permute-start(f32[384,128]{1,0:T(8,128)S(1)} %get-tuple-element.32), channel_id=1, source_target_pairs={{0,2},{1,3},{2,0},{3,1},{4,6},{5,7},{6,4},{7,5},{8,10},{9,11},{10,... | collective-permute-start | bytes 589832 | tf_op jit(solution)/shard_map/ppermute | solution.py:258
  5.1 0.3 collective-permute-done.1.refs_1_
  5.4 0.8 %collective-permute-done.2.refs_2_ = f32[384,128]{1,0:T(8,128)S(1)} collective-permute-done((f32[384,128]{1,0:T(8,128)S(1)}, f32[384,128]{1,0:T(8,128)S(1)}, u32[]{:S(2)}, u32[]{:S(2)}) %collective-permute-start.2) | collective-permute-done | bytes 196640 | tf_op jit(solution)/shard_map/ppermute | solution.py:258
  6.2 0.0 copy-start.1
  6.2 0.0 copy-start.2
  6.2 0.0 copy-start.3
  6.2 0.2 halo_rows.1
  6.4 1.3 %collective-permute-start.3 = (f32[2,128,256]{2,1,0:T(8,128)S(1)}, f32[2,128,256]{2,1,0:T(8,128)S(1)}, u32[]{:S(2)}, u32[]{:S(2)}) collective-permute-start(f32[2,128,256]{2,1,0:T(8,128)S(1)} %halo_rows.1), channel_id=1, source_target_pairs={{0,4},{1,5},{2,6},{3,7},{4,0},{5,1},{6,2},{7,3},{8,12},{9,13},{10,... | collective-permute-start | bytes 786440 | tf_op jit(solution)/shard_map/ppermute | solution.py:258
  7.7 0.0 copy-done.4
  7.7 0.1 broadcast_in_dim.21.spot_ref.refs_0_
  7.8 0.0 copy-start
  7.8 0.6 window.1
  8.4 0.8 %collective-permute-start.7 = (f32[2,128,256]{2,1,0:T(8,128)S(1)}, f32[2,128,256]{2,1,0:T(8,128)S(1)}, u32[]{:S(2)}, u32[]{:S(2)}) collective-permute-start(f32[2,128,256]{2,1,0:T(8,128)S(1)} %get-tuple-element.39.refs_2_), channel_id=1, source_target_pairs={{0,8},{1,9},{4,12},{5,13},{26,18},{27,19},{30,22},{31,23}} | collective-permute-start | bytes 786440 | tf_op jit(solution)/shard_map/ppermute | solution.py:258
  9.2 3.8 %collective-permute-start.6 = (f32[2,128,256]{2,1,0:T(8,128)S(1)}, f32[2,128,256]{2,1,0:T(8,128)S(1)}, u32[]{:S(2)}, u32[]{:S(2)}) collective-permute-start(f32[2,128,256]{2,1,0:T(8,128)S(1)} %get-tuple-element.39.refs_2_), channel_id=1, source_target_pairs={{10,18},{11,19},{14,22},{15,23},{16,8},{17,9},{20,12},{21,13}} | collective-permute-start | bytes 786440 | tf_op jit(solution)/shard_map/ppermute | solution.py:258
  13.0 0.7 %collective-permute-start.5 = (f32[2,128,256]{2,1,0:T(8,128)S(1)}, f32[2,128,256]{2,1,0:T(8,128)S(1)}, u32[]{:S(2)}, u32[]{:S(2)}) collective-permute-start(f32[2,128,256]{2,1,0:T(8,128)S(1)} %get-tuple-element.39.refs_2_), channel_id=1, source_target_pairs={{2,18},{3,19},{6,22},{7,23},{24,8},{25,9},{28,12},{29,13}} | collective-permute-start | bytes 786440 | tf_op jit(solution)/shard_map/ppermute | solution.py:258
  13.7 0.3 collective-permute-done.3.refs_0_
  14.0 0.1 join.1.refs_5_
  14.1 0.7 %collective-permute-start.10 = (f32[2,128,256]{2,1,0:T(8,128)S(1)}, f32[2,128,256]{2,1,0:T(8,128)S(1)}, u32[]{:S(2)}, u32[]{:S(2)}) collective-permute-start(f32[2,128,256]{2,1,0:T(8,128)S(1)} %join.1.refs_5_), channel_id=1, source_target_pairs={{2,18},{3,19},{6,22},{7,23},{24,8},{25,9},{28,12},{29,13}} | collective-permute-start | bytes 786440 | tf_op jit(solution)/shard_map/ppermute | solution.py:258
  14.8 3.8 %collective-permute-start.9 = (f32[2,128,256]{2,1,0:T(8,128)S(1)}, f32[2,128,256]{2,1,0:T(8,128)S(1)}, u32[]{:S(2)}, u32[]{:S(2)}) collective-permute-start(f32[2,128,256]{2,1,0:T(8,128)S(1)} %join.1.refs_5_), channel_id=1, source_target_pairs={{10,18},{11,19},{14,22},{15,23},{16,8},{17,9},{20,12},{21,13}} | collective-permute-start | bytes 786440 | tf_op jit(solution)/shard_map/ppermute | solution.py:258
  18.6 0.0 collective-permute-done.7.refs_3_
  18.6 0.7 %collective-permute-start.8 = (f32[2,128,256]{2,1,0:T(8,128)S(1)}, f32[2,128,256]{2,1,0:T(8,128)S(1)}, u32[]{:S(2)}, u32[]{:S(2)}) collective-permute-start(f32[2,128,256]{2,1,0:T(8,128)S(1)} %join.1.refs_5_), channel_id=1, source_target_pairs={{0,8},{1,9},{4,12},{5,13},{26,18},{27,19},{30,22},{31,23}} | collective-permute-start | bytes 786440 | tf_op jit(solution)/shard_map/ppermute | solution.py:258
  19.3 0.0 copy-done.1
  19.3 0.0 copy-done.2
  19.4 0.0 copy-done.3
  19.4 0.9 %prepare.1 = (f32[2,256,256]{2,1,0:T(8,128)S(1)}, f32[256,256]{1,0:T(8,128)S(1)}) custom-call(s32[1,2]{1,0:T(1,128)S(1)} %bitcast.11, f32[2,256,256]{2,1,0:T(8,128)S(1)} %copy-done.1, s32[256,256]{1,0:T(8,128)S(1)} %bitcast.8, bf16[2,256,256]{2,1,0:T(8,128)(2,1)S(1)} %copy-done.3), custom_call_target="tpu_custom_call" | custom-call | tf_op jit(solution)/shard_map/prepare/pallas_call | solution.py:442
  20.3 0.0 collective-permute-done.6.refs_1_
  20.3 0.3 collective-permute-start.4
  20.6 0.0 collective-permute-done.5.refs_0_
  20.6 2.7 %collective-permute-done.4.partner_ref.refs_1_ = s32[4,8,128]{2,1,0:T(8,128)S(1)} collective-permute-done((s32[4,8,128]{2,1,0:T(8,128)S(1)}, s32[4,8,128]{2,1,0:T(8,128)S(1)}, u32[]{:S(2)}, u32[]{:S(2)}) %collective-permute-start.4) | collective-permute-done | bytes 16416 | tf_op jit(solution)/shard_map/ppermute | solution.py:258
  23.2 0.0 collective-permute-done.10.refs_7_
  23.2 1.5 %collective-permute-done.9.refs_6_ = f32[2,128,256]{2,1,0:T(8,128)S(1)} collective-permute-done((f32[2,128,256]{2,1,0:T(8,128)S(1)}, f32[2,128,256]{2,1,0:T(8,128)S(1)}, u32[]{:S(2)}, u32[]{:S(2)}) %collective-permute-start.9) | collective-permute-done | bytes 262176 | tf_op jit(solution)/shard_map/ppermute | solution.py:258
  24.8 0.0 collective-permute-done.8.refs_4_
  24.8 0.0 copy-done
  24.8 6.1 %frame.1 = (f32[2,256,256]{2,1,0:T(8,128)S(1)}, f32[2,256,256]{2,1,0:T(8,128)S(1)}, f32[2,256,256]{2,1,0:T(8,128)S(1)}, f32[2,256,256]{2,1,0:T(8,128)S(1)}) custom-call(s32[4,8,128]{2,1,0:T(8,128)S(1)} %collective-permute-done.4.partner_ref.refs_1_, f32[2,256,256]{2,1,0:T(8,128)S(1)} %get-tuple-element.37.probe, f32[256,256]{1,0:T(8,128)S(1)} %get-tuple-element.38.seen, ...), custom_call_target="tpu_custom_call" | custom-call | tf_op jit(solution)/shard_map/frame/pallas_call | solution.py:499
  30.9 0.7 %collective-permute-start.11 = (f32[2,256,256]{2,1,0:T(8,128)S(1)}, f32[2,256,256]{2,1,0:T(8,128)S(1)}, u32[]{:S(2)}, u32[]{:S(2)}) collective-permute-start(f32[2,256,256]{2,1,0:T(8,128)S(1)} %get-tuple-element.41), channel_id=1, source_target_pairs={{8,24},{9,25},{12,28},{13,29},{18,2},{19,3},{22,6},{23,7}} | collective-permute-start | bytes 1572872 | tf_op jit(solution)/shard_map/ppermute | solution.py:258
  31.6 0.7 %collective-permute-start.12 = (f32[2,256,256]{2,1,0:T(8,128)S(1)}, f32[2,256,256]{2,1,0:T(8,128)S(1)}, u32[]{:S(2)}, u32[]{:S(2)}) collective-permute-start(f32[2,256,256]{2,1,0:T(8,128)S(1)} %get-tuple-element.42), channel_id=1, source_target_pairs={{8,0},{9,1},{12,4},{13,5},{18,26},{19,27},{22,30},{23,31}} | collective-permute-start | bytes 1572872 | tf_op jit(solution)/shard_map/ppermute | solution.py:258
  32.3 1.3 %collective-permute-start.13 = (f32[2,256,256]{2,1,0:T(8,128)S(1)}, f32[2,256,256]{2,1,0:T(8,128)S(1)}, u32[]{:S(2)}, u32[]{:S(2)}) collective-permute-start(f32[2,256,256]{2,1,0:T(8,128)S(1)} %get-tuple-element.43), channel_id=1, source_target_pairs={{8,16},{9,17},{12,20},{13,21},{18,10},{19,11},{22,14},{23,15}} | collective-permute-start | bytes 1572872 | tf_op jit(solution)/shard_map/ppermute | solution.py:258
  33.6 0.1 own_parts.1
  33.7 0.7 %collective-permute-start.15 = (f32[2,128,256]{2,1,0:T(8,128)S(1)}, f32[2,128,256]{2,1,0:T(8,128)S(1)}, u32[]{:S(2)}, u32[]{:S(2)}) collective-permute-start(f32[2,128,256]{2,1,0:T(8,128)S(1)} %own_parts.1), channel_id=1, source_target_pairs={{9,12},{12,9},{19,22},{22,19}} | collective-permute-start | bytes 786440 | tf_op jit(solution)/shard_map/ppermute | solution.py:258
  34.4 0.0 collective-permute-done.11.refs_0_
  34.4 0.0 collective-permute-done.12.refs_1_
  34.4 12.1 %collective-permute-done.13.refs_2_ = f32[2,256,256]{2,1,0:T(8,128)S(1)} collective-permute-done((f32[2,256,256]{2,1,0:T(8,128)S(1)}, f32[2,256,256]{2,1,0:T(8,128)S(1)}, u32[]{:S(2)}, u32[]{:S(2)}) %collective-permute-start.13) | collective-permute-done | bytes 524320 | tf_op jit(solution)/shard_map/ppermute | solution.py:258
  46.5 0.3 parts.1
  46.8 0.3 collective-permute-start.14
  47.1 0.0 collective-permute-done.15.refs_7_
  47.1 1.3 %collective-permute-start.16 = (f32[2,128,256]{2,1,0:T(8,128)S(1)}, f32[2,128,256]{2,1,0:T(8,128)S(1)}, u32[]{:S(2)}, u32[]{:S(2)}) collective-permute-start(f32[2,128,256]{2,1,0:T(8,128)S(1)} %get-tuple-element.48), channel_id=1, source_target_pairs={{0,4},{2,6},{5,1},{7,3},{8,12},{10,14},{13,9},{15,11},{16,20},{18,... | collective-permute-start | bytes 786440 | tf_op jit(solution)/shard_map/ppermute | solution.py:258
  48.4 4.1 %collective-permute-start.17 = (f32[2,128,256]{2,1,0:T(8,128)S(1)}, f32[2,128,256]{2,1,0:T(8,128)S(1)}, u32[]{:S(2)}, u32[]{:S(2)}) collective-permute-start(f32[2,128,256]{2,1,0:T(8,128)S(1)} %get-tuple-element.49), channel_id=1, source_target_pairs={{1,4},{3,6},{4,1},{6,3},{11,14},{14,11},{17,20},{20,17},{25,28},{2... | collective-permute-start | bytes 786440 | tf_op jit(solution)/shard_map/ppermute | solution.py:258
  52.5 0.2 keep.1.refs_2_
  52.7 3.3 %collective-permute-done.16.refs_5_ = f32[2,128,256]{2,1,0:T(8,128)S(1)} collective-permute-done((f32[2,128,256]{2,1,0:T(8,128)S(1)}, f32[2,128,256]{2,1,0:T(8,128)S(1)}, u32[]{:S(2)}, u32[]{:S(2)}) %collective-permute-start.16) | collective-permute-done | bytes 262176 | tf_op jit(solution)/shard_map/ppermute | solution.py:258
  56.0 0.5 collective-permute-done.17.refs_6_
  56.5 3.3 %collective-permute-done.14.refs_4_ = f32[2,192,256]{2,1,0:T(8,128)S(1)} collective-permute-done((f32[2,192,256]{2,1,0:T(8,128)S(1)}, f32[2,192,256]{2,1,0:T(8,128)S(1)}, u32[]{:S(2)}, u32[]{:S(2)}) %collective-permute-start.14) | collective-permute-done | bytes 393248 | tf_op jit(solution)/shard_map/ppermute | solution.py:258
  59.8 0.2 edge_terms.1
  60.0 1.5 %collective-permute-start.18 = (f32[2,192,128]{2,1,0:T(8,128)S(1)}, f32[2,192,128]{2,1,0:T(8,128)S(1)}, u32[]{:S(2)}, u32[]{:S(2)}) collective-permute-start(f32[2,192,128]{2,1,0:T(8,128)S(1)} %edge_terms.1), channel_id=1, source_target_pairs={{0,2},{1,3},{2,0},{3,1},{4,6},{5,7},{6,4},{7,5},{8,10},{9,11},{10,... | collective-permute-start | bytes 589832 | tf_op jit(solution)/shard_map/ppermute | solution.py:258
  61.5 1.0 %inner_terms.1 = (f32[192,384]{1,0:T(8,128)}, f32[192,384]{1,0:T(8,128)}, f32[1,2,192,128]{3,2,1,0:T(8,128)S(1)}) custom-call(s32[2,8,128]{2,1,0:T(8,128)S(1)} %broadcast_in_dim.21.spot_ref.refs_0_, s32[4,8,128]{2,1,0:T(8,128)S(1)} %collective-permute-done.4.partner_ref.refs_1_, f32[2,192,256]{2,1,0:T(8,128)S(1)} %keep.1.refs_2_, ...), custom_call_target="tpu_custom_call" | custom-call | flops 4194304 | bytes 2097152 | tf_op jit(solution)/shard_map/inner_terms/pallas_call | solution.py:690
  62.5 0.1 collective-permute-done.18.refs_0_
  62.5 0.7 %finish.1 = (f32[192,384]{1,0:T(8,128)}, f32[192,384]{1,0:T(8,128)}) custom-call(f32[192,384]{1,0:T(8,128)} %get-tuple-element.51.phase_in, f32[192,384]{1,0:T(8,128)} %get-tuple-element.52.absorb_in, f32[1,2,192,128]{3,2,1,0:T(8,128)S(1)} %get-tuple-element.53.inner_ref, ...), custom_call_target="tpu_custom_call", output_to_operand_aliasing={{0}: (0, {}), {1}: (1, {})} | custom-call | tf_op jit(solution)/shard_map/finish/pallas_call | solution.py:718
  (2 shorter events, 0.0 us)
Async XLA Ops:
  0.6 3.7 %collective-permute-start = (s32[1,2]{1,0:T(1,128)}, s32[1,2]{1,0:T(1,128)S(1)}, u32[]{:S(2)}, u32[]{:S(2)}) collective-permute-start(s32[1,2]{1,0:T(1,128)} %bitcast.9), channel_id=1, source_target_pairs={{0,4},{1,5},{2,6},{3,7},{4,0},{5,1},{6,2},{7,3},{8,12},{9,13},{10,... | collective-permute-start | bytes 32 | tf_op jit(solution)/shard_map/ppermute | solution.py:258
  3.3 4.4 %copy-start.4 = (s32[1,1,1,2]{3,2,1,0:T(1,128)S(1)}, s32[1,1,1,2]{3,2,1,0:T(1,128)}, u32[]{:S(2)}) copy-start(s32[1,1,1,2]{3,2,1,0:T(1,128)} %param.10) | copy-start | bytes 28
  3.3 2.1 %collective-permute-start.1 = (f32[384,128]{1,0:T(8,128)S(1)}, f32[384,128]{1,0:T(8,128)S(1)}, u32[]{:S(2)}, u32[]{:S(2)}) collective-permute-start(f32[384,128]{1,0:T(8,128)S(1)} %get-tuple-element.31), channel_id=1, source_target_pairs={{0,2},{1,3},{2,0},{3,1},{4,6},{5,7},{6,4},{7,5},{8,10},{9,11},{10,... | collective-permute-start | bytes 589832 | tf_op jit(solution)/shard_map/ppermute | solution.py:258
  4.4 1.8 %collective-permute-start.2 = (f32[384,128]{1,0:T(8,128)S(1)}, f32[384,128]{1,0:T(8,128)S(1)}, u32[]{:S(2)}, u32[]{:S(2)}) collective-permute-start(f32[384,128]{1,0:T(8,128)S(1)} %get-tuple-element.32), channel_id=1, source_target_pairs={{0,2},{1,3},{2,0},{3,1},{4,6},{5,7},{6,4},{7,5},{8,10},{9,11},{10,... | collective-permute-start | bytes 589832 | tf_op jit(solution)/shard_map/ppermute | solution.py:258
  6.2 13.2 %copy-start.1 = (f32[2,256,256]{2,1,0:T(8,128)S(1)}, f32[2,256,256]{2,1,0:T(8,128)}, u32[]{:S(2)}) copy-start(f32[2,256,256]{2,1,0:T(8,128)} %probe) | copy-start | bytes 1572868
  6.2 13.2 %copy-start.2 = (s32[1,1,1,256,256]{4,3,2,1,0:T(8,128)S(1)}, s32[1,1,1,256,256]{4,3,2,1,0:T(8,128)}, u32[]{:S(2)}) copy-start(s32[1,1,1,256,256]{4,3,2,1,0:T(8,128)} %param.11) | copy-start | bytes 786436
  6.2 13.2 %copy-start.3 = (bf16[2,256,256]{2,1,0:T(8,128)(2,1)S(1)}, bf16[2,256,256]{2,1,0:T(8,128)(2,1)}, u32[]{:S(2)}) copy-start(bf16[2,256,256]{2,1,0:T(8,128)(2,1)} %constant.4.clone.sort) | copy-start | bytes 786436
  6.4 7.6 %collective-permute-start.3 = (f32[2,128,256]{2,1,0:T(8,128)S(1)}, f32[2,128,256]{2,1,0:T(8,128)S(1)}, u32[]{:S(2)}, u32[]{:S(2)}) collective-permute-start(f32[2,128,256]{2,1,0:T(8,128)S(1)} %halo_rows.1), channel_id=1, source_target_pairs={{0,4},{1,5},{2,6},{3,7},{4,0},{5,1},{6,2},{7,3},{8,12},{9,13},{10,... | collective-permute-start | bytes 786440 | tf_op jit(solution)/shard_map/ppermute | solution.py:258
  7.8 17.0 %copy-start = (bf16[12,2,256,256]{3,2,1,0:T(8,128)(2,1)S(1)}, bf16[12,2,256,256]{3,2,1,0:T(8,128)(2,1)}, u32[]{:S(2)}) copy-start(bf16[12,2,256,256]{3,2,1,0:T(8,128)(2,1)} %constant.5.clone.tables) | copy-start | bytes 9437188
  8.4 10.2 %collective-permute-start.7 = (f32[2,128,256]{2,1,0:T(8,128)S(1)}, f32[2,128,256]{2,1,0:T(8,128)S(1)}, u32[]{:S(2)}, u32[]{:S(2)}) collective-permute-start(f32[2,128,256]{2,1,0:T(8,128)S(1)} %get-tuple-element.39.refs_2_), channel_id=1, source_target_pairs={{0,8},{1,9},{4,12},{5,13},{26,18},{27,19},{30,22},{31,23}} | collective-permute-start | bytes 786440 | tf_op jit(solution)/shard_map/ppermute | solution.py:258
  9.2 11.0 %collective-permute-start.6 = (f32[2,128,256]{2,1,0:T(8,128)S(1)}, f32[2,128,256]{2,1,0:T(8,128)S(1)}, u32[]{:S(2)}, u32[]{:S(2)}) collective-permute-start(f32[2,128,256]{2,1,0:T(8,128)S(1)} %get-tuple-element.39.refs_2_), channel_id=1, source_target_pairs={{10,18},{11,19},{14,22},{15,23},{16,8},{17,9},{20,12},{21,13}} | collective-permute-start | bytes 786440 | tf_op jit(solution)/shard_map/ppermute | solution.py:258
  13.0 7.5 %collective-permute-start.5 = (f32[2,128,256]{2,1,0:T(8,128)S(1)}, f32[2,128,256]{2,1,0:T(8,128)S(1)}, u32[]{:S(2)}, u32[]{:S(2)}) collective-permute-start(f32[2,128,256]{2,1,0:T(8,128)S(1)} %get-tuple-element.39.refs_2_), channel_id=1, source_target_pairs={{2,18},{3,19},{6,22},{7,23},{24,8},{25,9},{28,12},{29,13}} | collective-permute-start | bytes 786440 | tf_op jit(solution)/shard_map/ppermute | solution.py:258
  14.1 9.1 %collective-permute-start.10 = (f32[2,128,256]{2,1,0:T(8,128)S(1)}, f32[2,128,256]{2,1,0:T(8,128)S(1)}, u32[]{:S(2)}, u32[]{:S(2)}) collective-permute-start(f32[2,128,256]{2,1,0:T(8,128)S(1)} %join.1.refs_5_), channel_id=1, source_target_pairs={{2,18},{3,19},{6,22},{7,23},{24,8},{25,9},{28,12},{29,13}} | collective-permute-start | bytes 786440 | tf_op jit(solution)/shard_map/ppermute | solution.py:258
  14.8 10.0 %collective-permute-start.9 = (f32[2,128,256]{2,1,0:T(8,128)S(1)}, f32[2,128,256]{2,1,0:T(8,128)S(1)}, u32[]{:S(2)}, u32[]{:S(2)}) collective-permute-start(f32[2,128,256]{2,1,0:T(8,128)S(1)} %join.1.refs_5_), channel_id=1, source_target_pairs={{10,18},{11,19},{14,22},{15,23},{16,8},{17,9},{20,12},{21,13}} | collective-permute-start | bytes 786440 | tf_op jit(solution)/shard_map/ppermute | solution.py:258
  18.6 6.1 %collective-permute-start.8 = (f32[2,128,256]{2,1,0:T(8,128)S(1)}, f32[2,128,256]{2,1,0:T(8,128)S(1)}, u32[]{:S(2)}, u32[]{:S(2)}) collective-permute-start(f32[2,128,256]{2,1,0:T(8,128)S(1)} %join.1.refs_5_), channel_id=1, source_target_pairs={{0,8},{1,9},{4,12},{5,13},{26,18},{27,19},{30,22},{31,23}} | collective-permute-start | bytes 786440 | tf_op jit(solution)/shard_map/ppermute | solution.py:258
  20.3 2.9 %collective-permute-start.4 = (s32[4,8,128]{2,1,0:T(8,128)S(1)}, s32[4,8,128]{2,1,0:T(8,128)S(1)}, u32[]{:S(2)}, u32[]{:S(2)}) collective-permute-start(s32[4,8,128]{2,1,0:T(8,128)S(1)} %pad_add_fusion), channel_id=1, source_target_pairs={{0,1},{1,0},{2,3},{3,2},{4,5},{5,4},{6,7},{7,6},{8,9},{9,8},{10,11... | collective-permute-start | bytes 49160 | tf_op jit(solution)/shard_map/ppermute | solution.py:258
  30.9 3.5 %collective-permute-start.11 = (f32[2,256,256]{2,1,0:T(8,128)S(1)}, f32[2,256,256]{2,1,0:T(8,128)S(1)}, u32[]{:S(2)}, u32[]{:S(2)}) collective-permute-start(f32[2,256,256]{2,1,0:T(8,128)S(1)} %get-tuple-element.41), channel_id=1, source_target_pairs={{8,24},{9,25},{12,28},{13,29},{18,2},{19,3},{22,6},{23,7}} | collective-permute-start | bytes 1572872 | tf_op jit(solution)/shard_map/ppermute | solution.py:258
  31.6 2.8 %collective-permute-start.12 = (f32[2,256,256]{2,1,0:T(8,128)S(1)}, f32[2,256,256]{2,1,0:T(8,128)S(1)}, u32[]{:S(2)}, u32[]{:S(2)}) collective-permute-start(f32[2,256,256]{2,1,0:T(8,128)S(1)} %get-tuple-element.42), channel_id=1, source_target_pairs={{8,0},{9,1},{12,4},{13,5},{18,26},{19,27},{22,30},{23,31}} | collective-permute-start | bytes 1572872 | tf_op jit(solution)/shard_map/ppermute | solution.py:258
  32.3 14.2 %collective-permute-start.13 = (f32[2,256,256]{2,1,0:T(8,128)S(1)}, f32[2,256,256]{2,1,0:T(8,128)S(1)}, u32[]{:S(2)}, u32[]{:S(2)}) collective-permute-start(f32[2,256,256]{2,1,0:T(8,128)S(1)} %get-tuple-element.43), channel_id=1, source_target_pairs={{8,16},{9,17},{12,20},{13,21},{18,10},{19,11},{22,14},{23,15}} | collective-permute-start | bytes 1572872 | tf_op jit(solution)/shard_map/ppermute | solution.py:258
  33.7 13.4 %collective-permute-start.15 = (f32[2,128,256]{2,1,0:T(8,128)S(1)}, f32[2,128,256]{2,1,0:T(8,128)S(1)}, u32[]{:S(2)}, u32[]{:S(2)}) collective-permute-start(f32[2,128,256]{2,1,0:T(8,128)S(1)} %own_parts.1), channel_id=1, source_target_pairs={{9,12},{12,9},{19,22},{22,19}} | collective-permute-start | bytes 786440 | tf_op jit(solution)/shard_map/ppermute | solution.py:258
  46.8 13.0 %collective-permute-start.14 = (f32[2,192,256]{2,1,0:T(8,128)S(1)}, f32[2,192,256]{2,1,0:T(8,128)S(1)}, u32[]{:S(2)}, u32[]{:S(2)}) collective-permute-start(f32[2,192,256]{2,1,0:T(8,128)S(1)} %get-tuple-element.45), channel_id=1, source_target_pairs={{0,1},{1,0},{2,3},{3,2},{4,5},{5,4},{6,7},{7,6},{8,9},{9,8},{10,11... | collective-permute-start | bytes 1179656 | tf_op jit(solution)/shard_map/ppermute | solution.py:258
  47.1 8.9 %collective-permute-start.16 = (f32[2,128,256]{2,1,0:T(8,128)S(1)}, f32[2,128,256]{2,1,0:T(8,128)S(1)}, u32[]{:S(2)}, u32[]{:S(2)}) collective-permute-start(f32[2,128,256]{2,1,0:T(8,128)S(1)} %get-tuple-element.48), channel_id=1, source_target_pairs={{0,4},{2,6},{5,1},{7,3},{8,12},{10,14},{13,9},{15,11},{16,20},{18,... | collective-permute-start | bytes 786440 | tf_op jit(solution)/shard_map/ppermute | solution.py:258
  48.4 8.1 %collective-permute-start.17 = (f32[2,128,256]{2,1,0:T(8,128)S(1)}, f32[2,128,256]{2,1,0:T(8,128)S(1)}, u32[]{:S(2)}, u32[]{:S(2)}) collective-permute-start(f32[2,128,256]{2,1,0:T(8,128)S(1)} %get-tuple-element.49), channel_id=1, source_target_pairs={{1,4},{3,6},{4,1},{6,3},{11,14},{14,11},{17,20},{20,17},{25,28},{2... | collective-permute-start | bytes 786440 | tf_op jit(solution)/shard_map/ppermute | solution.py:258
  60.0 2.5 %collective-permute-start.18 = (f32[2,192,128]{2,1,0:T(8,128)S(1)}, f32[2,192,128]{2,1,0:T(8,128)S(1)}, u32[]{:S(2)}, u32[]{:S(2)}) collective-permute-start(f32[2,192,128]{2,1,0:T(8,128)S(1)} %edge_terms.1), channel_id=1, source_target_pairs={{0,2},{1,3},{2,0},{3,1},{4,6},{5,7},{6,4},{7,5},{8,10},{9,11},{10,... | collective-permute-start | bytes 589832 | tf_op jit(solution)/shard_map/ppermute | solution.py:258

commit v8 on v7

--- a/solution.py
+++ b/solution.py
@@ -367,7 +367,7 @@
         rims = trade_rows(strips)
 
         def window_kernel(spot_ref, *refs):
-            loaded, (whole, part) = refs[:-2], refs[-2:]
+            *loaded, whole = refs
             row, column = row_at(spot_ref), column_at(spot_ref)
             index = row_index((HALO, HALO))
             upper = in_band(index + HALO, row, 1)
@@ -378,6 +378,10 @@
                 bands = [jnp.where(upper, v, w) for v, w in zip(first, third)]
                 planes.append(choose_columns(bands, column))
             whole[0], whole[1] = transmission(*planes)
+
+        def part_kernel(spot_ref, *refs):
+            *loaded, part = refs
+            row, column = row_at(spot_ref), column_at(spot_ref)
             planes = []
             for plane in range(2):
                 bands = bands_of(*rows_of(loaded, plane, slice(HALO, 2 * HALO)))
@@ -386,14 +390,17 @@
             inside = in_band(row_index((HALO, frame)), row, 2)
             part[0], part[1] = jnp.where(inside, real, 1.0), jnp.where(inside, imag, 0.0)
 
-        whole, part = pl.pallas_call(
-            window_kernel,
-            out_shape=[sds((2, HALO, frame), f32)] * 2,
-            in_specs=[VMEM] * (2 + 2 * ways),
-            out_specs=[VMEM] * 2,
-            compiler_params=small,
-            name="window",
-        )(spot_tiles, tile, *sides)
+        def half_window(kernel, name):
+            return pl.pallas_call(
+                kernel,
+                out_shape=sds((2, HALO, frame), f32),
+                in_specs=[VMEM] * (2 + 2 * ways),
+                out_specs=VMEM,
+                compiler_params=small,
+                name=name,
+            )(spot_tiles, tile, *sides)
+
+        whole, part = half_window(window_kernel, "window"), half_window(part_kernel, "part")
 
         def to_owner(value):
             return [

time: 63.6 us -> 63.6 us (level)
  no operation moved by 1% of the time
where the time goes in v8:
time: 63.6 us; the launch traced here: 63.3 us
  starting transfers between devices  25.6 us (40%)
  waiting for transfers between devices  24.8 us (39%)
  Pallas kernels  10.5 us (17%)
  other arithmetic  1.32 us (2%)
  between operations  0.91 us (1%)
    ppermute x19, starting transfers between devices, move(): return lax.ppermute(value, AXES, everywhere(target_of))  25.6 us
    ppermute x19, waiting for transfers between devices, move(): return lax.ppermute(value, AXES, everywhere(target_of))  24.8 us
    pallas_call x1, Pallas kernels, shards(): pl.pallas_call(frame_kernel, out_shape=[sds((2, frame, frame), f32)] * 4,...  6.14 us
    another operation x1, other arithmetic, shards(): tile = jnp.stack([phase, absorb])  1.32 us
  transfers between devices with their start and end apart: 19, of which 10 were waited for; matrix products, arithmetic and copies ran while one was open for 2% of the time, Pallas kernels for 5%

profile of v8, /device:TPU:13, one launch (start us, length us, event | category | flops | bytes accessed | tf_op | source)
XLA Modules:
  0.0 63.3 jit_solution(7192639761473539311)
XLA Ops:
  0.6 1.3 %collective-permute-start = (s32[1,2]{1,0:T(1,128)}, s32[1,2]{1,0:T(1,128)S(1)}, u32[]{:S(2)}, u32[]{:S(2)}) collective-permute-start(s32[1,2]{1,0:T(1,128)} %bitcast.9), channel_id=1, source_target_pairs={{0,4},{1,5},{2,6},{3,7},{4,0},{5,1},{6,2},{7,3},{8,12},{9,13},{10,... | collective-permute-start | bytes 32 | tf_op jit(solution)/shard_map/ppermute | solution.py:258
  1.9 1.3 %pad_maximum_fusion.tile.refs_0_ = f32[2,384,384]{2,1,0:T(8,128)S(1)} fusion(f32[1,384,384]{2,1,0:T(8,128)} %bitcast.12, f32[1,384,384]{2,1,0:T(8,128)} %bitcast.13), kind=kLoop, calls=%fused_computation | loop fusion | flops 294912 | bytes 2359296 | tf_op jit(solution)/shard_map/stack | solution.py:304
  3.3 0.0 copy-start.4
  3.3 1.0 %collective-permute-start.1 = (f32[384,128]{1,0:T(8,128)S(1)}, f32[384,128]{1,0:T(8,128)S(1)}, u32[]{:S(2)}, u32[]{:S(2)}) collective-permute-start(f32[384,128]{1,0:T(8,128)S(1)} %get-tuple-element.29), channel_id=1, source_target_pairs={{0,2},{1,3},{2,0},{3,1},{4,6},{5,7},{6,4},{7,5},{8,10},{9,11},{10,... | collective-permute-start | bytes 589832 | tf_op jit(solution)/shard_map/ppermute | solution.py:258
  4.3 0.0 collective-permute-done
  4.3 0.1 broadcast_in_dim.23.refs_3_
  4.4 0.7 %collective-permute-start.2 = (f32[384,128]{1,0:T(8,128)S(1)}, f32[384,128]{1,0:T(8,128)S(1)}, u32[]{:S(2)}, u32[]{:S(2)}) collective-permute-start(f32[384,128]{1,0:T(8,128)S(1)} %get-tuple-element.30), channel_id=1, source_target_pairs={{0,2},{1,3},{2,0},{3,1},{4,6},{5,7},{6,4},{7,5},{8,10},{9,11},{10,... | collective-permute-start | bytes 589832 | tf_op jit(solution)/shard_map/ppermute | solution.py:258
  5.1 0.3 collective-permute-done.1.refs_1_
  5.4 0.8 %collective-permute-done.2.refs_2_ = f32[384,128]{1,0:T(8,128)S(1)} collective-permute-done((f32[384,128]{1,0:T(8,128)S(1)}, f32[384,128]{1,0:T(8,128)S(1)}, u32[]{:S(2)}, u32[]{:S(2)}) %collective-permute-start.2) | collective-permute-done | bytes 196640 | tf_op jit(solution)/shard_map/ppermute | solution.py:258
  6.2 0.2 halo_rows.1
  6.4 1.3 %collective-permute-start.3 = (f32[2,128,256]{2,1,0:T(8,128)S(1)}, f32[2,128,256]{2,1,0:T(8,128)S(1)}, u32[]{:S(2)}, u32[]{:S(2)}) collective-permute-start(f32[2,128,256]{2,1,0:T(8,128)S(1)} %halo_rows.1), channel_id=1, source_target_pairs={{0,4},{1,5},{2,6},{3,7},{4,0},{5,1},{6,2},{7,3},{8,12},{9,13},{10,... | collective-permute-start | bytes 786440 | tf_op jit(solution)/shard_map/ppermute | solution.py:258
  7.7 0.0 copy-done.4
  7.7 0.1 broadcast_in_dim.21.spot_ref.refs_0_
  7.8 0.0 copy-start.2
  7.8 0.0 copy-start.3
  7.8 0.3 window.1.refs_2_
  8.1 0.0 copy-start.1
  8.1 0.8 %collective-permute-start.7 = (f32[2,128,256]{2,1,0:T(8,128)S(1)}, f32[2,128,256]{2,1,0:T(8,128)S(1)}, u32[]{:S(2)}, u32[]{:S(2)}) collective-permute-start(f32[2,128,256]{2,1,0:T(8,128)S(1)} %window.1.refs_2_), channel_id=1, source_target_pairs={{0,8},{1,9},{4,12},{5,13},{26,18},{27,19},{30,22},{31,23}} | collective-permute-start | bytes 786440 | tf_op jit(solution)/shard_map/ppermute | solution.py:258
  9.0 3.8 %collective-permute-start.6 = (f32[2,128,256]{2,1,0:T(8,128)S(1)}, f32[2,128,256]{2,1,0:T(8,128)S(1)}, u32[]{:S(2)}, u32[]{:S(2)}) collective-permute-start(f32[2,128,256]{2,1,0:T(8,128)S(1)} %window.1.refs_2_), channel_id=1, source_target_pairs={{10,18},{11,19},{14,22},{15,23},{16,8},{17,9},{20,12},{21,13}} | collective-permute-start | bytes 786440 | tf_op jit(solution)/shard_map/ppermute | solution.py:258
  12.8 0.7 %collective-permute-start.5 = (f32[2,128,256]{2,1,0:T(8,128)S(1)}, f32[2,128,256]{2,1,0:T(8,128)S(1)}, u32[]{:S(2)}, u32[]{:S(2)}) collective-permute-start(f32[2,128,256]{2,1,0:T(8,128)S(1)} %window.1.refs_2_), channel_id=1, source_target_pairs={{2,18},{3,19},{6,22},{7,23},{24,8},{25,9},{28,12},{29,13}} | collective-permute-start | bytes 786440 | tf_op jit(solution)/shard_map/ppermute | solution.py:258
  13.5 0.0 copy-start
  13.5 0.3 part.1.part_ref
  13.8 0.3 collective-permute-done.3.refs_0_
  14.0 0.1 join.1.refs_5_
  14.1 0.8 %collective-permute-start.10 = (f32[2,128,256]{2,1,0:T(8,128)S(1)}, f32[2,128,256]{2,1,0:T(8,128)S(1)}, u32[]{:S(2)}, u32[]{:S(2)}) collective-permute-start(f32[2,128,256]{2,1,0:T(8,128)S(1)} %join.1.refs_5_), channel_id=1, source_target_pairs={{2,18},{3,19},{6,22},{7,23},{24,8},{25,9},{28,12},{29,13}} | collective-permute-start | bytes 786440 | tf_op jit(solution)/shard_map/ppermute | solution.py:258
  14.9 3.7 %collective-permute-start.9 = (f32[2,128,256]{2,1,0:T(8,128)S(1)}, f32[2,128,256]{2,1,0:T(8,128)S(1)}, u32[]{:S(2)}, u32[]{:S(2)}) collective-permute-start(f32[2,128,256]{2,1,0:T(8,128)S(1)} %join.1.refs_5_), channel_id=1, source_target_pairs={{10,18},{11,19},{14,22},{15,23},{16,8},{17,9},{20,12},{21,13}} | collective-permute-start | bytes 786440 | tf_op jit(solution)/shard_map/ppermute | solution.py:258
  18.6 0.0 collective-permute-done.7.refs_3_
  18.6 0.7 %collective-permute-start.8 = (f32[2,128,256]{2,1,0:T(8,128)S(1)}, f32[2,128,256]{2,1,0:T(8,128)S(1)}, u32[]{:S(2)}, u32[]{:S(2)}) collective-permute-start(f32[2,128,256]{2,1,0:T(8,128)S(1)} %join.1.refs_5_), channel_id=1, source_target_pairs={{0,8},{1,9},{4,12},{5,13},{26,18},{27,19},{30,22},{31,23}} | collective-permute-start | bytes 786440 | tf_op jit(solution)/shard_map/ppermute | solution.py:258
  19.3 0.0 copy-done.2
  19.3 0.0 copy-done.3
  19.4 0.0 copy-done.1
  19.4 0.9 %prepare.1 = (f32[2,256,256]{2,1,0:T(8,128)S(1)}, f32[256,256]{1,0:T(8,128)S(1)}) custom-call(s32[1,2]{1,0:T(1,128)S(1)} %bitcast.11, f32[2,256,256]{2,1,0:T(8,128)S(1)} %copy-done.1, s32[256,256]{1,0:T(8,128)S(1)} %bitcast.8, bf16[2,256,256]{2,1,0:T(8,128)(2,1)S(1)} %copy-done.3), custom_call_target="tpu_custom_call" | custom-call | tf_op jit(solution)/shard_map/prepare/pallas_call | solution.py:449
  20.3 0.0 collective-permute-done.6.refs_1_
  20.3 0.3 collective-permute-start.4
  20.6 0.0 collective-permute-done.5.refs_0_
  20.6 2.7 %collective-permute-done.4.partner_ref.refs_1_ = s32[4,8,128]{2,1,0:T(8,128)S(1)} collective-permute-done((s32[4,8,128]{2,1,0:T(8,128)S(1)}, s32[4,8,128]{2,1,0:T(8,128)S(1)}, u32[]{:S(2)}, u32[]{:S(2)}) %collective-permute-start.4) | collective-permute-done | bytes 16416 | tf_op jit(solution)/shard_map/ppermute | solution.py:258
  23.2 0.0 collective-permute-done.10.refs_7_
  23.2 1.3 %collective-permute-done.9.refs_6_ = f32[2,128,256]{2,1,0:T(8,128)S(1)} collective-permute-done((f32[2,128,256]{2,1,0:T(8,128)S(1)}, f32[2,128,256]{2,1,0:T(8,128)S(1)}, u32[]{:S(2)}, u32[]{:S(2)}) %collective-permute-start.9) | collective-permute-done | bytes 262176 | tf_op jit(solution)/shard_map/ppermute | solution.py:258
  24.5 0.0 collective-permute-done.8.refs_4_
  24.5 0.0 copy-done
  24.5 6.1 %frame.1 = (f32[2,256,256]{2,1,0:T(8,128)S(1)}, f32[2,256,256]{2,1,0:T(8,128)S(1)}, f32[2,256,256]{2,1,0:T(8,128)S(1)}, f32[2,256,256]{2,1,0:T(8,128)S(1)}) custom-call(s32[4,8,128]{2,1,0:T(8,128)S(1)} %collective-permute-done.4.partner_ref.refs_1_, f32[2,256,256]{2,1,0:T(8,128)S(1)} %get-tuple-element.34.probe, f32[256,256]{1,0:T(8,128)S(1)} %get-tuple-element.35.seen, ...), custom_call_target="tpu_custom_call" | custom-call | tf_op jit(solution)/shard_map/frame/pallas_call | solution.py:506
  30.7 0.7 %collective-permute-start.11 = (f32[2,256,256]{2,1,0:T(8,128)S(1)}, f32[2,256,256]{2,1,0:T(8,128)S(1)}, u32[]{:S(2)}, u32[]{:S(2)}) collective-permute-start(f32[2,256,256]{2,1,0:T(8,128)S(1)} %get-tuple-element.37), channel_id=1, source_target_pairs={{8,24},{9,25},{12,28},{13,29},{18,2},{19,3},{22,6},{23,7}} | collective-permute-start | bytes 1572872 | tf_op jit(solution)/shard_map/ppermute | solution.py:258
  31.4 0.7 %collective-permute-start.12 = (f32[2,256,256]{2,1,0:T(8,128)S(1)}, f32[2,256,256]{2,1,0:T(8,128)S(1)}, u32[]{:S(2)}, u32[]{:S(2)}) collective-permute-start(f32[2,256,256]{2,1,0:T(8,128)S(1)} %get-tuple-element.38), channel_id=1, source_target_pairs={{8,0},{9,1},{12,4},{13,5},{18,26},{19,27},{22,30},{23,31}} | collective-permute-start | bytes 1572872 | tf_op jit(solution)/shard_map/ppermute | solution.py:258
  32.1 1.3 %collective-permute-start.13 = (f32[2,256,256]{2,1,0:T(8,128)S(1)}, f32[2,256,256]{2,1,0:T(8,128)S(1)}, u32[]{:S(2)}, u32[]{:S(2)}) collective-permute-start(f32[2,256,256]{2,1,0:T(8,128)S(1)} %get-tuple-element.39), channel_id=1, source_target_pairs={{8,16},{9,17},{12,20},{13,21},{18,10},{19,11},{22,14},{23,15}} | collective-permute-start | bytes 1572872 | tf_op jit(solution)/shard_map/ppermute | solution.py:258
  33.4 0.1 own_parts.1
  33.5 0.7 %collective-permute-start.15 = (f32[2,128,256]{2,1,0:T(8,128)S(1)}, f32[2,128,256]{2,1,0:T(8,128)S(1)}, u32[]{:S(2)}, u32[]{:S(2)}) collective-permute-start(f32[2,128,256]{2,1,0:T(8,128)S(1)} %own_parts.1), channel_id=1, source_target_pairs={{9,12},{12,9},{19,22},{22,19}} | collective-permute-start | bytes 786440 | tf_op jit(solution)/shard_map/ppermute | solution.py:258
  34.2 0.0 collective-permute-done.11.refs_0_
  34.2 0.0 collective-permute-done.12.refs_1_
  34.2 12.3 %collective-permute-done.13.refs_2_ = f32[2,256,256]{2,1,0:T(8,128)S(1)} collective-permute-done((f32[2,256,256]{2,1,0:T(8,128)S(1)}, f32[2,256,256]{2,1,0:T(8,128)S(1)}, u32[]{:S(2)}, u32[]{:S(2)}) %collective-permute-start.13) | collective-permute-done | bytes 524320 | tf_op jit(solution)/shard_map/ppermute | solution.py:258
  46.5 0.3 parts.1
  46.8 0.3 collective-permute-start.14
  47.1 0.0 collective-permute-done.15.refs_7_
  47.1 1.3 %collective-permute-start.16 = (f32[2,128,256]{2,1,0:T(8,128)S(1)}, f32[2,128,256]{2,1,0:T(8,128)S(1)}, u32[]{:S(2)}, u32[]{:S(2)}) collective-permute-start(f32[2,128,256]{2,1,0:T(8,128)S(1)} %get-tuple-element.44), channel_id=1, source_target_pairs={{0,4},{2,6},{5,1},{7,3},{8,12},{10,14},{13,9},{15,11},{16,20},{18,... | collective-permute-start | bytes 786440 | tf_op jit(solution)/shard_map/ppermute | solution.py:258
  48.4 4.1 %collective-permute-start.17 = (f32[2,128,256]{2,1,0:T(8,128)S(1)}, f32[2,128,256]{2,1,0:T(8,128)S(1)}, u32[]{:S(2)}, u32[]{:S(2)}) collective-permute-start(f32[2,128,256]{2,1,0:T(8,128)S(1)} %get-tuple-element.45), channel_id=1, source_target_pairs={{1,4},{3,6},{4,1},{6,3},{11,14},{14,11},{17,20},{20,17},{25,28},{2... | collective-permute-start | bytes 786440 | tf_op jit(solution)/shard_map/ppermute | solution.py:258
  52.5 0.2 keep.1.refs_2_
  52.7 3.3 %collective-permute-done.16.refs_5_ = f32[2,128,256]{2,1,0:T(8,128)S(1)} collective-permute-done((f32[2,128,256]{2,1,0:T(8,128)S(1)}, f32[2,128,256]{2,1,0:T(8,128)S(1)}, u32[]{:S(2)}, u32[]{:S(2)}) %collective-permute-start.16) | collective-permute-done | bytes 262176 | tf_op jit(solution)/shard_map/ppermute | solution.py:258
  56.0 0.5 collective-permute-done.17.refs_6_
  56.5 3.3 %collective-permute-done.14.refs_4_ = f32[2,192,256]{2,1,0:T(8,128)S(1)} collective-permute-done((f32[2,192,256]{2,1,0:T(8,128)S(1)}, f32[2,192,256]{2,1,0:T(8,128)S(1)}, u32[]{:S(2)}, u32[]{:S(2)}) %collective-permute-start.14) | collective-permute-done | bytes 393248 | tf_op jit(solution)/shard_map/ppermute | solution.py:258
  59.8 0.2 edge_terms.1
  60.0 1.5 %collective-permute-start.18 = (f32[2,192,128]{2,1,0:T(8,128)S(1)}, f32[2,192,128]{2,1,0:T(8,128)S(1)}, u32[]{:S(2)}, u32[]{:S(2)}) collective-permute-start(f32[2,192,128]{2,1,0:T(8,128)S(1)} %edge_terms.1), channel_id=1, source_target_pairs={{0,2},{1,3},{2,0},{3,1},{4,6},{5,7},{6,4},{7,5},{8,10},{9,11},{10,... | collective-permute-start | bytes 589832 | tf_op jit(solution)/shard_map/ppermute | solution.py:258
  61.5 1.0 %inner_terms.1 = (f32[192,384]{1,0:T(8,128)}, f32[192,384]{1,0:T(8,128)}, f32[1,2,192,128]{3,2,1,0:T(8,128)S(1)}) custom-call(s32[2,8,128]{2,1,0:T(8,128)S(1)} %broadcast_in_dim.21.spot_ref.refs_0_, s32[4,8,128]{2,1,0:T(8,128)S(1)} %collective-permute-done.4.partner_ref.refs_1_, f32[2,192,256]{2,1,0:T(8,128)S(1)} %keep.1.refs_2_, ...), custom_call_target="tpu_custom_call" | custom-call | flops 4194304 | bytes 2097152 | tf_op jit(solution)/shard_map/inner_terms/pallas_call | solution.py:697
  62.5 0.1 collective-permute-done.18.refs_0_
  62.5 0.7 %finish.1 = (f32[192,384]{1,0:T(8,128)}, f32[192,384]{1,0:T(8,128)}) custom-call(f32[192,384]{1,0:T(8,128)} %get-tuple-element.47.phase_in, f32[192,384]{1,0:T(8,128)} %get-tuple-element.48.absorb_in, f32[1,2,192,128]{3,2,1,0:T(8,128)S(1)} %get-tuple-element.49.inner_ref, ...), custom_call_target="tpu_custom_call", output_to_operand_aliasing={{0}: (0, {}), {1}: (1, {})} | custom-call | tf_op jit(solution)/shard_map/finish/pallas_call | solution.py:725
  (2 shorter events, 0.0 us)
Async XLA Ops:
  0.6 3.7 %collective-permute-start = (s32[1,2]{1,0:T(1,128)}, s32[1,2]{1,0:T(1,128)S(1)}, u32[]{:S(2)}, u32[]{:S(2)}) collective-permute-start(s32[1,2]{1,0:T(1,128)} %bitcast.9), channel_id=1, source_target_pairs={{0,4},{1,5},{2,6},{3,7},{4,0},{5,1},{6,2},{7,3},{8,12},{9,13},{10,... | collective-permute-start | bytes 32 | tf_op jit(solution)/shard_map/ppermute | solution.py:258
  3.3 4.4 %copy-start.4 = (s32[1,1,1,2]{3,2,1,0:T(1,128)S(1)}, s32[1,1,1,2]{3,2,1,0:T(1,128)}, u32[]{:S(2)}) copy-start(s32[1,1,1,2]{3,2,1,0:T(1,128)} %param.10) | copy-start | bytes 28
  3.3 2.1 %collective-permute-start.1 = (f32[384,128]{1,0:T(8,128)S(1)}, f32[384,128]{1,0:T(8,128)S(1)}, u32[]{:S(2)}, u32[]{:S(2)}) collective-permute-start(f32[384,128]{1,0:T(8,128)S(1)} %get-tuple-element.29), channel_id=1, source_target_pairs={{0,2},{1,3},{2,0},{3,1},{4,6},{5,7},{6,4},{7,5},{8,10},{9,11},{10,... | collective-permute-start | bytes 589832 | tf_op jit(solution)/shard_map/ppermute | solution.py:258
  4.4 1.8 %collective-permute-start.2 = (f32[384,128]{1,0:T(8,128)S(1)}, f32[384,128]{1,0:T(8,128)S(1)}, u32[]{:S(2)}, u32[]{:S(2)}) collective-permute-start(f32[384,128]{1,0:T(8,128)S(1)} %get-tuple-element.30), channel_id=1, source_target_pairs={{0,2},{1,3},{2,0},{3,1},{4,6},{5,7},{6,4},{7,5},{8,10},{9,11},{10,... | collective-permute-start | bytes 589832 | tf_op jit(solution)/shard_map/ppermute | solution.py:258
  6.4 7.6 %collective-permute-start.3 = (f32[2,128,256]{2,1,0:T(8,128)S(1)}, f32[2,128,256]{2,1,0:T(8,128)S(1)}, u32[]{:S(2)}, u32[]{:S(2)}) collective-permute-start(f32[2,128,256]{2,1,0:T(8,128)S(1)} %halo_rows.1), channel_id=1, source_target_pairs={{0,4},{1,5},{2,6},{3,7},{4,0},{5,1},{6,2},{7,3},{8,12},{9,13},{10,... | collective-permute-start | bytes 786440 | tf_op jit(solution)/shard_map/ppermute | solution.py:258
  7.8 11.6 %copy-start.2 = (s32[1,1,1,256,256]{4,3,2,1,0:T(8,128)S(1)}, s32[1,1,1,256,256]{4,3,2,1,0:T(8,128)}, u32[]{:S(2)}) copy-start(s32[1,1,1,256,256]{4,3,2,1,0:T(8,128)} %param.11) | copy-start | bytes 786436
  7.8 11.6 %copy-start.3 = (bf16[2,256,256]{2,1,0:T(8,128)(2,1)S(1)}, bf16[2,256,256]{2,1,0:T(8,128)(2,1)}, u32[]{:S(2)}) copy-start(bf16[2,256,256]{2,1,0:T(8,128)(2,1)} %constant.4.clone.sort) | copy-start | bytes 786436
  8.1 11.2 %copy-start.1 = (f32[2,256,256]{2,1,0:T(8,128)S(1)}, f32[2,256,256]{2,1,0:T(8,128)}, u32[]{:S(2)}) copy-start(f32[2,256,256]{2,1,0:T(8,128)} %probe) | copy-start | bytes 1572868
  8.1 10.5 %collective-permute-start.7 = (f32[2,128,256]{2,1,0:T(8,128)S(1)}, f32[2,128,256]{2,1,0:T(8,128)S(1)}, u32[]{:S(2)}, u32[]{:S(2)}) collective-permute-start(f32[2,128,256]{2,1,0:T(8,128)S(1)} %window.1.refs_2_), channel_id=1, source_target_pairs={{0,8},{1,9},{4,12},{5,13},{26,18},{27,19},{30,22},{31,23}} | collective-permute-start | bytes 786440 | tf_op jit(solution)/shard_map/ppermute | solution.py:258
  9.0 11.3 %collective-permute-start.6 = (f32[2,128,256]{2,1,0:T(8,128)S(1)}, f32[2,128,256]{2,1,0:T(8,128)S(1)}, u32[]{:S(2)}, u32[]{:S(2)}) collective-permute-start(f32[2,128,256]{2,1,0:T(8,128)S(1)} %window.1.refs_2_), channel_id=1, source_target_pairs={{10,18},{11,19},{14,22},{15,23},{16,8},{17,9},{20,12},{21,13}} | collective-permute-start | bytes 786440 | tf_op jit(solution)/shard_map/ppermute | solution.py:258
  12.8 7.8 %collective-permute-start.5 = (f32[2,128,256]{2,1,0:T(8,128)S(1)}, f32[2,128,256]{2,1,0:T(8,128)S(1)}, u32[]{:S(2)}, u32[]{:S(2)}) collective-permute-start(f32[2,128,256]{2,1,0:T(8,128)S(1)} %window.1.refs_2_), channel_id=1, source_target_pairs={{2,18},{3,19},{6,22},{7,23},{24,8},{25,9},{28,12},{29,13}} | collective-permute-start | bytes 786440 | tf_op jit(solution)/shard_map/ppermute | solution.py:258
  13.5 11.0 %copy-start = (bf16[12,2,256,256]{3,2,1,0:T(8,128)(2,1)S(1)}, bf16[12,2,256,256]{3,2,1,0:T(8,128)(2,1)}, u32[]{:S(2)}) copy-start(bf16[12,2,256,256]{3,2,1,0:T(8,128)(2,1)} %constant.5.clone.tables) | copy-start | bytes 9437188
  14.1 9.1 %collective-permute-start.10 = (f32[2,128,256]{2,1,0:T(8,128)S(1)}, f32[2,128,256]{2,1,0:T(8,128)S(1)}, u32[]{:S(2)}, u32[]{:S(2)}) collective-permute-start(f32[2,128,256]{2,1,0:T(8,128)S(1)} %join.1.refs_5_), channel_id=1, source_target_pairs={{2,18},{3,19},{6,22},{7,23},{24,8},{25,9},{28,12},{29,13}} | collective-permute-start | bytes 786440 | tf_op jit(solution)/shard_map/ppermute | solution.py:258
  14.9 9.6 %collective-permute-start.9 = (f32[2,128,256]{2,1,0:T(8,128)S(1)}, f32[2,128,256]{2,1,0:T(8,128)S(1)}, u32[]{:S(2)}, u32[]{:S(2)}) collective-permute-start(f32[2,128,256]{2,1,0:T(8,128)S(1)} %join.1.refs_5_), channel_id=1, source_target_pairs={{10,18},{11,19},{14,22},{15,23},{16,8},{17,9},{20,12},{21,13}} | collective-permute-start | bytes 786440 | tf_op jit(solution)/shard_map/ppermute | solution.py:258
  18.6 5.9 %collective-permute-start.8 = (f32[2,128,256]{2,1,0:T(8,128)S(1)}, f32[2,128,256]{2,1,0:T(8,128)S(1)}, u32[]{:S(2)}, u32[]{:S(2)}) collective-permute-start(f32[2,128,256]{2,1,0:T(8,128)S(1)} %join.1.refs_5_), channel_id=1, source_target_pairs={{0,8},{1,9},{4,12},{5,13},{26,18},{27,19},{30,22},{31,23}} | collective-permute-start | bytes 786440 | tf_op jit(solution)/shard_map/ppermute | solution.py:258
  20.3 2.9 %collective-permute-start.4 = (s32[4,8,128]{2,1,0:T(8,128)S(1)}, s32[4,8,128]{2,1,0:T(8,128)S(1)}, u32[]{:S(2)}, u32[]{:S(2)}) collective-permute-start(s32[4,8,128]{2,1,0:T(8,128)S(1)} %pad_add_fusion), channel_id=1, source_target_pairs={{0,1},{1,0},{2,3},{3,2},{4,5},{5,4},{6,7},{7,6},{8,9},{9,8},{10,11... | collective-permute-start | bytes 49160 | tf_op jit(solution)/shard_map/ppermute | solution.py:258
  30.7 3.5 %collective-permute-start.11 = (f32[2,256,256]{2,1,0:T(8,128)S(1)}, f32[2,256,256]{2,1,0:T(8,128)S(1)}, u32[]{:S(2)}, u32[]{:S(2)}) collective-permute-start(f32[2,256,256]{2,1,0:T(8,128)S(1)} %get-tuple-element.37), channel_id=1, source_target_pairs={{8,24},{9,25},{12,28},{13,29},{18,2},{19,3},{22,6},{23,7}} | collective-permute-start | bytes 1572872 | tf_op jit(solution)/shard_map/ppermute | solution.py:258
  31.4 2.8 %collective-permute-start.12 = (f32[2,256,256]{2,1,0:T(8,128)S(1)}, f32[2,256,256]{2,1,0:T(8,128)S(1)}, u32[]{:S(2)}, u32[]{:S(2)}) collective-permute-start(f32[2,256,256]{2,1,0:T(8,128)S(1)} %get-tuple-element.38), channel_id=1, source_target_pairs={{8,0},{9,1},{12,4},{13,5},{18,26},{19,27},{22,30},{23,31}} | collective-permute-start | bytes 1572872 | tf_op jit(solution)/shard_map/ppermute | solution.py:258
  32.1 14.5 %collective-permute-start.13 = (f32[2,256,256]{2,1,0:T(8,128)S(1)}, f32[2,256,256]{2,1,0:T(8,128)S(1)}, u32[]{:S(2)}, u32[]{:S(2)}) collective-permute-start(f32[2,256,256]{2,1,0:T(8,128)S(1)} %get-tuple-element.39), channel_id=1, source_target_pairs={{8,16},{9,17},{12,20},{13,21},{18,10},{19,11},{22,14},{23,15}} | collective-permute-start | bytes 1572872 | tf_op jit(solution)/shard_map/ppermute | solution.py:258
  33.5 13.6 %collective-permute-start.15 = (f32[2,128,256]{2,1,0:T(8,128)S(1)}, f32[2,128,256]{2,1,0:T(8,128)S(1)}, u32[]{:S(2)}, u32[]{:S(2)}) collective-permute-start(f32[2,128,256]{2,1,0:T(8,128)S(1)} %own_parts.1), channel_id=1, source_target_pairs={{9,12},{12,9},{19,22},{22,19}} | collective-permute-start | bytes 786440 | tf_op jit(solution)/shard_map/ppermute | solution.py:258
  46.8 13.0 %collective-permute-start.14 = (f32[2,192,256]{2,1,0:T(8,128)S(1)}, f32[2,192,256]{2,1,0:T(8,128)S(1)}, u32[]{:S(2)}, u32[]{:S(2)}) collective-permute-start(f32[2,192,256]{2,1,0:T(8,128)S(1)} %get-tuple-element.41), channel_id=1, source_target_pairs={{0,1},{1,0},{2,3},{3,2},{4,5},{5,4},{6,7},{7,6},{8,9},{9,8},{10,11... | collective-permute-start | bytes 1179656 | tf_op jit(solution)/shard_map/ppermute | solution.py:258
  47.1 8.9 %collective-permute-start.16 = (f32[2,128,256]{2,1,0:T(8,128)S(1)}, f32[2,128,256]{2,1,0:T(8,128)S(1)}, u32[]{:S(2)}, u32[]{:S(2)}) collective-permute-start(f32[2,128,256]{2,1,0:T(8,128)S(1)} %get-tuple-element.44), channel_id=1, source_target_pairs={{0,4},{2,6},{5,1},{7,3},{8,12},{10,14},{13,9},{15,11},{16,20},{18,... | collective-permute-start | bytes 786440 | tf_op jit(solution)/shard_map/ppermute | solution.py:258
  48.4 8.1 %collective-permute-start.17 = (f32[2,128,256]{2,1,0:T(8,128)S(1)}, f32[2,128,256]{2,1,0:T(8,128)S(1)}, u32[]{:S(2)}, u32[]{:S(2)}) collective-permute-start(f32[2,128,256]{2,1,0:T(8,128)S(1)} %get-tuple-element.45), channel_id=1, source_target_pairs={{1,4},{3,6},{4,1},{6,3},{11,14},{14,11},{17,20},{20,17},{25,28},{2... | collective-permute-start | bytes 786440 | tf_op jit(solution)/shard_map/ppermute | solution.py:258
  60.0 2.5 %collective-permute-start.18 = (f32[2,192,128]{2,1,0:T(8,128)S(1)}, f32[2,192,128]{2,1,0:T(8,128)S(1)}, u32[]{:S(2)}, u32[]{:S(2)}) collective-permute-start(f32[2,192,128]{2,1,0:T(8,128)S(1)} %edge_terms.1), channel_id=1, source_target_pairs={{0,2},{1,3},{2,0},{3,1},{4,6},{5,7},{6,4},{7,5},{8,10},{9,11},{10,... | collective-permute-start | bytes 589832 | tf_op jit(solution)/shard_map/ppermute | solution.py:258

commit v9 on v7

--- a/solution.py
+++ b/solution.py
@@ -522,8 +522,8 @@
         far_terms = from_owner(terms[3], far_of)
         back = (
             far_terms,
+            from_owner(terms[2], middle_of),
             from_owner(terms[0], near_of),
-            from_owner(terms[2], middle_of),
             terms[1],
         )
 
@@ -531,7 +531,7 @@
             section, owner = place.section(), place.owner()
             near = 3 * (owner - 1)
             choice = jnp.where(
-                section == 3 - near, 0, jnp.where(section == near, 1, jnp.where(section == owner, 3, 2))
+                section == 3 - near, 0, jnp.where(section == near, 2, jnp.where(section == owner, 3, 1))
             )
             for number, ref in enumerate(refs):
 

time: 63.6 us -> 63.6 us (level)
  no operation moved by 1% of the time
where the time goes in v9:
time: 63.6 us; the launch traced here: 63.3 us
  starting transfers between devices  25.6 us (40%)
  waiting for transfers between devices  24.9 us (39%)
  Pallas kernels  10.5 us (17%)
  other arithmetic  1.32 us (2%)
  between operations  0.88 us (1%)
    ppermute x19, starting transfers between devices, move(): return lax.ppermute(value, AXES, everywhere(target_of))  25.6 us
    ppermute x19, waiting for transfers between devices, move(): return lax.ppermute(value, AXES, everywhere(target_of))  24.9 us
    pallas_call x1, Pallas kernels, shards(): pl.pallas_call(frame_kernel, out_shape=[sds((2, frame, frame), f32)] * 4,...  6.15 us
    another operation x1, other arithmetic, shards(): tile = jnp.stack([phase, absorb])  1.32 us
  transfers between devices with their start and end apart: 19, of which 10 were waited for; matrix products, arithmetic and copies ran while one was open for 2% of the time, Pallas kernels for 5%

profile of v9, /device:TPU:13, one launch (start us, length us, event | category | flops | bytes accessed | tf_op | source)
XLA Modules:
  0.0 63.3 jit_solution(10507630417013330576)
XLA Ops:
  0.6 1.3 %collective-permute-start = (s32[1,2]{1,0:T(1,128)}, s32[1,2]{1,0:T(1,128)S(1)}, u32[]{:S(2)}, u32[]{:S(2)}) collective-permute-start(s32[1,2]{1,0:T(1,128)} %bitcast.9), channel_id=1, source_target_pairs={{0,4},{1,5},{2,6},{3,7},{4,0},{5,1},{6,2},{7,3},{8,12},{9,13},{10,... | collective-permute-start | bytes 32 | tf_op jit(solution)/shard_map/ppermute | solution.py:258
  1.9 1.3 %pad_maximum_fusion.tile.refs_0_ = f32[2,384,384]{2,1,0:T(8,128)S(1)} fusion(f32[1,384,384]{2,1,0:T(8,128)} %bitcast.12, f32[1,384,384]{2,1,0:T(8,128)} %bitcast.13), kind=kLoop, calls=%fused_computation | loop fusion | flops 294912 | bytes 2359296 | tf_op jit(solution)/shard_map/stack | solution.py:304
  3.3 0.0 copy-start.4
  3.3 1.0 %collective-permute-start.1 = (f32[384,128]{1,0:T(8,128)S(1)}, f32[384,128]{1,0:T(8,128)S(1)}, u32[]{:S(2)}, u32[]{:S(2)}) collective-permute-start(f32[384,128]{1,0:T(8,128)S(1)} %get-tuple-element.31), channel_id=1, source_target_pairs={{0,2},{1,3},{2,0},{3,1},{4,6},{5,7},{6,4},{7,5},{8,10},{9,11},{10,... | collective-permute-start | bytes 589832 | tf_op jit(solution)/shard_map/ppermute | solution.py:258
  4.3 0.0 collective-permute-done
  4.3 0.1 broadcast_in_dim.23.refs_3_
  4.4 0.7 %collective-permute-start.2 = (f32[384,128]{1,0:T(8,128)S(1)}, f32[384,128]{1,0:T(8,128)S(1)}, u32[]{:S(2)}, u32[]{:S(2)}) collective-permute-start(f32[384,128]{1,0:T(8,128)S(1)} %get-tuple-element.32), channel_id=1, source_target_pairs={{0,2},{1,3},{2,0},{3,1},{4,6},{5,7},{6,4},{7,5},{8,10},{9,11},{10,... | collective-permute-start | bytes 589832 | tf_op jit(solution)/shard_map/ppermute | solution.py:258
  5.1 0.3 collective-permute-done.1.refs_1_
  5.4 0.8 %collective-permute-done.2.refs_2_ = f32[384,128]{1,0:T(8,128)S(1)} collective-permute-done((f32[384,128]{1,0:T(8,128)S(1)}, f32[384,128]{1,0:T(8,128)S(1)}, u32[]{:S(2)}, u32[]{:S(2)}) %collective-permute-start.2) | collective-permute-done | bytes 196640 | tf_op jit(solution)/shard_map/ppermute | solution.py:258
  6.2 0.0 copy-start.1
  6.2 0.0 copy-start.2
  6.2 0.0 copy-start.3
  6.2 0.2 halo_rows.1
  6.4 1.3 %collective-permute-start.3 = (f32[2,128,256]{2,1,0:T(8,128)S(1)}, f32[2,128,256]{2,1,0:T(8,128)S(1)}, u32[]{:S(2)}, u32[]{:S(2)}) collective-permute-start(f32[2,128,256]{2,1,0:T(8,128)S(1)} %halo_rows.1), channel_id=1, source_target_pairs={{0,4},{1,5},{2,6},{3,7},{4,0},{5,1},{6,2},{7,3},{8,12},{9,13},{10,... | collective-permute-start | bytes 786440 | tf_op jit(solution)/shard_map/ppermute | solution.py:258
  7.7 0.0 copy-done.4
  7.7 0.1 broadcast_in_dim.21.spot_ref.refs_0_
  7.8 0.0 copy-start
  7.8 0.6 window.1
  8.4 0.8 %collective-permute-start.7 = (f32[2,128,256]{2,1,0:T(8,128)S(1)}, f32[2,128,256]{2,1,0:T(8,128)S(1)}, u32[]{:S(2)}, u32[]{:S(2)}) collective-permute-start(f32[2,128,256]{2,1,0:T(8,128)S(1)} %get-tuple-element.39.refs_2_), channel_id=1, source_target_pairs={{0,8},{1,9},{4,12},{5,13},{26,18},{27,19},{30,22},{31,23}} | collective-permute-start | bytes 786440 | tf_op jit(solution)/shard_map/ppermute | solution.py:258
  9.2 3.8 %collective-permute-start.6 = (f32[2,128,256]{2,1,0:T(8,128)S(1)}, f32[2,128,256]{2,1,0:T(8,128)S(1)}, u32[]{:S(2)}, u32[]{:S(2)}) collective-permute-start(f32[2,128,256]{2,1,0:T(8,128)S(1)} %get-tuple-element.39.refs_2_), channel_id=1, source_target_pairs={{10,18},{11,19},{14,22},{15,23},{16,8},{17,9},{20,12},{21,13}} | collective-permute-start | bytes 786440 | tf_op jit(solution)/shard_map/ppermute | solution.py:258
  13.0 0.7 %collective-permute-start.5 = (f32[2,128,256]{2,1,0:T(8,128)S(1)}, f32[2,128,256]{2,1,0:T(8,128)S(1)}, u32[]{:S(2)}, u32[]{:S(2)}) collective-permute-start(f32[2,128,256]{2,1,0:T(8,128)S(1)} %get-tuple-element.39.refs_2_), channel_id=1, source_target_pairs={{2,18},{3,19},{6,22},{7,23},{24,8},{25,9},{28,12},{29,13}} | collective-permute-start | bytes 786440 | tf_op jit(solution)/shard_map/ppermute | solution.py:258
  13.7 0.3 collective-permute-done.3.refs_0_
  14.0 0.1 join.1.refs_5_
  14.1 0.7 %collective-permute-start.10 = (f32[2,128,256]{2,1,0:T(8,128)S(1)}, f32[2,128,256]{2,1,0:T(8,128)S(1)}, u32[]{:S(2)}, u32[]{:S(2)}) collective-permute-start(f32[2,128,256]{2,1,0:T(8,128)S(1)} %join.1.refs_5_), channel_id=1, source_target_pairs={{2,18},{3,19},{6,22},{7,23},{24,8},{25,9},{28,12},{29,13}} | collective-permute-start | bytes 786440 | tf_op jit(solution)/shard_map/ppermute | solution.py:258
  14.8 3.8 %collective-permute-start.9 = (f32[2,128,256]{2,1,0:T(8,128)S(1)}, f32[2,128,256]{2,1,0:T(8,128)S(1)}, u32[]{:S(2)}, u32[]{:S(2)}) collective-permute-start(f32[2,128,256]{2,1,0:T(8,128)S(1)} %join.1.refs_5_), channel_id=1, source_target_pairs={{10,18},{11,19},{14,22},{15,23},{16,8},{17,9},{20,12},{21,13}} | collective-permute-start | bytes 786440 | tf_op jit(solution)/shard_map/ppermute | solution.py:258
  18.6 0.0 collective-permute-done.7.refs_3_
  18.6 0.7 %collective-permute-start.8 = (f32[2,128,256]{2,1,0:T(8,128)S(1)}, f32[2,128,256]{2,1,0:T(8,128)S(1)}, u32[]{:S(2)}, u32[]{:S(2)}) collective-permute-start(f32[2,128,256]{2,1,0:T(8,128)S(1)} %join.1.refs_5_), channel_id=1, source_target_pairs={{0,8},{1,9},{4,12},{5,13},{26,18},{27,19},{30,22},{31,23}} | collective-permute-start | bytes 786440 | tf_op jit(solution)/shard_map/ppermute | solution.py:258
  19.3 0.0 copy-done.1
  19.3 0.0 copy-done.2
  19.4 0.0 copy-done.3
  19.4 0.9 %prepare.1 = (f32[2,256,256]{2,1,0:T(8,128)S(1)}, f32[256,256]{1,0:T(8,128)S(1)}) custom-call(s32[1,2]{1,0:T(1,128)S(1)} %bitcast.11, f32[2,256,256]{2,1,0:T(8,128)S(1)} %copy-done.1, s32[256,256]{1,0:T(8,128)S(1)} %bitcast.8, bf16[2,256,256]{2,1,0:T(8,128)(2,1)S(1)} %copy-done.3), custom_call_target="tpu_custom_call" | custom-call | tf_op jit(solution)/shard_map/prepare/pallas_call | solution.py:442
  20.3 0.0 collective-permute-done.6.refs_1_
  20.3 0.3 collective-permute-start.4
  20.6 0.0 collective-permute-done.5.refs_0_
  20.6 2.7 %collective-permute-done.4.partner_ref.refs_1_ = s32[4,8,128]{2,1,0:T(8,128)S(1)} collective-permute-done((s32[4,8,128]{2,1,0:T(8,128)S(1)}, s32[4,8,128]{2,1,0:T(8,128)S(1)}, u32[]{:S(2)}, u32[]{:S(2)}) %collective-permute-start.4) | collective-permute-done | bytes 16416 | tf_op jit(solution)/shard_map/ppermute | solution.py:258
  23.2 0.0 collective-permute-done.10.refs_7_
  23.2 1.5 %collective-permute-done.9.refs_6_ = f32[2,128,256]{2,1,0:T(8,128)S(1)} collective-permute-done((f32[2,128,256]{2,1,0:T(8,128)S(1)}, f32[2,128,256]{2,1,0:T(8,128)S(1)}, u32[]{:S(2)}, u32[]{:S(2)}) %collective-permute-start.9) | collective-permute-done | bytes 262176 | tf_op jit(solution)/shard_map/ppermute | solution.py:258
  24.8 0.0 collective-permute-done.8.refs_4_
  24.8 0.0 copy-done
  24.8 6.1 %frame.1 = (f32[2,256,256]{2,1,0:T(8,128)S(1)}, f32[2,256,256]{2,1,0:T(8,128)S(1)}, f32[2,256,256]{2,1,0:T(8,128)S(1)}, f32[2,256,256]{2,1,0:T(8,128)S(1)}) custom-call(s32[4,8,128]{2,1,0:T(8,128)S(1)} %collective-permute-done.4.partner_ref.refs_1_, f32[2,256,256]{2,1,0:T(8,128)S(1)} %get-tuple-element.37.probe, f32[256,256]{1,0:T(8,128)S(1)} %get-tuple-element.38.seen, ...), custom_call_target="tpu_custom_call" | custom-call | tf_op jit(solution)/shard_map/frame/pallas_call | solution.py:499
  30.9 0.7 %collective-permute-start.11 = (f32[2,256,256]{2,1,0:T(8,128)S(1)}, f32[2,256,256]{2,1,0:T(8,128)S(1)}, u32[]{:S(2)}, u32[]{:S(2)}) collective-permute-start(f32[2,256,256]{2,1,0:T(8,128)S(1)} %get-tuple-element.41), channel_id=1, source_target_pairs={{8,24},{9,25},{12,28},{13,29},{18,2},{19,3},{22,6},{23,7}} | collective-permute-start | bytes 1572872 | tf_op jit(solution)/shard_map/ppermute | solution.py:258
  31.6 1.3 %collective-permute-start.12 = (f32[2,256,256]{2,1,0:T(8,128)S(1)}, f32[2,256,256]{2,1,0:T(8,128)S(1)}, u32[]{:S(2)}, u32[]{:S(2)}) collective-permute-start(f32[2,256,256]{2,1,0:T(8,128)S(1)} %get-tuple-element.42), channel_id=1, source_target_pairs={{8,16},{9,17},{12,20},{13,21},{18,10},{19,11},{22,14},{23,15}} | collective-permute-start | bytes 1572872 | tf_op jit(solution)/shard_map/ppermute | solution.py:258
  32.9 0.7 %collective-permute-start.13 = (f32[2,256,256]{2,1,0:T(8,128)S(1)}, f32[2,256,256]{2,1,0:T(8,128)S(1)}, u32[]{:S(2)}, u32[]{:S(2)}) collective-permute-start(f32[2,256,256]{2,1,0:T(8,128)S(1)} %get-tuple-element.43), channel_id=1, source_target_pairs={{8,0},{9,1},{12,4},{13,5},{18,26},{19,27},{22,30},{23,31}} | collective-permute-start | bytes 1572872 | tf_op jit(solution)/shard_map/ppermute | solution.py:258
  33.6 0.1 own_parts.1
  33.7 0.7 %collective-permute-start.15 = (f32[2,128,256]{2,1,0:T(8,128)S(1)}, f32[2,128,256]{2,1,0:T(8,128)S(1)}, u32[]{:S(2)}, u32[]{:S(2)}) collective-permute-start(f32[2,128,256]{2,1,0:T(8,128)S(1)} %own_parts.1), channel_id=1, source_target_pairs={{9,12},{12,9},{19,22},{22,19}} | collective-permute-start | bytes 786440 | tf_op jit(solution)/shard_map/ppermute | solution.py:258
  34.4 0.0 collective-permute-done.11.refs_0_
  34.4 12.1 %collective-permute-done.12.refs_1_ = f32[2,256,256]{2,1,0:T(8,128)S(1)} collective-permute-done((f32[2,256,256]{2,1,0:T(8,128)S(1)}, f32[2,256,256]{2,1,0:T(8,128)S(1)}, u32[]{:S(2)}, u32[]{:S(2)}) %collective-permute-start.12) | collective-permute-done | bytes 524320 | tf_op jit(solution)/shard_map/ppermute | solution.py:258
  46.5 0.0 collective-permute-done.13.refs_2_
  46.5 0.3 parts.1
  46.8 0.3 collective-permute-start.14
  47.1 0.0 collective-permute-done.15.refs_7_
  47.1 1.3 %collective-permute-start.16 = (f32[2,128,256]{2,1,0:T(8,128)S(1)}, f32[2,128,256]{2,1,0:T(8,128)S(1)}, u32[]{:S(2)}, u32[]{:S(2)}) collective-permute-start(f32[2,128,256]{2,1,0:T(8,128)S(1)} %get-tuple-element.48), channel_id=1, source_target_pairs={{0,4},{2,6},{5,1},{7,3},{8,12},{10,14},{13,9},{15,11},{16,20},{18,... | collective-permute-start | bytes 786440 | tf_op jit(solution)/shard_map/ppermute | solution.py:258
  48.4 4.1 %collective-permute-start.17 = (f32[2,128,256]{2,1,0:T(8,128)S(1)}, f32[2,128,256]{2,1,0:T(8,128)S(1)}, u32[]{:S(2)}, u32[]{:S(2)}) collective-permute-start(f32[2,128,256]{2,1,0:T(8,128)S(1)} %get-tuple-element.49), channel_id=1, source_target_pairs={{1,4},{3,6},{4,1},{6,3},{11,14},{14,11},{17,20},{20,17},{25,28},{2... | collective-permute-start | bytes 786440 | tf_op jit(solution)/shard_map/ppermute | solution.py:258
  52.5 0.2 keep.1.refs_2_
  52.7 3.3 %collective-permute-done.16.refs_5_ = f32[2,128,256]{2,1,0:T(8,128)S(1)} collective-permute-done((f32[2,128,256]{2,1,0:T(8,128)S(1)}, f32[2,128,256]{2,1,0:T(8,128)S(1)}, u32[]{:S(2)}, u32[]{:S(2)}) %collective-permute-start.16) | collective-permute-done | bytes 262176 | tf_op jit(solution)/shard_map/ppermute | solution.py:258
  56.0 0.5 collective-permute-done.17.refs_6_
  56.5 3.3 %collective-permute-done.14.refs_4_ = f32[2,192,256]{2,1,0:T(8,128)S(1)} collective-permute-done((f32[2,192,256]{2,1,0:T(8,128)S(1)}, f32[2,192,256]{2,1,0:T(8,128)S(1)}, u32[]{:S(2)}, u32[]{:S(2)}) %collective-permute-start.14) | collective-permute-done | bytes 393248 | tf_op jit(solution)/shard_map/ppermute | solution.py:258
  59.8 0.2 edge_terms.1
  60.0 1.5 %collective-permute-start.18 = (f32[2,192,128]{2,1,0:T(8,128)S(1)}, f32[2,192,128]{2,1,0:T(8,128)S(1)}, u32[]{:S(2)}, u32[]{:S(2)}) collective-permute-start(f32[2,192,128]{2,1,0:T(8,128)S(1)} %edge_terms.1), channel_id=1, source_target_pairs={{0,2},{1,3},{2,0},{3,1},{4,6},{5,7},{6,4},{7,5},{8,10},{9,11},{10,... | collective-permute-start | bytes 589832 | tf_op jit(solution)/shard_map/ppermute | solution.py:258
  61.5 1.0 %inner_terms.1 = (f32[192,384]{1,0:T(8,128)}, f32[192,384]{1,0:T(8,128)}, f32[1,2,192,128]{3,2,1,0:T(8,128)S(1)}) custom-call(s32[2,8,128]{2,1,0:T(8,128)S(1)} %broadcast_in_dim.21.spot_ref.refs_0_, s32[4,8,128]{2,1,0:T(8,128)S(1)} %collective-permute-done.4.partner_ref.refs_1_, f32[2,192,256]{2,1,0:T(8,128)S(1)} %keep.1.refs_2_, ...), custom_call_target="tpu_custom_call" | custom-call | flops 4194304 | bytes 2097152 | tf_op jit(solution)/shard_map/inner_terms/pallas_call | solution.py:690
  62.5 0.1 collective-permute-done.18.refs_0_
  62.6 0.7 %finish.1 = (f32[192,384]{1,0:T(8,128)}, f32[192,384]{1,0:T(8,128)}) custom-call(f32[192,384]{1,0:T(8,128)} %get-tuple-element.51.phase_in, f32[192,384]{1,0:T(8,128)} %get-tuple-element.52.absorb_in, f32[1,2,192,128]{3,2,1,0:T(8,128)S(1)} %get-tuple-element.53.inner_ref, ...), custom_call_target="tpu_custom_call", output_to_operand_aliasing={{0}: (0, {}), {1}: (1, {})} | custom-call | tf_op jit(solution)/shard_map/finish/pallas_call | solution.py:718
  (2 shorter events, 0.0 us)
Async XLA Ops:
  0.6 3.7 %collective-permute-start = (s32[1,2]{1,0:T(1,128)}, s32[1,2]{1,0:T(1,128)S(1)}, u32[]{:S(2)}, u32[]{:S(2)}) collective-permute-start(s32[1,2]{1,0:T(1,128)} %bitcast.9), channel_id=1, source_target_pairs={{0,4},{1,5},{2,6},{3,7},{4,0},{5,1},{6,2},{7,3},{8,12},{9,13},{10,... | collective-permute-start | bytes 32 | tf_op jit(solution)/shard_map/ppermute | solution.py:258
  3.3 4.4 %copy-start.4 = (s32[1,1,1,2]{3,2,1,0:T(1,128)S(1)}, s32[1,1,1,2]{3,2,1,0:T(1,128)}, u32[]{:S(2)}) copy-start(s32[1,1,1,2]{3,2,1,0:T(1,128)} %param.10) | copy-start | bytes 28
  3.3 2.1 %collective-permute-start.1 = (f32[384,128]{1,0:T(8,128)S(1)}, f32[384,128]{1,0:T(8,128)S(1)}, u32[]{:S(2)}, u32[]{:S(2)}) collective-permute-start(f32[384,128]{1,0:T(8,128)S(1)} %get-tuple-element.31), channel_id=1, source_target_pairs={{0,2},{1,3},{2,0},{3,1},{4,6},{5,7},{6,4},{7,5},{8,10},{9,11},{10,... | collective-permute-start | bytes 589832 | tf_op jit(solution)/shard_map/ppermute | solution.py:258
  4.4 1.8 %collective-permute-start.2 = (f32[384,128]{1,0:T(8,128)S(1)}, f32[384,128]{1,0:T(8,128)S(1)}, u32[]{:S(2)}, u32[]{:S(2)}) collective-permute-start(f32[384,128]{1,0:T(8,128)S(1)} %get-tuple-element.32), channel_id=1, source_target_pairs={{0,2},{1,3},{2,0},{3,1},{4,6},{5,7},{6,4},{7,5},{8,10},{9,11},{10,... | collective-permute-start | bytes 589832 | tf_op jit(solution)/shard_map/ppermute | solution.py:258
  6.2 13.2 %copy-start.1 = (f32[2,256,256]{2,1,0:T(8,128)S(1)}, f32[2,256,256]{2,1,0:T(8,128)}, u32[]{:S(2)}) copy-start(f32[2,256,256]{2,1,0:T(8,128)} %probe) | copy-start | bytes 1572868
  6.2 13.2 %copy-start.2 = (s32[1,1,1,256,256]{4,3,2,1,0:T(8,128)S(1)}, s32[1,1,1,256,256]{4,3,2,1,0:T(8,128)}, u32[]{:S(2)}) copy-start(s32[1,1,1,256,256]{4,3,2,1,0:T(8,128)} %param.11) | copy-start | bytes 786436
  6.2 13.2 %copy-start.3 = (bf16[2,256,256]{2,1,0:T(8,128)(2,1)S(1)}, bf16[2,256,256]{2,1,0:T(8,128)(2,1)}, u32[]{:S(2)}) copy-start(bf16[2,256,256]{2,1,0:T(8,128)(2,1)} %constant.4.clone.sort) | copy-start | bytes 786436
  6.4 7.6 %collective-permute-start.3 = (f32[2,128,256]{2,1,0:T(8,128)S(1)}, f32[2,128,256]{2,1,0:T(8,128)S(1)}, u32[]{:S(2)}, u32[]{:S(2)}) collective-permute-start(f32[2,128,256]{2,1,0:T(8,128)S(1)} %halo_rows.1), channel_id=1, source_target_pairs={{0,4},{1,5},{2,6},{3,7},{4,0},{5,1},{6,2},{7,3},{8,12},{9,13},{10,... | collective-permute-start | bytes 786440 | tf_op jit(solution)/shard_map/ppermute | solution.py:258
  7.8 17.0 %copy-start = (bf16[12,2,256,256]{3,2,1,0:T(8,128)(2,1)S(1)}, bf16[12,2,256,256]{3,2,1,0:T(8,128)(2,1)}, u32[]{:S(2)}) copy-start(bf16[12,2,256,256]{3,2,1,0:T(8,128)(2,1)} %constant.5.clone.tables) | copy-start | bytes 9437188
  8.4 10.2 %collective-permute-start.7 = (f32[2,128,256]{2,1,0:T(8,128)S(1)}, f32[2,128,256]{2,1,0:T(8,128)S(1)}, u32[]{:S(2)}, u32[]{:S(2)}) collective-permute-start(f32[2,128,256]{2,1,0:T(8,128)S(1)} %get-tuple-element.39.refs_2_), channel_id=1, source_target_pairs={{0,8},{1,9},{4,12},{5,13},{26,18},{27,19},{30,22},{31,23}} | collective-permute-start | bytes 786440 | tf_op jit(solution)/shard_map/ppermute | solution.py:258
  9.2 11.0 %collective-permute-start.6 = (f32[2,128,256]{2,1,0:T(8,128)S(1)}, f32[2,128,256]{2,1,0:T(8,128)S(1)}, u32[]{:S(2)}, u32[]{:S(2)}) collective-permute-start(f32[2,128,256]{2,1,0:T(8,128)S(1)} %get-tuple-element.39.refs_2_), channel_id=1, source_target_pairs={{10,18},{11,19},{14,22},{15,23},{16,8},{17,9},{20,12},{21,13}} | collective-permute-start | bytes 786440 | tf_op jit(solution)/shard_map/ppermute | solution.py:258
  13.0 7.5 %collective-permute-start.5 = (f32[2,128,256]{2,1,0:T(8,128)S(1)}, f32[2,128,256]{2,1,0:T(8,128)S(1)}, u32[]{:S(2)}, u32[]{:S(2)}) collective-permute-start(f32[2,128,256]{2,1,0:T(8,128)S(1)} %get-tuple-element.39.refs_2_), channel_id=1, source_target_pairs={{2,18},{3,19},{6,22},{7,23},{24,8},{25,9},{28,12},{29,13}} | collective-permute-start | bytes 786440 | tf_op jit(solution)/shard_map/ppermute | solution.py:258
  14.1 9.1 %collective-permute-start.10 = (f32[2,128,256]{2,1,0:T(8,128)S(1)}, f32[2,128,256]{2,1,0:T(8,128)S(1)}, u32[]{:S(2)}, u32[]{:S(2)}) collective-permute-start(f32[2,128,256]{2,1,0:T(8,128)S(1)} %join.1.refs_5_), channel_id=1, source_target_pairs={{2,18},{3,19},{6,22},{7,23},{24,8},{25,9},{28,12},{29,13}} | collective-permute-start | bytes 786440 | tf_op jit(solution)/shard_map/ppermute | solution.py:258
  14.8 10.0 %collective-permute-start.9 = (f32[2,128,256]{2,1,0:T(8,128)S(1)}, f32[2,128,256]{2,1,0:T(8,128)S(1)}, u32[]{:S(2)}, u32[]{:S(2)}) collective-permute-start(f32[2,128,256]{2,1,0:T(8,128)S(1)} %join.1.refs_5_), channel_id=1, source_target_pairs={{10,18},{11,19},{14,22},{15,23},{16,8},{17,9},{20,12},{21,13}} | collective-permute-start | bytes 786440 | tf_op jit(solution)/shard_map/ppermute | solution.py:258
  18.6 6.1 %collective-permute-start.8 = (f32[2,128,256]{2,1,0:T(8,128)S(1)}, f32[2,128,256]{2,1,0:T(8,128)S(1)}, u32[]{:S(2)}, u32[]{:S(2)}) collective-permute-start(f32[2,128,256]{2,1,0:T(8,128)S(1)} %join.1.refs_5_), channel_id=1, source_target_pairs={{0,8},{1,9},{4,12},{5,13},{26,18},{27,19},{30,22},{31,23}} | collective-permute-start | bytes 786440 | tf_op jit(solution)/shard_map/ppermute | solution.py:258
  20.3 2.9 %collective-permute-start.4 = (s32[4,8,128]{2,1,0:T(8,128)S(1)}, s32[4,8,128]{2,1,0:T(8,128)S(1)}, u32[]{:S(2)}, u32[]{:S(2)}) collective-permute-start(s32[4,8,128]{2,1,0:T(8,128)S(1)} %pad_add_fusion), channel_id=1, source_target_pairs={{0,1},{1,0},{2,3},{3,2},{4,5},{5,4},{6,7},{7,6},{8,9},{9,8},{10,11... | collective-permute-start | bytes 49160 | tf_op jit(solution)/shard_map/ppermute | solution.py:258
  30.9 3.5 %collective-permute-start.11 = (f32[2,256,256]{2,1,0:T(8,128)S(1)}, f32[2,256,256]{2,1,0:T(8,128)S(1)}, u32[]{:S(2)}, u32[]{:S(2)}) collective-permute-start(f32[2,256,256]{2,1,0:T(8,128)S(1)} %get-tuple-element.41), channel_id=1, source_target_pairs={{8,24},{9,25},{12,28},{13,29},{18,2},{19,3},{22,6},{23,7}} | collective-permute-start | bytes 1572872 | tf_op jit(solution)/shard_map/ppermute | solution.py:258
  31.6 14.9 %collective-permute-start.12 = (f32[2,256,256]{2,1,0:T(8,128)S(1)}, f32[2,256,256]{2,1,0:T(8,128)S(1)}, u32[]{:S(2)}, u32[]{:S(2)}) collective-permute-start(f32[2,256,256]{2,1,0:T(8,128)S(1)} %get-tuple-element.42), channel_id=1, source_target_pairs={{8,16},{9,17},{12,20},{13,21},{18,10},{19,11},{22,14},{23,15}} | collective-permute-start | bytes 1572872 | tf_op jit(solution)/shard_map/ppermute | solution.py:258
  32.9 13.6 %collective-permute-start.13 = (f32[2,256,256]{2,1,0:T(8,128)S(1)}, f32[2,256,256]{2,1,0:T(8,128)S(1)}, u32[]{:S(2)}, u32[]{:S(2)}) collective-permute-start(f32[2,256,256]{2,1,0:T(8,128)S(1)} %get-tuple-element.43), channel_id=1, source_target_pairs={{8,0},{9,1},{12,4},{13,5},{18,26},{19,27},{22,30},{23,31}} | collective-permute-start | bytes 1572872 | tf_op jit(solution)/shard_map/ppermute | solution.py:258
  33.7 13.4 %collective-permute-start.15 = (f32[2,128,256]{2,1,0:T(8,128)S(1)}, f32[2,128,256]{2,1,0:T(8,128)S(1)}, u32[]{:S(2)}, u32[]{:S(2)}) collective-permute-start(f32[2,128,256]{2,1,0:T(8,128)S(1)} %own_parts.1), channel_id=1, source_target_pairs={{9,12},{12,9},{19,22},{22,19}} | collective-permute-start | bytes 786440 | tf_op jit(solution)/shard_map/ppermute | solution.py:258
  46.8 13.0 %collective-permute-start.14 = (f32[2,192,256]{2,1,0:T(8,128)S(1)}, f32[2,192,256]{2,1,0:T(8,128)S(1)}, u32[]{:S(2)}, u32[]{:S(2)}) collective-permute-start(f32[2,192,256]{2,1,0:T(8,128)S(1)} %get-tuple-element.45), channel_id=1, source_target_pairs={{0,1},{1,0},{2,3},{3,2},{4,5},{5,4},{6,7},{7,6},{8,9},{9,8},{10,11... | collective-permute-start | bytes 1179656 | tf_op jit(solution)/shard_map/ppermute | solution.py:258
  47.1 8.9 %collective-permute-start.16 = (f32[2,128,256]{2,1,0:T(8,128)S(1)}, f32[2,128,256]{2,1,0:T(8,128)S(1)}, u32[]{:S(2)}, u32[]{:S(2)}) collective-permute-start(f32[2,128,256]{2,1,0:T(8,128)S(1)} %get-tuple-element.48), channel_id=1, source_target_pairs={{0,4},{2,6},{5,1},{7,3},{8,12},{10,14},{13,9},{15,11},{16,20},{18,... | collective-permute-start | bytes 786440 | tf_op jit(solution)/shard_map/ppermute | solution.py:258
  48.4 8.1 %collective-permute-start.17 = (f32[2,128,256]{2,1,0:T(8,128)S(1)}, f32[2,128,256]{2,1,0:T(8,128)S(1)}, u32[]{:S(2)}, u32[]{:S(2)}) collective-permute-start(f32[2,128,256]{2,1,0:T(8,128)S(1)} %get-tuple-element.49), channel_id=1, source_target_pairs={{1,4},{3,6},{4,1},{6,3},{11,14},{14,11},{17,20},{20,17},{25,28},{2... | collective-permute-start | bytes 786440 | tf_op jit(solution)/shard_map/ppermute | solution.py:258
  60.0 2.5 %collective-permute-start.18 = (f32[2,192,128]{2,1,0:T(8,128)S(1)}, f32[2,192,128]{2,1,0:T(8,128)S(1)}, u32[]{:S(2)}, u32[]{:S(2)}) collective-permute-start(f32[2,192,128]{2,1,0:T(8,128)S(1)} %edge_terms.1), channel_id=1, source_target_pairs={{0,2},{1,3},{2,0},{3,1},{4,6},{5,7},{6,4},{7,5},{8,10},{9,11},{10,... | collective-permute-start | bytes 589832 | tf_op jit(solution)/shard_map/ppermute | solution.py:258

commit v10 on v7

--- a/solution.py
+++ b/solution.py
@@ -628,7 +628,7 @@
         def add_band(band, plane, refs):
             spot_ref, partner_ref, kept_ref, *spot_refs = refs[: 3 + ways]
             is_owner = place.section() == place.owner()
-            given, straight, late, early = (ref[plane] for ref in refs[3 + ways : count])
+            straight, given, late, early = (ref[plane] for ref in refs[3 + ways : count])
             across = jnp.where(is_owner, early, late)
             rep = place.rep()
             if ways == 1:
@@ -646,7 +646,7 @@
             early, late = jnp.concatenate([strip, gap], 0), jnp.concatenate([gap, strip], 0)
             return total + jnp.where(rep == 1, late, early)
 
-        pieces = (spot_tiles, spots_rep, kept, *spots_rows, given, came_straight, late_across, early_across)
+        pieces = (spot_tiles, spots_rep, kept, *spots_rows, came_straight, given, late_across, early_across)
         piece_specs = [VMEM] * len(pieces)
         count = len(piece_specs)
 

time: 63.6 us -> 63.6 us (level)
  no operation moved by 1% of the time
where the time goes in v10:
time: 63.6 us; the launch traced here: 63.3 us
  starting transfers between devices  25.6 us (40%)
  waiting for transfers between devices  24.9 us (39%)
  Pallas kernels  10.5 us (17%)
  other arithmetic  1.32 us (2%)
  between operations  0.89 us (1%)
    ppermute x19, starting transfers between devices, move(): return lax.ppermute(value, AXES, everywhere(target_of))  25.6 us
    ppermute x19, waiting for transfers between devices, move(): return lax.ppermute(value, AXES, everywhere(target_of))  24.9 us
    pallas_call x1, Pallas kernels, shards(): pl.pallas_call(frame_kernel, out_shape=[sds((2, frame, frame), f32)] * 4,...  6.15 us
    another operation x1, other arithmetic, shards(): tile = jnp.stack([phase, absorb])  1.32 us
  transfers between devices with their start and end apart: 19, of which 10 were waited for; matrix products, arithmetic and copies ran while one was open for 2% of the time, Pallas kernels for 5%

profile of v10, /device:TPU:13, one launch (start us, length us, event | category | flops | bytes accessed | tf_op | source)
XLA Modules:
  0.0 63.3 jit_solution(4948460330042444569)
XLA Ops:
  0.6 1.3 %collective-permute-start = (s32[1,2]{1,0:T(1,128)}, s32[1,2]{1,0:T(1,128)S(1)}, u32[]{:S(2)}, u32[]{:S(2)}) collective-permute-start(s32[1,2]{1,0:T(1,128)} %bitcast.9), channel_id=1, source_target_pairs={{0,4},{1,5},{2,6},{3,7},{4,0},{5,1},{6,2},{7,3},{8,12},{9,13},{10,... | collective-permute-start | bytes 32 | tf_op jit(solution)/shard_map/ppermute | solution.py:258
  1.9 1.3 %pad_maximum_fusion.tile.refs_0_ = f32[2,384,384]{2,1,0:T(8,128)S(1)} fusion(f32[1,384,384]{2,1,0:T(8,128)} %bitcast.12, f32[1,384,384]{2,1,0:T(8,128)} %bitcast.13), kind=kLoop, calls=%fused_computation | loop fusion | flops 294912 | bytes 2359296 | tf_op jit(solution)/shard_map/stack | solution.py:304
  3.3 0.0 copy-start.4
  3.3 1.0 %collective-permute-start.1 = (f32[384,128]{1,0:T(8,128)S(1)}, f32[384,128]{1,0:T(8,128)S(1)}, u32[]{:S(2)}, u32[]{:S(2)}) collective-permute-start(f32[384,128]{1,0:T(8,128)S(1)} %get-tuple-element.31), channel_id=1, source_target_pairs={{0,2},{1,3},{2,0},{3,1},{4,6},{5,7},{6,4},{7,5},{8,10},{9,11},{10,... | collective-permute-start | bytes 589832 | tf_op jit(solution)/shard_map/ppermute | solution.py:258
  4.3 0.0 collective-permute-done
  4.3 0.1 broadcast_in_dim.23.refs_3_
  4.4 0.7 %collective-permute-start.2 = (f32[384,128]{1,0:T(8,128)S(1)}, f32[384,128]{1,0:T(8,128)S(1)}, u32[]{:S(2)}, u32[]{:S(2)}) collective-permute-start(f32[384,128]{1,0:T(8,128)S(1)} %get-tuple-element.32), channel_id=1, source_target_pairs={{0,2},{1,3},{2,0},{3,1},{4,6},{5,7},{6,4},{7,5},{8,10},{9,11},{10,... | collective-permute-start | bytes 589832 | tf_op jit(solution)/shard_map/ppermute | solution.py:258
  5.1 0.3 collective-permute-done.1.refs_1_
  5.4 0.8 %collective-permute-done.2.refs_2_ = f32[384,128]{1,0:T(8,128)S(1)} collective-permute-done((f32[384,128]{1,0:T(8,128)S(1)}, f32[384,128]{1,0:T(8,128)S(1)}, u32[]{:S(2)}, u32[]{:S(2)}) %collective-permute-start.2) | collective-permute-done | bytes 196640 | tf_op jit(solution)/shard_map/ppermute | solution.py:258
  6.2 0.0 copy-start.1
  6.2 0.0 copy-start.2
  6.2 0.0 copy-start.3
  6.2 0.2 halo_rows.1
  6.4 1.3 %collective-permute-start.3 = (f32[2,128,256]{2,1,0:T(8,128)S(1)}, f32[2,128,256]{2,1,0:T(8,128)S(1)}, u32[]{:S(2)}, u32[]{:S(2)}) collective-permute-start(f32[2,128,256]{2,1,0:T(8,128)S(1)} %halo_rows.1), channel_id=1, source_target_pairs={{0,4},{1,5},{2,6},{3,7},{4,0},{5,1},{6,2},{7,3},{8,12},{9,13},{10,... | collective-permute-start | bytes 786440 | tf_op jit(solution)/shard_map/ppermute | solution.py:258
  7.7 0.0 copy-done.4
  7.7 0.1 broadcast_in_dim.21.spot_ref.refs_0_
  7.8 0.0 copy-start
  7.8 0.6 window.1
  8.4 0.8 %collective-permute-start.7 = (f32[2,128,256]{2,1,0:T(8,128)S(1)}, f32[2,128,256]{2,1,0:T(8,128)S(1)}, u32[]{:S(2)}, u32[]{:S(2)}) collective-permute-start(f32[2,128,256]{2,1,0:T(8,128)S(1)} %get-tuple-element.39.refs_2_), channel_id=1, source_target_pairs={{0,8},{1,9},{4,12},{5,13},{26,18},{27,19},{30,22},{31,23}} | collective-permute-start | bytes 786440 | tf_op jit(solution)/shard_map/ppermute | solution.py:258
  9.2 3.8 %collective-permute-start.6 = (f32[2,128,256]{2,1,0:T(8,128)S(1)}, f32[2,128,256]{2,1,0:T(8,128)S(1)}, u32[]{:S(2)}, u32[]{:S(2)}) collective-permute-start(f32[2,128,256]{2,1,0:T(8,128)S(1)} %get-tuple-element.39.refs_2_), channel_id=1, source_target_pairs={{10,18},{11,19},{14,22},{15,23},{16,8},{17,9},{20,12},{21,13}} | collective-permute-start | bytes 786440 | tf_op jit(solution)/shard_map/ppermute | solution.py:258
  13.0 0.7 %collective-permute-start.5 = (f32[2,128,256]{2,1,0:T(8,128)S(1)}, f32[2,128,256]{2,1,0:T(8,128)S(1)}, u32[]{:S(2)}, u32[]{:S(2)}) collective-permute-start(f32[2,128,256]{2,1,0:T(8,128)S(1)} %get-tuple-element.39.refs_2_), channel_id=1, source_target_pairs={{2,18},{3,19},{6,22},{7,23},{24,8},{25,9},{28,12},{29,13}} | collective-permute-start | bytes 786440 | tf_op jit(solution)/shard_map/ppermute | solution.py:258
  13.7 0.3 collective-permute-done.3.refs_0_
  14.0 0.1 join.1.refs_5_
  14.1 0.7 %collective-permute-start.10 = (f32[2,128,256]{2,1,0:T(8,128)S(1)}, f32[2,128,256]{2,1,0:T(8,128)S(1)}, u32[]{:S(2)}, u32[]{:S(2)}) collective-permute-start(f32[2,128,256]{2,1,0:T(8,128)S(1)} %join.1.refs_5_), channel_id=1, source_target_pairs={{2,18},{3,19},{6,22},{7,23},{24,8},{25,9},{28,12},{29,13}} | collective-permute-start | bytes 786440 | tf_op jit(solution)/shard_map/ppermute | solution.py:258
  14.8 3.8 %collective-permute-start.9 = (f32[2,128,256]{2,1,0:T(8,128)S(1)}, f32[2,128,256]{2,1,0:T(8,128)S(1)}, u32[]{:S(2)}, u32[]{:S(2)}) collective-permute-start(f32[2,128,256]{2,1,0:T(8,128)S(1)} %join.1.refs_5_), channel_id=1, source_target_pairs={{10,18},{11,19},{14,22},{15,23},{16,8},{17,9},{20,12},{21,13}} | collective-permute-start | bytes 786440 | tf_op jit(solution)/shard_map/ppermute | solution.py:258
  18.6 0.0 collective-permute-done.7.refs_3_
  18.6 0.7 %collective-permute-start.8 = (f32[2,128,256]{2,1,0:T(8,128)S(1)}, f32[2,128,256]{2,1,0:T(8,128)S(1)}, u32[]{:S(2)}, u32[]{:S(2)}) collective-permute-start(f32[2,128,256]{2,1,0:T(8,128)S(1)} %join.1.refs_5_), channel_id=1, source_target_pairs={{0,8},{1,9},{4,12},{5,13},{26,18},{27,19},{30,22},{31,23}} | collective-permute-start | bytes 786440 | tf_op jit(solution)/shard_map/ppermute | solution.py:258
  19.3 0.0 copy-done.1
  19.3 0.0 copy-done.2
  19.4 0.0 copy-done.3
  19.4 0.9 %prepare.1 = (f32[2,256,256]{2,1,0:T(8,128)S(1)}, f32[256,256]{1,0:T(8,128)S(1)}) custom-call(s32[1,2]{1,0:T(1,128)S(1)} %bitcast.11, f32[2,256,256]{2,1,0:T(8,128)S(1)} %copy-done.1, s32[256,256]{1,0:T(8,128)S(1)} %bitcast.8, bf16[2,256,256]{2,1,0:T(8,128)(2,1)S(1)} %copy-done.3), custom_call_target="tpu_custom_call" | custom-call | tf_op jit(solution)/shard_map/prepare/pallas_call | solution.py:442
  20.3 0.0 collective-permute-done.6.refs_1_
  20.3 0.3 collective-permute-start.4
  20.6 0.0 collective-permute-done.5.refs_0_
  20.6 2.7 %collective-permute-done.4.partner_ref.refs_1_ = s32[4,8,128]{2,1,0:T(8,128)S(1)} collective-permute-done((s32[4,8,128]{2,1,0:T(8,128)S(1)}, s32[4,8,128]{2,1,0:T(8,128)S(1)}, u32[]{:S(2)}, u32[]{:S(2)}) %collective-permute-start.4) | collective-permute-done | bytes 16416 | tf_op jit(solution)/shard_map/ppermute | solution.py:258
  23.2 0.0 collective-permute-done.10.refs_7_
  23.2 1.5 %collective-permute-done.9.refs_6_ = f32[2,128,256]{2,1,0:T(8,128)S(1)} collective-permute-done((f32[2,128,256]{2,1,0:T(8,128)S(1)}, f32[2,128,256]{2,1,0:T(8,128)S(1)}, u32[]{:S(2)}, u32[]{:S(2)}) %collective-permute-start.9) | collective-permute-done | bytes 262176 | tf_op jit(solution)/shard_map/ppermute | solution.py:258
  24.8 0.0 collective-permute-done.8.refs_4_
  24.8 0.0 copy-done
  24.8 6.1 %frame.1 = (f32[2,256,256]{2,1,0:T(8,128)S(1)}, f32[2,256,256]{2,1,0:T(8,128)S(1)}, f32[2,256,256]{2,1,0:T(8,128)S(1)}, f32[2,256,256]{2,1,0:T(8,128)S(1)}) custom-call(s32[4,8,128]{2,1,0:T(8,128)S(1)} %collective-permute-done.4.partner_ref.refs_1_, f32[2,256,256]{2,1,0:T(8,128)S(1)} %get-tuple-element.37.probe, f32[256,256]{1,0:T(8,128)S(1)} %get-tuple-element.38.seen, ...), custom_call_target="tpu_custom_call" | custom-call | tf_op jit(solution)/shard_map/frame/pallas_call | solution.py:499
  30.9 0.7 %collective-permute-start.11 = (f32[2,256,256]{2,1,0:T(8,128)S(1)}, f32[2,256,256]{2,1,0:T(8,128)S(1)}, u32[]{:S(2)}, u32[]{:S(2)}) collective-permute-start(f32[2,256,256]{2,1,0:T(8,128)S(1)} %get-tuple-element.41), channel_id=1, source_target_pairs={{8,24},{9,25},{12,28},{13,29},{18,2},{19,3},{22,6},{23,7}} | collective-permute-start | bytes 1572872 | tf_op jit(solution)/shard_map/ppermute | solution.py:258
  31.6 0.7 %collective-permute-start.12 = (f32[2,256,256]{2,1,0:T(8,128)S(1)}, f32[2,256,256]{2,1,0:T(8,128)S(1)}, u32[]{:S(2)}, u32[]{:S(2)}) collective-permute-start(f32[2,256,256]{2,1,0:T(8,128)S(1)} %get-tuple-element.42), channel_id=1, source_target_pairs={{8,0},{9,1},{12,4},{13,5},{18,26},{19,27},{22,30},{23,31}} | collective-permute-start | bytes 1572872 | tf_op jit(solution)/shard_map/ppermute | solution.py:258
  32.3 1.3 %collective-permute-start.13 = (f32[2,256,256]{2,1,0:T(8,128)S(1)}, f32[2,256,256]{2,1,0:T(8,128)S(1)}, u32[]{:S(2)}, u32[]{:S(2)}) collective-permute-start(f32[2,256,256]{2,1,0:T(8,128)S(1)} %get-tuple-element.43), channel_id=1, source_target_pairs={{8,16},{9,17},{12,20},{13,21},{18,10},{19,11},{22,14},{23,15}} | collective-permute-start | bytes 1572872 | tf_op jit(solution)/shard_map/ppermute | solution.py:258
  33.6 0.1 own_parts.1
  33.7 0.7 %collective-permute-start.14 = (f32[2,128,256]{2,1,0:T(8,128)S(1)}, f32[2,128,256]{2,1,0:T(8,128)S(1)}, u32[]{:S(2)}, u32[]{:S(2)}) collective-permute-start(f32[2,128,256]{2,1,0:T(8,128)S(1)} %own_parts.1), channel_id=1, source_target_pairs={{9,12},{12,9},{19,22},{22,19}} | collective-permute-start | bytes 786440 | tf_op jit(solution)/shard_map/ppermute | solution.py:258
  34.4 0.0 collective-permute-done.11.refs_0_
  34.4 0.0 collective-permute-done.12.refs_1_
  34.4 12.1 %collective-permute-done.13.refs_2_ = f32[2,256,256]{2,1,0:T(8,128)S(1)} collective-permute-done((f32[2,256,256]{2,1,0:T(8,128)S(1)}, f32[2,256,256]{2,1,0:T(8,128)S(1)}, u32[]{:S(2)}, u32[]{:S(2)}) %collective-permute-start.13) | collective-permute-done | bytes 524320 | tf_op jit(solution)/shard_map/ppermute | solution.py:258
  46.5 0.3 parts.1
  46.8 0.3 collective-permute-start.16
  47.1 0.0 collective-permute-done.14.refs_7_
  47.1 1.3 %collective-permute-start.15 = (f32[2,128,256]{2,1,0:T(8,128)S(1)}, f32[2,128,256]{2,1,0:T(8,128)S(1)}, u32[]{:S(2)}, u32[]{:S(2)}) collective-permute-start(f32[2,128,256]{2,1,0:T(8,128)S(1)} %get-tuple-element.47), channel_id=1, source_target_pairs={{0,4},{2,6},{5,1},{7,3},{8,12},{10,14},{13,9},{15,11},{16,20},{18,... | collective-permute-start | bytes 786440 | tf_op jit(solution)/shard_map/ppermute | solution.py:258
  48.4 4.1 %collective-permute-start.17 = (f32[2,128,256]{2,1,0:T(8,128)S(1)}, f32[2,128,256]{2,1,0:T(8,128)S(1)}, u32[]{:S(2)}, u32[]{:S(2)}) collective-permute-start(f32[2,128,256]{2,1,0:T(8,128)S(1)} %get-tuple-element.49), channel_id=1, source_target_pairs={{1,4},{3,6},{4,1},{6,3},{11,14},{14,11},{17,20},{20,17},{25,28},{2... | collective-permute-start | bytes 786440 | tf_op jit(solution)/shard_map/ppermute | solution.py:258
  52.5 0.2 keep.1.refs_2_
  52.7 3.3 %collective-permute-done.15.refs_4_ = f32[2,128,256]{2,1,0:T(8,128)S(1)} collective-permute-done((f32[2,128,256]{2,1,0:T(8,128)S(1)}, f32[2,128,256]{2,1,0:T(8,128)S(1)}, u32[]{:S(2)}, u32[]{:S(2)}) %collective-permute-start.15) | collective-permute-done | bytes 262176 | tf_op jit(solution)/shard_map/ppermute | solution.py:258
  56.0 0.5 collective-permute-done.17.refs_6_
  56.5 3.3 %collective-permute-done.16.refs_5_ = f32[2,192,256]{2,1,0:T(8,128)S(1)} collective-permute-done((f32[2,192,256]{2,1,0:T(8,128)S(1)}, f32[2,192,256]{2,1,0:T(8,128)S(1)}, u32[]{:S(2)}, u32[]{:S(2)}) %collective-permute-start.16) | collective-permute-done | bytes 393248 | tf_op jit(solution)/shard_map/ppermute | solution.py:258
  59.8 0.2 edge_terms.1
  60.0 1.5 %collective-permute-start.18 = (f32[2,192,128]{2,1,0:T(8,128)S(1)}, f32[2,192,128]{2,1,0:T(8,128)S(1)}, u32[]{:S(2)}, u32[]{:S(2)}) collective-permute-start(f32[2,192,128]{2,1,0:T(8,128)S(1)} %edge_terms.1), channel_id=1, source_target_pairs={{0,2},{1,3},{2,0},{3,1},{4,6},{5,7},{6,4},{7,5},{8,10},{9,11},{10,... | collective-permute-start | bytes 589832 | tf_op jit(solution)/shard_map/ppermute | solution.py:258
  61.5 1.0 %inner_terms.1 = (f32[192,384]{1,0:T(8,128)}, f32[192,384]{1,0:T(8,128)}, f32[1,2,192,128]{3,2,1,0:T(8,128)S(1)}) custom-call(s32[2,8,128]{2,1,0:T(8,128)S(1)} %broadcast_in_dim.21.spot_ref.refs_0_, s32[4,8,128]{2,1,0:T(8,128)S(1)} %collective-permute-done.4.partner_ref.refs_1_, f32[2,192,256]{2,1,0:T(8,128)S(1)} %keep.1.refs_2_, ...), custom_call_target="tpu_custom_call" | custom-call | flops 4194304 | bytes 2097152 | tf_op jit(solution)/shard_map/inner_terms/pallas_call | solution.py:690
  62.5 0.1 collective-permute-done.18.refs_0_
  62.5 0.7 %finish.1 = (f32[192,384]{1,0:T(8,128)}, f32[192,384]{1,0:T(8,128)}) custom-call(f32[192,384]{1,0:T(8,128)} %get-tuple-element.51.phase_in, f32[192,384]{1,0:T(8,128)} %get-tuple-element.52.absorb_in, f32[1,2,192,128]{3,2,1,0:T(8,128)S(1)} %get-tuple-element.53.inner_ref, ...), custom_call_target="tpu_custom_call", output_to_operand_aliasing={{0}: (0, {}), {1}: (1, {})} | custom-call | tf_op jit(solution)/shard_map/finish/pallas_call | solution.py:718
  (2 shorter events, 0.0 us)
Async XLA Ops:
  0.6 3.7 %collective-permute-start = (s32[1,2]{1,0:T(1,128)}, s32[1,2]{1,0:T(1,128)S(1)}, u32[]{:S(2)}, u32[]{:S(2)}) collective-permute-start(s32[1,2]{1,0:T(1,128)} %bitcast.9), channel_id=1, source_target_pairs={{0,4},{1,5},{2,6},{3,7},{4,0},{5,1},{6,2},{7,3},{8,12},{9,13},{10,... | collective-permute-start | bytes 32 | tf_op jit(solution)/shard_map/ppermute | solution.py:258
  3.3 4.4 %copy-start.4 = (s32[1,1,1,2]{3,2,1,0:T(1,128)S(1)}, s32[1,1,1,2]{3,2,1,0:T(1,128)}, u32[]{:S(2)}) copy-start(s32[1,1,1,2]{3,2,1,0:T(1,128)} %param.10) | copy-start | bytes 28
  3.3 2.1 %collective-permute-start.1 = (f32[384,128]{1,0:T(8,128)S(1)}, f32[384,128]{1,0:T(8,128)S(1)}, u32[]{:S(2)}, u32[]{:S(2)}) collective-permute-start(f32[384,128]{1,0:T(8,128)S(1)} %get-tuple-element.31), channel_id=1, source_target_pairs={{0,2},{1,3},{2,0},{3,1},{4,6},{5,7},{6,4},{7,5},{8,10},{9,11},{10,... | collective-permute-start | bytes 589832 | tf_op jit(solution)/shard_map/ppermute | solution.py:258
  4.4 1.8 %collective-permute-start.2 = (f32[384,128]{1,0:T(8,128)S(1)}, f32[384,128]{1,0:T(8,128)S(1)}, u32[]{:S(2)}, u32[]{:S(2)}) collective-permute-start(f32[384,128]{1,0:T(8,128)S(1)} %get-tuple-element.32), channel_id=1, source_target_pairs={{0,2},{1,3},{2,0},{3,1},{4,6},{5,7},{6,4},{7,5},{8,10},{9,11},{10,... | collective-permute-start | bytes 589832 | tf_op jit(solution)/shard_map/ppermute | solution.py:258
  6.2 13.2 %copy-start.1 = (f32[2,256,256]{2,1,0:T(8,128)S(1)}, f32[2,256,256]{2,1,0:T(8,128)}, u32[]{:S(2)}) copy-start(f32[2,256,256]{2,1,0:T(8,128)} %probe) | copy-start | bytes 1572868
  6.2 13.2 %copy-start.2 = (s32[1,1,1,256,256]{4,3,2,1,0:T(8,128)S(1)}, s32[1,1,1,256,256]{4,3,2,1,0:T(8,128)}, u32[]{:S(2)}) copy-start(s32[1,1,1,256,256]{4,3,2,1,0:T(8,128)} %param.11) | copy-start | bytes 786436
  6.2 13.2 %copy-start.3 = (bf16[2,256,256]{2,1,0:T(8,128)(2,1)S(1)}, bf16[2,256,256]{2,1,0:T(8,128)(2,1)}, u32[]{:S(2)}) copy-start(bf16[2,256,256]{2,1,0:T(8,128)(2,1)} %constant.4.clone.sort) | copy-start | bytes 786436
  6.4 7.6 %collective-permute-start.3 = (f32[2,128,256]{2,1,0:T(8,128)S(1)}, f32[2,128,256]{2,1,0:T(8,128)S(1)}, u32[]{:S(2)}, u32[]{:S(2)}) collective-permute-start(f32[2,128,256]{2,1,0:T(8,128)S(1)} %halo_rows.1), channel_id=1, source_target_pairs={{0,4},{1,5},{2,6},{3,7},{4,0},{5,1},{6,2},{7,3},{8,12},{9,13},{10,... | collective-permute-start | bytes 786440 | tf_op jit(solution)/shard_map/ppermute | solution.py:258
  7.8 17.0 %copy-start = (bf16[12,2,256,256]{3,2,1,0:T(8,128)(2,1)S(1)}, bf16[12,2,256,256]{3,2,1,0:T(8,128)(2,1)}, u32[]{:S(2)}) copy-start(bf16[12,2,256,256]{3,2,1,0:T(8,128)(2,1)} %constant.5.clone.tables) | copy-start | bytes 9437188
  8.4 10.2 %collective-permute-start.7 = (f32[2,128,256]{2,1,0:T(8,128)S(1)}, f32[2,128,256]{2,1,0:T(8,128)S(1)}, u32[]{:S(2)}, u32[]{:S(2)}) collective-permute-start(f32[2,128,256]{2,1,0:T(8,128)S(1)} %get-tuple-element.39.refs_2_), channel_id=1, source_target_pairs={{0,8},{1,9},{4,12},{5,13},{26,18},{27,19},{30,22},{31,23}} | collective-permute-start | bytes 786440 | tf_op jit(solution)/shard_map/ppermute | solution.py:258
  9.2 11.0 %collective-permute-start.6 = (f32[2,128,256]{2,1,0:T(8,128)S(1)}, f32[2,128,256]{2,1,0:T(8,128)S(1)}, u32[]{:S(2)}, u32[]{:S(2)}) collective-permute-start(f32[2,128,256]{2,1,0:T(8,128)S(1)} %get-tuple-element.39.refs_2_), channel_id=1, source_target_pairs={{10,18},{11,19},{14,22},{15,23},{16,8},{17,9},{20,12},{21,13}} | collective-permute-start | bytes 786440 | tf_op jit(solution)/shard_map/ppermute | solution.py:258
  13.0 7.5 %collective-permute-start.5 = (f32[2,128,256]{2,1,0:T(8,128)S(1)}, f32[2,128,256]{2,1,0:T(8,128)S(1)}, u32[]{:S(2)}, u32[]{:S(2)}) collective-permute-start(f32[2,128,256]{2,1,0:T(8,128)S(1)} %get-tuple-element.39.refs_2_), channel_id=1, source_target_pairs={{2,18},{3,19},{6,22},{7,23},{24,8},{25,9},{28,12},{29,13}} | collective-permute-start | bytes 786440 | tf_op jit(solution)/shard_map/ppermute | solution.py:258
  14.1 9.1 %collective-permute-start.10 = (f32[2,128,256]{2,1,0:T(8,128)S(1)}, f32[2,128,256]{2,1,0:T(8,128)S(1)}, u32[]{:S(2)}, u32[]{:S(2)}) collective-permute-start(f32[2,128,256]{2,1,0:T(8,128)S(1)} %join.1.refs_5_), channel_id=1, source_target_pairs={{2,18},{3,19},{6,22},{7,23},{24,8},{25,9},{28,12},{29,13}} | collective-permute-start | bytes 786440 | tf_op jit(solution)/shard_map/ppermute | solution.py:258
  14.8 10.0 %collective-permute-start.9 = (f32[2,128,256]{2,1,0:T(8,128)S(1)}, f32[2,128,256]{2,1,0:T(8,128)S(1)}, u32[]{:S(2)}, u32[]{:S(2)}) collective-permute-start(f32[2,128,256]{2,1,0:T(8,128)S(1)} %join.1.refs_5_), channel_id=1, source_target_pairs={{10,18},{11,19},{14,22},{15,23},{16,8},{17,9},{20,12},{21,13}} | collective-permute-start | bytes 786440 | tf_op jit(solution)/shard_map/ppermute | solution.py:258
  18.6 6.1 %collective-permute-start.8 = (f32[2,128,256]{2,1,0:T(8,128)S(1)}, f32[2,128,256]{2,1,0:T(8,128)S(1)}, u32[]{:S(2)}, u32[]{:S(2)}) collective-permute-start(f32[2,128,256]{2,1,0:T(8,128)S(1)} %join.1.refs_5_), channel_id=1, source_target_pairs={{0,8},{1,9},{4,12},{5,13},{26,18},{27,19},{30,22},{31,23}} | collective-permute-start | bytes 786440 | tf_op jit(solution)/shard_map/ppermute | solution.py:258
  20.3 2.9 %collective-permute-start.4 = (s32[4,8,128]{2,1,0:T(8,128)S(1)}, s32[4,8,128]{2,1,0:T(8,128)S(1)}, u32[]{:S(2)}, u32[]{:S(2)}) collective-permute-start(s32[4,8,128]{2,1,0:T(8,128)S(1)} %pad_add_fusion), channel_id=1, source_target_pairs={{0,1},{1,0},{2,3},{3,2},{4,5},{5,4},{6,7},{7,6},{8,9},{9,8},{10,11... | collective-permute-start | bytes 49160 | tf_op jit(solution)/shard_map/ppermute | solution.py:258
  30.9 3.5 %collective-permute-start.11 = (f32[2,256,256]{2,1,0:T(8,128)S(1)}, f32[2,256,256]{2,1,0:T(8,128)S(1)}, u32[]{:S(2)}, u32[]{:S(2)}) collective-permute-start(f32[2,256,256]{2,1,0:T(8,128)S(1)} %get-tuple-element.41), channel_id=1, source_target_pairs={{8,24},{9,25},{12,28},{13,29},{18,2},{19,3},{22,6},{23,7}} | collective-permute-start | bytes 1572872 | tf_op jit(solution)/shard_map/ppermute | solution.py:258
  31.6 2.8 %collective-permute-start.12 = (f32[2,256,256]{2,1,0:T(8,128)S(1)}, f32[2,256,256]{2,1,0:T(8,128)S(1)}, u32[]{:S(2)}, u32[]{:S(2)}) collective-permute-start(f32[2,256,256]{2,1,0:T(8,128)S(1)} %get-tuple-element.42), channel_id=1, source_target_pairs={{8,0},{9,1},{12,4},{13,5},{18,26},{19,27},{22,30},{23,31}} | collective-permute-start | bytes 1572872 | tf_op jit(solution)/shard_map/ppermute | solution.py:258
  32.3 14.2 %collective-permute-start.13 = (f32[2,256,256]{2,1,0:T(8,128)S(1)}, f32[2,256,256]{2,1,0:T(8,128)S(1)}, u32[]{:S(2)}, u32[]{:S(2)}) collective-permute-start(f32[2,256,256]{2,1,0:T(8,128)S(1)} %get-tuple-element.43), channel_id=1, source_target_pairs={{8,16},{9,17},{12,20},{13,21},{18,10},{19,11},{22,14},{23,15}} | collective-permute-start | bytes 1572872 | tf_op jit(solution)/shard_map/ppermute | solution.py:258
  33.7 13.4 %collective-permute-start.14 = (f32[2,128,256]{2,1,0:T(8,128)S(1)}, f32[2,128,256]{2,1,0:T(8,128)S(1)}, u32[]{:S(2)}, u32[]{:S(2)}) collective-permute-start(f32[2,128,256]{2,1,0:T(8,128)S(1)} %own_parts.1), channel_id=1, source_target_pairs={{9,12},{12,9},{19,22},{22,19}} | collective-permute-start | bytes 786440 | tf_op jit(solution)/shard_map/ppermute | solution.py:258
  46.8 13.0 %collective-permute-start.16 = (f32[2,192,256]{2,1,0:T(8,128)S(1)}, f32[2,192,256]{2,1,0:T(8,128)S(1)}, u32[]{:S(2)}, u32[]{:S(2)}) collective-permute-start(f32[2,192,256]{2,1,0:T(8,128)S(1)} %get-tuple-element.48), channel_id=1, source_target_pairs={{0,1},{1,0},{2,3},{3,2},{4,5},{5,4},{6,7},{7,6},{8,9},{9,8},{10,11... | collective-permute-start | bytes 1179656 | tf_op jit(solution)/shard_map/ppermute | solution.py:258
  47.1 8.9 %collective-permute-start.15 = (f32[2,128,256]{2,1,0:T(8,128)S(1)}, f32[2,128,256]{2,1,0:T(8,128)S(1)}, u32[]{:S(2)}, u32[]{:S(2)}) collective-permute-start(f32[2,128,256]{2,1,0:T(8,128)S(1)} %get-tuple-element.47), channel_id=1, source_target_pairs={{0,4},{2,6},{5,1},{7,3},{8,12},{10,14},{13,9},{15,11},{16,20},{18,... | collective-permute-start | bytes 786440 | tf_op jit(solution)/shard_map/ppermute | solution.py:258
  48.4 8.1 %collective-permute-start.17 = (f32[2,128,256]{2,1,0:T(8,128)S(1)}, f32[2,128,256]{2,1,0:T(8,128)S(1)}, u32[]{:S(2)}, u32[]{:S(2)}) collective-permute-start(f32[2,128,256]{2,1,0:T(8,128)S(1)} %get-tuple-element.49), channel_id=1, source_target_pairs={{1,4},{3,6},{4,1},{6,3},{11,14},{14,11},{17,20},{20,17},{25,28},{2... | collective-permute-start | bytes 786440 | tf_op jit(solution)/shard_map/ppermute | solution.py:258
  60.0 2.5 %collective-permute-start.18 = (f32[2,192,128]{2,1,0:T(8,128)S(1)}, f32[2,192,128]{2,1,0:T(8,128)S(1)}, u32[]{:S(2)}, u32[]{:S(2)}) collective-permute-start(f32[2,192,128]{2,1,0:T(8,128)S(1)} %edge_terms.1), channel_id=1, source_target_pairs={{0,2},{1,3},{2,0},{3,1},{4,6},{5,7},{6,4},{7,5},{8,10},{9,11},{10,... | collective-permute-start | bytes 589832 | tf_op jit(solution)/shard_map/ppermute | solution.py:258
